TPU v7x, 32 devices: a whole 2x2x4 slice. The times are simulated.
32 devices in a mesh: basis: 4 (over y, core), dp: 8 (over z, x).
Axes of the slice: x: 2, y: 2, z: 4, core: 2. Of those that a mesh axis runs over, the one named last changes fastest.
Arguments:
- gradient: bfloat16 [2048, 8192], P('basis', 'dp'), may hold values from -6 to 6
- left_basis: float32 [2048, 2048], P('basis', 'dp'), may hold values from -0.125 to 0.125
- right_basis: float32 [8192, 8192], P('basis', 'dp'), may hold values from -0.0625 to 0.0625
- first_moment: float32 [2048, 8192], P('basis', 'dp'), may hold values from -1.5 to 1.5
- second_moment: float32 [2048, 8192], P('basis', 'dp'), may hold values from 0.04 to 1
Outputs:
- first_new: float32 [2048, 8192], P('basis', 'dp')
- second_new: float32 [2048, 8192], P('basis', 'dp')
- update: bfloat16 [2048, 8192], P('dp', 'basis')
All inputs are finite; a program needn't handle non-finite values.
Results may differ from a plain program's by a relative error of at most 0.018.
Values may be sent and summed in bfloat16 or wider, within the bound.
No kernel may reach another device: no remote copies, remote signals or barrier semaphores. Data moves between devices by JAX's collectives and lax.ppermute only.
A program may use at most 128 MiB of HBM per device.

v0:
```python
import jax
import jax.numpy as jnp
from jax import lax
from jax.sharding import PartitionSpec as P

STEP = 4


beta_first = 0.95
beta_second = 0.95
epsilon = 1e-08

ROW_PARTS = 2
COL_PARTS = 2
OUT_PARTS = 2

low = jnp.bfloat16


def matmul(a, b):
    return lax.dot_general(a, b, (((1,), (0,)), ((), ())), preferred_element_type=jnp.float32)


def matmul_nt(a, b):
    return lax.dot_general(a, b, (((1,), (1,)), ((), ())), preferred_element_type=jnp.float32)


def per_device(gradient, left_basis, right_basis, first_moment, second_moment, *, nb, nd):
    nz = nb
    nx = nd // nz
    b = lax.axis_index("basis")
    d = lax.axis_index("dp")
    z, x = d // nx, d % nx
    bits = [1 << k for k in range(nb.bit_length() - 1)]
    x_bits = [1 << k for k in range(nx.bit_length() - 1)]

    def permute(value, target):
        pairs = []
        for bb in range(nb):
            for zz in range(nz):
                for xx in range(nx):
                    tb, tz, tx = target(bb, zz, xx)
                    pairs.append((bb * nd + zz * nx + xx, tb * nd + tz * nx + tx))
        return lax.ppermute(value, ("basis", "dp"), pairs)

    def move_b(value, t):
        return permute(value, lambda bb, zz, xx: (bb ^ t, zz, xx))

    def move_z(value, t):
        return permute(value, lambda bb, zz, xx: (bb, zz ^ t, xx))

    def move_x(value, u):
        return permute(value, lambda bb, zz, xx: (bb, zz, xx ^ u))

    def spread(beta):
        return (beta >> 1) ^ ((beta & 1) * (nz - 1))

    unspread = [0] * nz
    for beta in range(nb):
        unspread[spread(beta)] = beta

    def joined(mine, other, bit_set, axis):
        first = jnp.where(bit_set, other, mine)
        second = jnp.where(bit_set, mine, other)
        return jnp.stack([first, second], axis=axis)

    ff_block = right_basis.shape[1]
    rows = first_moment.shape[0]
    out_rows = left_basis.shape[1]
    whole = rows * nb

    path = [zz * nx for zz in range(nz)]
    for xx in range(1, nx):
        path += [zz * nx + xx for zz in (range(nz) if xx % 2 == 0 else reversed(range(nz)))]
    place = {dd: i for i, dd in enumerate(path)}

    part = rows // ROW_PARTS
    gathered = []
    for h in range(ROW_PARTS):
        piece = gradient[h * part : (h + 1) * part]
        piece = permute(piece, lambda bb, zz, xx: (bb, zz ^ spread(bb), xx))
        piece = permute(piece, lambda bb, zz, xx: (zz ^ spread(bb), zz, xx))
        gathered.append(lax.all_gather(piece, "dp", axis_index_groups=[path]))

    blocks = lax.all_gather(left_basis.astype(low).T, "dp", axis_index_groups=[path])
    left_t = jnp.concatenate([blocks[place[dd]] for dd in range(nd)], axis=0)
    for i, t in enumerate(reversed(bits)):
        left_t = joined(left_t, move_b(left_t, t), (b & t) != 0, 1 + i)
    left_t = left_t.reshape(whole, whole)
    left = left_t.T

    right = right_basis.astype(low)
    half = jnp.zeros((whole, ff_block), low)
    sources = jnp.array(unspread, jnp.int32)
    for h in range(ROW_PARTS):
        for zz in range(nz):
            total = 0.0
            for xx in range(nx):
                total = total + matmul(
                    gathered[h][place[zz * nx + xx]], right[xx * ff_block : (xx + 1) * ff_block]
                )
            start = sources[b ^ zz] * rows + h * part
            half = lax.dynamic_update_slice_in_dim(half, total.astype(low), start, 0)

    def left_t_rows(t):
        return lax.dynamic_slice_in_dim(left_t, (b ^ t) * rows, rows, 0)

    width = ff_block // COL_PARTS
    first_out, second_out, columns = [], [], []
    for j in range(COL_PARTS):
        cols = slice(j * width, (j + 1) * width)
        part_half = half[:, cols]
        gone = jnp.concatenate([matmul(left_t_rows(t), part_half).astype(low) for t in range(1, nb, 2)], axis=0)
        got = move_b(gone, 1)
        held = {}
        for i, t in enumerate(range(0, nb, 2)):
            held[t] = matmul(left_t_rows(t), part_half) + got[i * rows : (i + 1) * rows].astype(jnp.float32)
        for t in reversed(bits[1:]):
            away = [s for s in held if s & t]
            got = move_b(jnp.concatenate([held[s].astype(low) for s in away], axis=0), t)
            for i, s in enumerate(away):
                held[s ^ t] = held[s ^ t] + got[i * rows : (i + 1) * rows].astype(jnp.float32)
                del held[s]
        rotated = held[0]
        first_new = beta_first * first_moment[:, cols] + (1.0 - beta_first) * rotated
        second_new = beta_second * second_moment[:, cols] + (1.0 - beta_second) * rotated * rotated
        first_fix = 1.0 - beta_first**STEP
        second_fix = 1.0 - beta_second**STEP
        direction = first_new / first_fix / (jnp.sqrt(second_new / second_fix) + epsilon)
        first_out.append(first_new)
        second_out.append(second_new)
        column = direction.astype(low)
        axis = 0
        for t in reversed(bits):
            column = joined(column, move_b(column, t), (b & t) != 0, axis)
            axis += 1
        columns.append(column.reshape(whole, width))
    columns = lax.optimization_barrier(jnp.concatenate(columns, axis=1))

    update = []
    part = out_rows // OUT_PARTS
    for i in range(OUT_PARTS):
        rows_of = jnp.concatenate([left[dd * out_rows + i * part : dd * out_rows + (i + 1) * part] for dd in path], axis=0)
        rows_of = lax.optimization_barrier(rows_of)
        back = matmul(rows_of, columns).astype(low)
        total = matmul_nt(back, right).astype(low)
        update.append(lax.psum_scatter(total, "dp", scatter_dimension=0, axis_index_groups=[path], tiled=True))
    return (
        jnp.concatenate(first_out, axis=1),
        jnp.concatenate(second_out, axis=1),
        jnp.concatenate(update, axis=0),
    )


def solution(mesh):
    nb, nd = mesh.shape["basis"], mesh.shape["dp"]

    def run(*args):
        return per_device(*args, nb=nb, nd=nd)

    return jax.shard_map(
        run,
        mesh=mesh,
        in_specs=(
            P("basis", "dp"),
            P("basis", "dp"),
            P("basis", "dp"),
            P("basis", "dp"),
            P("basis", "dp"),
        ),
        out_specs=(P("basis", "dp"), P("basis", "dp"), P("dp", "basis")),
        check_vma=False,
    )
```

profile of v0, /device:TPU:0, one launch (start us, length us, event | category | flops | bytes accessed | tf_op | source)
XLA Modules:
  0.0 391.0 jit_solution(13248553176704226077)
XLA Ops:
  7.2 1.8 convert_bitcast_fusion
  9.1 1.3 fusion.158
  14.9 50.4 %all-gather.7.cloned.1.call-done = bf16[2048,512]{0,1:T(8,128)(2,1)} async-done(((bf16[256,512]{0,1:T(8,128)(2,1)}), bf16[2048,512]{0,1:T(8,128)(2,1)}) %all-gather.7.cloned.1.call-update) | async-done | bytes 2097168 | tf_op jit(solution)/shard_map/all_gather | solution.py:85
  65.3 1.0 slice_dynamic-update-slice_fusion.22
  66.3 1.0 slice_dynamic-update-slice_fusion.21
  67.3 1.0 slice_dynamic-update-slice_fusion.20
  68.3 1.0 slice_dynamic-update-slice_fusion.19
  69.3 1.0 slice_dynamic-update-slice_fusion.18
  70.2 1.0 slice_dynamic-update-slice_fusion.17
  71.2 1.1 slice_dynamic-update-slice_fusion.16
  72.4 12.2 %collective-permute-start = (bf16[2048,512]{0,1:T(8,128)(2,1)S(1)}, bf16[2048,512]{0,1:T(8,128)(2,1)}, u32[]{:S(2)}, u32[]{:S(2)}) collective-permute-start(bf16[2048,512]{0,1:T(8,128)(2,1)S(1)} %slice_dynamic-update-slice_fusion.16), channel_id=1, source_target_pairs={{0,16},{1,17},{2,18},{3,19},{4,20},{5,21},{6,22},{7,23},{8,24},{9,... | collective-permute-start | bytes 6291464 | tf_op jit(solution)/shard_map/ppermute | solution.py:44
  87.7 6.1 %convert_element_type.85 = bf16[2048,1024]{1,0:T(8,128)(2,1)} convert(f32[2048,1024]{1,0:T(8,128)} %param.8) | non-fusion elementwise | flops 2097152 | bytes 12582912 | tf_op jit(solution)/shard_map/convert_element_type | solution.py:92
  93.9 35.5 %collective-permute-done = bf16[2048,512]{0,1:T(8,128)(2,1)} collective-permute-done((bf16[2048,512]{0,1:T(8,128)(2,1)S(1)}, bf16[2048,512]{0,1:T(8,128)(2,1)}, u32[]{:S(2)}, u32[]{:S(2)}) %collective-permute-start) | collective-permute-done | bytes 2097184 | tf_op jit(solution)/shard_map/ppermute | solution.py:44
  129.4 2.5 select_bitcast_fusion.3
  131.9 2.6 pad_maximum_fusion.1
  134.6 1.9 collective-permute-start.1
  136.5 3.6 fusion.129
  140.2 2.7 fusion.126
  142.9 2.7 fusion.123
  145.6 1.7 fusion.120
  147.4 18.6 %all-gather.11.cloned.1.call-done = bf16[2048,1024]{1,0:T(8,128)(2,1)} async-done(((bf16[256,1024]{1,0:T(8,128)(2,1)}), bf16[2048,1024]{1,0:T(8,128)(2,1)}) %all-gather.11.cloned.1.call-update) | async-done | bytes 4194320 | tf_op jit(solution)/shard_map/all_gather | solution.py:83
  165.9 2.6 fusion.117
  168.9 2.0 fusion.114
  180.2 6.7 %select_bitcast_fusion.1 = (bf16[2048,2,1,512]{0,3,2,1:T(8,128)(2,1)}, bf16[2048,2,1,512]{0,3,2,1:T(8,128)(2,1)}) fusion(bf16[2048,2,512]{0,2,1:T(8,128)(2,1)} %collective-permute-done.1, pred[]{:T(512)S(6)} %ne.4, bf16[2048,1,512]{0,2,1:T(8,128)(2,1)S(1)} %copy-done.2, bf16[2048,1,512]{0,2,1:T(8,128)(2,1)S(1)} %get-tuple-element.30), kind=kLoop, calls=%fused_computation.4 | loop fusion | flops 6291456 | bytes 16777216 | tf_op jit(solution)/shard_map/stack | solution.py:65
  186.9 7.7 %pad_maximum_fusion = bf16[2048,2,2,512]{0,3,2,1:T(8,128)(2,1)} fusion(bf16[2048,2,1,512]{0,3,2,1:T(8,128)(2,1)} %get-tuple-element.26, bf16[2048,2,1,512]{0,3,2,1:T(8,128)(2,1)} %get-tuple-element.25), kind=kLoop, calls=%fused_computation | loop fusion | flops 4194304 | bytes 16777216 | tf_op jit(solution)/shard_map/stack | solution.py:65
  194.6 3.0 fusion.71
  197.6 2.9 fusion.66
  200.5 1.3 fusion.61
  201.8 1.3 fusion.56
  204.1 1.8 collective-permute-done.8
  205.9 1.3 fusion.76
  207.2 1.5 collective-permute-start.9
  208.8 1.3 fusion.81
  210.9 11.2 %collective-permute-done.9 = bf16[512,512]{1,0:T(8,128)(2,1)S(1)} collective-permute-done((bf16[512,512]{1,0:T(8,128)(2,1)S(1)}, bf16[512,512]{1,0:T(8,128)(2,1)S(1)}, u32[]{:S(2)}, u32[]{:S(2)}) %collective-permute-start.9) | collective-permute-done | bytes 524320 | tf_op jit(solution)/shard_map/ppermute | solution.py:44
  222.1 1.3 fusion.41
  223.4 9.2 %collective-permute-done.7 = bf16[512,512]{1,0:T(8,128)(2,1)S(1)} collective-permute-done((bf16[512,512]{1,0:T(8,128)(2,1)S(1)}, bf16[512,512]{1,0:T(8,128)(2,1)S(1)}, u32[]{:S(2)}, u32[]{:S(2)}) %collective-permute-start.7) | collective-permute-done | bytes 524320 | tf_op jit(solution)/shard_map/ppermute | solution.py:44
  232.6 3.9 %divide_convert_fusion.1 = (bf16[512,512]{1,0:T(8,128)(2,1)S(1)}, f32[512,512]{1,0:T(8,128)S(1)}, f32[512,512]{1,0:T(8,128)S(1)}, bf16[512,512]{1,0:T(8,128)(2,1...) fusion(f32[512,1024]{1,0:T(8,128)S(1)} %copy-done.15, f32[512,1024]{1,0:T(8,128)S(1)} %copy-done.16, ...), kind=kOutput, calls=%fused_computation.93 | convolution fusion | flops 1080557568 | bytes 15728644 | tf_op jit(solution)/shard_map/dot_general | solution.py:21
  236.5 1.5 collective-permute-start.12
  238.8 12.6 %collective-permute-done.12 = bf16[512,512]{1,0:T(8,128)(2,1)S(1)} collective-permute-done((bf16[512,512]{1,0:T(8,128)(2,1)S(1)}, bf16[512,512]{1,0:T(8,128)(2,1)S(1)}, u32[]{:S(2)}, u32[]{:S(2)}) %collective-permute-start.12) | collective-permute-done | bytes 524320 | tf_op jit(solution)/shard_map/ppermute | solution.py:44
  251.6 9.3 %collective-permute-done.10 = bf16[512,512]{1,0:T(8,128)(2,1)S(1)} collective-permute-done((bf16[512,512]{1,0:T(8,128)(2,1)S(1)}, bf16[512,512]{1,0:T(8,128)(2,1)S(1)}, u32[]{:S(2)}, u32[]{:S(2)}) %collective-permute-start.10) | collective-permute-done | bytes 524320 | tf_op jit(solution)/shard_map/ppermute | solution.py:44
  261.5 2.3 collective-permute-done.11
  265.6 2.6 pad_maximum_fusion.2
  268.3 14.5 %convolution_convert_fusion = bf16[1024,2048]{1,0:T(8,128)(2,1)} fusion(bf16[2048,1024]{1,0:T(8,128)(2,1)} %convert_element_type.85, bf16[1024,2048]{1,0:T(8,128)(2,1)} %copy-done.11, bf16[2048,1024]{1,0:T(8,128)(2,1)} %pad_maximum_fusion.2), kind=kOutput, calls=%fused_computation.5 | convolution fusion | flops 8593080320 | bytes 16777216 | tf_op jit(solution)/shard_map/dot_general | solution.py:25
  282.8 14.4 %convolution_convert_fusion.1 = bf16[1024,2048]{1,0:T(8,128)(2,1)} fusion(bf16[2048,1024]{1,0:T(8,128)(2,1)} %convert_element_type.85, bf16[1024,2048]{1,0:T(8,128)(2,1)} %copy-done.10, bf16[2048,1024]{1,0:T(8,128)(2,1)} %pad_maximum_fusion.2), kind=kOutput, calls=%fused_computation.6 | convolution fusion | flops 8593080320 | bytes 16777216 | tf_op jit(solution)/shard_map/dot_general | solution.py:25
  297.2 4.0 %pad_maximum_fusion.3 = (f32[512,1024]{1,0:T(8,128)}, f32[512,1024]{1,0:T(8,128)}) fusion(f32[512,512]{1,0:T(8,128)} %get-tuple-element.29, f32[512,512]{1,0:T(8,128)S(1)} %get-tuple-element.5, f32[512,512]{1,0:T(8,128)} %get-tuple-element.28, f32[512,512]{1,0:T(8,128)S(1)} %get-tuple-element.4), kind=kLoop, calls=%fused_computation.7 | loop fusion | flops 1048576 | bytes 8388608 | tf_op jit(solution)/shard_map/concatenate | solution.py:149
  301.3 30.3 %reduce-scatter.5.cloned.1.call-done = bf16[128,2048]{1,0:T(8,128)(2,1)} async-done(((bf16[1024,2048]{1,0:T(8,128)(2,1)}), bf16[128,2048]{1,0:T(8,128)(2,1)}) %reduce-scatter.5.cloned.1.call-update) | async-done | bytes 524304 | tf_op jit(solution)/shard_map/reduce_scatter | solution.py:147
  331.5 50.6 %reduce-scatter.3.cloned.1.call-done = bf16[128,2048]{1,0:T(8,128)(2,1)} async-done(((bf16[1024,2048]{1,0:T(8,128)(2,1)}), bf16[128,2048]{1,0:T(8,128)(2,1)}) %reduce-scatter.3.cloned.1.call-update) | async-done | bytes 524304 | tf_op jit(solution)/shard_map/reduce_scatter | solution.py:147
  382.2 2.3 pad_maximum_fusion.11
  (99 shorter events, 20.1 us)
Async XLA Ops:
  7.2 77.4 %copy-start.12 = (s32[4]{0:T(128)S(1)}, s32[4]{0:T(128)}, u32[]{:S(2)}) copy-start(s32[4]{0:T(128)} %constant.47.clone) | copy-start | bytes 52
  7.2 58.1 %all-gather.7.cloned.1.call-start = ((), (), s32[]{:S(2)}) async-start(), calls=%async_computation.4 | async-start | bytes 2359296 | tf_op jit(solution)/shard_map/all_gather | solution.py:85
  9.0 127.5 %all-gather.9.cloned.1.call-start = ((), (), s32[]{:S(2)}) async-start(), calls=%async_computation.5 | async-start | bytes 4718592 | tf_op jit(solution)/shard_map/all_gather | solution.py:83
  10.3 0.7 collective-permute-start.2
  11.1 0.7 collective-permute-start.3
  11.8 0.8 copy-start.8
  12.6 153.3 %all-gather.11.cloned.1.call-start = ((), (), s32[]{:S(2)}) async-start(), calls=%async_computation.6 | async-start | bytes 4718592 | tf_op jit(solution)/shard_map/all_gather | solution.py:83
  12.6 0.7 collective-permute-start.4
  13.4 0.7 collective-permute-start.5
  14.1 0.8 copy-start.9
  14.9 316.6 %reduce-scatter.5.cloned.1.call-start = ((), (), s32[]{:S(2)}) async-start(), calls=%async_computation.3 | async-start | bytes 4718592 | tf_op jit(solution)/shard_map/reduce_scatter | solution.py:147
  72.3 21.5 %copy-start.7 = (bf16[2048,512]{0,1:T(8,128)(2,1)}, bf16[2048,512]{0,1:T(8,128)(2,1)S(1)}, u32[]{:S(2)}) copy-start(bf16[2048,512]{0,1:T(8,128)(2,1)S(1)} %slice_dynamic-update-slice_fusion.16) | copy-start | bytes 6291460
  72.4 57.0 %collective-permute-start = (bf16[2048,512]{0,1:T(8,128)(2,1)S(1)}, bf16[2048,512]{0,1:T(8,128)(2,1)}, u32[]{:S(2)}, u32[]{:S(2)}) collective-permute-start(bf16[2048,512]{0,1:T(8,128)(2,1)S(1)} %slice_dynamic-update-slice_fusion.16), channel_id=1, source_target_pairs={{0,16},{1,17},{2,18},{3,19},{4,20},{5,21},{6,22},{7,23},{8,24},{9,... | collective-permute-start | bytes 6291464 | tf_op jit(solution)/shard_map/ppermute | solution.py:44
  131.9 2.7 copy-start.1
  134.6 45.5 %collective-permute-start.1 = (bf16[2048,2,512]{0,2,1:T(8,128)(2,1)}, bf16[2048,2,512]{0,2,1:T(8,128)(2,1)}, u32[]{:S(2)}, u32[]{:S(2)}) collective-permute-start(bf16[2048,2,512]{0,2,1:T(8,128)(2,1)} %pad_maximum_fusion.1), channel_id=1, source_target_pairs={{0,8},{1,9},{2,10},{3,11},{4,12},{5,13},{6,14},{7,15},{8,0},{9,1},... | collective-permute-start | bytes 12582920 | tf_op jit(solution)/shard_map/ppermute | solution.py:44
  136.5 3.6 copy-start.3
  165.9 3.0 copy-start.4
  165.9 5.0 %copy-start.14 = (bf16[2048,1024]{1,0:T(8,128)(2,1)S(1)}, bf16[2048,1024]{1,0:T(8,128)(2,1)}, u32[]{:S(2)}) copy-start(bf16[2048,1024]{1,0:T(8,128)(2,1)} %all-gather.11.cloned.1.call-done) | copy-start | bytes 12582916
  171.6 2.2 copy-start.13
  171.7 2.5 copy-start.19
  172.4 2.5 copy-start.18
  174.1 1.5 copy-start.17
  178.6 1.6 copy-start.2
  180.1 6.8 %copy-start.5 = (bf16[2048,1024]{1,0:T(8,128)(2,1)}, bf16[2048,1024]{1,0:T(8,128)(2,1)S(1)}, u32[]{:S(2)}) copy-start(bf16[2048,1024]{1,0:T(8,128)(2,1)S(1)} %fusion.101) | copy-start | bytes 12582916
  186.9 7.7 %copy-start.6 = (bf16[2048,1024]{1,0:T(8,128)(2,1)S(1)}, bf16[2048,1024]{1,0:T(8,128)(2,1)}, u32[]{:S(2)}) copy-start(bf16[2048,1024]{1,0:T(8,128)(2,1)} %copy-done.5) | copy-start | bytes 12582916
  194.6 5.9 %copy-start = (bf16[2048,2,2,512]{0,3,2,1:T(8,128)(2,1)S(1)}, bf16[2048,2,2,512]{0,3,2,1:T(8,128)(2,1)}, u32[]{:S(2)}) copy-start(bf16[2048,2,2,512]{0,3,2,1:T(8,128)(2,1)} %pad_maximum_fusion) | copy-start | bytes 25165828
  203.2 2.7 collective-permute-start.8
  203.4 5.4 %collective-permute-start.6 = (bf16[1024,512]{1,0:T(8,128)(2,1)S(1)}, bf16[1024,512]{1,0:T(8,128)(2,1)S(1)}, u32[]{:S(2)}, u32[]{:S(2)}) collective-permute-start(bf16[1024,512]{1,0:T(8,128)(2,1)S(1)} %pad_maximum_fusion.7), channel_id=1, source_target_pairs={{0,8},{1,9},{2,10},{3,11},{4,12},{5,13},{6,14},{7,15},{8,0},{9,1},... | collective-permute-start | bytes 3145736 | tf_op jit(solution)/shard_map/ppermute | solution.py:44
  207.2 14.8 %collective-permute-start.9 = (bf16[512,512]{1,0:T(8,128)(2,1)S(1)}, bf16[512,512]{1,0:T(8,128)(2,1)S(1)}, u32[]{:S(2)}, u32[]{:S(2)}) collective-permute-start(bf16[512,512]{1,0:T(8,128)(2,1)S(1)} %fusion.76), channel_id=1, source_target_pairs={{0,16},{1,17},{2,18},{3,19},{4,20},{5,21},{6,22},{7,23},{8,24},{9,... | collective-permute-start | bytes 1572872 | tf_op jit(solution)/shard_map/ppermute | solution.py:44
  210.1 22.4 %collective-permute-start.7 = (bf16[512,512]{1,0:T(8,128)(2,1)S(1)}, bf16[512,512]{1,0:T(8,128)(2,1)S(1)}, u32[]{:S(2)}, u32[]{:S(2)}) collective-permute-start(bf16[512,512]{1,0:T(8,128)(2,1)S(1)} %fusion.81), channel_id=1, source_target_pairs={{0,16},{1,17},{2,18},{3,19},{4,20},{5,21},{6,22},{7,23},{8,24},{9,... | collective-permute-start | bytes 1572872 | tf_op jit(solution)/shard_map/ppermute | solution.py:44
  210.8 21.8 %copy-start.15 = (f32[512,1024]{1,0:T(8,128)S(1)}, f32[512,1024]{1,0:T(8,128)}, u32[]{:S(2)}) copy-start(f32[512,1024]{1,0:T(8,128)} %param.10) | copy-start | bytes 6291460
  210.8 21.8 %copy-start.16 = (f32[512,1024]{1,0:T(8,128)S(1)}, f32[512,1024]{1,0:T(8,128)}, u32[]{:S(2)}) copy-start(f32[512,1024]{1,0:T(8,128)} %param.9) | copy-start | bytes 6291460
  236.5 14.9 %collective-permute-start.12 = (bf16[512,512]{1,0:T(8,128)(2,1)S(1)}, bf16[512,512]{1,0:T(8,128)(2,1)S(1)}, u32[]{:S(2)}, u32[]{:S(2)}) collective-permute-start(bf16[512,512]{1,0:T(8,128)(2,1)S(1)} %get-tuple-element.27), channel_id=1, source_target_pairs={{0,16},{1,17},{2,18},{3,19},{4,20},{5,21},{6,22},{7,23},{8,24},{9,... | collective-permute-start | bytes 1572872 | tf_op jit(solution)/shard_map/ppermute | solution.py:44
  238.1 22.8 %collective-permute-start.10 = (bf16[512,512]{1,0:T(8,128)(2,1)S(1)}, bf16[512,512]{1,0:T(8,128)(2,1)S(1)}, u32[]{:S(2)}, u32[]{:S(2)}) collective-permute-start(bf16[512,512]{1,0:T(8,128)(2,1)S(1)} %get-tuple-element.3), channel_id=1, source_target_pairs={{0,16},{1,17},{2,18},{3,19},{4,20},{5,21},{6,22},{7,23},{8,24},{9,... | collective-permute-start | bytes 1572872 | tf_op jit(solution)/shard_map/ppermute | solution.py:44
  251.5 10.0 %collective-permute-start.13 = (bf16[2,512,512]{2,1,0:T(8,128)(2,1)S(1)}, bf16[2,512,512]{2,1,0:T(8,128)(2,1)S(1)}, u32[]{:S(2)}, u32[]{:S(2)}) collective-permute-start(bf16[2,512,512]{2,1,0:T(8,128)(2,1)S(1)} %pad_maximum_fusion.10), channel_id=1, source_target_pairs={{0,8},{1,9},{2,10},{3,11},{4,12},{5,13},{6,14},{7,15},{8,0},{9,1},... | collective-permute-start | bytes 3145736 | tf_op jit(solution)/shard_map/ppermute | solution.py:44
  261.0 2.7 collective-permute-start.11
  261.5 2.6 copy-start.10
  261.5 3.3 copy-start.11
  282.7 99.4 %reduce-scatter.3.cloned.1.call-start = ((), (), s32[]{:S(2)}) async-start(), calls=%async_computation.2 | async-start | bytes 4718592 | tf_op jit(solution)/shard_map/reduce_scatter | solution.py:147
Sparse Core Ops, SparseCore 0:
  10.0 55.2 all-gather.6
  67.4 48.9 all-gather.8
  118.0 47.8 all-gather.10
  282.9 48.6 reduce-scatter.4
  333.7 48.4 reduce-scatter.2
where the time goes:
time: 392 us; the launch traced here: 391 us
  waiting for transfers between devices  232 us (59%)
  matrix products  68 us (17%)
  other arithmetic  37.7 us (10%)
  starting transfers between devices  22.1 us (6%)
  between operations  16.9 us (4%)
  local copies, waits for them, and re-layouts  14.5 us (4%)
    ppermute x14, waiting for transfers between devices, permute(): return lax.ppermute(value, ('basis', 'dp'), pairs)  81.8 us
    reduce_scatter x2, waiting for transfers between devices, per_device(): lax.psum_scatter(total, 'dp', scatter_dimension=0, axis_index_groups=[pat...  80.9 us
    all_gather x1, waiting for transfers between devices, per_device(): lax.all_gather(left_basis.astype(low).T, 'dp', axis_index_groups=[path])  50.4 us
    dot_general x24, matrix products, matmul(): lax.dot_general(a, b, (((1,), (0,)), ((), ())), preferred_element_type=jn...  39.2 us
    dot_general x2, matrix products, matmul_nt(): lax.dot_general(a, b, (((1,), (1,)), ((), ())), preferred_element_type=jn...  28.9 us
    ppermute x14, starting transfers between devices, permute(): return lax.ppermute(value, ('basis', 'dp'), pairs)  21.9 us
    another operation x11, other arithmetic, joined(): return jnp.stack([first, second], axis=axis)  20.7 us
    all_gather x2, waiting for transfers between devices, per_device(): gathered.append(lax.all_gather(piece, 'dp', axis_index_groups=[path]))  18.6 us
  transfers between devices with their start and end apart: 19, of which 11 were waited for; matrix products, arithmetic and copies ran while one was open for 17% of the time, Pallas kernels for 0%

commit v1 on v0

--- a/solution.py
+++ b/solution.py
@@ -10,9 +10,7 @@
 beta_second = 0.95
 epsilon = 1e-08
 
-ROW_PARTS = 2
 COL_PARTS = 2
-OUT_PARTS = 2
 
 low = jnp.bfloat16
 
@@ -74,33 +72,45 @@
         path += [zz * nx + xx for zz in (range(nz) if xx % 2 == 0 else reversed(range(nz)))]
     place = {dd: i for i, dd in enumerate(path)}
 
-    part = rows // ROW_PARTS
-    gathered = []
-    for h in range(ROW_PARTS):
-        piece = gradient[h * part : (h + 1) * part]
-        piece = permute(piece, lambda bb, zz, xx: (bb, zz ^ spread(bb), xx))
-        piece = permute(piece, lambda bb, zz, xx: (zz ^ spread(bb), zz, xx))
-        gathered.append(lax.all_gather(piece, "dp", axis_index_groups=[path]))
+    def after(value, *others):
+        return lax.optimization_barrier((value,) + others)[0]
 
-    blocks = lax.all_gather(left_basis.astype(low).T, "dp", axis_index_groups=[path])
-    left_t = jnp.concatenate([blocks[place[dd]] for dd in range(nd)], axis=0)
-    for i, t in enumerate(reversed(bits)):
-        left_t = joined(left_t, move_b(left_t, t), (b & t) != 0, 1 + i)
-    left_t = left_t.reshape(whole, whole)
-    left = left_t.T
+    left_t = left_basis.astype(low).T
+    piece = permute(gradient, lambda bb, zz, xx: (bb, zz ^ spread(bb), xx))
+    for i, t in enumerate(reversed(bits[1:])):
+        left_t = joined(left_t, move_z(left_t, t), (z & t) != 0, i)
+    piece, left_t = lax.optimization_barrier((piece, left_t))
+    piece = permute(piece, lambda bb, zz, xx: (zz ^ spread(bb), zz, xx))
+    gathered = lax.all_gather(piece, "dp", axis_index_groups=[path])
+    for i, u in enumerate(reversed(x_bits)):
+        left_t = joined(left_t, move_x(left_t, u), (x & u) != 0, len(bits) - 1 + i)
+    left_t = joined(left_t, move_z(left_t, bits[0]), (z & bits[0]) != 0, len(bits) - 1).reshape(whole, rows)
+    for t in reversed(bits):
+        left_t = jnp.concatenate([left_t, move_b(left_t, t)], axis=1)
+    order = [0]
+    for t in reversed(bits):
+        order = order + [s | t for s in order]
+    left_t, gathered = lax.optimization_barrier((left_t, gathered))
 
     right = right_basis.astype(low)
     half = jnp.zeros((whole, ff_block), low)
     sources = jnp.array(unspread, jnp.int32)
-    for h in range(ROW_PARTS):
-        for zz in range(nz):
-            total = 0.0
-            for xx in range(nx):
-                total = total + matmul(
-                    gathered[h][place[zz * nx + xx]], right[xx * ff_block : (xx + 1) * ff_block]
-                )
-            start = sources[b ^ zz] * rows + h * part
-            half = lax.dynamic_update_slice_in_dim(half, total.astype(low), start, 0)
+    places = jnp.array([order.index(t) for t in range(nb)], jnp.int32)
+    for zz in range(nz):
+        total = 0.0
+        for xx in range(nx):
+            total = total + matmul(gathered[place[zz * nx + xx]], right[xx * ff_block : (xx + 1) * ff_block])
+        start = places[sources[b ^ zz] ^ b] * rows
+        half = lax.dynamic_update_slice_in_dim(half, total.astype(low), start, 0)
+
+    left = jnp.concatenate(
+        [
+            lax.dynamic_slice_in_dim(left_t, places[b ^ (dd // nx)] * rows + dd % nx * out_rows, out_rows, 1).T
+            for dd in path
+        ],
+        axis=0,
+    )
+    left = lax.optimization_barrier(left)
 
     def left_t_rows(t):
         return lax.dynamic_slice_in_dim(left_t, (b ^ t) * rows, rows, 0)
@@ -110,6 +120,8 @@
     for j in range(COL_PARTS):
         cols = slice(j * width, (j + 1) * width)
         part_half = half[:, cols]
+        if j:
+            part_half = after(part_half, gone)
         gone = jnp.concatenate([matmul(left_t_rows(t), part_half).astype(low) for t in range(1, nb, 2)], axis=0)
         got = move_b(gone, 1)
         held = {}
@@ -122,14 +134,17 @@
                 held[s ^ t] = held[s ^ t] + got[i * rows : (i + 1) * rows].astype(jnp.float32)
                 del held[s]
         rotated = held[0]
-        first_new = beta_first * first_moment[:, cols] + (1.0 - beta_first) * rotated
-        second_new = beta_second * second_moment[:, cols] + (1.0 - beta_second) * rotated * rotated
+        moments = first_moment[:, cols], second_moment[:, cols]
+        if j:
+            moments = after(moments, previous)
+        first_new = beta_first * moments[0] + (1.0 - beta_first) * rotated
+        second_new = beta_second * moments[1] + (1.0 - beta_second) * rotated * rotated
         first_fix = 1.0 - beta_first**STEP
         second_fix = 1.0 - beta_second**STEP
         direction = first_new / first_fix / (jnp.sqrt(second_new / second_fix) + epsilon)
         first_out.append(first_new)
         second_out.append(second_new)
-        column = direction.astype(low)
+        column = previous = direction.astype(low)
         axis = 0
         for t in reversed(bits):
             column = joined(column, move_b(column, t), (b & t) != 0, axis)
@@ -137,18 +152,13 @@
         columns.append(column.reshape(whole, width))
     columns = lax.optimization_barrier(jnp.concatenate(columns, axis=1))
 
-    update = []
-    part = out_rows // OUT_PARTS
-    for i in range(OUT_PARTS):
-        rows_of = jnp.concatenate([left[dd * out_rows + i * part : dd * out_rows + (i + 1) * part] for dd in path], axis=0)
-        rows_of = lax.optimization_barrier(rows_of)
-        back = matmul(rows_of, columns).astype(low)
-        total = matmul_nt(back, right).astype(low)
-        update.append(lax.psum_scatter(total, "dp", scatter_dimension=0, axis_index_groups=[path], tiled=True))
+    back = lax.optimization_barrier(matmul(left, columns).astype(low))
+    total = matmul_nt(back, right).astype(low)
+    update = lax.psum_scatter(total, "dp", scatter_dimension=0, axis_index_groups=[path], tiled=True)
     return (
         jnp.concatenate(first_out, axis=1),
         jnp.concatenate(second_out, axis=1),
-        jnp.concatenate(update, axis=0),
+        update,
     )
 
 

time: 392 us -> 405 us (1.033)
  starting transfers between devices: 22.1 us -> 58.4 us
  other arithmetic: 37.7 us -> 22.5 us
  matrix products: 68 us -> 54.3 us
  between operations: 16.9 us -> 22 us
    ppermute x14 -> x15, waiting for transfers between devices: 81.8 us -> 154 us  [permute(): return lax.ppermute(value, ('basis', 'dp'), pairs)]
    all_gather x3 -> x1, waiting for transfers between devices: 68.9 us -> 0.01 us  [per_device(): gathered = lax.all_gather(piece, 'dp', axis_index_groups=[path])]
    ppermute x14 -> x15, starting transfers between devices: 21.9 us -> 58.3 us  [permute(): return lax.ppermute(value, ('basis', 'dp'), pairs)]
    another operation x11 -> x14, other arithmetic: 20.7 us -> 1.62 us  [joined(): return jnp.stack([first, second], axis=axis)]
    dot_general x2 -> x1, matrix products: 28.9 us -> 11 us  [matmul_nt(): lax.dot_general(a, b, (((1,), (1,)), ((), ())), preferred_element_type=jn...]
    concatenate x1 -> x2, other arithmetic: 2.28 us -> 9.34 us  [per_device(): left_t = jnp.concatenate([left_t, move_b(left_t, t)], axis=1)]
    dot_general x24 -> x17, matrix products: 39.2 us -> 43.4 us  [matmul(): lax.dot_general(a, b, (((1,), (0,)), ((), ())), preferred_element_type=jn...]
    unnamed x53 -> x44, local copies, waits for them, and re-layouts: 10.6 us -> 8.16 us
  transfers between devices with their start and end apart: 19 -> 17, of which waited for: 11 -> 10; matrix products, arithmetic and copies ran while one was open for 17% -> 10% of each run, Pallas kernels for 0% -> 0%
where the time goes in v1:
time: 405 us; the launch traced here: 404 us
  waiting for transfers between devices  236 us (58%)
  starting transfers between devices  58.4 us (14%)
  matrix products  54.3 us (13%)
  other arithmetic  22.5 us (6%)
  between operations  22 us (5%)
  local copies, waits for them, and re-layouts  10.7 us (3%)
    ppermute x15, waiting for transfers between devices, permute(): return lax.ppermute(value, ('basis', 'dp'), pairs)  154 us
    reduce_scatter x1, waiting for transfers between devices, per_device(): lax.psum_scatter(total, 'dp', scatter_dimension=0, axis_index_groups=[pat...  82.5 us
    ppermute x15, starting transfers between devices, permute(): return lax.ppermute(value, ('basis', 'dp'), pairs)  58.3 us
    dot_general x17, matrix products, matmul(): lax.dot_general(a, b, (((1,), (0,)), ((), ())), preferred_element_type=jn...  43.4 us
    dot_general x1, matrix products, matmul_nt(): lax.dot_general(a, b, (((1,), (1,)), ((), ())), preferred_element_type=jn...  11 us
    concatenate x2, other arithmetic, per_device(): left_t = jnp.concatenate([left_t, move_b(left_t, t)], axis=1)  9.34 us
    unnamed x44, local copies, waits for them, and re-layouts  8.16 us
  transfers between devices with their start and end apart: 17, of which 10 were waited for; matrix products, arithmetic and copies ran while one was open for 10% of the time, Pallas kernels for 0%

profile of v1, /device:TPU:0, one launch (start us, length us, event | category | flops | bytes accessed | tf_op | source)
XLA Modules:
  0.0 404.0 jit_solution(14600663176980392974)
XLA Ops:
  7.2 9.5 %collective-permute-start = (bf16[512,1024]{1,0:T(8,128)(2,1)}, bf16[512,1024]{1,0:T(8,128)(2,1)}, u32[]{:S(2)}, u32[]{:S(2)}) collective-permute-start(bf16[512,1024]{1,0:T(8,128)(2,1)} %param.7), channel_id=1, source_target_pairs={{0,0},{1,1},{2,2},{3,3},{4,4},{5,5},{6,6},{7,7},{8,14},{9,15},{10,... | collective-permute-start | bytes 3145736 | tf_op jit(solution)/shard_map/ppermute | solution.py:42
  16.7 1.2 copy.10
  17.9 4.1 %collective-permute-start.1 = (bf16[256,512]{1,0:T(8,128)(2,1)S(1)}, bf16[256,512]{1,0:T(8,128)(2,1)S(1)}, u32[]{:S(2)}, u32[]{:S(2)}) collective-permute-start(bf16[256,512]{1,0:T(8,128)(2,1)S(1)} %bitcast.109), channel_id=1, source_target_pairs={{0,4},{1,5},{2,6},{3,7},{4,0},{5,1},{6,2},{7,3},{8,12},{9,13},{10,... | collective-permute-start | bytes 786440 | tf_op jit(solution)/shard_map/ppermute | solution.py:42
  22.0 15.7 %collective-permute-done.1 = bf16[256,512]{1,0:T(8,128)(2,1)S(1)} collective-permute-done((bf16[256,512]{1,0:T(8,128)(2,1)S(1)}, bf16[256,512]{1,0:T(8,128)(2,1)S(1)}, u32[]{:S(2)}, u32[]{:S(2)}) %collective-permute-start.1) | collective-permute-done | bytes 262176 | tf_op jit(solution)/shard_map/ppermute | solution.py:42
  37.8 1.9 collective-permute-start.6
  39.7 1.0 copy-done.5
  40.7 1.6 collective-permute-start.2
  42.3 7.7 %collective-permute-done.2 = bf16[2,256,512]{2,1,0:T(8,128)(2,1)S(1)} collective-permute-done((bf16[2,256,512]{2,1,0:T(8,128)(2,1)S(1)}, bf16[2,256,512]{2,1,0:T(8,128)(2,1)S(1)}, u32[]{:S(2)}, u32[]{:S(2)}) %collective-permute-start.2) | collective-permute-done | bytes 524320 | tf_op jit(solution)/shard_map/ppermute | solution.py:42
  50.2 25.9 %collective-permute-start.3 = (bf16[2,2,256,512]{3,2,1,0:T(8,128)(2,1)S(1)}, bf16[2,2,256,512]{3,2,1,0:T(8,128)(2,1)S(1)}, u32[]{:S(2)}, u32[]{:S(2)}) collective-permute-start(bf16[2,2,256,512]{3,2,1,0:T(8,128)(2,1)S(1)} %pad_maximum_fusion.8), channel_id=1, source_target_pairs={{0,2},{1,3},{2,0},{3,1},{4,6},{5,7},{6,4},{7,5},{8,10},{9,11},{10,... | collective-permute-start | bytes 3145736 | tf_op jit(solution)/shard_map/ppermute | solution.py:42
  76.1 46.4 %collective-permute-done.3 = bf16[2,2,256,512]{3,2,1,0:T(8,128)(2,1)S(1)} collective-permute-done((bf16[2,2,256,512]{3,2,1,0:T(8,128)(2,1)S(1)}, bf16[2,2,256,512]{3,2,1,0:T(8,128)(2,1)S(1)}, u32[]{:S(2)}, u32[]{:S(2)}) %collective-permute-start.3) | collective-permute-done | bytes 1048608 | tf_op jit(solution)/shard_map/ppermute | solution.py:42
  122.9 10.3 %collective-permute-start.4 = (bf16[2048,512]{1,0:T(8,128)(2,1)S(1)}, bf16[2048,512]{1,0:T(8,128)(2,1)S(1)}, u32[]{:S(2)}, u32[]{:S(2)}) collective-permute-start(bf16[2048,512]{1,0:T(8,128)(2,1)S(1)} %bitcast.104), channel_id=1, source_target_pairs={{0,16},{1,17},{2,18},{3,19},{4,20},{5,21},{6,22},{7,23},{8,24},{9,... | collective-permute-start | bytes 6291464 | tf_op jit(solution)/shard_map/ppermute | solution.py:42
  133.1 45.4 %collective-permute-done.4 = bf16[2048,512]{1,0:T(8,128)(2,1)S(1)} collective-permute-done((bf16[2048,512]{1,0:T(8,128)(2,1)S(1)}, bf16[2048,512]{1,0:T(8,128)(2,1)S(1)}, u32[]{:S(2)}, u32[]{:S(2)}) %collective-permute-start.4) | collective-permute-done | bytes 2097184 | tf_op jit(solution)/shard_map/ppermute | solution.py:42
  178.5 2.7 pad_maximum_fusion.1
  184.4 0.7 fusion.112
  187.5 6.1 %convert_element_type.67 = bf16[2048,1024]{1,0:T(8,128)(2,1)} convert(f32[2048,1024]{1,0:T(8,128)} %param.9) | non-fusion elementwise | flops 2097152 | bytes 12582912 | tf_op jit(solution)/shard_map/convert_element_type | solution.py:95
  193.6 6.6 %pad_maximum_fusion = bf16[2048,2048]{1,0:T(8,128)(2,1)} fusion(bf16[2048,1024]{1,0:T(8,128)(2,1)} %collective-permute-done.5, bf16[2048,512]{1,0:T(8,128)(2,1)} %copy-done.2, bf16[2048,512]{1,0:T(8,128)(2,1)S(1)} %bitcast.106), kind=kLoop, calls=%fused_computation | loop fusion | flops 25165824 | bytes 16777216 | tf_op jit(solution)/shard_map/concatenate | solution.py:89
  200.2 3.3 fusion.34
  203.5 2.6 fusion.32
  206.4 1.3 fusion.30
  207.6 1.3 fusion.28
  209.4 1.3 fusion.16
  210.7 1.3 fusion.17
  212.0 1.3 fusion.18
  213.3 1.3 fusion.19
  214.8 0.8 slice-done.1
  215.7 1.2 fusion.68
  217.0 1.2 fusion.60
  218.2 1.0 pad_maximum_fusion.9
  219.7 1.2 fusion.73
  221.0 1.2 fusion.65
  225.0 1.4 bitcast_dynamic-update-slice_fusion.7
  226.4 3.9 fusion.79
  230.3 1.8 collective-permute-start.8
  232.1 1.4 bitcast_dynamic-update-slice_fusion.6
  233.5 3.1 fusion.76
  237.1 8.0 %collective-permute-done.8 = bf16[512,512]{1,0:T(8,128)(2,1)S(1)} collective-permute-done((bf16[512,512]{1,0:T(8,128)(2,1)S(1)}, bf16[512,512]{1,0:T(8,128)(2,1)S(1)}, u32[]{:S(2)}, u32[]{:S(2)}) %collective-permute-start.8) | collective-permute-done | bytes 524320 | tf_op jit(solution)/shard_map/ppermute | solution.py:42
  245.1 4.1 %divide_convert_fusion.1 = (bf16[512,512]{1,0:T(8,128)(2,1)S(1)}, f32[512,512]{1,0:T(8,128)S(1)}, f32[512,512]{1,0:T(8,128)}, f32[512,512]{1,0:T(8,128)S(1)}, f32[512,512]{1,0:T(8,128)S(1)}) fusion(f32[512,1024]{1,0:T(8,128)S(1)} %copy-done.10, f32[512,1024]{1,0:T(8,128)S(1)} %copy-done.11, bf16[512,512]{1,0:T(8,128)(2,1)S(1)} %collective-permute-done.8, ...), kind=kOutput, calls=%fused_computation.94 | convolution fusion | flops 1077673984 | bytes 14155780 | tf_op jit(solution)/shard_map/dot_general | solution.py:19
  249.2 6.7 %collective-permute-done.10 = bf16[512,512]{1,0:T(8,128)(2,1)S(1)} collective-permute-done((bf16[512,512]{1,0:T(8,128)(2,1)S(1)}, bf16[512,512]{1,0:T(8,128)(2,1)S(1)}, u32[]{:S(2)}, u32[]{:S(2)}) %collective-permute-start.10) | collective-permute-done | bytes 524320 | tf_op jit(solution)/shard_map/ppermute | solution.py:42
  255.9 4.3 %divide_convert_fusion = (bf16[512,512]{1,0:T(8,128)(2,1)S(1)}, f32[512,512]{1,0:T(8,128)}, f32[512,512]{1,0:T(8,128)}) fusion(f32[512,512]{1,0:T(8,128)S(1)} %get-tuple-element.16, f32[512,512]{1,0:T(8,128)S(1)} %get-tuple-element.14, bf16[512,512]{1,0:T(8,128)(2,1)S(1)} %collective-permute-done.10, bf16[1024,512]{1,0:T(8,128)(2,1)} %collective-permute-done.9, ...), kind=kOutput, calls=%fused_computation.91 | convolution fusion | flops 1077673984 | bytes 9961476 | tf_op jit(solution)/shard_map/dot_general | solution.py:19
  260.2 1.7 collective-permute-start.13
  262.7 12.3 %collective-permute-done.13 = bf16[512,512]{1,0:T(8,128)(2,1)S(1)} collective-permute-done((bf16[512,512]{1,0:T(8,128)(2,1)S(1)}, bf16[512,512]{1,0:T(8,128)(2,1)S(1)}, u32[]{:S(2)}, u32[]{:S(2)}) %collective-permute-start.13) | collective-permute-done | bytes 524320 | tf_op jit(solution)/shard_map/ppermute | solution.py:42
  275.3 9.7 %collective-permute-done.11 = bf16[512,512]{1,0:T(8,128)(2,1)S(1)} collective-permute-done((bf16[512,512]{1,0:T(8,128)(2,1)S(1)}, bf16[512,512]{1,0:T(8,128)(2,1)S(1)}, u32[]{:S(2)}, u32[]{:S(2)}) %collective-permute-start.11) | collective-permute-done | bytes 524320 | tf_op jit(solution)/shard_map/ppermute | solution.py:42
  286.2 1.7 collective-permute-done.12
  289.0 9.5 %convolution_convert_fusion.1 = bf16[2048,1024]{1,0:T(8,128)(2,1)S(1)} fusion(bf16[2048,2048]{0,1:T(8,128)(2,1)S(1)} %bitcast_dynamic-update-slice_fusion, bf16[2048,1024]{1,0:T(8,128)(2,1)S(1)} %pad_maximum_fusion.2), kind=kOutput, calls=%fused_computation.4 | convolution fusion | flops 8592031744 | bytes 16777216 | tf_op jit(solution)/shard_map/dot_general | solution.py:19
  298.5 11.0 %convolution_convert_fusion = bf16[2048,2048]{1,0:T(8,128)(2,1)} fusion(bf16[2048,1024]{1,0:T(8,128)(2,1)S(1)} %convolution_convert_fusion.1, bf16[2048,1024]{1,0:T(8,128)(2,1)S(1)} %copy-done.4), kind=kOutput, calls=%fused_computation.1 | convolution fusion | flops 8594128896 | bytes 16777216 | tf_op jit(solution)/shard_map/dot_general | solution.py:23
  309.5 1.2 copy-done.6
  311.0 3.7 pad_maximum_fusion.4
  314.7 82.5 %reduce-scatter.2.cloned.1.call-done = bf16[256,2048]{1,0:T(8,128)(2,1)} async-done(((bf16[2048,2048]{1,0:T(8,128)(2,1)}), bf16[256,2048]{1,0:T(8,128)(2,1)}) %reduce-scatter.2.cloned.1.call-update) | async-done | bytes 1048592 | tf_op jit(solution)/shard_map/reduce_scatter | solution.py:157
  (81 shorter events, 7.1 us)
Async XLA Ops:
  7.2 193.0 %all-gather.3.cloned.1.call-start = ((), (), s32[]{:S(2)}) async-start(), calls=%async_computation.2 | async-start | bytes 9437184 | tf_op jit(solution)/shard_map/all_gather | solution.py:84
  7.2 30.6 %collective-permute-start = (bf16[512,1024]{1,0:T(8,128)(2,1)}, bf16[512,1024]{1,0:T(8,128)(2,1)}, u32[]{:S(2)}, u32[]{:S(2)}) collective-permute-start(bf16[512,1024]{1,0:T(8,128)(2,1)} %param.7), channel_id=1, source_target_pairs={{0,0},{1,1},{2,2},{3,3},{4,4},{5,5},{6,6},{7,7},{8,14},{9,15},{10,... | collective-permute-start | bytes 3145736 | tf_op jit(solution)/shard_map/ppermute | solution.py:42
  17.9 19.8 %collective-permute-start.1 = (bf16[256,512]{1,0:T(8,128)(2,1)S(1)}, bf16[256,512]{1,0:T(8,128)(2,1)S(1)}, u32[]{:S(2)}, u32[]{:S(2)}) collective-permute-start(bf16[256,512]{1,0:T(8,128)(2,1)S(1)} %bitcast.109), channel_id=1, source_target_pairs={{0,4},{1,5},{2,6},{3,7},{4,0},{5,1},{6,2},{7,3},{8,12},{9,13},{10,... | collective-permute-start | bytes 786440 | tf_op jit(solution)/shard_map/ppermute | solution.py:42
  37.8 1.9 collective-permute-start.6
  39.7 1.0 copy-start.5
  40.7 356.5 %reduce-scatter.2.cloned.1.call-start = ((), (), s32[]{:S(2)}) async-start(), calls=%async_computation.1 | async-start | bytes 9437184 | tf_op jit(solution)/shard_map/reduce_scatter | solution.py:157
  40.7 9.2 %collective-permute-start.2 = (bf16[2,256,512]{2,1,0:T(8,128)(2,1)S(1)}, bf16[2,256,512]{2,1,0:T(8,128)(2,1)S(1)}, u32[]{:S(2)}, u32[]{:S(2)}) collective-permute-start(bf16[2,256,512]{2,1,0:T(8,128)(2,1)S(1)} %pad_maximum_fusion.13), channel_id=1, source_target_pairs={{0,1},{1,0},{2,3},{3,2},{4,5},{5,4},{6,7},{7,6},{8,9},{9,8},{10,11... | collective-permute-start | bytes 1572872 | tf_op jit(solution)/shard_map/ppermute | solution.py:42
  50.2 72.3 %collective-permute-start.3 = (bf16[2,2,256,512]{3,2,1,0:T(8,128)(2,1)S(1)}, bf16[2,2,256,512]{3,2,1,0:T(8,128)(2,1)S(1)}, u32[]{:S(2)}, u32[]{:S(2)}) collective-permute-start(bf16[2,2,256,512]{3,2,1,0:T(8,128)(2,1)S(1)} %pad_maximum_fusion.8), channel_id=1, source_target_pairs={{0,2},{1,3},{2,0},{3,1},{4,6},{5,7},{6,4},{7,5},{8,10},{9,11},{10,... | collective-permute-start | bytes 3145736 | tf_op jit(solution)/shard_map/ppermute | solution.py:42
  122.9 58.4 %copy-start.9 = (s32[4]{0:T(128)S(1)}, s32[4]{0:T(128)}, u32[]{:S(2)}) copy-start(s32[4]{0:T(128)} %constant.76.clone) | copy-start | bytes 52
  122.9 61.6 %copy-start.8 = (s32[4]{0:T(128)S(1)}, s32[4]{0:T(128)}, u32[]{:S(2)}) copy-start(s32[4]{0:T(128)} %constant.77.clone) | copy-start | bytes 52
  122.9 55.6 %collective-permute-start.4 = (bf16[2048,512]{1,0:T(8,128)(2,1)S(1)}, bf16[2048,512]{1,0:T(8,128)(2,1)S(1)}, u32[]{:S(2)}, u32[]{:S(2)}) collective-permute-start(bf16[2048,512]{1,0:T(8,128)(2,1)S(1)} %bitcast.104), channel_id=1, source_target_pairs={{0,16},{1,17},{2,18},{3,19},{4,20},{5,21},{6,22},{7,23},{8,24},{9,... | collective-permute-start | bytes 6291464 | tf_op jit(solution)/shard_map/ppermute | solution.py:42
  178.5 2.8 copy-start.2
  181.3 12.3 %collective-permute-start.5 = (bf16[2048,1024]{1,0:T(8,128)(2,1)}, bf16[2048,1024]{1,0:T(8,128)(2,1)}, u32[]{:S(2)}, u32[]{:S(2)}) collective-permute-start(bf16[2048,1024]{1,0:T(8,128)(2,1)} %pad_maximum_fusion.1), channel_id=1, source_target_pairs={{0,8},{1,9},{2,10},{3,11},{4,12},{5,13},{6,14},{7,15},{8,0},{9,1},... | collective-permute-start | bytes 12582920 | tf_op jit(solution)/shard_map/ppermute | solution.py:42
  200.2 3.3 copy-start.3
  200.2 6.0 %slice-start.4 = ((s8[8388608]{0:T(1024)(128)(4,1)}), s8[4194304]{0:T(1024)(128)(4,1)S(1)}, s32[]{:S(2)}) async-start(s8[8388608]{0:T(1024)(128)(4,1)} %bitcast.112), calls=%async_computation.7 | async-start | bytes 8388608
  203.5 2.8 slice-start.5
  212.0 2.9 slice-start
  213.3 2.4 slice-start.1
  214.6 2.4 copy-start
  219.3 7.1 %collective-permute-start.7 = (bf16[1024,512]{1,0:T(8,128)(2,1)}, bf16[1024,512]{1,0:T(8,128)(2,1)}, u32[]{:S(2)}, u32[]{:S(2)}) collective-permute-start(bf16[1024,512]{1,0:T(8,128)(2,1)} %pad_maximum_fusion.9), channel_id=1, source_target_pairs={{0,8},{1,9},{2,10},{3,11},{4,12},{5,13},{6,14},{7,15},{8,0},{9,1},... | collective-permute-start | bytes 3145736 | tf_op jit(solution)/shard_map/ppermute | solution.py:42
  222.3 11.2 %collective-permute-start.9 = (bf16[1024,512]{1,0:T(8,128)(2,1)S(1)}, bf16[1024,512]{1,0:T(8,128)(2,1)}, u32[]{:S(2)}, u32[]{:S(2)}) collective-permute-start(bf16[1024,512]{1,0:T(8,128)(2,1)S(1)} %pad_maximum_fusion.10), channel_id=1, source_target_pairs={{0,8},{1,9},{2,10},{3,11},{4,12},{5,13},{6,14},{7,15},{8,0},{9,1},... | collective-permute-start | bytes 3145736 | tf_op jit(solution)/shard_map/ppermute | solution.py:42
  226.3 18.8 %slice-start.2 = ((s8[8388608]{0:T(1024)(128)(4,1)}), s8[4194304]{0:T(1024)(128)(4,1)S(1)}, s32[]{:S(2)}) async-start(s8[8388608]{0:T(1024)(128)(4,1)} %bitcast.102), calls=%async_computation.5 | async-start | bytes 8388608
  226.3 18.7 %copy-start.10 = (f32[512,1024]{1,0:T(8,128)S(1)}, f32[512,1024]{1,0:T(8,128)}, u32[]{:S(2)}) copy-start(f32[512,1024]{1,0:T(8,128)} %param.10) | copy-start | bytes 6291460
  226.4 18.7 %copy-start.11 = (f32[512,1024]{1,0:T(8,128)S(1)}, f32[512,1024]{1,0:T(8,128)}, u32[]{:S(2)}) copy-start(f32[512,1024]{1,0:T(8,128)} %param.11) | copy-start | bytes 6291460
  230.3 14.8 %slice-start.3 = ((s8[8388608]{0:T(1024)(128)(4,1)}), s8[4194304]{0:T(1024)(128)(4,1)S(1)}, s32[]{:S(2)}) async-start(s8[8388608]{0:T(1024)(128)(4,1)} %bitcast.102), calls=%async_computation.6 | async-start | bytes 8388608
  230.3 14.8 %collective-permute-start.8 = (bf16[512,512]{1,0:T(8,128)(2,1)S(1)}, bf16[512,512]{1,0:T(8,128)(2,1)S(1)}, u32[]{:S(2)}, u32[]{:S(2)}) collective-permute-start(bf16[512,512]{1,0:T(8,128)(2,1)S(1)} %fusion.79), channel_id=1, source_target_pairs={{0,16},{1,17},{2,18},{3,19},{4,20},{5,21},{6,22},{7,23},{8,24},{9,... | collective-permute-start | bytes 1572872 | tf_op jit(solution)/shard_map/ppermute | solution.py:42
  233.5 11.6 %copy-start.1 = (bf16[2048,1024]{1,0:T(8,128)(2,1)S(1)}, bf16[2048,1024]{1,0:T(8,128)(2,1)}, u32[]{:S(2)}) copy-start(bf16[2048,1024]{1,0:T(8,128)(2,1)} %copy-done) | copy-start | bytes 12582916
  236.6 19.3 %collective-permute-start.10 = (bf16[512,512]{1,0:T(8,128)(2,1)S(1)}, bf16[512,512]{1,0:T(8,128)(2,1)S(1)}, u32[]{:S(2)}, u32[]{:S(2)}) collective-permute-start(bf16[512,512]{1,0:T(8,128)(2,1)S(1)} %fusion.76), channel_id=1, source_target_pairs={{0,16},{1,17},{2,18},{3,19},{4,20},{5,21},{6,22},{7,23},{8,24},{9,... | collective-permute-start | bytes 1572872 | tf_op jit(solution)/shard_map/ppermute | solution.py:42
  260.2 14.8 %collective-permute-start.13 = (bf16[512,512]{1,0:T(8,128)(2,1)S(1)}, bf16[512,512]{1,0:T(8,128)(2,1)S(1)}, u32[]{:S(2)}, u32[]{:S(2)}) collective-permute-start(bf16[512,512]{1,0:T(8,128)(2,1)S(1)} %get-tuple-element.17), channel_id=1, source_target_pairs={{0,16},{1,17},{2,18},{3,19},{4,20},{5,21},{6,22},{7,23},{8,24},{9,... | collective-permute-start | bytes 1572872 | tf_op jit(solution)/shard_map/ppermute | solution.py:42
  262.2 22.8 %collective-permute-start.11 = (bf16[512,512]{1,0:T(8,128)(2,1)S(1)}, bf16[512,512]{1,0:T(8,128)(2,1)S(1)}, u32[]{:S(2)}, u32[]{:S(2)}) collective-permute-start(bf16[512,512]{1,0:T(8,128)(2,1)S(1)} %get-tuple-element.20), channel_id=1, source_target_pairs={{0,16},{1,17},{2,18},{3,19},{4,20},{5,21},{6,22},{7,23},{8,24},{9,... | collective-permute-start | bytes 1572872 | tf_op jit(solution)/shard_map/ppermute | solution.py:42
  275.2 10.5 %collective-permute-start.14 = (bf16[2,512,512]{2,1,0:T(8,128)(2,1)S(1)}, bf16[2,512,512]{2,1,0:T(8,128)(2,1)S(1)}, u32[]{:S(2)}, u32[]{:S(2)}) collective-permute-start(bf16[2,512,512]{2,1,0:T(8,128)(2,1)S(1)} %pad_maximum_fusion.12), channel_id=1, source_target_pairs={{0,8},{1,9},{2,10},{3,11},{4,12},{5,13},{6,14},{7,15},{8,0},{9,1},... | collective-permute-start | bytes 3145736 | tf_op jit(solution)/shard_map/ppermute | solution.py:42
  285.2 2.7 collective-permute-start.12
  289.0 9.5 %copy-start.4 = (bf16[2048,1024]{1,0:T(8,128)(2,1)S(1)}, bf16[2048,1024]{1,0:T(8,128)(2,1)}, u32[]{:S(2)}) copy-start(bf16[2048,1024]{1,0:T(8,128)(2,1)} %convert_element_type.67) | copy-start | bytes 12582916
  309.5 1.2 copy-start.6
  309.5 1.5 copy-start.7
Sparse Core Ops, SparseCore 0:
  40.8 134.8 all-gather.2
  309.6 87.5 reduce-scatter.1

commit v2 on v1

v2 whole, which is shorter than its diff:
```python
import functools

import jax
import jax.numpy as jnp
from jax import lax
from jax.experimental import pallas as pl
from jax.experimental.pallas import tpu as pltpu
from jax.sharding import PartitionSpec as P

STEP = 4


beta_first = 0.95
beta_second = 0.95
epsilon = 1e-08

COL_PARTS = 2

VMEM_BYTES = 48 * 1024 * 1024

low = jnp.bfloat16


def matmul(a, b):
    return lax.dot_general(a, b, (((1,), (0,)), ((), ())), preferred_element_type=jnp.float32)


def matmul_tn(a, b):
    return lax.dot_general(a, b, (((0,), (0,)), ((), ())), preferred_element_type=jnp.float32)


def matmul_nt(a, b):
    return lax.dot_general(a, b, (((1,), (1,)), ((), ())), preferred_element_type=jnp.float32)


def cost(flops, *arrays):
    size = sum(a.size * a.dtype.itemsize for a in arrays)
    return pl.CostEstimate(flops=flops, bytes_accessed=size, transcendentals=0)


def half_rotation(gathered, right, places, nz, parts):
    count, rows, cols = gathered.shape
    nx = count // nz
    width = right.shape[1] // parts

    def kernel(places_ref, *refs):
        blocks, right_ref, outs = refs[:nx], refs[nx], refs[nx + 1 :]
        for j, out in enumerate(outs):
            total = matmul(blocks[0][...], right_ref[:cols, j * width : (j + 1) * width])
            for i in range(1, nx):
                total += matmul(blocks[i][...], right_ref[i * cols : (i + 1) * cols, j * width : (j + 1) * width])
            out[...] = total.astype(out.dtype)

    def block_of(i):
        if i % 2 == 0:
            return pl.BlockSpec((None, rows, cols), lambda k, p: (i * nz + k, 0, 0))
        return pl.BlockSpec((None, rows, cols), lambda k, p: (i * nz + nz - 1 - k, 0, 0))

    outs = [jax.ShapeDtypeStruct((nz * rows, width), low)] * parts
    return pl.pallas_call(
        kernel,
        out_shape=outs,
        grid_spec=pltpu.PrefetchScalarGridSpec(
            num_scalar_prefetch=1,
            grid=(nz,),
            in_specs=[block_of(i) for i in range(nx)]
            + [pl.BlockSpec(right.shape, lambda k, p: (0, 0), pipeline_mode=pl.Buffered(1))],
            out_specs=[pl.BlockSpec((rows, width), lambda k, p: (p[k], 0))] * parts,
        ),
        compiler_params=pltpu.CompilerParams(vmem_limit_bytes=VMEM_BYTES),
        cost_estimate=cost(2 * gathered.size * right.shape[1], gathered, right, *outs),
        name="half_rotation",
    )(places, *([gathered] * nx), right)


def back_rotation(columns, right, places, block):
    parts = len(columns)
    total_rows, width = columns[0].shape
    count = total_rows // block

    def kernel(places_ref, *refs):
        rows_of, right_ref, out = refs[:parts], refs[parts], refs[parts + 1]
        total = matmul_nt(rows_of[0][...], right_ref[:, :width])
        for j in range(1, parts):
            total += matmul_nt(rows_of[j][...], right_ref[:, j * width : (j + 1) * width])
        out[...] = total.astype(out.dtype)

    out = jax.ShapeDtypeStruct((total_rows, right.shape[0]), low)
    return pl.pallas_call(
        kernel,
        out_shape=out,
        grid_spec=pltpu.PrefetchScalarGridSpec(
            num_scalar_prefetch=1,
            grid=(count,),
            in_specs=[pl.BlockSpec((block, width), lambda k, p: (p[k], 0))] * parts
            + [pl.BlockSpec(right.shape, lambda k, p: (0, 0), pipeline_mode=pl.Buffered(1))],
            out_specs=pl.BlockSpec((block, right.shape[0]), lambda k, p: (k, 0)),
        ),
        compiler_params=pltpu.CompilerParams(vmem_limit_bytes=VMEM_BYTES),
        cost_estimate=cost(2 * total_rows * right.size, right, out, *columns),
        name="back_rotation",
    )(places, *columns, right)


def per_device(gradient, left_basis, right_basis, first_moment, second_moment, *, nb, nd):
    nz = nb
    nx = nd // nz
    b = lax.axis_index("basis")
    d = lax.axis_index("dp")
    z, x = d // nx, d % nx
    bits = [1 << k for k in range(nb.bit_length() - 1)]
    x_bits = [1 << k for k in range(nx.bit_length() - 1)]

    def permute(value, target):
        pairs = []
        for bb in range(nb):
            for zz in range(nz):
                for xx in range(nx):
                    tb, tz, tx = target(bb, zz, xx)
                    pairs.append((bb * nd + zz * nx + xx, tb * nd + tz * nx + tx))
        return lax.ppermute(value, ("basis", "dp"), pairs)

    def move_b(value, t):
        return permute(value, lambda bb, zz, xx: (bb ^ t, zz, xx))

    def move_z(value, t):
        return permute(value, lambda bb, zz, xx: (bb, zz ^ t, xx))

    def move_x(value, u):
        return permute(value, lambda bb, zz, xx: (bb, zz, xx ^ u))

    def spread(beta):
        return (beta >> 1) ^ ((beta & 1) * (nz - 1))

    unspread = [0] * nz
    for beta in range(nb):
        unspread[spread(beta)] = beta

    def joined(mine, other, bit_set, axis):
        first = jnp.where(bit_set, other, mine)
        second = jnp.where(bit_set, mine, other)
        return jnp.stack([first, second], axis=axis)

    def after(value, *others):
        return lax.optimization_barrier((value,) + others)[0]

    ff_block = right_basis.shape[1]
    rows = first_moment.shape[0]
    out_rows = left_basis.shape[1]
    whole = rows * nb

    path = []
    for xx in range(nx):
        path += [zz * nx + xx for zz in (range(nz) if xx % 2 == 0 else reversed(range(nz)))]

    order = [0]
    for t in reversed(bits):
        order = order + [s | t for s in order]
    half_places = [[order.index(unspread[bb ^ zz] ^ bb) for zz in range(nz)] for bb in range(nb)]
    back_places = [[order.index(bb ^ (dd // nx)) * nx + dd % nx for dd in path] for bb in range(nb)]
    half_places = jnp.array(half_places, jnp.int32)[b]
    back_places = jnp.array(back_places, jnp.int32)[b]

    left_t = left_basis.astype(low).T
    right = right_basis.astype(low)
    piece = permute(gradient, lambda bb, zz, xx: (bb, zz ^ spread(bb), xx))
    for i, u in enumerate(reversed(x_bits)):
        left_t = joined(left_t, move_x(left_t, u), (x & u) != 0, i)
    for i, t in enumerate(reversed(bits[1:])):
        left_t = joined(left_t, move_z(left_t, t), (z & t) != 0, i)
    piece, left_t, right, half_places, back_places = lax.optimization_barrier(
        (piece, left_t, right, half_places, back_places)
    )
    piece = permute(piece, lambda bb, zz, xx: (zz ^ spread(bb), zz, xx))
    gathered = lax.all_gather(piece, "dp", axis_index_groups=[path])
    left_t = joined(left_t, move_z(left_t, bits[0]), (z & bits[0]) != 0, len(bits) - 1).reshape(whole, rows)
    for t in reversed(bits):
        left_t = jnp.concatenate([left_t, move_b(left_t, t)], axis=1)
    left_t, gathered = lax.optimization_barrier((left_t, gathered))

    half = list(half_rotation(gathered, right, half_places, nz, COL_PARTS))

    def product(t, j):
        rows_of = lax.dynamic_slice_in_dim(left_t, (b ^ t) * rows, rows, 0)
        return matmul(rows_of, half[j]).astype(low)

    width = ff_block // COL_PARTS
    first_out, second_out, back = [], [], []
    for j in range(COL_PARTS):
        cols = slice(j * width, (j + 1) * width)
        if j:
            half[j] = after(half[j], gone)
        gone = lax.optimization_barrier([product(t, j) for t in range(1, nb, 2)])
        gots = [move_b(value, 1) for value in gone]
        held = dict(zip(range(0, nb, 2), lax.optimization_barrier([product(t, j) for t in range(0, nb, 2)])))
        held = {t: held[t].astype(jnp.float32) + got.astype(jnp.float32) for t, got in zip(held, gots)}
        for t in reversed(bits[1:]):
            for s in [s for s in held if s & t]:
                held[s ^ t] = held[s ^ t] + move_b(held.pop(s).astype(low), t).astype(jnp.float32)
        rotated = held[0]
        moments = first_moment[:, cols], second_moment[:, cols]
        if j:
            moments = after(moments, previous)
        first_new = beta_first * moments[0] + (1.0 - beta_first) * rotated
        second_new = beta_second * moments[1] + (1.0 - beta_second) * rotated * rotated
        first_fix = 1.0 - beta_first**STEP
        second_fix = 1.0 - beta_second**STEP
        direction = first_new / first_fix / (jnp.sqrt(second_new / second_fix) + epsilon)
        first_out.append(first_new)
        second_out.append(second_new)
        column = previous = direction.astype(low)
        axis = 0
        for t in reversed(bits):
            column = joined(column, move_b(column, t), (b & t) != 0, axis)
            axis += 1
        column = lax.optimization_barrier(column.reshape(whole, width))
        back.append(lax.optimization_barrier(matmul_tn(left_t, column).astype(low)))

    total = back_rotation(back, right, back_places, out_rows)
    update = lax.psum_scatter(total, "dp", scatter_dimension=0, axis_index_groups=[path], tiled=True)
    return (
        jnp.concatenate(first_out, axis=1),
        jnp.concatenate(second_out, axis=1),
        update,
    )


def solution(mesh):
    nb, nd = mesh.shape["basis"], mesh.shape["dp"]

    return jax.shard_map(
        functools.partial(per_device, nb=nb, nd=nd),
        mesh=mesh,
        in_specs=(
            P("basis", "dp"),
            P("basis", "dp"),
            P("basis", "dp"),
            P("basis", "dp"),
            P("basis", "dp"),
        ),
        out_specs=(P("basis", "dp"), P("basis", "dp"), P("dp", "basis")),
        check_vma=False,
    )
```

time: 405 us -> 390 us (0.963)
  matrix products: 54.3 us -> 23.7 us
  Pallas kernels: 0 us -> 27.2 us
  waiting for transfers between devices: 236 us -> 218 us
  starting transfers between devices: 58.4 us -> 70 us
  between operations: 22 us -> 14.3 us
  other arithmetic: 22.5 us -> 29 us
  local copies, waits for them, and re-layouts: 10.7 us -> 6.13 us
    dot_general x17 -> x8, matrix products: 43.4 us -> 9.95 us  [matmul(): lax.dot_general(a, b, (((1,), (0,)), ((), ())), preferred_element_type=jn...]
    pallas_call x0 -> x2, Pallas kernels: none -> 27.2 us  [the longest x1 14.2 us: back_rotation(): pl.pallas_call(kernel, out_shape=out, grid_spec=pltpu.PrefetchScalarGridS...]
    ppermute x15 -> x17, waiting for transfers between devices: 154 us -> 138 us  [permute(): return lax.ppermute(value, ('basis', 'dp'), pairs)]
    ppermute x15 -> x17, starting transfers between devices: 58.3 us -> 69.9 us  [permute(): return lax.ppermute(value, ('basis', 'dp'), pairs)]
    convert_element_type x0 -> x4, other arithmetic: none -> 4.29 us  [the longest x2 4.02 us: per_device(): column = previous = direction.astype(low)]
    unnamed x44 -> x25, local copies, waits for them, and re-layouts: 8.16 us -> 4.49 us
    dot_general x1 -> x2, matrix products: 11 us -> 13.7 us  [matmul_tn(): lax.dot_general(a, b, (((0,), (0,)), ((), ())), preferred_element_type=jn...]
  transfers between devices with their start and end apart: 17 -> 19, of which waited for: 10 -> 10; matrix products, arithmetic and copies ran while one was open for 10% -> 11% of each run, Pallas kernels for 0% -> 0%
where the time goes in v2:
time: 390 us; the launch traced here: 389 us
  waiting for transfers between devices  218 us (56%)
  starting transfers between devices  70 us (18%)
  other arithmetic  29 us (7%)
  Pallas kernels  27.2 us (7%)
  matrix products  23.7 us (6%)
  between operations  14.3 us (4%)
  local copies, waits for them, and re-layouts  6.13 us (2%)
    ppermute x17, waiting for transfers between devices, permute(): return lax.ppermute(value, ('basis', 'dp'), pairs)  138 us
    reduce_scatter x1, waiting for transfers between devices, per_device(): lax.psum_scatter(total, 'dp', scatter_dimension=0, axis_index_groups=[pat...  80.9 us
    ppermute x17, starting transfers between devices, permute(): return lax.ppermute(value, ('basis', 'dp'), pairs)  69.9 us
    pallas_call x1, Pallas kernels, back_rotation(): pl.pallas_call(kernel, out_shape=out, grid_spec=pltpu.PrefetchScalarGridS...  14.2 us
    dot_general x2, matrix products, matmul_tn(): lax.dot_general(a, b, (((0,), (0,)), ((), ())), preferred_element_type=jn...  13.7 us
    pallas_call x1, Pallas kernels, half_rotation(): pl.pallas_call(kernel, out_shape=outs, grid_spec=pltpu.PrefetchScalarGrid...  13 us
    dot_general x8, matrix products, matmul(): lax.dot_general(a, b, (((1,), (0,)), ((), ())), preferred_element_type=jn...  9.95 us
    concatenate x2, other arithmetic, per_device(): left_t = jnp.concatenate([left_t, move_b(left_t, t)], axis=1)  9.31 us
  transfers between devices with their start and end apart: 19, of which 10 were waited for; matrix products, arithmetic and copies ran while one was open for 11% of the time, Pallas kernels for 0%

profile of v2, /device:TPU:0, one launch (start us, length us, event | category | flops | bytes accessed | tf_op | source)
XLA Modules:
  0.0 388.8 jit_solution(351598984685252984)
XLA Ops:
  7.2 1.2 copy.10
  8.4 3.0 collective-permute-start.1
  11.4 9.5 %collective-permute-start = (bf16[512,1024]{1,0:T(8,128)(2,1)}, bf16[512,1024]{1,0:T(8,128)(2,1)}, u32[]{:S(2)}, u32[]{:S(2)}) collective-permute-start(bf16[512,1024]{1,0:T(8,128)(2,1)} %param.7), channel_id=1, source_target_pairs={{0,0},{1,1},{2,2},{3,3},{4,4},{5,5},{6,6},{7,7},{8,14},{9,15},{10,... | collective-permute-start | bytes 3145736 | tf_op jit(solution)/shard_map/ppermute | solution.py:121
  21.0 2.7 collective-permute-start.2
  23.6 6.0 %convert_element_type.79.refs_2_ = bf16[2048,1024]{1,0:T(8,128)(2,1)} convert(f32[2048,1024]{1,0:T(8,128)} %param.9) | non-fusion elementwise | flops 2097152 | bytes 12582912 | tf_op jit(solution)/shard_map/convert_element_type | solution.py:165
  29.7 0.7 fusion.50.places_ref
  30.4 0.7 fusion.51.places_ref
  31.0 20.3 %collective-permute-done.2 = bf16[2,256,512]{2,1,0:T(8,128)(2,1)S(1)} collective-permute-done((bf16[2,256,512]{2,1,0:T(8,128)(2,1)S(1)}, bf16[2,256,512]{2,1,0:T(8,128)(2,1)S(1)}, u32[]{:S(2)}, u32[]{:S(2)}) %collective-permute-start.2) | collective-permute-done | bytes 524320 | tf_op jit(solution)/shard_map/ppermute | solution.py:121
  51.6 1.9 collective-permute-start.6
  53.5 1.0 copy-done.8
  54.5 17.1 %collective-permute-start.3 = (bf16[2,2,256,512]{3,2,1,0:T(8,128)(2,1)S(1)}, bf16[2,2,256,512]{3,2,1,0:T(8,128)(2,1)S(1)}, u32[]{:S(2)}, u32[]{:S(2)}) collective-permute-start(bf16[2,2,256,512]{3,2,1,0:T(8,128)(2,1)S(1)} %pad_maximum_fusion.7), channel_id=1, source_target_pairs={{0,2},{1,3},{2,0},{3,1},{4,6},{5,7},{6,4},{7,5},{8,10},{9,11},{10,... | collective-permute-start | bytes 3145736 | tf_op jit(solution)/shard_map/ppermute | solution.py:121
  71.6 19.4 %collective-permute-done.3 = bf16[2,2,256,512]{3,2,1,0:T(8,128)(2,1)S(1)} collective-permute-done((bf16[2,2,256,512]{3,2,1,0:T(8,128)(2,1)S(1)}, bf16[2,2,256,512]{3,2,1,0:T(8,128)(2,1)S(1)}, u32[]{:S(2)}, u32[]{:S(2)}) %collective-permute-start.3) | collective-permute-done | bytes 1048608 | tf_op jit(solution)/shard_map/ppermute | solution.py:121
  91.4 30.1 %collective-permute-start.4 = (bf16[2048,512]{1,0:T(8,128)(2,1)S(1)}, bf16[2048,512]{1,0:T(8,128)(2,1)S(1)}, u32[]{:S(2)}, u32[]{:S(2)}) collective-permute-start(bf16[2048,512]{1,0:T(8,128)(2,1)S(1)} %bitcast.54), channel_id=1, source_target_pairs={{0,16},{1,17},{2,18},{3,19},{4,20},{5,21},{6,22},{7,23},{8,24},{9,... | collective-permute-start | bytes 6291464 | tf_op jit(solution)/shard_map/ppermute | solution.py:121
  121.5 46.1 %collective-permute-done.4 = bf16[2048,512]{1,0:T(8,128)(2,1)S(1)} collective-permute-done((bf16[2048,512]{1,0:T(8,128)(2,1)S(1)}, bf16[2048,512]{1,0:T(8,128)(2,1)S(1)}, u32[]{:S(2)}, u32[]{:S(2)}) %collective-permute-start.4) | collective-permute-done | bytes 2097184 | tf_op jit(solution)/shard_map/ppermute | solution.py:121
  167.6 2.7 pad_maximum_fusion.1
  170.3 7.5 %collective-permute-done.5 = bf16[2048,1024]{1,0:T(8,128)(2,1)} collective-permute-done((bf16[2048,1024]{1,0:T(8,128)(2,1)}, bf16[2048,1024]{1,0:T(8,128)(2,1)}, u32[]{:S(2)}, u32[]{:S(2)}) %collective-permute-start.5) | collective-permute-done | bytes 4194336 | tf_op jit(solution)/shard_map/ppermute | solution.py:121
  177.8 6.7 %pad_maximum_fusion = bf16[2048,2048]{1,0:T(8,128)(2,1)} fusion(bf16[2048,1024]{1,0:T(8,128)(2,1)} %collective-permute-done.5, bf16[2048,512]{1,0:T(8,128)(2,1)} %copy-done.1, bf16[2048,512]{1,0:T(8,128)(2,1)S(1)} %bitcast.56), kind=kLoop, calls=%fused_computation | loop fusion | flops 25165824 | bytes 16777216 | tf_op jit(solution)/shard_map/concatenate | solution.py:178
  184.4 13.0 %half_rotation.1 = (bf16[2048,512]{1,0:T(8,128)(2,1)S(1)}, bf16[2048,512]{1,0:T(8,128)(2,1)S(1)}) custom-call(s32[4]{0:T(128)S(1)} %fusion.50.places_ref, bf16[8,512,1024]{2,1,0:T(8,128)(2,1)} %bitcast.62, bf16[8,512,1024]{2,1,0:T(8,128)(2,1)} %bitcast.63, bf16[2048,1024]{1,0:T(8,128)(2,1)} %convert_element_type.79.refs_2_), custom_call_target="tpu_custom_call" | custom-call | flops 8589934592 | bytes 16777216 | tf_op jit(solution)/shard_map/half_rotation/pallas_call | solution.py:60
  197.4 1.2 fusion.34
  198.7 1.2 fusion.28
  200.1 0.4 collective-permute-start.7
  200.5 1.2 fusion.37
  201.8 1.2 fusion.31
  203.0 1.2 fusion.22
  204.3 1.2 fusion.16
  205.7 1.2 fusion.25
  207.1 1.8 collective-permute-start.9
  208.9 1.2 fusion.19
  210.5 0.4 collective-permute-start.12
  210.9 11.1 %collective-permute-done.9 = bf16[512,512]{1,0:T(8,128)(2,1)S(1)} collective-permute-done((bf16[512,512]{1,0:T(8,128)(2,1)S(1)}, bf16[512,512]{1,0:T(8,128)(2,1)S(1)}, u32[]{:S(2)}, u32[]{:S(2)}) %collective-permute-start.9) | collective-permute-done | bytes 524320 | tf_op jit(solution)/shard_map/ppermute | solution.py:121
  222.0 1.9 divide_convert_fusion.1
  223.8 8.8 %collective-permute-done.12 = bf16[512,512]{1,0:T(8,128)(2,1)S(1)} collective-permute-done((bf16[512,512]{1,0:T(8,128)(2,1)S(1)}, bf16[512,512]{1,0:T(8,128)(2,1)S(1)}, u32[]{:S(2)}, u32[]{:S(2)}) %collective-permute-start.12) | collective-permute-done | bytes 524320 | tf_op jit(solution)/shard_map/ppermute | solution.py:121
  232.6 2.1 divide_convert_fusion
  234.8 1.7 collective-permute-start.15
  236.8 12.8 %collective-permute-done.15 = bf16[512,512]{1,0:T(8,128)(2,1)S(1)} collective-permute-done((bf16[512,512]{1,0:T(8,128)(2,1)S(1)}, bf16[512,512]{1,0:T(8,128)(2,1)S(1)}, u32[]{:S(2)}, u32[]{:S(2)}) %collective-permute-start.15) | collective-permute-done | bytes 524320 | tf_op jit(solution)/shard_map/ppermute | solution.py:121
  249.6 0.8 copy-done.9
  250.4 9.1 %collective-permute-done.13 = bf16[512,512]{1,0:T(8,128)(2,1)} collective-permute-done((bf16[512,512]{1,0:T(8,128)(2,1)S(1)}, bf16[512,512]{1,0:T(8,128)(2,1)}, u32[]{:S(2)}, u32[]{:S(2)}) %collective-permute-start.13) | collective-permute-done | bytes 524320 | tf_op jit(solution)/shard_map/ppermute | solution.py:121
  259.5 1.7 select_bitcast_fusion.7
  261.2 1.1 pad_maximum_fusion.9
  262.3 0.6 collective-permute-start.14
  262.9 2.3 collective-permute-done.16
  265.2 1.5 select_bitcast_fusion.1
  267.1 8.9 %convolution_convert_fusion.refs_1_ = bf16[2048,512]{1,0:T(8,128)(2,1)S(1)} fusion(bf16[2048,2048]{1,0:T(8,128)(2,1)} %pad_maximum_fusion, bf16[2048,512]{1,0:T(8,128)(2,1)S(1)} %bitcast.60), kind=kOutput, calls=%fused_computation.2 | convolution fusion | flops 4296015872 | bytes 12582912 | tf_op jit(solution)/shard_map/dot_general | solution.py:29
  276.6 4.8 %convolution_convert_fusion.1.refs_0_ = bf16[2048,512]{1,0:T(8,128)(2,1)S(1)} fusion(bf16[2048,2048]{1,0:T(8,128)(2,1)S(1)} %bitcast.58, bf16[2048,512]{1,0:T(8,128)(2,1)S(1)} %bitcast.59), kind=kOutput, calls=%fused_computation.3 | convolution fusion | flops 4296015872 | bytes 12582912 | tf_op jit(solution)/shard_map/dot_general | solution.py:29
  281.4 14.2 %back_rotation.1 = bf16[2048,2048]{1,0:T(8,128)(2,1)} custom-call(s32[8]{0:T(128)S(1)} %fusion.51.places_ref, bf16[2048,512]{1,0:T(8,128)(2,1)S(1)} %convolution_convert_fusion.1.refs_0_, bf16[2048,512]{1,0:T(8,128)(2,1)S(1)} %convolution_convert_fusion.refs_1_, bf16[2048,1024]{1,0:T(8,128)(2,1)} %convert_element_type.79.refs_2_), custom_call_target="tpu_custom_call" | custom-call | flops 8589934592 | bytes 16777216 | tf_op jit(solution)/shard_map/back_rotation/pallas_call | solution.py:89
  295.6 1.2 copy-done.2
  297.1 3.9 %pad_maximum_fusion.3 = (f32[512,1024]{1,0:T(8,128)}, f32[512,1024]{1,0:T(8,128)}) fusion(f32[512,512]{1,0:T(8,128)} %get-tuple-element.45, f32[512,512]{1,0:T(8,128)S(1)} %get-tuple-element.47, f32[512,512]{1,0:T(8,128)S(1)} %copy-done.3, f32[512,512]{1,0:T(8,128)S(1)} %copy-done.2), kind=kLoop, calls=%fused_computation.5 | loop fusion | flops 1048576 | bytes 8388608 | tf_op jit(solution)/shard_map/concatenate | solution.py:222
  301.0 80.9 %reduce-scatter.2.cloned.1.call-done = bf16[256,2048]{1,0:T(8,128)(2,1)} async-done(((bf16[2048,2048]{1,0:T(8,128)(2,1)}), bf16[256,2048]{1,0:T(8,128)(2,1)}) %reduce-scatter.2.cloned.1.call-update) | async-done | bytes 1048592 | tf_op jit(solution)/shard_map/reduce_scatter | solution.py:220
  (55 shorter events, 3.1 us)
Async XLA Ops:
  7.2 177.2 %all-gather.3.cloned.1.call-start = ((), (), s32[]{:S(2)}) async-start(), calls=%async_computation.2 | async-start | bytes 9437184 | tf_op jit(solution)/shard_map/all_gather | solution.py:175
  8.4 12.5 %collective-permute-start.1 = (bf16[256,512]{1,0:T(8,128)(2,1)S(1)}, bf16[256,512]{1,0:T(8,128)(2,1)S(1)}, u32[]{:S(2)}, u32[]{:S(2)}) collective-permute-start(bf16[256,512]{1,0:T(8,128)(2,1)S(1)} %bitcast.61), channel_id=1, source_target_pairs={{0,1},{1,0},{2,3},{3,2},{4,5},{5,4},{6,7},{7,6},{8,9},{9,8},{10,11... | collective-permute-start | bytes 786440 | tf_op jit(solution)/shard_map/ppermute | solution.py:121
  11.4 40.2 %collective-permute-start = (bf16[512,1024]{1,0:T(8,128)(2,1)}, bf16[512,1024]{1,0:T(8,128)(2,1)}, u32[]{:S(2)}, u32[]{:S(2)}) collective-permute-start(bf16[512,1024]{1,0:T(8,128)(2,1)} %param.7), channel_id=1, source_target_pairs={{0,0},{1,1},{2,2},{3,3},{4,4},{5,5},{6,6},{7,7},{8,14},{9,15},{10,... | collective-permute-start | bytes 3145736 | tf_op jit(solution)/shard_map/ppermute | solution.py:121
  21.0 30.4 %collective-permute-start.2 = (bf16[2,256,512]{2,1,0:T(8,128)(2,1)S(1)}, bf16[2,256,512]{2,1,0:T(8,128)(2,1)S(1)}, u32[]{:S(2)}, u32[]{:S(2)}) collective-permute-start(bf16[2,256,512]{2,1,0:T(8,128)(2,1)S(1)} %pad_maximum_fusion.10), channel_id=1, source_target_pairs={{0,4},{1,5},{2,6},{3,7},{4,0},{5,1},{6,2},{7,3},{8,12},{9,13},{10,... | collective-permute-start | bytes 1572872 | tf_op jit(solution)/shard_map/ppermute | solution.py:121
  51.6 1.9 collective-permute-start.6
  53.5 1.0 copy-start.8
  54.4 327.5 %reduce-scatter.2.cloned.1.call-start = ((), (), s32[]{:S(2)}) async-start(), calls=%async_computation.1 | async-start | bytes 9437184 | tf_op jit(solution)/shard_map/reduce_scatter | solution.py:220
  54.5 36.6 %collective-permute-start.3 = (bf16[2,2,256,512]{3,2,1,0:T(8,128)(2,1)S(1)}, bf16[2,2,256,512]{3,2,1,0:T(8,128)(2,1)S(1)}, u32[]{:S(2)}, u32[]{:S(2)}) collective-permute-start(bf16[2,2,256,512]{3,2,1,0:T(8,128)(2,1)S(1)} %pad_maximum_fusion.7), channel_id=1, source_target_pairs={{0,2},{1,3},{2,0},{3,1},{4,6},{5,7},{6,4},{7,5},{8,10},{9,11},{10,... | collective-permute-start | bytes 3145736 | tf_op jit(solution)/shard_map/ppermute | solution.py:121
  91.4 76.2 %collective-permute-start.4 = (bf16[2048,512]{1,0:T(8,128)(2,1)S(1)}, bf16[2048,512]{1,0:T(8,128)(2,1)S(1)}, u32[]{:S(2)}, u32[]{:S(2)}) collective-permute-start(bf16[2048,512]{1,0:T(8,128)(2,1)S(1)} %bitcast.54), channel_id=1, source_target_pairs={{0,16},{1,17},{2,18},{3,19},{4,20},{5,21},{6,22},{7,23},{8,24},{9,... | collective-permute-start | bytes 6291464 | tf_op jit(solution)/shard_map/ppermute | solution.py:121
  167.6 2.7 copy-start.1
  170.2 7.5 %collective-permute-start.5 = (bf16[2048,1024]{1,0:T(8,128)(2,1)}, bf16[2048,1024]{1,0:T(8,128)(2,1)}, u32[]{:S(2)}, u32[]{:S(2)}) collective-permute-start(bf16[2048,1024]{1,0:T(8,128)(2,1)} %pad_maximum_fusion.1), channel_id=1, source_target_pairs={{0,8},{1,9},{2,10},{3,11},{4,12},{5,13},{6,14},{7,15},{8,0},{9,1},... | collective-permute-start | bytes 12582920 | tf_op jit(solution)/shard_map/ppermute | solution.py:121
  184.4 13.0 %copy-start = (bf16[2048,2048]{1,0:T(8,128)(2,1)S(1)}, bf16[2048,2048]{1,0:T(8,128)(2,1)}, u32[]{:S(2)}) copy-start(bf16[2048,2048]{1,0:T(8,128)(2,1)} %pad_maximum_fusion) | copy-start | bytes 25165828
  199.9 7.0 %collective-permute-start.8 = (bf16[512,512]{1,0:T(8,128)(2,1)S(1)}, bf16[512,512]{1,0:T(8,128)(2,1)S(1)}, u32[]{:S(2)}, u32[]{:S(2)}) collective-permute-start(bf16[512,512]{1,0:T(8,128)(2,1)S(1)} %fusion.34), channel_id=1, source_target_pairs={{0,8},{1,9},{2,10},{3,11},{4,12},{5,13},{6,14},{7,15},{8,0},{9,1},... | collective-permute-start | bytes 1572872 | tf_op jit(solution)/shard_map/ppermute | solution.py:121
  200.1 10.7 %collective-permute-start.7 = (bf16[512,512]{1,0:T(8,128)(2,1)S(1)}, bf16[512,512]{1,0:T(8,128)(2,1)S(1)}, u32[]{:S(2)}, u32[]{:S(2)}) collective-permute-start(bf16[512,512]{1,0:T(8,128)(2,1)S(1)} %fusion.28), channel_id=1, source_target_pairs={{0,8},{1,9},{2,10},{3,11},{4,12},{5,13},{6,14},{7,15},{8,0},{9,1},... | collective-permute-start | bytes 1572872 | tf_op jit(solution)/shard_map/ppermute | solution.py:121
  205.5 4.8 %collective-permute-start.11 = (bf16[512,512]{1,0:T(8,128)(2,1)S(1)}, bf16[512,512]{1,0:T(8,128)(2,1)S(1)}, u32[]{:S(2)}, u32[]{:S(2)}) collective-permute-start(bf16[512,512]{1,0:T(8,128)(2,1)S(1)} %fusion.37), channel_id=1, source_target_pairs={{0,8},{1,9},{2,10},{3,11},{4,12},{5,13},{6,14},{7,15},{8,0},{9,1},... | collective-permute-start | bytes 1572872 | tf_op jit(solution)/shard_map/ppermute | solution.py:121
  207.1 14.8 %collective-permute-start.9 = (bf16[512,512]{1,0:T(8,128)(2,1)S(1)}, bf16[512,512]{1,0:T(8,128)(2,1)S(1)}, u32[]{:S(2)}, u32[]{:S(2)}) collective-permute-start(bf16[512,512]{1,0:T(8,128)(2,1)S(1)} %add_convert_fusion.1), channel_id=1, source_target_pairs={{0,16},{1,17},{2,18},{3,19},{4,20},{5,21},{6,22},{7,23},{8,24},{9,... | collective-permute-start | bytes 1572872 | tf_op jit(solution)/shard_map/ppermute | solution.py:121
  208.9 13.0 %copy-start.4 = (f32[512,1024]{1,0:T(8,128)S(1)}, f32[512,1024]{1,0:T(8,128)}, u32[]{:S(2)}) copy-start(f32[512,1024]{1,0:T(8,128)} %param.10) | copy-start | bytes 6291460
  208.9 13.0 %copy-start.5 = (f32[512,1024]{1,0:T(8,128)S(1)}, f32[512,1024]{1,0:T(8,128)}, u32[]{:S(2)}) copy-start(f32[512,1024]{1,0:T(8,128)} %param.11) | copy-start | bytes 6291460
  210.2 13.6 %collective-permute-start.10 = (bf16[512,512]{1,0:T(8,128)(2,1)S(1)}, bf16[512,512]{1,0:T(8,128)(2,1)S(1)}, u32[]{:S(2)}, u32[]{:S(2)}) collective-permute-start(bf16[512,512]{1,0:T(8,128)(2,1)S(1)} %fusion.31), channel_id=1, source_target_pairs={{0,8},{1,9},{2,10},{3,11},{4,12},{5,13},{6,14},{7,15},{8,0},{9,1},... | collective-permute-start | bytes 1572872 | tf_op jit(solution)/shard_map/ppermute | solution.py:121
  210.5 22.1 %collective-permute-start.12 = (bf16[512,512]{1,0:T(8,128)(2,1)S(1)}, bf16[512,512]{1,0:T(8,128)(2,1)S(1)}, u32[]{:S(2)}, u32[]{:S(2)}) collective-permute-start(bf16[512,512]{1,0:T(8,128)(2,1)S(1)} %add_convert_fusion), channel_id=1, source_target_pairs={{0,16},{1,17},{2,18},{3,19},{4,20},{5,21},{6,22},{7,23},{8,24},{9,... | collective-permute-start | bytes 1572872 | tf_op jit(solution)/shard_map/ppermute | solution.py:121
  223.8 12.7 %copy-start.6 = (bf16[512,512]{1,0:T(8,128)(2,1)}, bf16[512,512]{1,0:T(8,128)(2,1)S(1)}, u32[]{:S(2)}) copy-start(bf16[512,512]{1,0:T(8,128)(2,1)S(1)} %get-tuple-element.46) | copy-start | bytes 1572868
  234.8 14.9 %copy-start.7 = (bf16[512,512]{1,0:T(8,128)(2,1)}, bf16[512,512]{1,0:T(8,128)(2,1)S(1)}, u32[]{:S(2)}) copy-start(bf16[512,512]{1,0:T(8,128)(2,1)S(1)} %get-tuple-element.43) | copy-start | bytes 1572868
  234.8 14.8 %collective-permute-start.15 = (bf16[512,512]{1,0:T(8,128)(2,1)S(1)}, bf16[512,512]{1,0:T(8,128)(2,1)S(1)}, u32[]{:S(2)}, u32[]{:S(2)}) collective-permute-start(bf16[512,512]{1,0:T(8,128)(2,1)S(1)} %get-tuple-element.43), channel_id=1, source_target_pairs={{0,16},{1,17},{2,18},{3,19},{4,20},{5,21},{6,22},{7,23},{8,24},{9,... | collective-permute-start | bytes 1572872 | tf_op jit(solution)/shard_map/ppermute | solution.py:121
  236.5 23.0 %collective-permute-start.13 = (bf16[512,512]{1,0:T(8,128)(2,1)S(1)}, bf16[512,512]{1,0:T(8,128)(2,1)}, u32[]{:S(2)}, u32[]{:S(2)}) collective-permute-start(bf16[512,512]{1,0:T(8,128)(2,1)S(1)} %get-tuple-element.46), channel_id=1, source_target_pairs={{0,16},{1,17},{2,18},{3,19},{4,20},{5,21},{6,22},{7,23},{8,24},{9,... | collective-permute-start | bytes 1572872 | tf_op jit(solution)/shard_map/ppermute | solution.py:121
  249.6 0.8 copy-start.9
  262.2 3.0 collective-permute-start.16
  262.3 13.7 %collective-permute-start.14 = (bf16[2,512,512]{2,1,0:T(8,128)(2,1)S(1)}, bf16[2,512,512]{2,1,0:T(8,128)(2,1)S(1)}, u32[]{:S(2)}, u32[]{:S(2)}) collective-permute-start(bf16[2,512,512]{2,1,0:T(8,128)(2,1)S(1)} %pad_maximum_fusion.8), channel_id=1, source_target_pairs={{0,8},{1,9},{2,10},{3,11},{4,12},{5,13},{6,14},{7,15},{8,0},{9,1},... | collective-permute-start | bytes 3145736 | tf_op jit(solution)/shard_map/ppermute | solution.py:121
  266.9 9.6 %slice-start = ((s8[8388608]{0:T(1024)(128)(4,1)}), s8[4194304]{0:T(1024)(128)(4,1)S(1)}, s32[]{:S(2)}) async-start(s8[8388608]{0:T(1024)(128)(4,1)} %bitcast.57), calls=%async_computation.3 | async-start | bytes 8388608
  267.1 9.5 %slice-start.1 = ((s8[8388608]{0:T(1024)(128)(4,1)}), s8[4194304]{0:T(1024)(128)(4,1)S(1)}, s32[]{:S(2)}) async-start(s8[8388608]{0:T(1024)(128)(4,1)} %bitcast.57), calls=%async_computation.4 | async-start | bytes 8388608
  295.6 1.2 copy-start.2
  295.6 1.5 copy-start.3
Sparse Core Ops, SparseCore 0:
  54.6 120.2 all-gather.2
  295.8 86.1 reduce-scatter.1

commit v3 on v2

--- a/solution.py
+++ b/solution.py
@@ -23,14 +23,6 @@
 
 def matmul(a, b):
     return lax.dot_general(a, b, (((1,), (0,)), ((), ())), preferred_element_type=jnp.float32)
-
-
-def matmul_tn(a, b):
-    return lax.dot_general(a, b, (((0,), (0,)), ((), ())), preferred_element_type=jnp.float32)
-
-
-def matmul_nt(a, b):
-    return lax.dot_general(a, b, (((1,), (1,)), ((), ())), preferred_element_type=jnp.float32)
 
 
 def cost(flops, *arrays):
@@ -73,33 +65,29 @@
     )(places, *([gathered] * nx), right)
 
 
-def back_rotation(columns, right, places, block):
+def back_rotation(columns, right_t, block):
     parts = len(columns)
     total_rows, width = columns[0].shape
-    count = total_rows // block
-
-    def kernel(places_ref, *refs):
+
+    def kernel(*refs):
         rows_of, right_ref, out = refs[:parts], refs[parts], refs[parts + 1]
-        total = matmul_nt(rows_of[0][...], right_ref[:, :width])
+        total = matmul(rows_of[0][...], right_ref[:width])
         for j in range(1, parts):
-            total += matmul_nt(rows_of[j][...], right_ref[:, j * width : (j + 1) * width])
+            total += matmul(rows_of[j][...], right_ref[j * width : (j + 1) * width])
         out[...] = total.astype(out.dtype)
 
-    out = jax.ShapeDtypeStruct((total_rows, right.shape[0]), low)
+    out = jax.ShapeDtypeStruct((total_rows, right_t.shape[1]), low)
     return pl.pallas_call(
         kernel,
         out_shape=out,
-        grid_spec=pltpu.PrefetchScalarGridSpec(
-            num_scalar_prefetch=1,
-            grid=(count,),
-            in_specs=[pl.BlockSpec((block, width), lambda k, p: (p[k], 0))] * parts
-            + [pl.BlockSpec(right.shape, lambda k, p: (0, 0), pipeline_mode=pl.Buffered(1))],
-            out_specs=pl.BlockSpec((block, right.shape[0]), lambda k, p: (k, 0)),
-        ),
+        grid=(total_rows // block,),
+        in_specs=[pl.BlockSpec((block, width), lambda k: (k, 0))] * parts
+        + [pl.BlockSpec(right_t.shape, lambda k: (0, 0), pipeline_mode=pl.Buffered(1))],
+        out_specs=pl.BlockSpec((block, right_t.shape[1]), lambda k: (k, 0)),
         compiler_params=pltpu.CompilerParams(vmem_limit_bytes=VMEM_BYTES),
-        cost_estimate=cost(2 * total_rows * right.size, right, out, *columns),
+        cost_estimate=cost(2 * total_rows * right_t.size, right_t, out, *columns),
         name="back_rotation",
-    )(places, *columns, right)
+    )(*columns, right_t)
 
 
 def per_device(gradient, left_basis, right_basis, first_moment, second_moment, *, nb, nd):
@@ -157,26 +145,32 @@
     for t in reversed(bits):
         order = order + [s | t for s in order]
     half_places = [[order.index(unspread[bb ^ zz] ^ bb) for zz in range(nz)] for bb in range(nb)]
-    back_places = [[order.index(bb ^ (dd // nx)) * nx + dd % nx for dd in path] for bb in range(nb)]
     half_places = jnp.array(half_places, jnp.int32)[b]
-    back_places = jnp.array(back_places, jnp.int32)[b]
+    order_of = jnp.array([order.index(t) for t in range(nb)], jnp.int32)
+    path_places = [order_of[b ^ (dd // nx)] * rows + dd % nx * out_rows for dd in path]
 
     left_t = left_basis.astype(low).T
     right = right_basis.astype(low)
+    right_t = right.T
     piece = permute(gradient, lambda bb, zz, xx: (bb, zz ^ spread(bb), xx))
-    for i, u in enumerate(reversed(x_bits)):
-        left_t = joined(left_t, move_x(left_t, u), (x & u) != 0, i)
-    for i, t in enumerate(reversed(bits[1:])):
+    for i, t in enumerate(reversed(bits)):
         left_t = joined(left_t, move_z(left_t, t), (z & t) != 0, i)
-    piece, left_t, right, half_places, back_places = lax.optimization_barrier(
-        (piece, left_t, right, half_places, back_places)
+    piece, left_t, right, right_t, half_places, path_places = lax.optimization_barrier(
+        (piece, left_t, right, right_t, half_places, path_places)
     )
     piece = permute(piece, lambda bb, zz, xx: (zz ^ spread(bb), zz, xx))
     gathered = lax.all_gather(piece, "dp", axis_index_groups=[path])
-    left_t = joined(left_t, move_z(left_t, bits[0]), (z & bits[0]) != 0, len(bits) - 1).reshape(whole, rows)
+    for i, u in enumerate(reversed(x_bits)):
+        other, piece = lax.optimization_barrier((move_x(left_t, u), piece))
+        left_t = joined(left_t, other, (x & u) != 0, len(bits) + i)
+    left_t = left_t.reshape(whole, rows)
     for t in reversed(bits):
         left_t = jnp.concatenate([left_t, move_b(left_t, t)], axis=1)
-    left_t, gathered = lax.optimization_barrier((left_t, gathered))
+    left_t = lax.optimization_barrier(left_t)
+    left = jnp.concatenate(
+        [lax.dynamic_slice_in_dim(left_t, start, out_rows, 1).T for start in path_places], axis=0
+    )
+    left_t, left, gathered = lax.optimization_barrier((left_t, left, gathered))
 
     half = list(half_rotation(gathered, right, half_places, nz, COL_PARTS))
 
@@ -185,7 +179,7 @@
         return matmul(rows_of, half[j]).astype(low)
 
     width = ff_block // COL_PARTS
-    first_out, second_out, back = [], [], []
+    first_out, second_out, back, joins = [], [], [], []
     for j in range(COL_PARTS):
         cols = slice(j * width, (j + 1) * width)
         if j:
@@ -196,8 +190,11 @@
         held = {t: held[t].astype(jnp.float32) + got.astype(jnp.float32) for t, got in zip(held, gots)}
         for t in reversed(bits[1:]):
             for s in [s for s in held if s & t]:
-                held[s ^ t] = held[s ^ t] + move_b(held.pop(s).astype(low), t).astype(jnp.float32)
-        rotated = held[0]
+                away = held.pop(s).astype(low)
+                if j:
+                    away = after(away, summed)
+                held[s ^ t] = held[s ^ t] + move_b(away, t).astype(jnp.float32)
+        rotated = summed = held[0]
         moments = first_moment[:, cols], second_moment[:, cols]
         if j:
             moments = after(moments, previous)
@@ -211,12 +208,16 @@
         column = previous = direction.astype(low)
         axis = 0
         for t in reversed(bits):
-            column = joined(column, move_b(column, t), (b & t) != 0, axis)
+            other = move_b(column, t)
+            if j:
+                other = after(other, joins[axis])
+            column = joined(column, other, (b & t) != 0, axis)
+            joins[axis : axis + 1] = [column]
             axis += 1
         column = lax.optimization_barrier(column.reshape(whole, width))
-        back.append(lax.optimization_barrier(matmul_tn(left_t, column).astype(low)))
-
-    total = back_rotation(back, right, back_places, out_rows)
+        back.append(lax.optimization_barrier(matmul(left, column).astype(low)))
+
+    total = back_rotation(back, right_t, rows)
     update = lax.psum_scatter(total, "dp", scatter_dimension=0, axis_index_groups=[path], tiled=True)
     return (
         jnp.concatenate(first_out, axis=1),

time: 390 us -> 394 us (1.010)
  local copies, waits for them, and re-layouts: 6.13 us -> 33.4 us
  waiting for transfers between devices: 218 us -> 202 us
  starting transfers between devices: 70 us -> 62.8 us
  other arithmetic: 29 us -> 22.9 us
  matrix products: 23.7 us -> 28.7 us
    ppermute x17, waiting for transfers between devices: 138 us -> 114 us  [permute(): return lax.ppermute(value, ('basis', 'dp'), pairs)]
    unnamed x25 -> x35, local copies, waits for them, and re-layouts: 4.49 us -> 23.8 us
    dot_general x8 -> x10, matrix products: 9.95 us -> 28.7 us  [matmul(): lax.dot_general(a, b, (((1,), (0,)), ((), ())), preferred_element_type=jn...]
    dot_general x2 -> x0, matrix products: 13.7 us -> none  [matmul_tn(): lax.dot_general(a, b, (((0,), (0,)), ((), ())), preferred_element_type=jn...]
    reduce_scatter x1, waiting for transfers between devices: 80.9 us -> 88.3 us  [per_device(): lax.psum_scatter(total, 'dp', scatter_dimension=0, axis_index_groups=[pat...]
    ppermute x17, starting transfers between devices: 69.9 us -> 62.8 us  [permute(): return lax.ppermute(value, ('basis', 'dp'), pairs)]
    optimization_barrier x0 -> x1, local copies, waits for them, and re-layouts: none -> 6.43 us  [per_device(): lax.optimization_barrier((piece, left_t, right, right_t, half_places, pat...]
    convert_element_type x3 -> x2, other arithmetic: 6.3 us -> 1.1 us  [per_device(): away = held.pop(s).astype(low)]
  transfers between devices with their start and end apart: 19 -> 19, of which waited for: 10 -> 10; matrix products, arithmetic and copies ran while one was open for 11% -> 17% of each run, Pallas kernels for 0% -> 0%
where the time goes in v3:
time: 394 us; the launch traced here: 393 us
  waiting for transfers between devices  202 us (51%)
  starting transfers between devices  62.8 us (16%)
  local copies, waits for them, and re-layouts  33.4 us (8%)
  matrix products  28.7 us (7%)
  Pallas kernels  26.2 us (7%)
  other arithmetic  22.9 us (6%)
  between operations  17 us (4%)
    ppermute x17, waiting for transfers between devices, permute(): return lax.ppermute(value, ('basis', 'dp'), pairs)  114 us
    reduce_scatter x1, waiting for transfers between devices, per_device(): lax.psum_scatter(total, 'dp', scatter_dimension=0, axis_index_groups=[pat...  88.3 us
    ppermute x17, starting transfers between devices, permute(): return lax.ppermute(value, ('basis', 'dp'), pairs)  62.8 us
    dot_general x10, matrix products, matmul(): lax.dot_general(a, b, (((1,), (0,)), ((), ())), preferred_element_type=jn...  28.7 us
    unnamed x35, local copies, waits for them, and re-layouts  23.8 us
    pallas_call x1, Pallas kernels, half_rotation(): pl.pallas_call(kernel, out_shape=outs, grid_spec=pltpu.PrefetchScalarGrid...  13.2 us
    pallas_call x1, Pallas kernels, back_rotation(): pl.pallas_call(kernel, out_shape=out, grid=(total_rows // block,), in_spe...  13 us
  transfers between devices with their start and end apart: 19, of which 10 were waited for; matrix products, arithmetic and copies ran while one was open for 17% of the time, Pallas kernels for 0%

profile of v3, /device:TPU:0, one launch (start us, length us, event | category | flops | bytes accessed | tf_op | source)
XLA Modules:
  0.0 393.0 jit_solution(1512928491915214618)
XLA Ops:
  7.2 1.2 copy.12
  8.4 4.1 %collective-permute-start.1 = (bf16[256,512]{1,0:T(8,128)(2,1)S(1)}, bf16[256,512]{1,0:T(8,128)(2,1)S(1)}, u32[]{:S(2)}, u32[]{:S(2)}) collective-permute-start(bf16[256,512]{1,0:T(8,128)(2,1)S(1)} %bitcast.81), channel_id=1, source_target_pairs={{0,4},{1,5},{2,6},{3,7},{4,0},{5,1},{6,2},{7,3},{8,12},{9,13},{10,... | collective-permute-start | bytes 786440 | tf_op jit(solution)/shard_map/ppermute | solution.py:109
  12.5 1.9 collective-permute-start
  14.4 22.1 %collective-permute-done.1 = bf16[256,512]{1,0:T(8,128)(2,1)S(1)} collective-permute-done((bf16[256,512]{1,0:T(8,128)(2,1)S(1)}, bf16[256,512]{1,0:T(8,128)(2,1)S(1)}, u32[]{:S(2)}, u32[]{:S(2)}) %collective-permute-start.1) | collective-permute-done | bytes 262176 | tf_op jit(solution)/shard_map/ppermute | solution.py:109
  40.0 7.4 %copy.14 = bf16[2048,1024]{0,1:T(8,128)(2,1)} copy(f32[2048,1024]{1,0:T(8,128)} %param.9) | data formatting | bytes 12582912 | tf_op args[2]
  50.1 1.9 collective-permute-start.4
  53.0 1.3 collective-permute-start.3
  54.3 13.6 %collective-permute-done.3 = bf16[2,2,256,512]{3,2,1,0:T(8,128)(2,1)S(1)} collective-permute-done((bf16[2,2,256,512]{3,2,1,0:T(8,128)(2,1)S(1)}, bf16[2,2,256,512]{3,2,1,0:T(8,128)(2,1)S(1)}, u32[]{:S(2)}, u32[]{:S(2)}) %collective-permute-start.3) | collective-permute-done | bytes 1048608 | tf_op jit(solution)/shard_map/ppermute | solution.py:109
  68.2 47.2 %collective-permute-start.5 = (bf16[2048,512]{1,0:T(8,128)(2,1)S(1)}, bf16[2048,512]{1,0:T(8,128)(2,1)S(1)}, u32[]{:S(2)}, u32[]{:S(2)}) collective-permute-start(bf16[2048,512]{1,0:T(8,128)(2,1)S(1)} %bitcast.75), channel_id=1, source_target_pairs={{0,16},{1,17},{2,18},{3,19},{4,20},{5,21},{6,22},{7,23},{8,24},{9,... | collective-permute-start | bytes 6291464 | tf_op jit(solution)/shard_map/ppermute | solution.py:109
  115.5 39.1 %collective-permute-done.5 = bf16[2048,512]{1,0:T(8,128)(2,1)S(1)} collective-permute-done((bf16[2048,512]{1,0:T(8,128)(2,1)S(1)}, bf16[2048,512]{1,0:T(8,128)(2,1)S(1)}, u32[]{:S(2)}, u32[]{:S(2)}) %collective-permute-start.5) | collective-permute-done | bytes 2097184 | tf_op jit(solution)/shard_map/ppermute | solution.py:109
  154.6 2.7 pad_maximum_fusion.1
  157.3 6.4 %copy.16.refs_2_ = bf16[2048,1024]{1,0:T(8,128)(2,1)} copy(bf16[2048,1024]{0,1:T(8,128)(2,1)} %copy.14) | data formatting | bytes 8388608 | tf_op jit(solution)/shard_map/optimization_barrier | solution.py:158
  164.8 3.8 pad_maximum_fusion
  168.6 1.8 bitcast_dynamic-update-slice_fusion.7
  170.4 2.1 bitcast_dynamic-update-slice_fusion.6
  172.5 1.6 bitcast_dynamic-update-slice_fusion.5
  174.1 1.6 bitcast_dynamic-update-slice_fusion.4
  175.6 1.5 bitcast_dynamic-update-slice_fusion.3
  177.1 1.5 bitcast_dynamic-update-slice_fusion.2
  178.6 1.5 bitcast_dynamic-update-slice_fusion.1
  180.1 1.5 bitcast_dynamic-update-slice_fusion
  181.7 13.2 %half_rotation.1 = (bf16[2048,512]{1,0:T(8,128)(2,1)S(1)}, bf16[2048,512]{1,0:T(8,128)(2,1)S(1)}) custom-call(s32[4]{0:T(128)S(1)} %fusion.50.places_ref, bf16[8,512,1024]{2,1,0:T(8,128)(2,1)} %bitcast.82, bf16[8,512,1024]{2,1,0:T(8,128)(2,1)} %bitcast.83, bf16[2048,1024]{1,0:T(8,128)(2,1)} %copy.16.refs_2_), custom_call_target="tpu_custom_call" | custom-call | flops 8589934592 | bytes 16777216 | tf_op jit(solution)/shard_map/half_rotation/pallas_call | solution.py:52
  194.9 1.2 fusion.22
  196.1 1.2 fusion.34
  197.4 1.2 fusion.28
  198.8 1.2 fusion.16
  200.5 1.2 fusion.37
  201.9 1.9 collective-permute-start.9
  203.8 2.0 fusion.31
  205.8 1.2 fusion.25
  207.1 8.9 %collective-permute-done.9 = bf16[512,512]{1,0:T(8,128)(2,1)S(1)} collective-permute-done((bf16[512,512]{1,0:T(8,128)(2,1)S(1)}, bf16[512,512]{1,0:T(8,128)(2,1)S(1)}, u32[]{:S(2)}, u32[]{:S(2)}) %collective-permute-start.9) | collective-permute-done | bytes 524320 | tf_op jit(solution)/shard_map/ppermute | solution.py:109
  216.0 2.2 divide_convert_fusion.1
  218.2 1.7 collective-permute-start.13
  220.0 2.1 fusion.19
  223.3 9.9 %collective-permute-done.13 = bf16[512,512]{1,0:T(8,128)(2,1)} collective-permute-done((bf16[512,512]{1,0:T(8,128)(2,1)S(1)}, bf16[512,512]{1,0:T(8,128)(2,1)}, u32[]{:S(2)}, u32[]{:S(2)}) %collective-permute-start.13) | collective-permute-done | bytes 524320 | tf_op jit(solution)/shard_map/ppermute | solution.py:109
  233.2 1.3 select_bitcast_fusion.9
  235.5 7.2 %collective-permute-done.12 = bf16[512,512]{1,0:T(8,128)(2,1)} collective-permute-done((bf16[512,512]{1,0:T(8,128)(2,1)}, bf16[512,512]{1,0:T(8,128)(2,1)}, u32[]{:S(2)}, u32[]{:S(2)}) %collective-permute-start.12) | collective-permute-done | bytes 524320 | tf_op jit(solution)/shard_map/ppermute | solution.py:109
  242.8 3.3 divide_convert_fusion
  246.1 1.7 collective-permute-start.15
  247.8 10.8 %collective-permute-done.15 = bf16[512,512]{1,0:T(8,128)(2,1)S(1)} collective-permute-done((bf16[512,512]{1,0:T(8,128)(2,1)}, bf16[512,512]{1,0:T(8,128)(2,1)S(1)}, u32[]{:S(2)}, u32[]{:S(2)}) %collective-permute-start.15) | collective-permute-done | bytes 524320 | tf_op jit(solution)/shard_map/ppermute | solution.py:109
  258.6 1.1 select_bitcast_fusion.7
  259.9 1.4 select_bitcast_fusion.3
  261.6 8.7 %convolution_convert_fusion.1.refs_0_ = bf16[2048,512]{1,0:T(8,128)(2,1)S(1)} fusion(bf16[2048,2048]{0,1:T(8,128)(2,1)} %bitcast_dynamic-update-slice_fusion, bf16[2048,512]{1,0:T(8,128)(2,1)S(1)} %bitcast.80), kind=kOutput, calls=%fused_computation.3 | convolution fusion | flops 4296015872 | bytes 12582912 | tf_op jit(solution)/shard_map/dot_general | solution.py:25
  270.8 8.5 %convolution_convert_fusion.refs_1_ = bf16[2048,512]{1,0:T(8,128)(2,1)S(1)} fusion(bf16[2048,2048]{0,1:T(8,128)(2,1)} %bitcast_dynamic-update-slice_fusion, bf16[2048,512]{1,0:T(8,128)(2,1)S(1)} %bitcast.79), kind=kOutput, calls=%fused_computation.2 | convolution fusion | flops 4296015872 | bytes 12582912 | tf_op jit(solution)/shard_map/dot_general | solution.py:25
  279.3 13.0 %back_rotation.1 = bf16[2048,2048]{1,0:T(8,128)(2,1)} custom-call(bf16[2048,512]{1,0:T(8,128)(2,1)S(1)} %convolution_convert_fusion.1.refs_0_, bf16[2048,512]{1,0:T(8,128)(2,1)S(1)} %convolution_convert_fusion.refs_1_, bf16[1024,2048]{1,0:T(8,128)(2,1)} %bitcast.78), custom_call_target="tpu_custom_call" | custom-call | flops 8589934592 | bytes 16777216 | tf_op jit(solution)/shard_map/back_rotation/pallas_call | solution.py:80
  292.4 1.2 copy-done.3
  294.2 3.7 pad_maximum_fusion.3
  297.9 88.3 %reduce-scatter.2.cloned.1.call-done = bf16[256,2048]{1,0:T(8,128)(2,1)} async-done(((bf16[2048,2048]{1,0:T(8,128)(2,1)}), bf16[256,2048]{1,0:T(8,128)(2,1)}) %reduce-scatter.2.cloned.1.call-update) | async-done | bytes 1048592 | tf_op jit(solution)/shard_map/reduce_scatter | solution.py:221
  (66 shorter events, 10.8 us)
Async XLA Ops:
  7.2 29.5 %copy-start.11 = (s32[4]{0:T(128)S(1)}, s32[4]{0:T(128)}, u32[]{:S(2)}) copy-start(s32[4]{0:T(128)} %constant.66.clone) | copy-start | bytes 52
  7.2 174.5 %all-gather.3.cloned.1.call-start = ((), (), s32[]{:S(2)}) async-start(), calls=%async_computation.2 | async-start | bytes 9437184 | tf_op jit(solution)/shard_map/all_gather | solution.py:162
  8.4 28.1 %collective-permute-start.1 = (bf16[256,512]{1,0:T(8,128)(2,1)S(1)}, bf16[256,512]{1,0:T(8,128)(2,1)S(1)}, u32[]{:S(2)}, u32[]{:S(2)}) collective-permute-start(bf16[256,512]{1,0:T(8,128)(2,1)S(1)} %bitcast.81), channel_id=1, source_target_pairs={{0,4},{1,5},{2,6},{3,7},{4,0},{5,1},{6,2},{7,3},{8,12},{9,13},{10,... | collective-permute-start | bytes 786440 | tf_op jit(solution)/shard_map/ppermute | solution.py:109
  12.5 36.6 %collective-permute-start = (bf16[512,1024]{1,0:T(8,128)(2,1)}, bf16[512,1024]{1,0:T(8,128)(2,1)S(1)}, u32[]{:S(2)}, u32[]{:S(2)}) collective-permute-start(bf16[512,1024]{1,0:T(8,128)(2,1)} %param.7), channel_id=1, source_target_pairs={{0,0},{1,1},{2,2},{3,3},{4,4},{5,5},{6,6},{7,7},{8,14},{9,15},{10,... | collective-permute-start | bytes 3145736 | tf_op jit(solution)/shard_map/ppermute | solution.py:109
  36.6 12.3 %collective-permute-start.2 = (bf16[2,256,512]{2,1,0:T(8,128)(2,1)S(1)}, bf16[2,256,512]{2,1,0:T(8,128)(2,1)S(1)}, u32[]{:S(2)}, u32[]{:S(2)}) collective-permute-start(bf16[2,256,512]{2,1,0:T(8,128)(2,1)S(1)} %pad_maximum_fusion.10), channel_id=1, source_target_pairs={{0,2},{1,3},{2,0},{3,1},{4,6},{5,7},{6,4},{7,5},{8,10},{9,11},{10,... | collective-permute-start | bytes 1572872 | tf_op jit(solution)/shard_map/ppermute | solution.py:109
  49.1 1.0 copy-start.12
  50.1 1.9 collective-permute-start.4
  52.0 1.0 copy-start.9
  53.0 333.2 %reduce-scatter.2.cloned.1.call-start = ((), (), s32[]{:S(2)}) async-start(), calls=%async_computation.1 | async-start | bytes 9437184 | tf_op jit(solution)/shard_map/reduce_scatter | solution.py:221
  53.0 14.9 %collective-permute-start.3 = (bf16[2,2,256,512]{3,2,1,0:T(8,128)(2,1)S(1)}, bf16[2,2,256,512]{3,2,1,0:T(8,128)(2,1)S(1)}, u32[]{:S(2)}, u32[]{:S(2)}) collective-permute-start(bf16[2,2,256,512]{3,2,1,0:T(8,128)(2,1)S(1)} %pad_maximum_fusion.7), channel_id=1, source_target_pairs={{0,1},{1,0},{2,3},{3,2},{4,5},{5,4},{6,7},{7,6},{8,9},{9,8},{10,11... | collective-permute-start | bytes 3145736 | tf_op jit(solution)/shard_map/ppermute | solution.py:109
  68.2 86.3 %collective-permute-start.5 = (bf16[2048,512]{1,0:T(8,128)(2,1)S(1)}, bf16[2048,512]{1,0:T(8,128)(2,1)S(1)}, u32[]{:S(2)}, u32[]{:S(2)}) collective-permute-start(bf16[2048,512]{1,0:T(8,128)(2,1)S(1)} %bitcast.75), channel_id=1, source_target_pairs={{0,16},{1,17},{2,18},{3,19},{4,20},{5,21},{6,22},{7,23},{8,24},{9,... | collective-permute-start | bytes 6291464 | tf_op jit(solution)/shard_map/ppermute | solution.py:109
  154.5 2.7 copy-start.2
  157.3 7.5 %collective-permute-start.6 = (bf16[2048,1024]{1,0:T(8,128)(2,1)}, bf16[2048,1024]{1,0:T(8,128)(2,1)}, u32[]{:S(2)}, u32[]{:S(2)}) collective-permute-start(bf16[2048,1024]{1,0:T(8,128)(2,1)} %pad_maximum_fusion.1), channel_id=1, source_target_pairs={{0,8},{1,9},{2,10},{3,11},{4,12},{5,13},{6,14},{7,15},{8,0},{9,1},... | collective-permute-start | bytes 12582920 | tf_op jit(solution)/shard_map/ppermute | solution.py:109
  168.6 11.5 %copy-start = (bf16[2048,2048]{1,0:T(8,128)(2,1)}, bf16[2048,2048]{1,0:T(8,128)(2,1)S(1)}, u32[]{:S(2)}) copy-start(bf16[2048,2048]{1,0:T(8,128)(2,1)S(1)} %pad_maximum_fusion) | copy-start | bytes 25165828
  181.7 13.2 %copy-start.1 = (bf16[2048,2048]{1,0:T(8,128)(2,1)S(1)}, bf16[2048,2048]{1,0:T(8,128)(2,1)}, u32[]{:S(2)}) copy-start(bf16[2048,2048]{1,0:T(8,128)(2,1)} %copy-done) | copy-start | bytes 25165828
  198.6 3.1 collective-permute-start.8
  200.1 7.0 %collective-permute-start.7 = (bf16[512,512]{1,0:T(8,128)(2,1)S(1)}, bf16[512,512]{1,0:T(8,128)(2,1)S(1)}, u32[]{:S(2)}, u32[]{:S(2)}) collective-permute-start(bf16[512,512]{1,0:T(8,128)(2,1)S(1)} %fusion.28), channel_id=1, source_target_pairs={{0,8},{1,9},{2,10},{3,11},{4,12},{5,13},{6,14},{7,15},{8,0},{9,1},... | collective-permute-start | bytes 1572872 | tf_op jit(solution)/shard_map/ppermute | solution.py:109
  201.9 14.1 %collective-permute-start.9 = (bf16[512,512]{1,0:T(8,128)(2,1)S(1)}, bf16[512,512]{1,0:T(8,128)(2,1)S(1)}, u32[]{:S(2)}, u32[]{:S(2)}) collective-permute-start(bf16[512,512]{1,0:T(8,128)(2,1)S(1)} %add_convert_fusion.1), channel_id=1, source_target_pairs={{0,16},{1,17},{2,18},{3,19},{4,20},{5,21},{6,22},{7,23},{8,24},{9,... | collective-permute-start | bytes 1572872 | tf_op jit(solution)/shard_map/ppermute | solution.py:109
  205.8 10.2 %copy-start.6 = (f32[512,1024]{1,0:T(8,128)S(1)}, f32[512,1024]{1,0:T(8,128)}, u32[]{:S(2)}) copy-start(f32[512,1024]{1,0:T(8,128)} %param.10) | copy-start | bytes 6291460
  205.8 10.2 %copy-start.7 = (f32[512,1024]{1,0:T(8,128)S(1)}, f32[512,1024]{1,0:T(8,128)}, u32[]{:S(2)}) copy-start(f32[512,1024]{1,0:T(8,128)} %param.11) | copy-start | bytes 6291460
  205.8 16.2 %collective-permute-start.11 = (bf16[512,512]{1,0:T(8,128)(2,1)S(1)}, bf16[512,512]{1,0:T(8,128)(2,1)S(1)}, u32[]{:S(2)}, u32[]{:S(2)}) collective-permute-start(bf16[512,512]{1,0:T(8,128)(2,1)S(1)} %fusion.37), channel_id=1, source_target_pairs={{0,8},{1,9},{2,10},{3,11},{4,12},{5,13},{6,14},{7,15},{8,0},{9,1},... | collective-permute-start | bytes 1572872 | tf_op jit(solution)/shard_map/ppermute | solution.py:109
  218.2 3.8 copy-start.8
  218.2 15.0 %collective-permute-start.13 = (bf16[512,512]{1,0:T(8,128)(2,1)S(1)}, bf16[512,512]{1,0:T(8,128)(2,1)}, u32[]{:S(2)}, u32[]{:S(2)}) collective-permute-start(bf16[512,512]{1,0:T(8,128)(2,1)S(1)} %get-tuple-element.72), channel_id=1, source_target_pairs={{0,16},{1,17},{2,18},{3,19},{4,20},{5,21},{6,22},{7,23},{8,24},{9,... | collective-permute-start | bytes 1572872 | tf_op jit(solution)/shard_map/ppermute | solution.py:109
  222.0 13.5 %collective-permute-start.10 = (bf16[512,512]{1,0:T(8,128)(2,1)}, bf16[512,512]{1,0:T(8,128)(2,1)}, u32[]{:S(2)}, u32[]{:S(2)}) collective-permute-start(bf16[512,512]{1,0:T(8,128)(2,1)} %fusion.31), channel_id=1, source_target_pairs={{0,8},{1,9},{2,10},{3,11},{4,12},{5,13},{6,14},{7,15},{8,0},{9,1},... | collective-permute-start | bytes 1572872 | tf_op jit(solution)/shard_map/ppermute | solution.py:109
  223.0 19.8 %collective-permute-start.12 = (bf16[512,512]{1,0:T(8,128)(2,1)}, bf16[512,512]{1,0:T(8,128)(2,1)}, u32[]{:S(2)}, u32[]{:S(2)}) collective-permute-start(bf16[512,512]{1,0:T(8,128)(2,1)} %add_convert_fusion), channel_id=1, source_target_pairs={{0,16},{1,17},{2,18},{3,19},{4,20},{5,21},{6,22},{7,23},{8,24},{9,... | collective-permute-start | bytes 1572872 | tf_op jit(solution)/shard_map/ppermute | solution.py:109
  223.3 19.5 %copy-start.10 = (bf16[512,512]{1,0:T(8,128)(2,1)S(1)}, bf16[512,512]{1,0:T(8,128)(2,1)}, u32[]{:S(2)}) copy-start(bf16[512,512]{1,0:T(8,128)(2,1)} %fusion.19) | copy-start | bytes 1572868
  235.5 24.4 %collective-permute-start.14 = (bf16[2,512,512]{2,1,0:T(8,128)(2,1)}, bf16[2,512,512]{2,1,0:T(8,128)(2,1)}, u32[]{:S(2)}, u32[]{:S(2)}) collective-permute-start(bf16[2,512,512]{2,1,0:T(8,128)(2,1)} %pad_maximum_fusion.8), channel_id=1, source_target_pairs={{0,8},{1,9},{2,10},{3,11},{4,12},{5,13},{6,14},{7,15},{8,0},{9,1},... | collective-permute-start | bytes 3145736 | tf_op jit(solution)/shard_map/ppermute | solution.py:109
  246.1 12.5 %collective-permute-start.15 = (bf16[512,512]{1,0:T(8,128)(2,1)}, bf16[512,512]{1,0:T(8,128)(2,1)S(1)}, u32[]{:S(2)}, u32[]{:S(2)}) collective-permute-start(bf16[512,512]{1,0:T(8,128)(2,1)} %get-tuple-element.69), channel_id=1, source_target_pairs={{0,16},{1,17},{2,18},{3,19},{4,20},{5,21},{6,22},{7,23},{8,24},{9,... | collective-permute-start | bytes 1572872 | tf_op jit(solution)/shard_map/ppermute | solution.py:109
  259.8 10.5 %collective-permute-start.16 = (bf16[2,512,512]{2,1,0:T(8,128)(2,1)S(1)}, bf16[2,512,512]{2,1,0:T(8,128)(2,1)S(1)}, u32[]{:S(2)}, u32[]{:S(2)}) collective-permute-start(bf16[2,512,512]{2,1,0:T(8,128)(2,1)S(1)} %pad_maximum_fusion.9), channel_id=1, source_target_pairs={{0,8},{1,9},{2,10},{3,11},{4,12},{5,13},{6,14},{7,15},{8,0},{9,1},... | collective-permute-start | bytes 3145736 | tf_op jit(solution)/shard_map/ppermute | solution.py:109
  292.3 1.2 copy-start.3
  292.3 1.5 copy-start.4
  292.3 1.9 copy-start.5
Sparse Core Ops, SparseCore 0:
  53.1 114.8 all-gather.2
  292.5 93.6 reduce-scatter.1

commit v4 on v3

--- a/solution.py
+++ b/solution.py
@@ -14,6 +14,7 @@
 beta_second = 0.95
 epsilon = 1e-08
 
+ROW_PARTS = 2
 COL_PARTS = 2
 
 VMEM_BYTES = 48 * 1024 * 1024
@@ -23,6 +24,10 @@
 
 def matmul(a, b):
     return lax.dot_general(a, b, (((1,), (0,)), ((), ())), preferred_element_type=jnp.float32)
+
+
+def matmul_nt(a, b):
+    return lax.dot_general(a, b, (((1,), (1,)), ((), ())), preferred_element_type=jnp.float32)
 
 
 def cost(flops, *arrays):
@@ -30,13 +35,13 @@
     return pl.CostEstimate(flops=flops, bytes_accessed=size, transcendentals=0)
 
 
-def half_rotation(gathered, right, places, nz, parts):
+def half_rotation(gathered, right, places, nz, parts, part, row_parts, held):
     count, rows, cols = gathered.shape
     nx = count // nz
     width = right.shape[1] // parts
 
     def kernel(places_ref, *refs):
-        blocks, right_ref, outs = refs[:nx], refs[nx], refs[nx + 1 :]
+        blocks, right_ref, outs = refs[:nx], refs[nx], refs[-parts:]
         for j, out in enumerate(outs):
             total = matmul(blocks[0][...], right_ref[:cols, j * width : (j + 1) * width])
             for i in range(1, nx):
@@ -48,7 +53,7 @@
             return pl.BlockSpec((None, rows, cols), lambda k, p: (i * nz + k, 0, 0))
         return pl.BlockSpec((None, rows, cols), lambda k, p: (i * nz + nz - 1 - k, 0, 0))
 
-    outs = [jax.ShapeDtypeStruct((nz * rows, width), low)] * parts
+    outs = [jax.ShapeDtypeStruct((nz * rows * row_parts, width), low)] * parts
     return pl.pallas_call(
         kernel,
         out_shape=outs,
@@ -56,38 +61,15 @@
             num_scalar_prefetch=1,
             grid=(nz,),
             in_specs=[block_of(i) for i in range(nx)]
-            + [pl.BlockSpec(right.shape, lambda k, p: (0, 0), pipeline_mode=pl.Buffered(1))],
-            out_specs=[pl.BlockSpec((rows, width), lambda k, p: (p[k], 0))] * parts,
+            + [pl.BlockSpec(right.shape, lambda k, p: (0, 0), pipeline_mode=pl.Buffered(1))]
+            + [pl.BlockSpec(memory_space=pl.ANY)] * len(held),
+            out_specs=[pl.BlockSpec((rows, width), lambda k, p: (p[k] * row_parts + part, 0))] * parts,
         ),
+        input_output_aliases={nx + 2 + j: j for j in range(len(held))},
         compiler_params=pltpu.CompilerParams(vmem_limit_bytes=VMEM_BYTES),
         cost_estimate=cost(2 * gathered.size * right.shape[1], gathered, right, *outs),
         name="half_rotation",
-    )(places, *([gathered] * nx), right)
-
-
-def back_rotation(columns, right_t, block):
-    parts = len(columns)
-    total_rows, width = columns[0].shape
-
-    def kernel(*refs):
-        rows_of, right_ref, out = refs[:parts], refs[parts], refs[parts + 1]
-        total = matmul(rows_of[0][...], right_ref[:width])
-        for j in range(1, parts):
-            total += matmul(rows_of[j][...], right_ref[j * width : (j + 1) * width])
-        out[...] = total.astype(out.dtype)
-
-    out = jax.ShapeDtypeStruct((total_rows, right_t.shape[1]), low)
-    return pl.pallas_call(
-        kernel,
-        out_shape=out,
-        grid=(total_rows // block,),
-        in_specs=[pl.BlockSpec((block, width), lambda k: (k, 0))] * parts
-        + [pl.BlockSpec(right_t.shape, lambda k: (0, 0), pipeline_mode=pl.Buffered(1))],
-        out_specs=pl.BlockSpec((block, right_t.shape[1]), lambda k: (k, 0)),
-        compiler_params=pltpu.CompilerParams(vmem_limit_bytes=VMEM_BYTES),
-        cost_estimate=cost(2 * total_rows * right_t.size, right_t, out, *columns),
-        name="back_rotation",
-    )(*columns, right_t)
+    )(places, *([gathered] * nx), right, *held)
 
 
 def per_device(gradient, left_basis, right_basis, first_moment, second_moment, *, nb, nd):
@@ -149,37 +131,68 @@
     order_of = jnp.array([order.index(t) for t in range(nb)], jnp.int32)
     path_places = [order_of[b ^ (dd // nx)] * rows + dd % nx * out_rows for dd in path]
 
+    def together(*values):
+        return lax.optimization_barrier(values)
+
     left_t = left_basis.astype(low).T
     right = right_basis.astype(low)
-    right_t = right.T
-    piece = permute(gradient, lambda bb, zz, xx: (bb, zz ^ spread(bb), xx))
-    for i, t in enumerate(reversed(bits)):
-        left_t = joined(left_t, move_z(left_t, t), (z & t) != 0, i)
-    piece, left_t, right, right_t, half_places, path_places = lax.optimization_barrier(
-        (piece, left_t, right, right_t, half_places, path_places)
-    )
-    piece = permute(piece, lambda bb, zz, xx: (zz ^ spread(bb), zz, xx))
-    gathered = lax.all_gather(piece, "dp", axis_index_groups=[path])
-    for i, u in enumerate(reversed(x_bits)):
-        other, piece = lax.optimization_barrier((move_x(left_t, u), piece))
-        left_t = joined(left_t, other, (x & u) != 0, len(bits) + i)
-    left_t = left_t.reshape(whole, rows)
-    for t in reversed(bits):
-        left_t = jnp.concatenate([left_t, move_b(left_t, t)], axis=1)
-    left_t = lax.optimization_barrier(left_t)
+    part = rows // ROW_PARTS
+    pieces = [gradient[h * part : (h + 1) * part] for h in range(ROW_PARTS)]
+
+    def across(piece):
+        return permute(piece, lambda bb, zz, xx: (bb, zz ^ spread(bb), xx))
+
+    def along(piece):
+        return permute(piece, lambda bb, zz, xx: (zz ^ spread(bb), zz, xx))
+
+    def gather(piece):
+        return lax.all_gather(piece, "dp", axis_index_groups=[path])
+
+    def left_steps():
+        value = left_t
+        for i, t in enumerate(reversed(bits)):
+            value = joined(value, (yield move_z(value, t)), (z & t) != 0, i)
+        for i, u in enumerate(reversed(x_bits)):
+            value = joined(value, (yield move_x(value, u)), (x & u) != 0, len(bits) + i)
+        value = value.reshape(whole, rows)
+        for t in reversed(bits):
+            value = jnp.concatenate([value, (yield move_b(value, t))], axis=1)
+        yield value
+
+    steps = left_steps()
+    step = next(steps)
+    gathered = []
+    pieces[0] = across(pieces[0])
+    for h in range(ROW_PARTS):
+        pieces[h], step, right, half_places = together(pieces[h], step, right, half_places)
+        moved = along(pieces[h])
+        if h + 1 < ROW_PARTS:
+            pieces[h + 1] = across(after(pieces[h + 1], pieces[h]))
+        step = steps.send(step)
+        gathered.append(gather(moved))
+        if h + 1 < ROW_PARTS:
+            pieces[h + 1], step, _ = together(pieces[h + 1], step, moved)
+        else:
+            step, _ = together(step, moved)
+    left_t = step
+    while left_t.shape != (whole, whole):
+        left_t = steps.send(left_t)
+    left_t, gathered[-1] = together(left_t, gathered[-1])
     left = jnp.concatenate(
         [lax.dynamic_slice_in_dim(left_t, start, out_rows, 1).T for start in path_places], axis=0
     )
-    left_t, left, gathered = lax.optimization_barrier((left_t, left, gathered))
-
-    half = list(half_rotation(gathered, right, half_places, nz, COL_PARTS))
+    left = lax.optimization_barrier(left)
+
+    half = []
+    for h in range(ROW_PARTS):
+        half = list(half_rotation(gathered[h], right, half_places, nz, COL_PARTS, h, ROW_PARTS, half))
 
     def product(t, j):
         rows_of = lax.dynamic_slice_in_dim(left_t, (b ^ t) * rows, rows, 0)
         return matmul(rows_of, half[j]).astype(low)
 
     width = ff_block // COL_PARTS
-    first_out, second_out, back, joins = [], [], [], []
+    first_out, second_out, columns, joins = [], [], [], []
     for j in range(COL_PARTS):
         cols = slice(j * width, (j + 1) * width)
         if j:
@@ -193,8 +206,9 @@
                 away = held.pop(s).astype(low)
                 if j:
                     away = after(away, summed)
-                held[s ^ t] = held[s ^ t] + move_b(away, t).astype(jnp.float32)
-        rotated = summed = held[0]
+                arrived = move_b(away, t)
+                held[s ^ t] = held[s ^ t] + arrived.astype(jnp.float32)
+        rotated, summed = held[0], arrived
         moments = first_moment[:, cols], second_moment[:, cols]
         if j:
             moments = after(moments, previous)
@@ -214,10 +228,11 @@
             column = joined(column, other, (b & t) != 0, axis)
             joins[axis : axis + 1] = [column]
             axis += 1
-        column = lax.optimization_barrier(column.reshape(whole, width))
-        back.append(lax.optimization_barrier(matmul(left, column).astype(low)))
-
-    total = back_rotation(back, right_t, rows)
+        columns.append(column.reshape(whole, width))
+
+    columns = lax.optimization_barrier(jnp.concatenate(columns, axis=1))
+    back = lax.optimization_barrier(matmul(left, columns).astype(low))
+    total = matmul_nt(back, right).astype(low)
     update = lax.psum_scatter(total, "dp", scatter_dimension=0, axis_index_groups=[path], tiled=True)
     return (
         jnp.concatenate(first_out, axis=1),

time: 394 us -> 397 us (level)
  local copies, waits for them, and re-layouts: 33.4 us -> 15.8 us
  starting transfers between devices: 62.8 us -> 77.5 us
  waiting for transfers between devices: 202 us -> 215 us
  Pallas kernels: 26.2 us -> 17 us
    ppermute x17 -> x19, waiting for transfers between devices: 114 us -> 132 us  [permute(): return lax.ppermute(value, ('basis', 'dp'), pairs)]
    ppermute x17 -> x19, starting transfers between devices: 62.8 us -> 77.4 us  [permute(): return lax.ppermute(value, ('basis', 'dp'), pairs)]
    pallas_call x1 -> x0, Pallas kernels: 13 us -> none  [back_rotation(): pl.pallas_call(kernel, out_shape=out, grid=(total_rows // block,), in_spe...]
    unnamed x35 -> x40, local copies, waits for them, and re-layouts: 23.8 us -> 12.8 us
    dot_general x0 -> x1, matrix products: none -> 10.9 us  [matmul_nt(): lax.dot_general(a, b, (((1,), (1,)), ((), ())), preferred_element_type=jn...]
    dot_general x10 -> x9, matrix products: 28.7 us -> 19.1 us  [matmul(): lax.dot_general(a, b, (((1,), (0,)), ((), ())), preferred_element_type=jn...]
    optimization_barrier x1 -> x0, local copies, waits for them, and re-layouts: 6.43 us -> none  [per_device(): lax.optimization_barrier((piece, left_t, right, right_t, half_places, pat...]
    convert_element_type x0 -> x1, other arithmetic: none -> 6.11 us  [per_device(): right = right_basis.astype(low)]
  transfers between devices with their start and end apart: 19 -> 22, of which waited for: 10 -> 9; matrix products, arithmetic and copies ran while one was open for 17% -> 8% of each run, Pallas kernels for 0% -> 2%
where the time goes in v4:
time: 397 us; the launch traced here: 396 us
  waiting for transfers between devices  215 us (54%)
  starting transfers between devices  77.5 us (20%)
  matrix products  30.1 us (8%)
  other arithmetic  24.3 us (6%)
  Pallas kernels  17 us (4%)
  between operations  16.9 us (4%)
  local copies, waits for them, and re-layouts  15.8 us (4%)
    ppermute x19, waiting for transfers between devices, permute(): return lax.ppermute(value, ('basis', 'dp'), pairs)  132 us
    reduce_scatter x1, waiting for transfers between devices, per_device(): lax.psum_scatter(total, 'dp', scatter_dimension=0, axis_index_groups=[pat...  82.4 us
    ppermute x19, starting transfers between devices, permute(): return lax.ppermute(value, ('basis', 'dp'), pairs)  77.4 us
    dot_general x9, matrix products, matmul(): lax.dot_general(a, b, (((1,), (0,)), ((), ())), preferred_element_type=jn...  19.1 us
    pallas_call x2, Pallas kernels, half_rotation(): pl.pallas_call(kernel, out_shape=outs, grid_spec=pltpu.PrefetchScalarGrid...  17 us
    unnamed x40, local copies, waits for them, and re-layouts  12.8 us
    dot_general x1, matrix products, matmul_nt(): lax.dot_general(a, b, (((1,), (1,)), ((), ())), preferred_element_type=jn...  10.9 us
    concatenate x2, other arithmetic, left_steps(): value = jnp.concatenate([value, (yield move_b(value, t))], axis=1)  8.93 us
  transfers between devices with their start and end apart: 22, of which 9 were waited for; matrix products, arithmetic and copies ran while one was open for 8% of the time, Pallas kernels for 2%

profile of v4, /device:TPU:0, one launch (start us, length us, event | category | flops | bytes accessed | tf_op | source)
XLA Modules:
  0.0 396.4 jit_solution(7330854242555629348)
XLA Ops:
  7.2 1.3 fusion.53
  8.5 0.7 collective-permute-start
  9.2 1.2 copy.12
  10.4 4.1 %collective-permute-start.1 = (bf16[256,512]{1,0:T(8,128)(2,1)S(1)}, bf16[256,512]{1,0:T(8,128)(2,1)S(1)}, u32[]{:S(2)}, u32[]{:S(2)}) collective-permute-start(bf16[256,512]{1,0:T(8,128)(2,1)S(1)} %bitcast.82), channel_id=1, source_target_pairs={{0,4},{1,5},{2,6},{3,7},{4,0},{5,1},{6,2},{7,3},{8,12},{9,13},{10,... | collective-permute-start | bytes 786440 | tf_op jit(solution)/shard_map/ppermute | solution.py:91
  14.5 6.1 %convert_element_type.79.refs_2_ = bf16[2048,1024]{1,0:T(8,128)(2,1)} convert(f32[2048,1024]{1,0:T(8,128)} %param.9) | non-fusion elementwise | flops 2097152 | bytes 12582912 | tf_op jit(solution)/shard_map/convert_element_type | solution.py:138
  20.6 0.7 fusion.50.places_ref
  21.3 11.6 %collective-permute-done.1 = bf16[256,512]{1,0:T(8,128)(2,1)S(1)} collective-permute-done((bf16[256,512]{1,0:T(8,128)(2,1)S(1)}, bf16[256,512]{1,0:T(8,128)(2,1)S(1)}, u32[]{:S(2)}, u32[]{:S(2)}) %collective-permute-start.1) | collective-permute-done | bytes 262176 | tf_op jit(solution)/shard_map/ppermute | solution.py:91
  32.8 0.7 collective-permute-start.4
  33.5 0.8 copy-done.10
  34.4 0.7 collective-permute-start.2
  35.2 11.4 %collective-permute-start.3 = (bf16[2,256,512]{2,1,0:T(8,128)(2,1)S(1)}, bf16[2,256,512]{2,1,0:T(8,128)(2,1)S(1)}, u32[]{:S(2)}, u32[]{:S(2)}) collective-permute-start(bf16[2,256,512]{2,1,0:T(8,128)(2,1)S(1)} %pad_maximum_fusion.11), channel_id=1, source_target_pairs={{0,2},{1,3},{2,0},{3,1},{4,6},{5,7},{6,4},{7,5},{8,10},{9,11},{10,... | collective-permute-start | bytes 1572872 | tf_op jit(solution)/shard_map/ppermute | solution.py:91
  46.7 7.2 %collective-permute-done.3 = bf16[2,256,512]{2,1,0:T(8,128)(2,1)S(1)} collective-permute-done((bf16[2,256,512]{2,1,0:T(8,128)(2,1)S(1)}, bf16[2,256,512]{2,1,0:T(8,128)(2,1)S(1)}, u32[]{:S(2)}, u32[]{:S(2)}) %collective-permute-start.3) | collective-permute-done | bytes 524320 | tf_op jit(solution)/shard_map/ppermute | solution.py:91
  54.0 1.6 collective-permute-start.5
  55.6 5.3 %collective-permute-start.6 = (bf16[256,1024]{1,0:T(8,128)(2,1)}, bf16[256,1024]{1,0:T(8,128)(2,1)}, u32[]{:S(2)}, u32[]{:S(2)}) collective-permute-start(bf16[256,1024]{1,0:T(8,128)(2,1)} %copy-done.13), channel_id=1, source_target_pairs={{0,0},{1,1},{2,10},{3,11},{4,20},{5,21},{6,30},{7,31},{8,24},{9,25... | collective-permute-start | bytes 1572872 | tf_op jit(solution)/shard_map/ppermute | solution.py:91
  61.0 28.7 %collective-permute-done.5 = bf16[2,2,256,512]{3,2,1,0:T(8,128)(2,1)S(1)} collective-permute-done((bf16[2,2,256,512]{3,2,1,0:T(8,128)(2,1)S(1)}, bf16[2,2,256,512]{3,2,1,0:T(8,128)(2,1)S(1)}, u32[]{:S(2)}, u32[]{:S(2)}) %collective-permute-start.5) | collective-permute-done | bytes 1048608 | tf_op jit(solution)/shard_map/ppermute | solution.py:91
  90.0 45.8 %collective-permute-start.7 = (bf16[2048,512]{1,0:T(8,128)(2,1)S(1)}, bf16[2048,512]{1,0:T(8,128)(2,1)S(1)}, u32[]{:S(2)}, u32[]{:S(2)}) collective-permute-start(bf16[2048,512]{1,0:T(8,128)(2,1)S(1)} %bitcast.75), channel_id=1, source_target_pairs={{0,16},{1,17},{2,18},{3,19},{4,20},{5,21},{6,22},{7,23},{8,24},{9,... | collective-permute-start | bytes 6291464 | tf_op jit(solution)/shard_map/ppermute | solution.py:91
  135.8 44.0 %collective-permute-done.7 = bf16[2048,512]{1,0:T(8,128)(2,1)S(1)} collective-permute-done((bf16[2048,512]{1,0:T(8,128)(2,1)S(1)}, bf16[2048,512]{1,0:T(8,128)(2,1)S(1)}, u32[]{:S(2)}, u32[]{:S(2)}) %collective-permute-start.7) | collective-permute-done | bytes 2097184 | tf_op jit(solution)/shard_map/ppermute | solution.py:91
  179.8 1.3 copy-done.6
  181.1 2.7 pad_maximum_fusion.1
  187.2 8.4 %half_rotation.2 = (bf16[2048,512]{1,0:T(8,128)(2,1)S(1)}, bf16[2048,512]{1,0:T(8,128)(2,1)S(1)}) custom-call(s32[4]{0:T(128)S(1)} %fusion.50.places_ref, bf16[8,256,1024]{2,1,0:T(8,128)(2,1)} %bitcast.85, bf16[8,256,1024]{2,1,0:T(8,128)(2,1)} %bitcast.86, bf16[2048,1024]{1,0:T(8,128)(2,1)} %convert_element_type.79.refs_2_), custom_call_target="tpu_custom_call" | custom-call | flops 4294967296 | bytes 12582912 | tf_op jit(solution)/shard_map/half_rotation/pallas_call | solution.py:57
  195.6 1.3 copy-done
  196.9 6.3 %pad_maximum_fusion = bf16[2048,2048]{1,0:T(8,128)(2,1)} fusion(bf16[2048,1024]{1,0:T(8,128)(2,1)} %collective-permute-done.8, bf16[2048,512]{1,0:T(8,128)(2,1)S(1)} %copy-done.7, bf16[2048,512]{1,0:T(8,128)(2,1)S(1)} %bitcast.77), kind=kLoop, calls=%fused_computation | loop fusion | flops 25165824 | bytes 16777216 | tf_op jit(solution)/shard_map/concatenate | solution.py:159
  203.2 1.6 copy-done.1
  204.8 8.5 %half_rotation.3 = (bf16[2048,512]{1,0:T(8,128)(2,1)S(1)}, bf16[2048,512]{1,0:T(8,128)(2,1)S(1)}) custom-call(s32[4]{0:T(128)S(1)} %fusion.50.places_ref, bf16[8,256,1024]{2,1,0:T(8,128)(2,1)} %bitcast.78, bf16[8,256,1024]{2,1,0:T(8,128)(2,1)} %bitcast.79, ...), custom_call_target="tpu_custom_call", output_to_operand_aliasing={{0}: (4, {}), {1}: (5, {})} | custom-call | flops 4294967296 | bytes 12582912 | tf_op jit(solution)/shard_map/half_rotation/pallas_call | solution.py:57
  213.4 1.2 fusion.28
  214.6 1.2 fusion.34
  215.9 1.2 fusion.31
  217.1 1.2 fusion.37
  218.9 1.2 fusion.19
  220.2 1.2 fusion.16
  222.0 1.2 fusion.22
  223.5 1.2 fusion.25
  225.0 1.8 collective-permute-start.11
  227.2 12.1 %collective-permute-done.11 = bf16[512,512]{1,0:T(8,128)(2,1)S(1)} collective-permute-done((bf16[512,512]{1,0:T(8,128)(2,1)S(1)}, bf16[512,512]{1,0:T(8,128)(2,1)S(1)}, u32[]{:S(2)}, u32[]{:S(2)}) %collective-permute-start.11) | collective-permute-done | bytes 524320 | tf_op jit(solution)/shard_map/ppermute | solution.py:91
  239.3 1.7 collective-permute-start.14
  241.2 0.9 divide_convert_fusion.1
  242.5 11.6 %collective-permute-done.14 = bf16[512,512]{1,0:T(8,128)(2,1)S(1)} collective-permute-done((bf16[512,512]{1,0:T(8,128)(2,1)S(1)}, bf16[512,512]{1,0:T(8,128)(2,1)S(1)}, u32[]{:S(2)}, u32[]{:S(2)}) %collective-permute-start.14) | collective-permute-done | bytes 524320 | tf_op jit(solution)/shard_map/ppermute | solution.py:91
  254.1 1.8 divide_convert_fusion
  256.0 1.7 collective-permute-start.17
  257.9 7.5 %collective-permute-done.15 = bf16[512,512]{1,0:T(8,128)(2,1)S(1)} collective-permute-done((bf16[512,512]{1,0:T(8,128)(2,1)S(1)}, bf16[512,512]{1,0:T(8,128)(2,1)S(1)}, u32[]{:S(2)}, u32[]{:S(2)}) %collective-permute-start.15) | collective-permute-done | bytes 524320 | tf_op jit(solution)/shard_map/ppermute | solution.py:91
  265.6 9.6 %collective-permute-done.17 = bf16[512,512]{1,0:T(8,128)(2,1)S(1)} collective-permute-done((bf16[512,512]{1,0:T(8,128)(2,1)S(1)}, bf16[512,512]{1,0:T(8,128)(2,1)S(1)}, u32[]{:S(2)}, u32[]{:S(2)}) %collective-permute-start.17) | collective-permute-done | bytes 524320 | tf_op jit(solution)/shard_map/ppermute | solution.py:91
  276.5 2.9 copy-done.11
  280.8 1.2 slice-done
  282.0 1.4 slice-done.1
  283.3 9.2 %convolution_convert_fusion.1 = bf16[2048,1024]{1,0:T(8,128)(2,1)S(1)} fusion(bf16[2048,2048]{0,1:T(8,128)(2,1)S(1)} %bitcast.84, bf16[2048,1024]{1,0:T(8,128)(2,1)S(1)} %pad_maximum_fusion.2), kind=kOutput, calls=%fused_computation.4 | convolution fusion | flops 8592031744 | bytes 16777216 | tf_op jit(solution)/shard_map/dot_general | solution.py:26
  292.5 10.9 %convolution_convert_fusion = bf16[2048,2048]{1,0:T(8,128)(2,1)} fusion(bf16[2048,1024]{1,0:T(8,128)(2,1)S(1)} %convolution_convert_fusion.1, bf16[2048,1024]{1,0:T(8,128)(2,1)S(1)} %copy-done.5), kind=kOutput, calls=%fused_computation.1 | convolution fusion | flops 8594128896 | bytes 16777216 | tf_op jit(solution)/shard_map/dot_general | solution.py:30
  303.5 3.9 pad_maximum_fusion.4
  307.4 82.4 %reduce-scatter.2.cloned.1.call-done = bf16[256,2048]{1,0:T(8,128)(2,1)} async-done(((bf16[2048,2048]{1,0:T(8,128)(2,1)}), bf16[256,2048]{1,0:T(8,128)(2,1)}) %reduce-scatter.2.cloned.1.call-update) | async-done | bytes 1048592 | tf_op jit(solution)/shard_map/reduce_scatter | solution.py:236
  (81 shorter events, 6.8 us)
Async XLA Ops:
  7.2 180.0 %all-gather.7.cloned.1.call-start = ((), (), s32[]{:S(2)}) async-start(), calls=%async_computation.3 | async-start | bytes 4718592 | tf_op jit(solution)/shard_map/all_gather | solution.py:149
  8.5 24.3 %collective-permute-start = (bf16[256,1024]{1,0:T(8,128)(2,1)S(1)}, bf16[256,1024]{1,0:T(8,128)(2,1)S(1)}, u32[]{:S(2)}, u32[]{:S(2)}) collective-permute-start(bf16[256,1024]{1,0:T(8,128)(2,1)S(1)} %get-tuple-element.87), channel_id=1, source_target_pairs={{0,0},{1,1},{2,2},{3,3},{4,4},{5,5},{6,6},{7,7},{8,14},{9,15},{10,... | collective-permute-start | bytes 1572872 | tf_op jit(solution)/shard_map/ppermute | solution.py:91
  10.4 22.5 %collective-permute-start.1 = (bf16[256,512]{1,0:T(8,128)(2,1)S(1)}, bf16[256,512]{1,0:T(8,128)(2,1)S(1)}, u32[]{:S(2)}, u32[]{:S(2)}) collective-permute-start(bf16[256,512]{1,0:T(8,128)(2,1)S(1)} %bitcast.82), channel_id=1, source_target_pairs={{0,4},{1,5},{2,6},{3,7},{4,0},{5,1},{6,2},{7,3},{8,12},{9,13},{10,... | collective-permute-start | bytes 786440 | tf_op jit(solution)/shard_map/ppermute | solution.py:91
  32.8 0.7 collective-permute-start.4
  33.5 0.8 copy-start.10
  34.4 168.8 %all-gather.5.cloned.1.call-start = ((), (), s32[]{:S(2)}) async-start(), calls=%async_computation.2 | async-start | bytes 4718592 | tf_op jit(solution)/shard_map/all_gather | solution.py:149
  34.4 12.3 %collective-permute-start.2 = (bf16[256,1024]{1,0:T(8,128)(2,1)S(1)}, bf16[256,1024]{1,0:T(8,128)(2,1)S(1)}, u32[]{:S(2)}, u32[]{:S(2)}) collective-permute-start(bf16[256,1024]{1,0:T(8,128)(2,1)S(1)} %get-tuple-element.36), channel_id=1, source_target_pairs={{0,0},{1,1},{2,2},{3,3},{4,4},{5,5},{6,6},{7,7},{8,14},{9,15},{10,... | collective-permute-start | bytes 1572872 | tf_op jit(solution)/shard_map/ppermute | solution.py:91
  35.2 18.6 %collective-permute-start.3 = (bf16[2,256,512]{2,1,0:T(8,128)(2,1)S(1)}, bf16[2,256,512]{2,1,0:T(8,128)(2,1)S(1)}, u32[]{:S(2)}, u32[]{:S(2)}) collective-permute-start(bf16[2,256,512]{2,1,0:T(8,128)(2,1)S(1)} %pad_maximum_fusion.11), channel_id=1, source_target_pairs={{0,2},{1,3},{2,0},{3,1},{4,6},{5,7},{6,4},{7,5},{8,10},{9,11},{10,... | collective-permute-start | bytes 1572872 | tf_op jit(solution)/shard_map/ppermute | solution.py:91
  46.7 7.2 %copy-start.13 = (bf16[256,1024]{1,0:T(8,128)(2,1)}, bf16[256,1024]{1,0:T(8,128)(2,1)S(1)}, u32[]{:S(2)}) copy-start(bf16[256,1024]{1,0:T(8,128)(2,1)S(1)} %collective-permute-done.2) | copy-start | bytes 1572868
  54.0 35.6 %collective-permute-start.5 = (bf16[2,2,256,512]{3,2,1,0:T(8,128)(2,1)S(1)}, bf16[2,2,256,512]{3,2,1,0:T(8,128)(2,1)S(1)}, u32[]{:S(2)}, u32[]{:S(2)}) collective-permute-start(bf16[2,2,256,512]{3,2,1,0:T(8,128)(2,1)S(1)} %pad_maximum_fusion.8), channel_id=1, source_target_pairs={{0,1},{1,0},{2,3},{3,2},{4,5},{5,4},{6,7},{7,6},{8,9},{9,8},{10,11... | collective-permute-start | bytes 3145736 | tf_op jit(solution)/shard_map/ppermute | solution.py:91
  55.6 5.3 %collective-permute-start.6 = (bf16[256,1024]{1,0:T(8,128)(2,1)}, bf16[256,1024]{1,0:T(8,128)(2,1)}, u32[]{:S(2)}, u32[]{:S(2)}) collective-permute-start(bf16[256,1024]{1,0:T(8,128)(2,1)} %copy-done.13), channel_id=1, source_target_pairs={{0,0},{1,1},{2,10},{3,11},{4,20},{5,21},{6,30},{7,31},{8,24},{9,25... | collective-permute-start | bytes 1572872 | tf_op jit(solution)/shard_map/ppermute | solution.py:91
  61.0 328.9 %reduce-scatter.2.cloned.1.call-start = ((), (), s32[]{:S(2)}) async-start(), calls=%async_computation.1 | async-start | bytes 9437184 | tf_op jit(solution)/shard_map/reduce_scatter | solution.py:236
  90.0 93.8 %copy-start.3 = (bf16[2,2,2,256,512]{4,3,2,1,0:T(8,128)(2,1)}, bf16[2,2,2,256,512]{4,3,2,1,0:T(8,128)(2,1)S(1)}, u32[]{:S(2)}) copy-start(bf16[2,2,2,256,512]{4,3,2,1,0:T(8,128)(2,1)S(1)} %pad_maximum_fusion.3) | copy-start | bytes 6291460
  90.0 93.8 %copy-start.12 = (s32[4]{0:T(128)S(1)}, s32[4]{0:T(128)}, u32[]{:S(2)}) copy-start(s32[4]{0:T(128)} %constant.71.clone) | copy-start | bytes 52
  90.0 89.8 %collective-permute-start.7 = (bf16[2048,512]{1,0:T(8,128)(2,1)S(1)}, bf16[2048,512]{1,0:T(8,128)(2,1)S(1)}, u32[]{:S(2)}, u32[]{:S(2)}) collective-permute-start(bf16[2048,512]{1,0:T(8,128)(2,1)S(1)} %bitcast.75), channel_id=1, source_target_pairs={{0,16},{1,17},{2,18},{3,19},{4,20},{5,21},{6,22},{7,23},{8,24},{9,... | collective-permute-start | bytes 6291464 | tf_op jit(solution)/shard_map/ppermute | solution.py:91
  179.8 1.3 copy-start.6
  183.8 13.1 %collective-permute-start.8 = (bf16[2048,1024]{1,0:T(8,128)(2,1)}, bf16[2048,1024]{1,0:T(8,128)(2,1)}, u32[]{:S(2)}, u32[]{:S(2)}) collective-permute-start(bf16[2048,1024]{1,0:T(8,128)(2,1)} %pad_maximum_fusion.1), channel_id=1, source_target_pairs={{0,8},{1,9},{2,10},{3,11},{4,12},{5,13},{6,14},{7,15},{8,0},{9,1},... | collective-permute-start | bytes 12582920 | tf_op jit(solution)/shard_map/ppermute | solution.py:91
  187.1 9.8 %copy-start.4 = (bf16[2,2,2,256,512]{4,3,2,1,0:T(8,128)(2,1)S(1)}, bf16[2,2,2,256,512]{4,3,2,1,0:T(8,128)(2,1)}, u32[]{:S(2)}) copy-start(bf16[2,2,2,256,512]{4,3,2,1,0:T(8,128)(2,1)} %copy-done.3) | copy-start | bytes 6291460
  187.2 9.8 %copy-start.7 = (bf16[2048,512]{1,0:T(8,128)(2,1)S(1)}, bf16[2048,512]{1,0:T(8,128)(2,1)}, u32[]{:S(2)}) copy-start(bf16[2048,512]{1,0:T(8,128)(2,1)} %copy-done.6) | copy-start | bytes 6291460
  195.6 1.3 copy-start
  203.2 1.6 copy-start.1
  204.8 8.6 %copy-start.2 = (bf16[2048,2048]{1,0:T(8,128)(2,1)S(1)}, bf16[2048,2048]{1,0:T(8,128)(2,1)}, u32[]{:S(2)}) copy-start(bf16[2048,2048]{1,0:T(8,128)(2,1)} %pad_maximum_fusion) | copy-start | bytes 25165828
  218.4 6.4 %collective-permute-start.10 = (bf16[512,512]{1,0:T(8,128)(2,1)S(1)}, bf16[512,512]{1,0:T(8,128)(2,1)S(1)}, u32[]{:S(2)}, u32[]{:S(2)}) collective-permute-start(bf16[512,512]{1,0:T(8,128)(2,1)S(1)} %fusion.34), channel_id=1, source_target_pairs={{0,8},{1,9},{2,10},{3,11},{4,12},{5,13},{6,14},{7,15},{8,0},{9,1},... | collective-permute-start | bytes 1572872 | tf_op jit(solution)/shard_map/ppermute | solution.py:91
  221.4 19.8 %collective-permute-start.9 = (bf16[512,512]{1,0:T(8,128)(2,1)S(1)}, bf16[512,512]{1,0:T(8,128)(2,1)S(1)}, u32[]{:S(2)}, u32[]{:S(2)}) collective-permute-start(bf16[512,512]{1,0:T(8,128)(2,1)S(1)} %fusion.28), channel_id=1, source_target_pairs={{0,8},{1,9},{2,10},{3,11},{4,12},{5,13},{6,14},{7,15},{8,0},{9,1},... | collective-permute-start | bytes 1572872 | tf_op jit(solution)/shard_map/ppermute | solution.py:91
  221.5 5.6 %collective-permute-start.13 = (bf16[512,512]{1,0:T(8,128)(2,1)S(1)}, bf16[512,512]{1,0:T(8,128)(2,1)S(1)}, u32[]{:S(2)}, u32[]{:S(2)}) collective-permute-start(bf16[512,512]{1,0:T(8,128)(2,1)S(1)} %fusion.37), channel_id=1, source_target_pairs={{0,8},{1,9},{2,10},{3,11},{4,12},{5,13},{6,14},{7,15},{8,0},{9,1},... | collective-permute-start | bytes 1572872 | tf_op jit(solution)/shard_map/ppermute | solution.py:91
  223.2 19.3 %collective-permute-start.12 = (bf16[512,512]{1,0:T(8,128)(2,1)S(1)}, bf16[512,512]{1,0:T(8,128)(2,1)S(1)}, u32[]{:S(2)}, u32[]{:S(2)}) collective-permute-start(bf16[512,512]{1,0:T(8,128)(2,1)S(1)} %fusion.31), channel_id=1, source_target_pairs={{0,8},{1,9},{2,10},{3,11},{4,12},{5,13},{6,14},{7,15},{8,0},{9,1},... | collective-permute-start | bytes 1572872 | tf_op jit(solution)/shard_map/ppermute | solution.py:91
  224.9 16.3 %copy-start.8 = (f32[512,1024]{1,0:T(8,128)S(1)}, f32[512,1024]{1,0:T(8,128)}, u32[]{:S(2)}) copy-start(f32[512,1024]{1,0:T(8,128)} %param.10) | copy-start | bytes 6291460
  224.9 16.3 %copy-start.9 = (f32[512,1024]{1,0:T(8,128)S(1)}, f32[512,1024]{1,0:T(8,128)}, u32[]{:S(2)}) copy-start(f32[512,1024]{1,0:T(8,128)} %param.11) | copy-start | bytes 6291460
  225.0 14.3 %collective-permute-start.11 = (bf16[512,512]{1,0:T(8,128)(2,1)S(1)}, bf16[512,512]{1,0:T(8,128)(2,1)S(1)}, u32[]{:S(2)}, u32[]{:S(2)}) collective-permute-start(bf16[512,512]{1,0:T(8,128)(2,1)S(1)} %add_convert_fusion.1), channel_id=1, source_target_pairs={{0,16},{1,17},{2,18},{3,19},{4,20},{5,21},{6,22},{7,23},{8,24},{9,... | collective-permute-start | bytes 1572872 | tf_op jit(solution)/shard_map/ppermute | solution.py:91
  239.3 14.8 %collective-permute-start.14 = (bf16[512,512]{1,0:T(8,128)(2,1)S(1)}, bf16[512,512]{1,0:T(8,128)(2,1)S(1)}, u32[]{:S(2)}, u32[]{:S(2)}) collective-permute-start(bf16[512,512]{1,0:T(8,128)(2,1)S(1)} %add_convert_fusion), channel_id=1, source_target_pairs={{0,16},{1,17},{2,18},{3,19},{4,20},{5,21},{6,22},{7,23},{8,24},{9,... | collective-permute-start | bytes 1572872 | tf_op jit(solution)/shard_map/ppermute | solution.py:91
  242.2 23.2 %collective-permute-start.15 = (bf16[512,512]{1,0:T(8,128)(2,1)S(1)}, bf16[512,512]{1,0:T(8,128)(2,1)S(1)}, u32[]{:S(2)}, u32[]{:S(2)}) collective-permute-start(bf16[512,512]{1,0:T(8,128)(2,1)S(1)} %get-tuple-element.70), channel_id=1, source_target_pairs={{0,16},{1,17},{2,18},{3,19},{4,20},{5,21},{6,22},{7,23},{8,24},{9,... | collective-permute-start | bytes 1572872 | tf_op jit(solution)/shard_map/ppermute | solution.py:91
  256.0 19.3 %collective-permute-start.17 = (bf16[512,512]{1,0:T(8,128)(2,1)S(1)}, bf16[512,512]{1,0:T(8,128)(2,1)S(1)}, u32[]{:S(2)}, u32[]{:S(2)}) collective-permute-start(bf16[512,512]{1,0:T(8,128)(2,1)S(1)} %get-tuple-element.67), channel_id=1, source_target_pairs={{0,16},{1,17},{2,18},{3,19},{4,20},{5,21},{6,22},{7,23},{8,24},{9,... | collective-permute-start | bytes 1572872 | tf_op jit(solution)/shard_map/ppermute | solution.py:91
  265.6 10.6 %collective-permute-start.16 = (bf16[2,512,512]{2,1,0:T(8,128)(2,1)S(1)}, bf16[2,512,512]{2,1,0:T(8,128)(2,1)S(1)}, u32[]{:S(2)}, u32[]{:S(2)}) collective-permute-start(bf16[2,512,512]{2,1,0:T(8,128)(2,1)S(1)} %pad_maximum_fusion.9), channel_id=1, source_target_pairs={{0,8},{1,9},{2,10},{3,11},{4,12},{5,13},{6,14},{7,15},{8,0},{9,1},... | collective-permute-start | bytes 3145736 | tf_op jit(solution)/shard_map/ppermute | solution.py:91
  275.5 4.1 %collective-permute-start.18 = (bf16[2,512,512]{2,1,0:T(8,128)(2,1)S(1)}, bf16[2,512,512]{2,1,0:T(8,128)(2,1)S(1)}, u32[]{:S(2)}, u32[]{:S(2)}) collective-permute-start(bf16[2,512,512]{2,1,0:T(8,128)(2,1)S(1)} %pad_maximum_fusion.10), channel_id=1, source_target_pairs={{0,8},{1,9},{2,10},{3,11},{4,12},{5,13},{6,14},{7,15},{8,0},{9,1},... | collective-permute-start | bytes 3145736 | tf_op jit(solution)/shard_map/ppermute | solution.py:91
  276.2 3.3 copy-start.11
  279.8 2.2 slice-start
  280.1 3.2 slice-start.1
  283.3 9.2 %copy-start.5 = (bf16[2048,1024]{1,0:T(8,128)(2,1)S(1)}, bf16[2048,1024]{1,0:T(8,128)(2,1)}, u32[]{:S(2)}) copy-start(bf16[2048,1024]{1,0:T(8,128)(2,1)} %convert_element_type.79.refs_2_) | copy-start | bytes 12582916
Sparse Core Ops, SparseCore 0:
  34.5 85.1 all-gather.6
  121.2 58.4 all-gather.4
  303.6 86.1 reduce-scatter.1

commit v5 on v3

--- a/solution.py
+++ b/solution.py
@@ -16,13 +16,17 @@
 
 COL_PARTS = 2
 
-VMEM_BYTES = 48 * 1024 * 1024
+VMEM_BYTES = 20 * 1024 * 1024
 
 low = jnp.bfloat16
 
 
 def matmul(a, b):
     return lax.dot_general(a, b, (((1,), (0,)), ((), ())), preferred_element_type=jnp.float32)
+
+
+def matmul_nt(a, b):
+    return lax.dot_general(a, b, (((1,), (1,)), ((), ())), preferred_element_type=jnp.float32)
 
 
 def cost(flops, *arrays):
@@ -65,31 +69,6 @@
     )(places, *([gathered] * nx), right)
 
 
-def back_rotation(columns, right_t, block):
-    parts = len(columns)
-    total_rows, width = columns[0].shape
-
-    def kernel(*refs):
-        rows_of, right_ref, out = refs[:parts], refs[parts], refs[parts + 1]
-        total = matmul(rows_of[0][...], right_ref[:width])
-        for j in range(1, parts):
-            total += matmul(rows_of[j][...], right_ref[j * width : (j + 1) * width])
-        out[...] = total.astype(out.dtype)
-
-    out = jax.ShapeDtypeStruct((total_rows, right_t.shape[1]), low)
-    return pl.pallas_call(
-        kernel,
-        out_shape=out,
-        grid=(total_rows // block,),
-        in_specs=[pl.BlockSpec((block, width), lambda k: (k, 0))] * parts
-        + [pl.BlockSpec(right_t.shape, lambda k: (0, 0), pipeline_mode=pl.Buffered(1))],
-        out_specs=pl.BlockSpec((block, right_t.shape[1]), lambda k: (k, 0)),
-        compiler_params=pltpu.CompilerParams(vmem_limit_bytes=VMEM_BYTES),
-        cost_estimate=cost(2 * total_rows * right_t.size, right_t, out, *columns),
-        name="back_rotation",
-    )(*columns, right_t)
-
-
 def per_device(gradient, left_basis, right_basis, first_moment, second_moment, *, nb, nd):
     nz = nb
     nx = nd // nz
@@ -149,52 +128,63 @@
     order_of = jnp.array([order.index(t) for t in range(nb)], jnp.int32)
     path_places = [order_of[b ^ (dd // nx)] * rows + dd % nx * out_rows for dd in path]
 
+    def together(*values):
+        return lax.optimization_barrier(values)
+
     left_t = left_basis.astype(low).T
     right = right_basis.astype(low)
-    right_t = right.T
-    piece = permute(gradient, lambda bb, zz, xx: (bb, zz ^ spread(bb), xx))
+
+    def across(piece):
+        return permute(piece, lambda bb, zz, xx: (bb, zz ^ spread(bb), xx))
+
+    def along(piece):
+        return permute(piece, lambda bb, zz, xx: (zz ^ spread(bb), zz, xx))
+
+    piece = across(gradient)
     for i, t in enumerate(reversed(bits)):
         left_t = joined(left_t, move_z(left_t, t), (z & t) != 0, i)
-    piece, left_t, right, right_t, half_places, path_places = lax.optimization_barrier(
-        (piece, left_t, right, right_t, half_places, path_places)
-    )
-    piece = permute(piece, lambda bb, zz, xx: (zz ^ spread(bb), zz, xx))
+    piece, left_t, right, half_places = together(piece, left_t, right, half_places)
+    piece = along(piece)
+    for i, u in enumerate(reversed(x_bits)):
+        other, piece = together(move_x(left_t, u), piece)
+        left_t = joined(left_t, other, (x & u) != 0, len(bits) + i)
     gathered = lax.all_gather(piece, "dp", axis_index_groups=[path])
-    for i, u in enumerate(reversed(x_bits)):
-        other, piece = lax.optimization_barrier((move_x(left_t, u), piece))
-        left_t = joined(left_t, other, (x & u) != 0, len(bits) + i)
     left_t = left_t.reshape(whole, rows)
     for t in reversed(bits):
         left_t = jnp.concatenate([left_t, move_b(left_t, t)], axis=1)
-    left_t = lax.optimization_barrier(left_t)
+    left_t, gathered = together(left_t, gathered)
     left = jnp.concatenate(
         [lax.dynamic_slice_in_dim(left_t, start, out_rows, 1).T for start in path_places], axis=0
     )
-    left_t, left, gathered = lax.optimization_barrier((left_t, left, gathered))
-
-    half = list(half_rotation(gathered, right, half_places, nz, COL_PARTS))
-
-    def product(t, j):
+    left = lax.optimization_barrier(left)
+
+    half = half_rotation(gathered, right, half_places, nz, COL_PARTS)
+
+    odd = sorted(range(1, nb, 2), key=lambda t: -t)
+    groups = odd[: nb // 4], odd[nb // 4 :]
+    turns = [(t ^ f, j) for group in groups for j in range(COL_PARTS) for t in group for f in (0, 1)]
+    products = {}
+    last = None
+    for t, j in turns:
         rows_of = lax.dynamic_slice_in_dim(left_t, (b ^ t) * rows, rows, 0)
-        return matmul(rows_of, half[j]).astype(low)
+        part = half[j] if last is None else after(half[j], last)
+        last = products[t, j] = lax.optimization_barrier(matmul(rows_of, part).astype(low))
 
     width = ff_block // COL_PARTS
-    first_out, second_out, back, joins = [], [], [], []
+    first_out, second_out, columns, joins = [], [], [], []
     for j in range(COL_PARTS):
         cols = slice(j * width, (j + 1) * width)
-        if j:
-            half[j] = after(half[j], gone)
-        gone = lax.optimization_barrier([product(t, j) for t in range(1, nb, 2)])
-        gots = [move_b(value, 1) for value in gone]
-        held = dict(zip(range(0, nb, 2), lax.optimization_barrier([product(t, j) for t in range(0, nb, 2)])))
-        held = {t: held[t].astype(jnp.float32) + got.astype(jnp.float32) for t, got in zip(held, gots)}
+        held = {}
+        for t in odd:
+            held[t ^ 1] = products[t ^ 1, j].astype(jnp.float32) + move_b(products[t, j], 1).astype(jnp.float32)
         for t in reversed(bits[1:]):
             for s in [s for s in held if s & t]:
                 away = held.pop(s).astype(low)
                 if j:
                     away = after(away, summed)
-                held[s ^ t] = held[s ^ t] + move_b(away, t).astype(jnp.float32)
-        rotated = summed = held[0]
+                arrived = move_b(away, t)
+                held[s ^ t] = held[s ^ t] + arrived.astype(jnp.float32)
+        rotated, summed = held[0], arrived
         moments = first_moment[:, cols], second_moment[:, cols]
         if j:
             moments = after(moments, previous)
@@ -214,10 +204,11 @@
             column = joined(column, other, (b & t) != 0, axis)
             joins[axis : axis + 1] = [column]
             axis += 1
-        column = lax.optimization_barrier(column.reshape(whole, width))
-        back.append(lax.optimization_barrier(matmul(left, column).astype(low)))
-
-    total = back_rotation(back, right_t, rows)
+        columns.append(column.reshape(whole, width))
+
+    columns = lax.optimization_barrier(jnp.concatenate(columns, axis=1))
+    back = lax.optimization_barrier(matmul(left, columns).astype(low))
+    total = matmul_nt(back, right).astype(low)
     update = lax.psum_scatter(total, "dp", scatter_dimension=0, axis_index_groups=[path], tiled=True)
     return (
         jnp.concatenate(first_out, axis=1),

time: 394 us -> 368 us (0.934)
  waiting for transfers between devices: 202 us -> 241 us
  starting transfers between devices: 62.8 us -> 31.7 us
  local copies, waits for them, and re-layouts: 33.4 us -> 12 us
  Pallas kernels: 26.2 us -> 10.2 us
    ppermute x17, starting transfers between devices: 62.8 us -> 31.6 us  [permute(): return lax.ppermute(value, ('basis', 'dp'), pairs)]
    all_gather x1, waiting for transfers between devices: 0.01 us -> 27.1 us  [per_device(): gathered = lax.all_gather(piece, 'dp', axis_index_groups=[path])]
    ppermute x17, waiting for transfers between devices: 114 us -> 129 us  [permute(): return lax.ppermute(value, ('basis', 'dp'), pairs)]
    unnamed x35 -> x26, local copies, waits for them, and re-layouts: 23.8 us -> 10.3 us
    pallas_call x1 -> x0, Pallas kernels: 13 us -> none  [back_rotation(): pl.pallas_call(kernel, out_shape=out, grid=(total_rows // block,), in_spe...]
    dot_general x0 -> x1, matrix products: none -> 11 us  [matmul_nt(): lax.dot_general(a, b, (((1,), (1,)), ((), ())), preferred_element_type=jn...]
    dot_general x10 -> x9, matrix products: 28.7 us -> 19.8 us  [matmul(): lax.dot_general(a, b, (((1,), (0,)), ((), ())), preferred_element_type=jn...]
    optimization_barrier x1 -> x0, local copies, waits for them, and re-layouts: 6.43 us -> none  [per_device(): lax.optimization_barrier((piece, left_t, right, right_t, half_places, pat...]
  transfers between devices with their start and end apart: 19 -> 19, of which waited for: 10 -> 12; matrix products, arithmetic and copies ran while one was open for 17% -> 9% of each run, Pallas kernels for 0% -> 0%
where the time goes in v5:
time: 368 us; the launch traced here: 367 us
  waiting for transfers between devices  241 us (65%)
  starting transfers between devices  31.7 us (9%)
  matrix products  30.7 us (8%)
  other arithmetic  24.3 us (7%)
  between operations  17 us (5%)
  local copies, waits for them, and re-layouts  12 us (3%)
  Pallas kernels  10.2 us (3%)
    ppermute x17, waiting for transfers between devices, permute(): return lax.ppermute(value, ('basis', 'dp'), pairs)  129 us
    reduce_scatter x1, waiting for transfers between devices, per_device(): lax.psum_scatter(total, 'dp', scatter_dimension=0, axis_index_groups=[pat...  84.8 us
    ppermute x17, starting transfers between devices, permute(): return lax.ppermute(value, ('basis', 'dp'), pairs)  31.6 us
    all_gather x1, waiting for transfers between devices, per_device(): gathered = lax.all_gather(piece, 'dp', axis_index_groups=[path])  27.1 us
    dot_general x9, matrix products, matmul(): lax.dot_general(a, b, (((1,), (0,)), ((), ())), preferred_element_type=jn...  19.8 us
    dot_general x1, matrix products, matmul_nt(): lax.dot_general(a, b, (((1,), (1,)), ((), ())), preferred_element_type=jn...  11 us
    unnamed x26, local copies, waits for them, and re-layouts  10.3 us
    pallas_call x1, Pallas kernels, half_rotation(): pl.pallas_call(kernel, out_shape=outs, grid_spec=pltpu.PrefetchScalarGrid...  10.2 us
  transfers between devices with their start and end apart: 19, of which 12 were waited for; matrix products, arithmetic and copies ran while one was open for 9% of the time, Pallas kernels for 0%

profile of v5, /device:TPU:0, one launch (start us, length us, event | category | flops | bytes accessed | tf_op | source)
XLA Modules:
  0.0 366.7 jit_solution(17127481515471024742)
XLA Ops:
  7.2 1.2 copy.10
  8.4 4.1 %collective-permute-start.1 = (bf16[256,512]{1,0:T(8,128)(2,1)S(1)}, bf16[256,512]{1,0:T(8,128)(2,1)S(1)}, u32[]{:S(2)}, u32[]{:S(2)}) collective-permute-start(bf16[256,512]{1,0:T(8,128)(2,1)S(1)} %bitcast.81), channel_id=1, source_target_pairs={{0,4},{1,5},{2,6},{3,7},{4,0},{5,1},{6,2},{7,3},{8,12},{9,13},{10,... | collective-permute-start | bytes 786440 | tf_op jit(solution)/shard_map/ppermute | solution.py:88
  12.5 9.5 %collective-permute-start = (bf16[512,1024]{1,0:T(8,128)(2,1)}, bf16[512,1024]{1,0:T(8,128)(2,1)}, u32[]{:S(2)}, u32[]{:S(2)}) collective-permute-start(bf16[512,1024]{1,0:T(8,128)(2,1)} %param.7), channel_id=1, source_target_pairs={{0,0},{1,1},{2,2},{3,3},{4,4},{5,5},{6,6},{7,7},{8,14},{9,15},{10,... | collective-permute-start | bytes 3145736 | tf_op jit(solution)/shard_map/ppermute | solution.py:88
  22.0 14.5 %collective-permute-done.1 = bf16[256,512]{1,0:T(8,128)(2,1)S(1)} collective-permute-done((bf16[256,512]{1,0:T(8,128)(2,1)S(1)}, bf16[256,512]{1,0:T(8,128)(2,1)S(1)}, u32[]{:S(2)}, u32[]{:S(2)}) %collective-permute-start.1) | collective-permute-done | bytes 262176 | tf_op jit(solution)/shard_map/ppermute | solution.py:88
  36.7 6.0 %convert_element_type.79.refs_2_ = bf16[2048,1024]{1,0:T(8,128)(2,1)} convert(f32[2048,1024]{1,0:T(8,128)} %param.9) | non-fusion elementwise | flops 2097152 | bytes 12582912 | tf_op jit(solution)/shard_map/convert_element_type | solution.py:135
  42.7 0.7 fusion.50.places_ref
  43.4 5.6 %collective-permute-done.2 = bf16[2,256,512]{2,1,0:T(8,128)(2,1)S(1)} collective-permute-done((bf16[2,256,512]{2,1,0:T(8,128)(2,1)S(1)}, bf16[2,256,512]{2,1,0:T(8,128)(2,1)S(1)}, u32[]{:S(2)}, u32[]{:S(2)}) %collective-permute-start.2) | collective-permute-done | bytes 524320 | tf_op jit(solution)/shard_map/ppermute | solution.py:88
  49.1 1.3 collective-permute-start.3
  50.4 1.9 collective-permute-start.4
  52.3 20.0 %collective-permute-done.3 = bf16[2,2,256,512]{3,2,1,0:T(8,128)(2,1)S(1)} collective-permute-done((bf16[2,2,256,512]{3,2,1,0:T(8,128)(2,1)S(1)}, bf16[2,2,256,512]{3,2,1,0:T(8,128)(2,1)S(1)}, u32[]{:S(2)}, u32[]{:S(2)}) %collective-permute-start.3) | collective-permute-done | bytes 1048608 | tf_op jit(solution)/shard_map/ppermute | solution.py:88
  72.3 1.0 copy-done.7
  73.7 8.5 %collective-permute-start.5 = (bf16[2048,512]{1,0:T(8,128)(2,1)S(1)}, bf16[2048,512]{1,0:T(8,128)(2,1)S(1)}, u32[]{:S(2)}, u32[]{:S(2)}) collective-permute-start(bf16[2048,512]{1,0:T(8,128)(2,1)S(1)} %bitcast.76), channel_id=1, source_target_pairs={{0,16},{1,17},{2,18},{3,19},{4,20},{5,21},{6,22},{7,23},{8,24},{9,... | collective-permute-start | bytes 6291464 | tf_op jit(solution)/shard_map/ppermute | solution.py:88
  82.2 42.4 %collective-permute-done.5 = bf16[2048,512]{1,0:T(8,128)(2,1)S(1)} collective-permute-done((bf16[2048,512]{1,0:T(8,128)(2,1)S(1)}, bf16[2048,512]{1,0:T(8,128)(2,1)S(1)}, u32[]{:S(2)}, u32[]{:S(2)}) %collective-permute-start.5) | collective-permute-done | bytes 2097184 | tf_op jit(solution)/shard_map/ppermute | solution.py:88
  124.6 1.3 copy-done.4
  125.9 2.6 pad_maximum_fusion.1
  128.5 0.6 fusion.53
  131.7 4.3 %collective-permute-done.6 = bf16[2048,1024]{1,0:T(8,128)(2,1)} collective-permute-done((bf16[2048,1024]{1,0:T(8,128)(2,1)}, bf16[2048,1024]{1,0:T(8,128)(2,1)}, u32[]{:S(2)}, u32[]{:S(2)}) %collective-permute-start.6) | collective-permute-done | bytes 4194336 | tf_op jit(solution)/shard_map/ppermute | solution.py:88
  136.0 6.6 %pad_maximum_fusion = bf16[2048,2048]{1,0:T(8,128)(2,1)} fusion(bf16[2048,1024]{1,0:T(8,128)(2,1)} %collective-permute-done.6, bf16[2048,512]{1,0:T(8,128)(2,1)} %copy-done.4, bf16[2048,512]{1,0:T(8,128)(2,1)S(1)} %bitcast.78), kind=kLoop, calls=%fused_computation | loop fusion | flops 25165824 | bytes 16777216 | tf_op jit(solution)/shard_map/concatenate | solution.py:154
  142.6 27.1 %all-gather.3.cloned.1.call-done = bf16[4096,1024]{1,0:T(8,128)(2,1)} async-done(((bf16[512,1024]{1,0:T(8,128)(2,1)}), bf16[4096,1024]{1,0:T(8,128)(2,1)}) %all-gather.3.cloned.1.call-update) | async-done | bytes 8388624 | tf_op jit(solution)/shard_map/all_gather | solution.py:151
  169.8 2.2 copy-done
  172.0 3.4 copy-done.2
  175.3 10.2 %half_rotation.1 = (bf16[2048,512]{1,0:T(8,128)(2,1)S(1)}, bf16[2048,512]{1,0:T(8,128)(2,1)S(1)}) custom-call(s32[4]{0:T(128)S(1)} %fusion.50.places_ref, bf16[8,512,1024]{2,1,0:T(8,128)(2,1)S(1)} %bitcast.74, bf16[8,512,1024]{2,1,0:T(8,128)(2,1)S(1)} %bitcast.75, bf16[2048,1024]{1,0:T(8,128)(2,1)S(1)} %copy-done), custom_call_target="tpu_custom_call" | custom-call | flops 8589934592 | bytes 16777216 | tf_op jit(solution)/shard_map/half_rotation/pallas_call | solution.py:56
  185.6 1.3 fusion.34
  186.9 1.3 fusion.28
  188.1 1.3 fusion.37
  189.5 0.5 collective-permute-start.8
  190.0 1.3 fusion.31
  191.2 1.3 fusion.22
  192.5 1.3 fusion.16
  193.8 1.3 fusion.25
  195.2 0.4 collective-permute-start.7
  195.9 1.3 fusion.19
  197.3 1.4 collective-permute-start.9
  199.3 11.9 %collective-permute-done.9 = bf16[512,512]{1,0:T(8,128)(2,1)S(1)} collective-permute-done((bf16[512,512]{1,0:T(8,128)(2,1)S(1)}, bf16[512,512]{1,0:T(8,128)(2,1)S(1)}, u32[]{:S(2)}, u32[]{:S(2)}) %collective-permute-start.9) | collective-permute-done | bytes 524320 | tf_op jit(solution)/shard_map/ppermute | solution.py:88
  211.2 1.5 collective-permute-start.12
  212.8 0.9 divide_convert_fusion.1
  213.7 0.6 collective-permute-start.13
  214.3 11.7 %collective-permute-done.12 = bf16[512,512]{1,0:T(8,128)(2,1)S(1)} collective-permute-done((bf16[512,512]{1,0:T(8,128)(2,1)S(1)}, bf16[512,512]{1,0:T(8,128)(2,1)S(1)}, u32[]{:S(2)}, u32[]{:S(2)}) %collective-permute-start.12) | collective-permute-done | bytes 524320 | tf_op jit(solution)/shard_map/ppermute | solution.py:88
  226.0 1.8 divide_convert_fusion
  227.8 1.5 collective-permute-start.15
  229.5 7.8 %collective-permute-done.13 = bf16[512,512]{1,0:T(8,128)(2,1)S(1)} collective-permute-done((bf16[512,512]{1,0:T(8,128)(2,1)S(1)}, bf16[512,512]{1,0:T(8,128)(2,1)S(1)}, u32[]{:S(2)}, u32[]{:S(2)}) %collective-permute-start.13) | collective-permute-done | bytes 524320 | tf_op jit(solution)/shard_map/ppermute | solution.py:88
  237.5 9.0 %collective-permute-done.15 = bf16[512,512]{1,0:T(8,128)(2,1)S(1)} collective-permute-done((bf16[512,512]{1,0:T(8,128)(2,1)S(1)}, bf16[512,512]{1,0:T(8,128)(2,1)S(1)}, u32[]{:S(2)}, u32[]{:S(2)}) %collective-permute-start.15) | collective-permute-done | bytes 524320 | tf_op jit(solution)/shard_map/ppermute | solution.py:88
  247.9 1.7 collective-permute-done.16
  250.0 0.6 pad_maximum_fusion.2
  250.7 9.7 %convolution_convert_fusion.1 = bf16[2048,1024]{1,0:T(8,128)(2,1)S(1)} fusion(bf16[2048,2048]{0,1:T(8,128)(2,1)S(1)} %bitcast_dynamic-update-slice_fusion, bf16[2048,1024]{1,0:T(8,128)(2,1)S(1)} %pad_maximum_fusion.2), kind=kOutput, calls=%fused_computation.4 | convolution fusion | flops 8592031744 | bytes 16777216 | tf_op jit(solution)/shard_map/dot_general | solution.py:25
  260.4 11.0 %convolution_convert_fusion = bf16[2048,2048]{1,0:T(8,128)(2,1)} fusion(bf16[2048,1024]{1,0:T(8,128)(2,1)S(1)} %convolution_convert_fusion.1, bf16[2048,1024]{1,0:T(8,128)(2,1)S(1)} %copy-done.1), kind=kOutput, calls=%fused_computation.1 | convolution fusion | flops 8594128896 | bytes 16777216 | tf_op jit(solution)/shard_map/dot_general | solution.py:29
  271.4 3.7 %pad_maximum_fusion.4 = (f32[512,1024]{1,0:T(8,128)}, f32[512,1024]{1,0:T(8,128)}) fusion(f32[512,512]{1,0:T(8,128)} %get-tuple-element.49, f32[512,512]{1,0:T(8,128)S(1)} %get-tuple-element.51, f32[512,512]{1,0:T(8,128)S(1)} %get-tuple-element.48, f32[512,512]{1,0:T(8,128)S(1)} %get-tuple-element.52), kind=kLoop, calls=%fused_computation.6 | loop fusion | flops 1048576 | bytes 8388608 | tf_op jit(solution)/shard_map/concatenate | solution.py:214
  275.1 84.8 %reduce-scatter.2.cloned.1.call-done = bf16[256,2048]{1,0:T(8,128)(2,1)} async-done(((bf16[2048,2048]{1,0:T(8,128)(2,1)}), bf16[256,2048]{1,0:T(8,128)(2,1)}) %reduce-scatter.2.cloned.1.call-update) | async-done | bytes 1048592 | tf_op jit(solution)/shard_map/reduce_scatter | solution.py:212
  (57 shorter events, 4.2 us)
Async XLA Ops:
  7.2 162.6 %all-gather.3.cloned.1.call-start = ((), (), s32[]{:S(2)}) async-start(), calls=%async_computation.2 | async-start | bytes 9437184 | tf_op jit(solution)/shard_map/all_gather | solution.py:151
  8.4 28.1 %collective-permute-start.1 = (bf16[256,512]{1,0:T(8,128)(2,1)S(1)}, bf16[256,512]{1,0:T(8,128)(2,1)S(1)}, u32[]{:S(2)}, u32[]{:S(2)}) collective-permute-start(bf16[256,512]{1,0:T(8,128)(2,1)S(1)} %bitcast.81), channel_id=1, source_target_pairs={{0,4},{1,5},{2,6},{3,7},{4,0},{5,1},{6,2},{7,3},{8,12},{9,13},{10,... | collective-permute-start | bytes 786440 | tf_op jit(solution)/shard_map/ppermute | solution.py:88
  12.5 36.6 %collective-permute-start = (bf16[512,1024]{1,0:T(8,128)(2,1)}, bf16[512,1024]{1,0:T(8,128)(2,1)}, u32[]{:S(2)}, u32[]{:S(2)}) collective-permute-start(bf16[512,1024]{1,0:T(8,128)(2,1)} %param.7), channel_id=1, source_target_pairs={{0,0},{1,1},{2,2},{3,3},{4,4},{5,5},{6,6},{7,7},{8,14},{9,15},{10,... | collective-permute-start | bytes 3145736 | tf_op jit(solution)/shard_map/ppermute | solution.py:88
  36.6 12.3 %collective-permute-start.2 = (bf16[2,256,512]{2,1,0:T(8,128)(2,1)S(1)}, bf16[2,256,512]{2,1,0:T(8,128)(2,1)S(1)}, u32[]{:S(2)}, u32[]{:S(2)}) collective-permute-start(bf16[2,256,512]{2,1,0:T(8,128)(2,1)S(1)} %pad_maximum_fusion.11), channel_id=1, source_target_pairs={{0,2},{1,3},{2,0},{3,1},{4,6},{5,7},{6,4},{7,5},{8,10},{9,11},{10,... | collective-permute-start | bytes 1572872 | tf_op jit(solution)/shard_map/ppermute | solution.py:88
  49.1 23.1 %collective-permute-start.3 = (bf16[2,2,256,512]{3,2,1,0:T(8,128)(2,1)S(1)}, bf16[2,2,256,512]{3,2,1,0:T(8,128)(2,1)S(1)}, u32[]{:S(2)}, u32[]{:S(2)}) collective-permute-start(bf16[2,2,256,512]{3,2,1,0:T(8,128)(2,1)S(1)} %pad_maximum_fusion.8), channel_id=1, source_target_pairs={{0,1},{1,0},{2,3},{3,2},{4,5},{5,4},{6,7},{7,6},{8,9},{9,8},{10,11... | collective-permute-start | bytes 3145736 | tf_op jit(solution)/shard_map/ppermute | solution.py:88
  50.4 21.8 %collective-permute-start.4 = (bf16[512,1024]{1,0:T(8,128)(2,1)}, bf16[512,1024]{1,0:T(8,128)(2,1)S(1)}, u32[]{:S(2)}, u32[]{:S(2)}) collective-permute-start(bf16[512,1024]{1,0:T(8,128)(2,1)} %collective-permute-done), channel_id=1, source_target_pairs={{0,0},{1,1},{2,10},{3,11},{4,20},{5,21},{6,30},{7,31},{8,24},{9,25... | collective-permute-start | bytes 3145736 | tf_op jit(solution)/shard_map/ppermute | solution.py:88
  72.3 1.0 copy-start.7
  73.3 286.6 %reduce-scatter.2.cloned.1.call-start = ((), (), s32[]{:S(2)}) async-start(), calls=%async_computation.1 | async-start | bytes 9437184 | tf_op jit(solution)/shard_map/reduce_scatter | solution.py:212
  73.7 54.8 %copy-start.8 = (s32[4]{0:T(128)S(1)}, s32[4]{0:T(128)}, u32[]{:S(2)}) copy-start(s32[4]{0:T(128)} %constant.71.clone) | copy-start | bytes 52
  73.7 50.9 %collective-permute-start.5 = (bf16[2048,512]{1,0:T(8,128)(2,1)S(1)}, bf16[2048,512]{1,0:T(8,128)(2,1)S(1)}, u32[]{:S(2)}, u32[]{:S(2)}) collective-permute-start(bf16[2048,512]{1,0:T(8,128)(2,1)S(1)} %bitcast.76), channel_id=1, source_target_pairs={{0,16},{1,17},{2,18},{3,19},{4,20},{5,21},{6,22},{7,23},{8,24},{9,... | collective-permute-start | bytes 6291464 | tf_op jit(solution)/shard_map/ppermute | solution.py:88
  124.6 1.3 copy-start.4
  128.5 7.5 %collective-permute-start.6 = (bf16[2048,1024]{1,0:T(8,128)(2,1)}, bf16[2048,1024]{1,0:T(8,128)(2,1)}, u32[]{:S(2)}, u32[]{:S(2)}) collective-permute-start(bf16[2048,1024]{1,0:T(8,128)(2,1)} %pad_maximum_fusion.1), channel_id=1, source_target_pairs={{0,8},{1,9},{2,10},{3,11},{4,12},{5,13},{6,14},{7,15},{8,0},{9,1},... | collective-permute-start | bytes 12582920 | tf_op jit(solution)/shard_map/ppermute | solution.py:88
  169.8 2.2 copy-start
  172.0 3.4 copy-start.2
  175.3 10.2 %copy-start.3 = (bf16[2048,2048]{1,0:T(8,128)(2,1)S(1)}, bf16[2048,2048]{1,0:T(8,128)(2,1)}, u32[]{:S(2)}) copy-start(bf16[2048,2048]{1,0:T(8,128)(2,1)} %pad_maximum_fusion) | copy-start | bytes 25165828
  189.4 9.8 %collective-permute-start.11 = (bf16[512,512]{1,0:T(8,128)(2,1)S(1)}, bf16[512,512]{1,0:T(8,128)(2,1)S(1)}, u32[]{:S(2)}, u32[]{:S(2)}) collective-permute-start(bf16[512,512]{1,0:T(8,128)(2,1)S(1)} %fusion.37), channel_id=1, source_target_pairs={{0,8},{1,9},{2,10},{3,11},{4,12},{5,13},{6,14},{7,15},{8,0},{9,1},... | collective-permute-start | bytes 1572872 | tf_op jit(solution)/shard_map/ppermute | solution.py:88
  189.5 7.7 %collective-permute-start.8 = (bf16[512,512]{1,0:T(8,128)(2,1)S(1)}, bf16[512,512]{1,0:T(8,128)(2,1)S(1)}, u32[]{:S(2)}, u32[]{:S(2)}) collective-permute-start(bf16[512,512]{1,0:T(8,128)(2,1)S(1)} %fusion.34), channel_id=1, source_target_pairs={{0,8},{1,9},{2,10},{3,11},{4,12},{5,13},{6,14},{7,15},{8,0},{9,1},... | collective-permute-start | bytes 1572872 | tf_op jit(solution)/shard_map/ppermute | solution.py:88
  195.0 19.3 %collective-permute-start.10 = (bf16[512,512]{1,0:T(8,128)(2,1)S(1)}, bf16[512,512]{1,0:T(8,128)(2,1)S(1)}, u32[]{:S(2)}, u32[]{:S(2)}) collective-permute-start(bf16[512,512]{1,0:T(8,128)(2,1)S(1)} %fusion.25), channel_id=1, source_target_pairs={{0,8},{1,9},{2,10},{3,11},{4,12},{5,13},{6,14},{7,15},{8,0},{9,1},... | collective-permute-start | bytes 1572872 | tf_op jit(solution)/shard_map/ppermute | solution.py:88
  195.2 17.6 %collective-permute-start.7 = (bf16[512,512]{1,0:T(8,128)(2,1)S(1)}, bf16[512,512]{1,0:T(8,128)(2,1)S(1)}, u32[]{:S(2)}, u32[]{:S(2)}) collective-permute-start(bf16[512,512]{1,0:T(8,128)(2,1)S(1)} %fusion.22), channel_id=1, source_target_pairs={{0,8},{1,9},{2,10},{3,11},{4,12},{5,13},{6,14},{7,15},{8,0},{9,1},... | collective-permute-start | bytes 1572872 | tf_op jit(solution)/shard_map/ppermute | solution.py:88
  197.3 15.5 %copy-start.5 = (f32[512,1024]{1,0:T(8,128)S(1)}, f32[512,1024]{1,0:T(8,128)}, u32[]{:S(2)}) copy-start(f32[512,1024]{1,0:T(8,128)} %param.10) | copy-start | bytes 6291460
  197.3 15.5 %copy-start.6 = (f32[512,1024]{1,0:T(8,128)S(1)}, f32[512,1024]{1,0:T(8,128)}, u32[]{:S(2)}) copy-start(f32[512,1024]{1,0:T(8,128)} %param.11) | copy-start | bytes 6291460
  197.3 13.9 %collective-permute-start.9 = (bf16[512,512]{1,0:T(8,128)(2,1)S(1)}, bf16[512,512]{1,0:T(8,128)(2,1)S(1)}, u32[]{:S(2)}, u32[]{:S(2)}) collective-permute-start(bf16[512,512]{1,0:T(8,128)(2,1)S(1)} %add_convert_fusion.1), channel_id=1, source_target_pairs={{0,16},{1,17},{2,18},{3,19},{4,20},{5,21},{6,22},{7,23},{8,24},{9,... | collective-permute-start | bytes 1572872 | tf_op jit(solution)/shard_map/ppermute | solution.py:88
  211.2 14.9 %collective-permute-start.12 = (bf16[512,512]{1,0:T(8,128)(2,1)S(1)}, bf16[512,512]{1,0:T(8,128)(2,1)S(1)}, u32[]{:S(2)}, u32[]{:S(2)}) collective-permute-start(bf16[512,512]{1,0:T(8,128)(2,1)S(1)} %add_convert_fusion), channel_id=1, source_target_pairs={{0,16},{1,17},{2,18},{3,19},{4,20},{5,21},{6,22},{7,23},{8,24},{9,... | collective-permute-start | bytes 1572872 | tf_op jit(solution)/shard_map/ppermute | solution.py:88
  213.7 23.6 %collective-permute-start.13 = (bf16[512,512]{1,0:T(8,128)(2,1)S(1)}, bf16[512,512]{1,0:T(8,128)(2,1)S(1)}, u32[]{:S(2)}, u32[]{:S(2)}) collective-permute-start(bf16[512,512]{1,0:T(8,128)(2,1)S(1)} %get-tuple-element.50), channel_id=1, source_target_pairs={{0,16},{1,17},{2,18},{3,19},{4,20},{5,21},{6,22},{7,23},{8,24},{9,... | collective-permute-start | bytes 1572872 | tf_op jit(solution)/shard_map/ppermute | solution.py:88
  227.8 18.7 %collective-permute-start.15 = (bf16[512,512]{1,0:T(8,128)(2,1)S(1)}, bf16[512,512]{1,0:T(8,128)(2,1)S(1)}, u32[]{:S(2)}, u32[]{:S(2)}) collective-permute-start(bf16[512,512]{1,0:T(8,128)(2,1)S(1)} %get-tuple-element.47), channel_id=1, source_target_pairs={{0,16},{1,17},{2,18},{3,19},{4,20},{5,21},{6,22},{7,23},{8,24},{9,... | collective-permute-start | bytes 1572872 | tf_op jit(solution)/shard_map/ppermute | solution.py:88
  237.5 9.9 %collective-permute-start.14 = (bf16[2,512,512]{2,1,0:T(8,128)(2,1)S(1)}, bf16[2,512,512]{2,1,0:T(8,128)(2,1)S(1)}, u32[]{:S(2)}, u32[]{:S(2)}) collective-permute-start(bf16[2,512,512]{2,1,0:T(8,128)(2,1)S(1)} %pad_maximum_fusion.9), channel_id=1, source_target_pairs={{0,8},{1,9},{2,10},{3,11},{4,12},{5,13},{6,14},{7,15},{8,0},{9,1},... | collective-permute-start | bytes 3145736 | tf_op jit(solution)/shard_map/ppermute | solution.py:88
  246.8 2.7 collective-permute-start.16
  250.7 9.7 %copy-start.1 = (bf16[2048,1024]{1,0:T(8,128)(2,1)S(1)}, bf16[2048,1024]{1,0:T(8,128)(2,1)}, u32[]{:S(2)}) copy-start(bf16[2048,1024]{1,0:T(8,128)(2,1)} %convert_element_type.79.refs_2_) | copy-start | bytes 12582916
Sparse Core Ops, SparseCore 0:
  73.4 96.3 all-gather.2
  271.5 88.3 reduce-scatter.1

commit v6 on v5

--- a/solution.py
+++ b/solution.py
@@ -16,7 +16,7 @@
 
 COL_PARTS = 2
 
-VMEM_BYTES = 20 * 1024 * 1024
+VMEM_BYTES = 54 * 1024 * 1024
 
 low = jnp.bfloat16
 
@@ -34,13 +34,13 @@
     return pl.CostEstimate(flops=flops, bytes_accessed=size, transcendentals=0)
 
 
-def half_rotation(gathered, right, places, nz, parts):
+def half_rotation(gathered, right, places, nz, parts, part, row_parts, held):
     count, rows, cols = gathered.shape
     nx = count // nz
     width = right.shape[1] // parts
 
     def kernel(places_ref, *refs):
-        blocks, right_ref, outs = refs[:nx], refs[nx], refs[nx + 1 :]
+        blocks, right_ref, outs = refs[:nx], refs[nx], refs[-parts:]
         for j, out in enumerate(outs):
             total = matmul(blocks[0][...], right_ref[:cols, j * width : (j + 1) * width])
             for i in range(1, nx):
@@ -52,7 +52,7 @@
             return pl.BlockSpec((None, rows, cols), lambda k, p: (i * nz + k, 0, 0))
         return pl.BlockSpec((None, rows, cols), lambda k, p: (i * nz + nz - 1 - k, 0, 0))
 
-    outs = [jax.ShapeDtypeStruct((nz * rows, width), low)] * parts
+    outs = [jax.ShapeDtypeStruct((nz * rows * row_parts, width), low)] * parts
     return pl.pallas_call(
         kernel,
         out_shape=outs,
@@ -60,13 +60,15 @@
             num_scalar_prefetch=1,
             grid=(nz,),
             in_specs=[block_of(i) for i in range(nx)]
-            + [pl.BlockSpec(right.shape, lambda k, p: (0, 0), pipeline_mode=pl.Buffered(1))],
-            out_specs=[pl.BlockSpec((rows, width), lambda k, p: (p[k], 0))] * parts,
+            + [pl.BlockSpec(right.shape, lambda k, p: (0, 0), pipeline_mode=pl.Buffered(1))]
+            + [pl.BlockSpec(memory_space=pl.ANY)] * len(held),
+            out_specs=[pl.BlockSpec((rows, width), lambda k, p: (p[k] * row_parts + part, 0))] * parts,
         ),
+        input_output_aliases={nx + 2 + j: j for j in range(len(held))},
         compiler_params=pltpu.CompilerParams(vmem_limit_bytes=VMEM_BYTES),
         cost_estimate=cost(2 * gathered.size * right.shape[1], gathered, right, *outs),
         name="half_rotation",
-    )(places, *([gathered] * nx), right)
+    )(places, *([gathered] * nx), right, *held)
 
 
 def per_device(gradient, left_basis, right_basis, first_moment, second_moment, *, nb, nd):
@@ -140,54 +142,70 @@
     def along(piece):
         return permute(piece, lambda bb, zz, xx: (zz ^ spread(bb), zz, xx))
 
-    piece = across(gradient)
-    for i, t in enumerate(reversed(bits)):
+    part = rows // 2
+    first, second = gradient[:part], gradient[part:]
+    first = across(first)
+    for i, t in enumerate(reversed(bits[1:])):
         left_t = joined(left_t, move_z(left_t, t), (z & t) != 0, i)
-    piece, left_t, right, half_places = together(piece, left_t, right, half_places)
-    piece = along(piece)
+    first, left_t, right, half_places = together(first, left_t, right, half_places)
+    left_t = joined(left_t, move_z(left_t, bits[0]), (z & bits[0]) != 0, len(bits) - 1)
+    first, second, left_t = together(along(first), across(after(second, first)), left_t)
+    gathered = [lax.all_gather(first, "dp", axis_index_groups=[path])]
+    second = along(second)
     for i, u in enumerate(reversed(x_bits)):
-        other, piece = together(move_x(left_t, u), piece)
+        other, second = together(move_x(left_t, u), second)
         left_t = joined(left_t, other, (x & u) != 0, len(bits) + i)
-    gathered = lax.all_gather(piece, "dp", axis_index_groups=[path])
+    gathered.append(lax.all_gather(second, "dp", axis_index_groups=[path]))
     left_t = left_t.reshape(whole, rows)
     for t in reversed(bits):
         left_t = jnp.concatenate([left_t, move_b(left_t, t)], axis=1)
-    left_t, gathered = together(left_t, gathered)
+    left_t, gathered[1] = together(left_t, gathered[1])
+    half = []
+    for h in range(2):
+        half = list(half_rotation(gathered[h], right, half_places, nz, COL_PARTS, h, 2, half))
+
+    products = {}
+    last = None
+    odd = sorted(range(1, nb, 2), key=lambda t: -t)
+    held = [{} for _ in range(COL_PARTS)]
+    for group in (odd[: nb // 4], odd[nb // 4 :]):
+        for j in range(COL_PARTS):
+            for t in (t for pair in group for t in (pair, pair ^ 1)):
+                rows_of = lax.dynamic_slice_in_dim(left_t, (b ^ t) * rows, rows, 0)
+                part = half[j] if last is None else after(half[j], last)
+                last = products[t, j] = lax.optimization_barrier(matmul(rows_of, part).astype(low))
+        for j in range(COL_PARTS):
+            for t in group:
+                got = move_b(products[t, j], 1)
+                held[j][t ^ 1] = products[t ^ 1, j].astype(jnp.float32) + got.astype(jnp.float32)
+        last = held[0][group[-1] ^ 1] = lax.optimization_barrier(held[0][group[-1] ^ 1].astype(low))
+    held[0] = {t: value.astype(jnp.float32) for t, value in held[0].items()}
+
+    arrived = []
+    for j in range(COL_PARTS):
+        for t in reversed(bits[1:]):
+            for s in [s for s in held[j] if s & t]:
+                away = held[j].pop(s).astype(low)
+                if j:
+                    away = after(away, arrived[j - 1])
+                got = move_b(away, t)
+                held[j][s ^ t] = held[j][s ^ t] + got.astype(jnp.float32)
+        arrived.append(got)
+
+    source = after(left_t, arrived[0])
     left = jnp.concatenate(
-        [lax.dynamic_slice_in_dim(left_t, start, out_rows, 1).T for start in path_places], axis=0
+        [lax.dynamic_slice_in_dim(source, start, out_rows, 1).T for start in path_places], axis=0
     )
     left = lax.optimization_barrier(left)
 
-    half = half_rotation(gathered, right, half_places, nz, COL_PARTS)
-
-    odd = sorted(range(1, nb, 2), key=lambda t: -t)
-    groups = odd[: nb // 4], odd[nb // 4 :]
-    turns = [(t ^ f, j) for group in groups for j in range(COL_PARTS) for t in group for f in (0, 1)]
-    products = {}
-    last = None
-    for t, j in turns:
-        rows_of = lax.dynamic_slice_in_dim(left_t, (b ^ t) * rows, rows, 0)
-        part = half[j] if last is None else after(half[j], last)
-        last = products[t, j] = lax.optimization_barrier(matmul(rows_of, part).astype(low))
-
     width = ff_block // COL_PARTS
-    first_out, second_out, columns, joins = [], [], [], []
+    first_out, second_out, directions = [], [], []
     for j in range(COL_PARTS):
         cols = slice(j * width, (j + 1) * width)
-        held = {}
-        for t in odd:
-            held[t ^ 1] = products[t ^ 1, j].astype(jnp.float32) + move_b(products[t, j], 1).astype(jnp.float32)
-        for t in reversed(bits[1:]):
-            for s in [s for s in held if s & t]:
-                away = held.pop(s).astype(low)
-                if j:
-                    away = after(away, summed)
-                arrived = move_b(away, t)
-                held[s ^ t] = held[s ^ t] + arrived.astype(jnp.float32)
-        rotated, summed = held[0], arrived
+        rotated = held[j][0]
         moments = first_moment[:, cols], second_moment[:, cols]
         if j:
-            moments = after(moments, previous)
+            moments = after(moments, directions[-1])
         first_new = beta_first * moments[0] + (1.0 - beta_first) * rotated
         second_new = beta_second * moments[1] + (1.0 - beta_second) * rotated * rotated
         first_fix = 1.0 - beta_first**STEP
@@ -195,19 +213,22 @@
         direction = first_new / first_fix / (jnp.sqrt(second_new / second_fix) + epsilon)
         first_out.append(first_new)
         second_out.append(second_new)
-        column = previous = direction.astype(low)
-        axis = 0
-        for t in reversed(bits):
+        directions.append(direction.astype(low))
+
+    back, joins = [], []
+    for j, column in enumerate(directions):
+        for axis, t in enumerate(reversed(bits)):
             other = move_b(column, t)
             if j:
-                other = after(other, joins[axis])
+                other = after(other, joins[axis], back[-1])
+            elif not axis:
+                other = after(other, left, directions[-1])
             column = joined(column, other, (b & t) != 0, axis)
             joins[axis : axis + 1] = [column]
-            axis += 1
-        columns.append(column.reshape(whole, width))
-
-    columns = lax.optimization_barrier(jnp.concatenate(columns, axis=1))
-    back = lax.optimization_barrier(matmul(left, columns).astype(low))
+        column = lax.optimization_barrier(column.reshape(whole, width))
+        back.append(lax.optimization_barrier(matmul(left, column).astype(low)))
+
+    back = lax.optimization_barrier(jnp.concatenate(back, axis=1))
     total = matmul_nt(back, right).astype(low)
     update = lax.psum_scatter(total, "dp", scatter_dimension=0, axis_index_groups=[path], tiled=True)
     return (

time: 368 us -> 362 us (0.984)
  waiting for transfers between devices: 241 us -> 191 us
  starting transfers between devices: 31.7 us -> 51.9 us
  Pallas kernels: 10.2 us -> 18.7 us
  other arithmetic: 24.3 us -> 30.2 us
  matrix products: 30.7 us -> 36.2 us
  local copies, waits for them, and re-layouts: 12 us -> 16.8 us
    ppermute x17 -> x19, waiting for transfers between devices: 129 us -> 97.9 us  [permute(): return lax.ppermute(value, ('basis', 'dp'), pairs)]
    ppermute x17 -> x19, starting transfers between devices: 31.6 us -> 51.7 us  [permute(): return lax.ppermute(value, ('basis', 'dp'), pairs)]
    all_gather x1 -> x2, waiting for transfers between devices: 27.1 us -> 9.57 us  [the longest x1 9.55 us: per_device(): gathered.append(lax.all_gather(second, 'dp', axis_index_groups=[path]))]
    pallas_call x1 -> x2, Pallas kernels: 10.2 us -> 18.7 us  [half_rotation(): pl.pallas_call(kernel, out_shape=outs, grid_spec=pltpu.PrefetchScalarGrid...]
    dot_general x9 -> x10, matrix products: 19.8 us -> 25.3 us  [matmul(): lax.dot_general(a, b, (((1,), (0,)), ((), ())), preferred_element_type=jn...]
    another operation x14, other arithmetic: 1.68 us -> 6.08 us  [joined(): return jnp.stack([first, second], axis=axis)]
    unnamed x26 -> x38, local copies, waits for them, and re-layouts: 10.3 us -> 13.2 us
  transfers between devices with their start and end apart: 19 -> 22, of which waited for: 12 -> 12; matrix products, arithmetic and copies ran while one was open for 9% -> 14% of each run, Pallas kernels for 0% -> 3%
where the time goes in v6:
time: 362 us; the launch traced here: 361 us
  waiting for transfers between devices  191 us (53%)
  starting transfers between devices  51.9 us (14%)
  matrix products  36.2 us (10%)
  other arithmetic  30.2 us (8%)
  Pallas kernels  18.7 us (5%)
  between operations  16.9 us (5%)
  local copies, waits for them, and re-layouts  16.8 us (5%)
    ppermute x19, waiting for transfers between devices, permute(): return lax.ppermute(value, ('basis', 'dp'), pairs)  97.9 us
    reduce_scatter x1, waiting for transfers between devices, per_device(): lax.psum_scatter(total, 'dp', scatter_dimension=0, axis_index_groups=[pat...  83.1 us
    ppermute x19, starting transfers between devices, permute(): return lax.ppermute(value, ('basis', 'dp'), pairs)  51.7 us
    dot_general x10, matrix products, matmul(): lax.dot_general(a, b, (((1,), (0,)), ((), ())), preferred_element_type=jn...  25.3 us
    pallas_call x2, Pallas kernels, half_rotation(): pl.pallas_call(kernel, out_shape=outs, grid_spec=pltpu.PrefetchScalarGrid...  18.7 us
    unnamed x38, local copies, waits for them, and re-layouts  13.2 us
    dot_general x1, matrix products, matmul_nt(): lax.dot_general(a, b, (((1,), (1,)), ((), ())), preferred_element_type=jn...  10.9 us
    all_gather x1, waiting for transfers between devices, per_device(): gathered.append(lax.all_gather(second, 'dp', axis_index_groups=[path]))  9.55 us
  transfers between devices with their start and end apart: 22, of which 12 were waited for; matrix products, arithmetic and copies ran while one was open for 14% of the time, Pallas kernels for 3%

profile of v6, /device:TPU:0, one launch (start us, length us, event | category | flops | bytes accessed | tf_op | source)
XLA Modules:
  0.0 361.3 jit_solution(7735635876576497075)
XLA Ops:
  7.2 1.2 copy.12
  8.4 4.1 %collective-permute-start.1 = (bf16[256,512]{1,0:T(8,128)(2,1)S(1)}, bf16[256,512]{1,0:T(8,128)(2,1)S(1)}, u32[]{:S(2)}, u32[]{:S(2)}) collective-permute-start(bf16[256,512]{1,0:T(8,128)(2,1)S(1)} %bitcast.84), channel_id=1, source_target_pairs={{0,4},{1,5},{2,6},{3,7},{4,0},{5,1},{6,2},{7,3},{8,12},{9,13},{10,... | collective-permute-start | bytes 786440 | tf_op jit(solution)/shard_map/ppermute | solution.py:90
  12.5 1.3 fusion.53
  14.5 6.1 %convert_element_type.90.refs_2_ = bf16[2048,1024]{1,0:T(8,128)(2,1)} convert(f32[2048,1024]{1,0:T(8,128)} %param.9) | non-fusion elementwise | flops 2097152 | bytes 12582912 | tf_op jit(solution)/shard_map/convert_element_type | solution.py:137
  20.6 1.3 fusion.50.places_ref
  21.9 9.0 %collective-permute-done.1 = bf16[256,512]{1,0:T(8,128)(2,1)S(1)} collective-permute-done((bf16[256,512]{1,0:T(8,128)(2,1)S(1)}, bf16[256,512]{1,0:T(8,128)(2,1)S(1)}, u32[]{:S(2)}, u32[]{:S(2)}) %collective-permute-start.1) | collective-permute-done | bytes 262176 | tf_op jit(solution)/shard_map/ppermute | solution.py:90
  32.5 10.6 %collective-permute-done.4 = bf16[2,256,512]{2,1,0:T(8,128)(2,1)S(1)} collective-permute-done((bf16[2,256,512]{2,1,0:T(8,128)(2,1)S(1)}, bf16[2,256,512]{2,1,0:T(8,128)(2,1)S(1)}, u32[]{:S(2)}, u32[]{:S(2)}) %collective-permute-start.4) | collective-permute-done | bytes 524320 | tf_op jit(solution)/shard_map/ppermute | solution.py:90
  44.1 2.2 collective-permute-start.5
  47.8 15.5 %collective-permute-done.5 = bf16[2,2,256,512]{3,2,1,0:T(8,128)(2,1)S(1)} collective-permute-done((bf16[2,2,256,512]{3,2,1,0:T(8,128)(2,1)S(1)}, bf16[2,2,256,512]{3,2,1,0:T(8,128)(2,1)S(1)}, u32[]{:S(2)}, u32[]{:S(2)}) %collective-permute-start.5) | collective-permute-done | bytes 1048608 | tf_op jit(solution)/shard_map/ppermute | solution.py:90
  63.4 1.1 select_bitcast_fusion.5
  64.5 1.5 pad_maximum_fusion.3
  66.1 36.5 %collective-permute-start.7 = (bf16[2048,512]{1,0:T(8,128)(2,1)S(1)}, bf16[2048,512]{1,0:T(8,128)(2,1)S(1)}, u32[]{:S(2)}, u32[]{:S(2)}) collective-permute-start(bf16[2048,512]{1,0:T(8,128)(2,1)S(1)} %bitcast.77), channel_id=1, source_target_pairs={{0,16},{1,17},{2,18},{3,19},{4,20},{5,21},{6,22},{7,23},{8,24},{9,... | collective-permute-start | bytes 6291464 | tf_op jit(solution)/shard_map/ppermute | solution.py:90
  102.5 37.1 %collective-permute-done.7 = bf16[2048,512]{1,0:T(8,128)(2,1)S(1)} collective-permute-done((bf16[2048,512]{1,0:T(8,128)(2,1)S(1)}, bf16[2048,512]{1,0:T(8,128)(2,1)S(1)}, u32[]{:S(2)}, u32[]{:S(2)}) %collective-permute-start.7) | collective-permute-done | bytes 2097184 | tf_op jit(solution)/shard_map/ppermute | solution.py:90
  139.6 1.4 copy-done.2
  141.0 2.7 pad_maximum_fusion.1
  146.9 9.2 %half_rotation.2 = (bf16[2048,512]{1,0:T(8,128)(2,1)}, bf16[2048,512]{1,0:T(8,128)(2,1)}) custom-call(s32[4]{0:T(128)} %fusion.50.places_ref, bf16[8,256,1024]{2,1,0:T(8,128)(2,1)} %bitcast.87, bf16[8,256,1024]{2,1,0:T(8,128)(2,1)} %bitcast.88, bf16[2048,1024]{1,0:T(8,128)(2,1)} %convert_element_type.90.refs_2_), custom_call_target="tpu_custom_call" | custom-call | flops 4294967296 | bytes 12582912 | tf_op jit(solution)/shard_map/half_rotation/pallas_call | solution.py:56
  156.2 6.3 %pad_maximum_fusion = bf16[2048,2048]{1,0:T(8,128)(2,1)} fusion(bf16[2048,1024]{1,0:T(8,128)(2,1)} %collective-permute-done.8, bf16[2048,512]{1,0:T(8,128)(2,1)S(1)} %copy-done.3, bf16[2048,512]{1,0:T(8,128)(2,1)S(1)} %bitcast.79), kind=kLoop, calls=%fused_computation | loop fusion | flops 25165824 | bytes 16777216 | tf_op jit(solution)/shard_map/concatenate | solution.py:161
  162.5 9.5 %all-gather.5.cloned.1.call-done = bf16[2048,1024]{1,0:T(8,128)(2,1)} async-done(((bf16[256,1024]{1,0:T(8,128)(2,1)}), bf16[2048,1024]{1,0:T(8,128)(2,1)}) %all-gather.5.cloned.1.call-update) | async-done | bytes 4194320 | tf_op jit(solution)/shard_map/all_gather | solution.py:158
  172.0 9.5 %half_rotation.3 = (bf16[2048,512]{1,0:T(8,128)(2,1)}, bf16[2048,512]{1,0:T(8,128)(2,1)}) custom-call(s32[4]{0:T(128)} %fusion.50.places_ref, bf16[8,256,1024]{2,1,0:T(8,128)(2,1)} %bitcast.80, bf16[8,256,1024]{2,1,0:T(8,128)(2,1)} %bitcast.81, bf16[2048,1024]{1,0:T(8,128)(2,1)} %convert_element_type.90.refs_2_, ...), custom_call_target="tpu_custom_call", output_to_operand_aliasing={{0}: (4, {}), {1}: (5, {})} | custom-call | flops 4294967296 | bytes 12582912 | tf_op jit(solution)/shard_map/half_rotation/pallas_call | solution.py:56
  181.5 3.0 fusion.34
  184.6 1.3 fusion.28
  186.1 1.3 fusion.37
  187.7 1.3 fusion.31
  189.1 1.5 collective-permute-start.11
  190.7 1.3 fusion.22
  191.9 1.3 fusion.16
  193.2 1.3 fusion.25
  195.1 1.3 fusion.19
  196.5 6.8 %collective-permute-done.11 = bf16[512,512]{1,0:T(8,128)(2,1)S(1)} collective-permute-done((bf16[512,512]{1,0:T(8,128)(2,1)S(1)}, bf16[512,512]{1,0:T(8,128)(2,1)S(1)}, u32[]{:S(2)}, u32[]{:S(2)}) %collective-permute-start.11) | collective-permute-done | bytes 524320 | tf_op jit(solution)/shard_map/ppermute | solution.py:90
  203.3 1.5 collective-permute-start.14
  204.9 1.8 divide_convert_fusion.1
  208.5 3.3 copy-done.11
  211.8 6.4 %collective-permute-done.14 = bf16[512,512]{1,0:T(8,128)(2,1)S(1)} collective-permute-done((bf16[512,512]{1,0:T(8,128)(2,1)S(1)}, bf16[512,512]{1,0:T(8,128)(2,1)S(1)}, u32[]{:S(2)}, u32[]{:S(2)}) %collective-permute-start.14) | collective-permute-done | bytes 524320 | tf_op jit(solution)/shard_map/ppermute | solution.py:90
  218.1 2.1 divide_convert_fusion
  220.3 7.5 %collective-permute-done.15 = bf16[512,512]{1,0:T(8,128)(2,1)S(1)} collective-permute-done((bf16[512,512]{1,0:T(8,128)(2,1)S(1)}, bf16[512,512]{1,0:T(8,128)(2,1)S(1)}, u32[]{:S(2)}, u32[]{:S(2)}) %collective-permute-start.15) | collective-permute-done | bytes 524320 | tf_op jit(solution)/shard_map/ppermute | solution.py:90
  227.8 1.1 pad_maximum_fusion.9
  228.9 1.5 collective-permute-start.17
  230.4 1.5 collective-permute-done.16
  231.9 1.4 select_bitcast_fusion.3
  233.6 8.7 %convolution_convert_fusion.2 = bf16[2048,512]{1,0:T(8,128)(2,1)S(1)} fusion(bf16[2048,2048]{0,1:T(8,128)(2,1)} %copy-done.11, bf16[2048,512]{1,0:T(8,128)(2,1)S(1)} %bitcast.83), kind=kOutput, calls=%fused_computation.5 | convolution fusion | flops 4296015872 | bytes 12582912 | tf_op jit(solution)/shard_map/dot_general | solution.py:25
  243.5 2.6 collective-permute-done.18
  246.7 1.8 slice-done.1
  248.5 4.8 %convolution_convert_fusion.1 = bf16[2048,512]{1,0:T(8,128)(2,1)S(1)} fusion(bf16[2048,2048]{0,1:T(8,128)(2,1)S(1)} %bitcast.86, bf16[2048,512]{1,0:T(8,128)(2,1)S(1)} %bitcast.82), kind=kOutput, calls=%fused_computation.4 | convolution fusion | flops 4296015872 | bytes 12582912 | tf_op jit(solution)/shard_map/dot_general | solution.py:25
  253.9 1.5 copy-done.1
  255.5 10.9 %convolution_convert_fusion = bf16[2048,2048]{1,0:T(8,128)(2,1)} fusion(bf16[2048,1024]{1,0:T(8,128)(2,1)S(1)} %pad_maximum_fusion.2, bf16[2048,1024]{1,0:T(8,128)(2,1)S(1)} %copy-done.1), kind=kOutput, calls=%fused_computation.1 | convolution fusion | flops 8594128896 | bytes 16777216 | tf_op jit(solution)/shard_map/dot_general | solution.py:29
  266.4 1.2 copy-done.4
  267.6 4.1 %pad_maximum_fusion.4 = (f32[512,1024]{1,0:T(8,128)}, f32[512,1024]{1,0:T(8,128)}) fusion(f32[512,512]{1,0:T(8,128)} %get-tuple-element.65, f32[512,512]{1,0:T(8,128)S(1)} %get-tuple-element.67, f32[512,512]{1,0:T(8,128)} %get-tuple-element.64, f32[512,512]{1,0:T(8,128)S(1)} %copy-done.4), kind=kLoop, calls=%fused_computation.7 | loop fusion | flops 1048576 | bytes 8388608 | tf_op jit(solution)/shard_map/concatenate | solution.py:235
  271.7 83.1 %reduce-scatter.2.cloned.1.call-done = bf16[256,2048]{1,0:T(8,128)(2,1)} async-done(((bf16[2048,2048]{1,0:T(8,128)(2,1)}), bf16[256,2048]{1,0:T(8,128)(2,1)}) %reduce-scatter.2.cloned.1.call-update) | async-done | bytes 1048592 | tf_op jit(solution)/shard_map/reduce_scatter | solution.py:233
  (81 shorter events, 11.6 us)
Async XLA Ops:
  7.2 139.7 %all-gather.7.cloned.1.call-start = ((), (), s32[]{:S(2)}) async-start(), calls=%async_computation.3 | async-start | bytes 4718592 | tf_op jit(solution)/shard_map/all_gather | solution.py:153
  8.4 22.5 %collective-permute-start.1 = (bf16[256,512]{1,0:T(8,128)(2,1)S(1)}, bf16[256,512]{1,0:T(8,128)(2,1)S(1)}, u32[]{:S(2)}, u32[]{:S(2)}) collective-permute-start(bf16[256,512]{1,0:T(8,128)(2,1)S(1)} %bitcast.84), channel_id=1, source_target_pairs={{0,4},{1,5},{2,6},{3,7},{4,0},{5,1},{6,2},{7,3},{8,12},{9,13},{10,... | collective-permute-start | bytes 786440 | tf_op jit(solution)/shard_map/ppermute | solution.py:90
  13.8 17.2 %collective-permute-start = (bf16[256,1024]{1,0:T(8,128)(2,1)S(1)}, bf16[256,1024]{1,0:T(8,128)(2,1)S(1)}, u32[]{:S(2)}, u32[]{:S(2)}) collective-permute-start(bf16[256,1024]{1,0:T(8,128)(2,1)S(1)} %get-tuple-element.84), channel_id=1, source_target_pairs={{0,0},{1,1},{2,2},{3,3},{4,4},{5,5},{6,6},{7,7},{8,14},{9,15},{10,... | collective-permute-start | bytes 1572872 | tf_op jit(solution)/shard_map/ppermute | solution.py:90
  31.0 12.1 %collective-permute-start.4 = (bf16[2,256,512]{2,1,0:T(8,128)(2,1)S(1)}, bf16[2,256,512]{2,1,0:T(8,128)(2,1)S(1)}, u32[]{:S(2)}, u32[]{:S(2)}) collective-permute-start(bf16[2,256,512]{2,1,0:T(8,128)(2,1)S(1)} %pad_maximum_fusion.11), channel_id=1, source_target_pairs={{0,2},{1,3},{2,0},{3,1},{4,6},{5,7},{6,4},{7,5},{8,10},{9,11},{10,... | collective-permute-start | bytes 1572872 | tf_op jit(solution)/shard_map/ppermute | solution.py:90
  31.1 12.2 %collective-permute-start.2 = (bf16[256,1024]{1,0:T(8,128)(2,1)S(1)}, bf16[256,1024]{1,0:T(8,128)(2,1)S(1)}, u32[]{:S(2)}, u32[]{:S(2)}) collective-permute-start(bf16[256,1024]{1,0:T(8,128)(2,1)S(1)} %collective-permute-done), channel_id=1, source_target_pairs={{0,0},{1,1},{2,10},{3,11},{4,20},{5,21},{6,30},{7,31},{8,24},{9,25... | collective-permute-start | bytes 1572872 | tf_op jit(solution)/shard_map/ppermute | solution.py:90
  31.8 11.5 %collective-permute-start.3 = (bf16[256,1024]{1,0:T(8,128)(2,1)S(1)}, bf16[256,1024]{1,0:T(8,128)(2,1)S(1)}, u32[]{:S(2)}, u32[]{:S(2)}) collective-permute-start(bf16[256,1024]{1,0:T(8,128)(2,1)S(1)} %get-tuple-element.34), channel_id=1, source_target_pairs={{0,0},{1,1},{2,2},{3,3},{4,4},{5,5},{6,6},{7,7},{8,14},{9,15},{10,... | collective-permute-start | bytes 1572872 | tf_op jit(solution)/shard_map/ppermute | solution.py:90
  43.2 0.8 copy-start.9
  44.1 128.0 %all-gather.5.cloned.1.call-start = ((), (), s32[]{:S(2)}) async-start(), calls=%async_computation.2 | async-start | bytes 4718592 | tf_op jit(solution)/shard_map/all_gather | solution.py:158
  44.1 19.3 %collective-permute-start.5 = (bf16[2,2,256,512]{3,2,1,0:T(8,128)(2,1)S(1)}, bf16[2,2,256,512]{3,2,1,0:T(8,128)(2,1)S(1)}, u32[]{:S(2)}, u32[]{:S(2)}) collective-permute-start(bf16[2,2,256,512]{3,2,1,0:T(8,128)(2,1)S(1)} %pad_maximum_fusion.8), channel_id=1, source_target_pairs={{0,1},{1,0},{2,3},{3,2},{4,5},{5,4},{6,7},{7,6},{8,9},{9,8},{10,11... | collective-permute-start | bytes 3145736 | tf_op jit(solution)/shard_map/ppermute | solution.py:90
  46.3 0.7 collective-permute-start.6
  47.1 0.8 copy-start.10
  64.5 290.3 %reduce-scatter.2.cloned.1.call-start = ((), (), s32[]{:S(2)}) async-start(), calls=%async_computation.1 | async-start | bytes 9437184 | tf_op jit(solution)/shard_map/reduce_scatter | solution.py:233
  66.0 77.6 %copy-start.12 = (s32[4]{0:T(128)S(1)}, s32[4]{0:T(128)}, u32[]{:S(2)}) copy-start(s32[4]{0:T(128)} %constant.71.clone) | copy-start | bytes 52
  66.1 73.5 %collective-permute-start.7 = (bf16[2048,512]{1,0:T(8,128)(2,1)S(1)}, bf16[2048,512]{1,0:T(8,128)(2,1)S(1)}, u32[]{:S(2)}, u32[]{:S(2)}) collective-permute-start(bf16[2048,512]{1,0:T(8,128)(2,1)S(1)} %bitcast.77), channel_id=1, source_target_pairs={{0,16},{1,17},{2,18},{3,19},{4,20},{5,21},{6,22},{7,23},{8,24},{9,... | collective-permute-start | bytes 6291464 | tf_op jit(solution)/shard_map/ppermute | solution.py:90
  139.6 1.4 copy-start.2
  143.6 12.5 %collective-permute-start.8 = (bf16[2048,1024]{1,0:T(8,128)(2,1)}, bf16[2048,1024]{1,0:T(8,128)(2,1)}, u32[]{:S(2)}, u32[]{:S(2)}) collective-permute-start(bf16[2048,1024]{1,0:T(8,128)(2,1)} %pad_maximum_fusion.1), channel_id=1, source_target_pairs={{0,8},{1,9},{2,10},{3,11},{4,12},{5,13},{6,14},{7,15},{8,0},{9,1},... | collective-permute-start | bytes 12582920 | tf_op jit(solution)/shard_map/ppermute | solution.py:90
  146.9 9.2 %copy-start.3 = (bf16[2048,512]{1,0:T(8,128)(2,1)S(1)}, bf16[2048,512]{1,0:T(8,128)(2,1)}, u32[]{:S(2)}) copy-start(bf16[2048,512]{1,0:T(8,128)(2,1)} %copy-done.2) | copy-start | bytes 6291460
  172.0 9.5 %copy-start = (bf16[2048,2048]{1,0:T(8,128)(2,1)S(1)}, bf16[2048,2048]{1,0:T(8,128)(2,1)}, u32[]{:S(2)}) copy-start(bf16[2048,2048]{1,0:T(8,128)(2,1)} %pad_maximum_fusion) | copy-start | bytes 25165828
  181.5 3.1 copy-start.7
  184.5 1.6 copy-start.8
  184.5 4.5 %collective-permute-start.9 = (bf16[512,512]{1,0:T(8,128)(2,1)S(1)}, bf16[512,512]{1,0:T(8,128)(2,1)S(1)}, u32[]{:S(2)}, u32[]{:S(2)}) collective-permute-start(bf16[512,512]{1,0:T(8,128)(2,1)S(1)} %fusion.34), channel_id=1, source_target_pairs={{0,8},{1,9},{2,10},{3,11},{4,12},{5,13},{6,14},{7,15},{8,0},{9,1},... | collective-permute-start | bytes 1572872 | tf_op jit(solution)/shard_map/ppermute | solution.py:90
  187.4 9.0 %collective-permute-start.13 = (bf16[512,512]{1,0:T(8,128)(2,1)S(1)}, bf16[512,512]{1,0:T(8,128)(2,1)S(1)}, u32[]{:S(2)}, u32[]{:S(2)}) collective-permute-start(bf16[512,512]{1,0:T(8,128)(2,1)S(1)} %fusion.37), channel_id=1, source_target_pairs={{0,8},{1,9},{2,10},{3,11},{4,12},{5,13},{6,14},{7,15},{8,0},{9,1},... | collective-permute-start | bytes 1572872 | tf_op jit(solution)/shard_map/ppermute | solution.py:90
  189.1 14.1 %collective-permute-start.11 = (bf16[512,512]{1,0:T(8,128)(2,1)S(1)}, bf16[512,512]{1,0:T(8,128)(2,1)S(1)}, u32[]{:S(2)}, u32[]{:S(2)}) collective-permute-start(bf16[512,512]{1,0:T(8,128)(2,1)S(1)} %add_convert_fusion.2), channel_id=1, source_target_pairs={{0,16},{1,17},{2,18},{3,19},{4,20},{5,21},{6,22},{7,23},{8,24},{9,... | collective-permute-start | bytes 1572872 | tf_op jit(solution)/shard_map/ppermute | solution.py:90
  194.5 10.4 %copy-start.5 = (f32[512,1024]{1,0:T(8,128)S(1)}, f32[512,1024]{1,0:T(8,128)}, u32[]{:S(2)}) copy-start(f32[512,1024]{1,0:T(8,128)} %param.10) | copy-start | bytes 6291460
  194.5 10.4 %copy-start.6 = (f32[512,1024]{1,0:T(8,128)S(1)}, f32[512,1024]{1,0:T(8,128)}, u32[]{:S(2)}) copy-start(f32[512,1024]{1,0:T(8,128)} %param.11) | copy-start | bytes 6291460
  194.5 14.0 %collective-permute-start.12 = (bf16[512,512]{1,0:T(8,128)(2,1)S(1)}, bf16[512,512]{1,0:T(8,128)(2,1)S(1)}, u32[]{:S(2)}, u32[]{:S(2)}) collective-permute-start(bf16[512,512]{1,0:T(8,128)(2,1)S(1)} %fusion.25), channel_id=1, source_target_pairs={{0,8},{1,9},{2,10},{3,11},{4,12},{5,13},{6,14},{7,15},{8,0},{9,1},... | collective-permute-start | bytes 1572872 | tf_op jit(solution)/shard_map/ppermute | solution.py:90
  194.6 10.2 %collective-permute-start.10 = (bf16[512,512]{1,0:T(8,128)(2,1)S(1)}, bf16[512,512]{1,0:T(8,128)(2,1)S(1)}, u32[]{:S(2)}, u32[]{:S(2)}) collective-permute-start(bf16[512,512]{1,0:T(8,128)(2,1)S(1)} %fusion.22), channel_id=1, source_target_pairs={{0,8},{1,9},{2,10},{3,11},{4,12},{5,13},{6,14},{7,15},{8,0},{9,1},... | collective-permute-start | bytes 1572872 | tf_op jit(solution)/shard_map/ppermute | solution.py:90
  203.3 14.9 %collective-permute-start.14 = (bf16[512,512]{1,0:T(8,128)(2,1)S(1)}, bf16[512,512]{1,0:T(8,128)(2,1)S(1)}, u32[]{:S(2)}, u32[]{:S(2)}) collective-permute-start(bf16[512,512]{1,0:T(8,128)(2,1)S(1)} %add_convert_fusion), channel_id=1, source_target_pairs={{0,16},{1,17},{2,18},{3,19},{4,20},{5,21},{6,22},{7,23},{8,24},{9,... | collective-permute-start | bytes 1572872 | tf_op jit(solution)/shard_map/ppermute | solution.py:90
  206.7 21.1 %collective-permute-start.15 = (bf16[512,512]{1,0:T(8,128)(2,1)S(1)}, bf16[512,512]{1,0:T(8,128)(2,1)S(1)}, u32[]{:S(2)}, u32[]{:S(2)}) collective-permute-start(bf16[512,512]{1,0:T(8,128)(2,1)S(1)} %get-tuple-element.66), channel_id=1, source_target_pairs={{0,16},{1,17},{2,18},{3,19},{4,20},{5,21},{6,22},{7,23},{8,24},{9,... | collective-permute-start | bytes 1572872 | tf_op jit(solution)/shard_map/ppermute | solution.py:90
  208.4 3.3 copy-start.11
  228.9 3.0 collective-permute-start.16
  228.9 14.3 %collective-permute-start.17 = (bf16[512,512]{1,0:T(8,128)(2,1)S(1)}, bf16[512,512]{1,0:T(8,128)(2,1)S(1)}, u32[]{:S(2)}, u32[]{:S(2)}) collective-permute-start(bf16[512,512]{1,0:T(8,128)(2,1)S(1)} %get-tuple-element.63), channel_id=1, source_target_pairs={{0,16},{1,17},{2,18},{3,19},{4,20},{5,21},{6,22},{7,23},{8,24},{9,... | collective-permute-start | bytes 1572872 | tf_op jit(solution)/shard_map/ppermute | solution.py:90
  243.2 3.4 slice-start
  243.4 2.7 collective-permute-start.18
  246.3 2.2 slice-start.1
  253.3 2.2 copy-start.1
  266.4 1.2 copy-start.4
Sparse Core Ops, SparseCore 0:
  44.2 66.0 all-gather.6
  111.8 60.1 all-gather.4
  266.5 88.1 reduce-scatter.1

commit v7 on v6

--- a/solution.py
+++ b/solution.py
@@ -18,15 +18,13 @@
 
 VMEM_BYTES = 54 * 1024 * 1024
 
+BLOCK = 256
+
 low = jnp.bfloat16
 
 
 def matmul(a, b):
     return lax.dot_general(a, b, (((1,), (0,)), ((), ())), preferred_element_type=jnp.float32)
-
-
-def matmul_nt(a, b):
-    return lax.dot_general(a, b, (((1,), (1,)), ((), ())), preferred_element_type=jnp.float32)
 
 
 def cost(flops, *arrays):
@@ -34,41 +32,85 @@
     return pl.CostEstimate(flops=flops, bytes_accessed=size, transcendentals=0)
 
 
-def half_rotation(gathered, right, places, nz, parts, part, row_parts, held):
+def half_rotation(gathered, right, places, nz, parts, prior):
     count, rows, cols = gathered.shape
     nx = count // nz
     width = right.shape[1] // parts
-
-    def kernel(places_ref, *refs):
-        blocks, right_ref, outs = refs[:nx], refs[nx], refs[-parts:]
+    block = min(BLOCK, width)
+    per = width // block
+    halves = 2 if prior else 1
+
+    def kernel(places_ref, blocks_ref, right_ref, *refs):
+        prior_refs, outs = refs[:-parts], refs[-parts:]
+        step = pl.program_id(0)
+        totals = [
+            matmul(blocks_ref[i * nz : (i + 1) * nz].reshape(nz * rows, cols), right_ref[i * cols : (i + 1) * cols])
+            for i in range(nx)
+        ]
         for j, out in enumerate(outs):
-            total = matmul(blocks[0][...], right_ref[:cols, j * width : (j + 1) * width])
-            for i in range(1, nx):
-                total += matmul(blocks[i][...], right_ref[i * cols : (i + 1) * cols, j * width : (j + 1) * width])
-            out[...] = total.astype(out.dtype)
-
-    def block_of(i):
-        if i % 2 == 0:
-            return pl.BlockSpec((None, rows, cols), lambda k, p: (i * nz + k, 0, 0))
-        return pl.BlockSpec((None, rows, cols), lambda k, p: (i * nz + nz - 1 - k, 0, 0))
-
-    outs = [jax.ShapeDtypeStruct((nz * rows * row_parts, width), low)] * parts
+
+            @pl.when(step // per == j)
+            def _():
+                for k in range(nz):
+                    total = totals[0][k * rows : (k + 1) * rows]
+                    for i in range(1, nx):
+                        at = k if i % 2 == 0 else nz - 1 - k
+                        total = total + totals[i][at * rows : (at + 1) * rows]
+                    total = total.astype(out.dtype)
+                    if prior:
+                        start = pl.multiple_of(places_ref[k] * (2 * rows), 2 * rows)
+                        out[pl.ds(start, rows)] = prior_refs[j][k * rows : (k + 1) * rows]
+                        out[pl.ds(start + rows, rows)] = total
+                    else:
+                        out[k * rows : (k + 1) * rows] = total
+
+    def part_block(j, height):
+        return pl.BlockSpec((height, block), lambda n, p: (0, jnp.clip(n - j * per, 0, per - 1)))
+
+    outs = [jax.ShapeDtypeStruct((nz * rows * halves, width), low)] * parts
     return pl.pallas_call(
         kernel,
         out_shape=outs,
         grid_spec=pltpu.PrefetchScalarGridSpec(
             num_scalar_prefetch=1,
-            grid=(nz,),
-            in_specs=[block_of(i) for i in range(nx)]
-            + [pl.BlockSpec(right.shape, lambda k, p: (0, 0), pipeline_mode=pl.Buffered(1))]
-            + [pl.BlockSpec(memory_space=pl.ANY)] * len(held),
-            out_specs=[pl.BlockSpec((rows, width), lambda k, p: (p[k] * row_parts + part, 0))] * parts,
+            grid=(parts * per,),
+            in_specs=[
+                pl.BlockSpec(gathered.shape, lambda n, p: (0, 0, 0), pipeline_mode=pl.Buffered(1)),
+                pl.BlockSpec((nx * cols, block), lambda n, p: (0, n)),
+            ]
+            + [part_block(j, nz * rows) for j in range(len(prior))],
+            out_specs=[part_block(j, nz * rows * halves) for j in range(parts)],
         ),
-        input_output_aliases={nx + 2 + j: j for j in range(len(held))},
         compiler_params=pltpu.CompilerParams(vmem_limit_bytes=VMEM_BYTES),
         cost_estimate=cost(2 * gathered.size * right.shape[1], gathered, right, *outs),
         name="half_rotation",
-    )(places, *([gathered] * nx), right, *held)
+    )(places, gathered, right, *prior)
+
+
+def back_rotation(columns, right_t):
+    parts = len(columns)
+    rows, width = columns[0].shape
+    block = min(BLOCK, right_t.shape[1])
+
+    def kernel(*refs):
+        rows_of, right_ref, out = refs[:parts], refs[parts], refs[parts + 1]
+        total = matmul(rows_of[0][...], right_ref[:width])
+        for j in range(1, parts):
+            total += matmul(rows_of[j][...], right_ref[j * width : (j + 1) * width])
+        out[...] = total.astype(out.dtype)
+
+    out = jax.ShapeDtypeStruct((rows, right_t.shape[1]), low)
+    return pl.pallas_call(
+        kernel,
+        out_shape=out,
+        grid=(right_t.shape[1] // block,),
+        in_specs=[pl.BlockSpec((rows, width), lambda n: (0, 0), pipeline_mode=pl.Buffered(1))] * parts
+        + [pl.BlockSpec((right_t.shape[0], block), lambda n: (0, n))],
+        out_specs=pl.BlockSpec((rows, block), lambda n: (0, n)),
+        compiler_params=pltpu.CompilerParams(vmem_limit_bytes=VMEM_BYTES),
+        cost_estimate=cost(2 * rows * right_t.size, right_t, out, *columns),
+        name="back_rotation",
+    )(*columns, right_t)
 
 
 def per_device(gradient, left_basis, right_basis, first_moment, second_moment, *, nb, nd):
@@ -127,14 +169,25 @@
         order = order + [s | t for s in order]
     half_places = [[order.index(unspread[bb ^ zz] ^ bb) for zz in range(nz)] for bb in range(nb)]
     half_places = jnp.array(half_places, jnp.int32)[b]
-    order_of = jnp.array([order.index(t) for t in range(nb)], jnp.int32)
-    path_places = [order_of[b ^ (dd // nx)] * rows + dd % nx * out_rows for dd in path]
+    paths = [path if bb % 2 == 0 else path[::-1] for bb in range(nb)]
+    groups = [[bb * nd + dd for dd in paths[bb]] for bb in range(nb)]
+    path_places = [[order.index(bb ^ (dd // nx)) * rows + dd % nx * out_rows for dd in paths[bb]] for bb in range(nb)]
+    path_places = jnp.array(path_places, jnp.int32)[b]
 
     def together(*values):
         return lax.optimization_barrier(values)
 
     left_t = left_basis.astype(low).T
-    right = right_basis.astype(low)
+    ff_rows = right_basis.shape[0] // nx
+    first_x = (b & 1) * (nx - 1)
+    right = jnp.concatenate(
+        [
+            lax.dynamic_slice_in_dim(right_basis, (first_x + (1 - 2 * (b & 1)) * i) * ff_rows, ff_rows, 0).astype(low)
+            for i in range(nx)
+        ],
+        axis=0,
+    )
+    right_t = right_basis.astype(low).T
 
     def across(piece):
         return permute(piece, lambda bb, zz, xx: (bb, zz ^ spread(bb), xx))
@@ -147,22 +200,22 @@
     first = across(first)
     for i, t in enumerate(reversed(bits[1:])):
         left_t = joined(left_t, move_z(left_t, t), (z & t) != 0, i)
-    first, left_t, right, half_places = together(first, left_t, right, half_places)
+    first, left_t, right, half_places, path_places = together(first, left_t, right, half_places, path_places)
     left_t = joined(left_t, move_z(left_t, bits[0]), (z & bits[0]) != 0, len(bits) - 1)
     first, second, left_t = together(along(first), across(after(second, first)), left_t)
-    gathered = [lax.all_gather(first, "dp", axis_index_groups=[path])]
+    gathered = [lax.all_gather(first, ("basis", "dp"), axis_index_groups=groups)]
     second = along(second)
     for i, u in enumerate(reversed(x_bits)):
         other, second = together(move_x(left_t, u), second)
         left_t = joined(left_t, other, (x & u) != 0, len(bits) + i)
-    gathered.append(lax.all_gather(second, "dp", axis_index_groups=[path]))
+    gathered.append(lax.all_gather(second, ("basis", "dp"), axis_index_groups=groups))
     left_t = left_t.reshape(whole, rows)
     for t in reversed(bits):
         left_t = jnp.concatenate([left_t, move_b(left_t, t)], axis=1)
-    left_t, gathered[1] = together(left_t, gathered[1])
+    left_t, right_t, gathered[1] = together(left_t, right_t, gathered[1])
     half = []
     for h in range(2):
-        half = list(half_rotation(gathered[h], right, half_places, nz, COL_PARTS, h, 2, half))
+        half = half_rotation(gathered[h], right, half_places, nz, COL_PARTS, half)
 
     products = {}
     last = None
@@ -194,7 +247,7 @@
 
     source = after(left_t, arrived[0])
     left = jnp.concatenate(
-        [lax.dynamic_slice_in_dim(source, start, out_rows, 1).T for start in path_places], axis=0
+        [lax.dynamic_slice_in_dim(source, path_places[i], out_rows, 1).T for i in range(nd)], axis=0
     )
     left = lax.optimization_barrier(left)
 
@@ -228,9 +281,8 @@
         column = lax.optimization_barrier(column.reshape(whole, width))
         back.append(lax.optimization_barrier(matmul(left, column).astype(low)))
 
-    back = lax.optimization_barrier(jnp.concatenate(back, axis=1))
-    total = matmul_nt(back, right).astype(low)
-    update = lax.psum_scatter(total, "dp", scatter_dimension=0, axis_index_groups=[path], tiled=True)
+    total = back_rotation(back, right_t)
+    update = lax.psum_scatter(total, ("basis", "dp"), scatter_dimension=0, axis_index_groups=groups, tiled=True)
     return (
         jnp.concatenate(first_out, axis=1),
         jnp.concatenate(second_out, axis=1),

time: 362 us -> 381 us (1.052)
  Pallas kernels: 18.7 us -> 35.4 us
  between operations: 16.9 us -> 29.3 us
  local copies, waits for them, and re-layouts: 16.8 us -> 27.6 us
  waiting for transfers between devices: 191 us -> 181 us
  matrix products: 36.2 us -> 26.9 us
  other arithmetic: 30.2 us -> 26.1 us
    pallas_call x0 -> x1, Pallas kernels: none -> 14.2 us  [back_rotation(): pl.pallas_call(kernel, out_shape=out, grid=(right_t.shape[1] // block,),...]
    dot_general x1 -> x0, matrix products: 10.9 us -> none  [matmul_nt(): lax.dot_general(a, b, (((1,), (1,)), ((), ())), preferred_element_type=jn...]
    all_gather x2, waiting for transfers between devices: 9.57 us -> 0.02 us  [the longest x1 0.02 us: per_device(): lax.all_gather(first, ('basis', 'dp'), axis_index_groups=groups)]
    convert_element_type x1 -> x0, other arithmetic: 6.12 us -> none  [per_device(): right = right_basis.astype(low)]
    unnamed x38 -> x37, local copies, waits for them, and re-layouts: 13.2 us -> 18.7 us
    convert_element_type x0 -> x1, local copies, waits for them, and re-layouts: none -> 4.13 us  [per_device(): lax.dynamic_slice_in_dim(right_basis, (first_x + (1 - 2 * (b & 1)) * i) *...]
  transfers between devices with their start and end apart: 22 -> 22, of which waited for: 12 -> 11; matrix products, arithmetic and copies ran while one was open for 14% -> 16% of each run, Pallas kernels for 3% -> 3%
where the time goes in v7:
time: 381 us; the launch traced here: 380 us
  waiting for transfers between devices  181 us (48%)
  starting transfers between devices  53.7 us (14%)
  Pallas kernels  35.4 us (9%)
  between operations  29.3 us (8%)
  local copies, waits for them, and re-layouts  27.6 us (7%)
  matrix products  26.9 us (7%)
  other arithmetic  26.1 us (7%)
    ppermute x19, waiting for transfers between devices, permute(): return lax.ppermute(value, ('basis', 'dp'), pairs)  95.4 us
    reduce_scatter x1, waiting for transfers between devices, per_device(): lax.psum_scatter(total, ('basis', 'dp'), scatter_dimension=0, axis_index_...  85.8 us
    ppermute x19, starting transfers between devices, permute(): return lax.ppermute(value, ('basis', 'dp'), pairs)  53.6 us
    dot_general x10, matrix products, matmul(): lax.dot_general(a, b, (((1,), (0,)), ((), ())), preferred_element_type=jn...  26.9 us
    pallas_call x2, Pallas kernels, half_rotation(): pl.pallas_call(kernel, out_shape=outs, grid_spec=pltpu.PrefetchScalarGrid...  21.2 us
    unnamed x37, local copies, waits for them, and re-layouts  18.7 us
    pallas_call x1, Pallas kernels, back_rotation(): pl.pallas_call(kernel, out_shape=out, grid=(right_t.shape[1] // block,),...  14.2 us
    concatenate x2, other arithmetic, per_device(): left_t = jnp.concatenate([left_t, move_b(left_t, t)], axis=1)  8.97 us
  transfers between devices with their start and end apart: 22, of which 11 were waited for; matrix products, arithmetic and copies ran while one was open for 16% of the time, Pallas kernels for 3%

profile of v7, /device:TPU:0, one launch (start us, length us, event | category | flops | bytes accessed | tf_op | source)
XLA Modules:
  0.0 380.2 jit_solution(9453447435161474764)
XLA Ops:
  7.2 1.3 fusion.54
  9.4 4.1 %collective-permute-start.1 = (bf16[256,512]{1,0:T(8,128)(2,1)S(1)}, bf16[256,512]{1,0:T(8,128)(2,1)S(1)}, u32[]{:S(2)}, u32[]{:S(2)}) collective-permute-start(bf16[256,512]{1,0:T(8,128)(2,1)S(1)} %bitcast.90), channel_id=1, source_target_pairs={{0,4},{1,5},{2,6},{3,7},{4,0},{5,1},{6,2},{7,3},{8,12},{9,13},{10,... | collective-permute-start | bytes 786440 | tf_op jit(solution)/shard_map/ppermute | solution.py:132
  13.5 4.1 %dynamic-slice_convert_fusion.1 = (bf16[1024,1024]{1,0:T(8,128)(2,1)S(1)}, bf16[1024,1024]{1,0:T(8,128)(2,1)S(1)}) fusion(f32[2048,1024]{1,0:T(8,128)} %param.9, s32[]{:T(128)S(6)} %select_n.143, s32[]{:T(128)S(6)} %select_n.144), kind=kLoop, calls=%fused_computation.5 | loop fusion | bytes 8388616 | tf_op jit(solution)/shard_map/convert_element_type | solution.py:185
  17.6 2.4 pad_maximum_fusion.1.right_ref
  20.0 1.3 fusion.50.places_ref
  22.0 9.6 %collective-permute-done.1 = bf16[256,512]{1,0:T(8,128)(2,1)S(1)} collective-permute-done((bf16[256,512]{1,0:T(8,128)(2,1)S(1)}, bf16[256,512]{1,0:T(8,128)(2,1)S(1)}, u32[]{:S(2)}, u32[]{:S(2)}) %collective-permute-start.1) | collective-permute-done | bytes 262176 | tf_op jit(solution)/shard_map/ppermute | solution.py:132
  31.7 1.5 collective-permute-start.4
  34.6 11.4 %collective-permute-done.4 = bf16[2,256,512]{2,1,0:T(8,128)(2,1)S(1)} collective-permute-done((bf16[2,256,512]{2,1,0:T(8,128)(2,1)S(1)}, bf16[2,256,512]{2,1,0:T(8,128)(2,1)S(1)}, u32[]{:S(2)}, u32[]{:S(2)}) %collective-permute-start.4) | collective-permute-done | bytes 524320 | tf_op jit(solution)/shard_map/ppermute | solution.py:132
  47.0 1.8 collective-permute-start.5
  49.6 0.8 copy-done.8
  50.4 15.1 %collective-permute-done.5 = bf16[2,2,256,512]{3,2,1,0:T(8,128)(2,1)S(1)} collective-permute-done((bf16[2,2,256,512]{3,2,1,0:T(8,128)(2,1)S(1)}, bf16[2,2,256,512]{3,2,1,0:T(8,128)(2,1)S(1)}, u32[]{:S(2)}, u32[]{:S(2)}) %collective-permute-start.5) | collective-permute-done | bytes 1048608 | tf_op jit(solution)/shard_map/ppermute | solution.py:132
  65.5 1.1 select_bitcast_fusion.5
  66.7 1.5 pad_maximum_fusion.3
  68.2 36.4 %collective-permute-start.7 = (bf16[2048,512]{1,0:T(8,128)(2,1)S(1)}, bf16[2048,512]{1,0:T(8,128)(2,1)S(1)}, u32[]{:S(2)}, u32[]{:S(2)}) collective-permute-start(bf16[2048,512]{1,0:T(8,128)(2,1)S(1)} %bitcast.84), channel_id=1, source_target_pairs={{0,16},{1,17},{2,18},{3,19},{4,20},{5,21},{6,22},{7,23},{8,24},{9,... | collective-permute-start | bytes 6291464 | tf_op jit(solution)/shard_map/ppermute | solution.py:132
  104.6 37.5 %collective-permute-done.7 = bf16[2048,512]{1,0:T(8,128)(2,1)S(1)} collective-permute-done((bf16[2048,512]{1,0:T(8,128)(2,1)S(1)}, bf16[2048,512]{1,0:T(8,128)(2,1)S(1)}, u32[]{:S(2)}, u32[]{:S(2)}) %collective-permute-start.7) | collective-permute-done | bytes 2097184 | tf_op jit(solution)/shard_map/ppermute | solution.py:132
  142.1 2.7 pad_maximum_fusion.2
  144.8 7.4 %copy.14 = bf16[2048,1024]{0,1:T(8,128)(2,1)} copy(f32[2048,1024]{1,0:T(8,128)} %param.9) | data formatting | bytes 12582912 | tf_op args[2]
  167.9 9.9 %half_rotation.2 = (bf16[1024,512]{1,0:T(8,128)(2,1)}, bf16[1024,512]{1,0:T(8,128)(2,1)}) custom-call(s32[4]{0:T(128)} %fusion.50.places_ref, bf16[8,256,1024]{2,1,0:T(8,128)(2,1)} %bitcast.93, bf16[2048,1024]{1,0:T(8,128)(2,1)} %pad_maximum_fusion.1.right_ref), custom_call_target="tpu_custom_call" | custom-call | flops 4294967296 | bytes 10485760 | tf_op jit(solution)/shard_map/half_rotation/pallas_call | solution.py:71
  177.9 6.3 %pad_maximum_fusion = bf16[2048,2048]{1,0:T(8,128)(2,1)} fusion(bf16[2048,1024]{1,0:T(8,128)(2,1)} %collective-permute-done.8, bf16[2048,512]{1,0:T(8,128)(2,1)S(1)} %copy-done.2, bf16[2048,512]{1,0:T(8,128)(2,1)S(1)} %bitcast.86), kind=kLoop, calls=%fused_computation | loop fusion | flops 25165824 | bytes 16777216 | tf_op jit(solution)/shard_map/concatenate | solution.py:214
  184.1 11.3 %half_rotation.3 = (bf16[2048,512]{1,0:T(8,128)(2,1)}, bf16[2048,512]{1,0:T(8,128)(2,1)}) custom-call(s32[4]{0:T(128)} %fusion.50.places_ref, bf16[8,256,1024]{2,1,0:T(8,128)(2,1)} %bitcast.94, bf16[2048,1024]{1,0:T(8,128)(2,1)} %pad_maximum_fusion.1.right_ref, bf16[1024,512]{1,0:T(8,128)(2,1)} %get-tuple-element.47.refs_0_, ...), custom_call_target="tpu_custom_call" | custom-call | flops 4294967296 | bytes 12582912 | tf_op jit(solution)/shard_map/half_rotation/pallas_call | solution.py:71
  195.4 3.0 fusion.34
  199.0 1.3 fusion.28
  200.2 1.3 fusion.37
  201.8 1.3 fusion.31
  203.2 1.8 collective-permute-start.11
  205.0 1.3 fusion.22
  206.3 1.3 fusion.16
  207.6 1.3 fusion.25
  209.4 1.3 fusion.19
  210.8 6.5 %collective-permute-done.11 = bf16[512,512]{1,0:T(8,128)(2,1)S(1)} collective-permute-done((bf16[512,512]{1,0:T(8,128)(2,1)S(1)}, bf16[512,512]{1,0:T(8,128)(2,1)S(1)}, u32[]{:S(2)}, u32[]{:S(2)}) %collective-permute-start.11) | collective-permute-done | bytes 524320 | tf_op jit(solution)/shard_map/ppermute | solution.py:132
  217.4 1.7 collective-permute-start.14
  219.3 1.8 divide_convert_fusion.1
  225.2 3.3 copy-done.9
  228.5 3.8 collective-permute-done.14
  232.3 2.3 divide_convert_fusion
  234.6 7.3 %collective-permute-done.15 = bf16[512,512]{1,0:T(8,128)(2,1)S(1)} collective-permute-done((bf16[512,512]{1,0:T(8,128)(2,1)S(1)}, bf16[512,512]{1,0:T(8,128)(2,1)S(1)}, u32[]{:S(2)}, u32[]{:S(2)}) %collective-permute-start.15) | collective-permute-done | bytes 524320 | tf_op jit(solution)/shard_map/ppermute | solution.py:132
  242.0 1.1 pad_maximum_fusion.9
  243.1 1.7 collective-permute-start.17
  244.8 1.3 collective-permute-done.16
  246.1 1.4 select_bitcast_fusion.3
  247.8 9.4 %convolution_convert_fusion.1.refs_0_ = bf16[2048,512]{1,0:T(8,128)(2,1)} fusion(bf16[2048,2048]{0,1:T(8,128)(2,1)} %copy-done.9, bf16[2048,512]{1,0:T(8,128)(2,1)S(1)} %bitcast.89), kind=kOutput, calls=%fused_computation.7 | convolution fusion | flops 4296015872 | bytes 12582912 | tf_op jit(solution)/shard_map/dot_general | solution.py:27
  257.7 2.6 collective-permute-done.18
  260.9 1.8 slice-done.1
  262.7 5.7 %convolution_convert_fusion.refs_1_ = bf16[2048,512]{1,0:T(8,128)(2,1)} fusion(bf16[2048,2048]{0,1:T(8,128)(2,1)S(1)} %bitcast.92, bf16[2048,512]{1,0:T(8,128)(2,1)S(1)} %bitcast.88), kind=kOutput, calls=%fused_computation.6 | convolution fusion | flops 4296015872 | bytes 12582912 | tf_op jit(solution)/shard_map/dot_general | solution.py:27
  268.4 14.2 %back_rotation.1 = bf16[2048,2048]{1,0:T(8,128)(2,1)} custom-call(bf16[2048,512]{1,0:T(8,128)(2,1)} %convolution_convert_fusion.1.refs_0_, bf16[2048,512]{1,0:T(8,128)(2,1)} %convolution_convert_fusion.refs_1_, bf16[1024,2048]{1,0:T(8,128)(2,1)} %bitcast.87), custom_call_target="tpu_custom_call" | custom-call | flops 8589934592 | bytes 16777216 | tf_op jit(solution)/shard_map/back_rotation/pallas_call | solution.py:103
  282.6 1.2 copy-done.3
  283.8 4.1 %pad_maximum_fusion.4 = (f32[512,1024]{1,0:T(8,128)}, f32[512,1024]{1,0:T(8,128)}) fusion(f32[512,512]{1,0:T(8,128)} %get-tuple-element.69, f32[512,512]{1,0:T(8,128)S(1)} %get-tuple-element.71, f32[512,512]{1,0:T(8,128)} %get-tuple-element.68, f32[512,512]{1,0:T(8,128)S(1)} %copy-done.3), kind=kLoop, calls=%fused_computation.9 | loop fusion | flops 1048576 | bytes 8388608 | tf_op jit(solution)/shard_map/concatenate | solution.py:287
  287.9 85.8 %reduce-scatter.2.cloned.1.call-done = bf16[256,2048]{1,0:T(8,128)(2,1)} async-done(((bf16[2048,2048]{1,0:T(8,128)(2,1)}), bf16[256,2048]{1,0:T(8,128)(2,1)}) %reduce-scatter.2.cloned.1.call-update) | async-done | bytes 1048592 | tf_op jit(solution)/shard_map/reduce_scatter | solution.py:285
  (81 shorter events, 12.8 us)
Async XLA Ops:
  7.2 2.1 copy-start.6
  7.2 160.8 %all-gather.7.cloned.1.call-start = ((), (), s32[]{:S(2)}) async-start(), calls=%async_computation.3 | async-start | bytes 4718592 | tf_op jit(solution)/shard_map/all_gather | solution.py:206
  8.5 23.2 %collective-permute-start = (bf16[256,1024]{1,0:T(8,128)(2,1)S(1)}, bf16[256,1024]{1,0:T(8,128)(2,1)S(1)}, u32[]{:S(2)}, u32[]{:S(2)}) collective-permute-start(bf16[256,1024]{1,0:T(8,128)(2,1)S(1)} %get-tuple-element.90), channel_id=1, source_target_pairs={{0,0},{1,1},{2,2},{3,3},{4,4},{5,5},{6,6},{7,7},{8,14},{9,15},{10,... | collective-permute-start | bytes 1572872 | tf_op jit(solution)/shard_map/ppermute | solution.py:132
  9.4 22.2 %collective-permute-start.1 = (bf16[256,512]{1,0:T(8,128)(2,1)S(1)}, bf16[256,512]{1,0:T(8,128)(2,1)S(1)}, u32[]{:S(2)}, u32[]{:S(2)}) collective-permute-start(bf16[256,512]{1,0:T(8,128)(2,1)S(1)} %bitcast.90), channel_id=1, source_target_pairs={{0,4},{1,5},{2,6},{3,7},{4,0},{5,1},{6,2},{7,3},{8,12},{9,13},{10,... | collective-permute-start | bytes 786440 | tf_op jit(solution)/shard_map/ppermute | solution.py:132
  31.7 14.3 %collective-permute-start.4 = (bf16[2,256,512]{2,1,0:T(8,128)(2,1)S(1)}, bf16[2,256,512]{2,1,0:T(8,128)(2,1)S(1)}, u32[]{:S(2)}, u32[]{:S(2)}) collective-permute-start(bf16[2,256,512]{2,1,0:T(8,128)(2,1)S(1)} %pad_maximum_fusion.11), channel_id=1, source_target_pairs={{0,2},{1,3},{2,0},{3,1},{4,6},{5,7},{6,4},{7,5},{8,10},{9,11},{10,... | collective-permute-start | bytes 1572872 | tf_op jit(solution)/shard_map/ppermute | solution.py:132
  33.2 13.0 %collective-permute-start.2 = (bf16[256,1024]{1,0:T(8,128)(2,1)S(1)}, bf16[256,1024]{1,0:T(8,128)(2,1)S(1)}, u32[]{:S(2)}, u32[]{:S(2)}) collective-permute-start(bf16[256,1024]{1,0:T(8,128)(2,1)S(1)} %collective-permute-done), channel_id=1, source_target_pairs={{0,0},{1,1},{2,10},{3,11},{4,20},{5,21},{6,30},{7,31},{8,24},{9,25... | collective-permute-start | bytes 1572872 | tf_op jit(solution)/shard_map/ppermute | solution.py:132
  33.9 12.3 %collective-permute-start.3 = (bf16[256,1024]{1,0:T(8,128)(2,1)S(1)}, bf16[256,1024]{1,0:T(8,128)(2,1)S(1)}, u32[]{:S(2)}, u32[]{:S(2)}) collective-permute-start(bf16[256,1024]{1,0:T(8,128)(2,1)S(1)} %get-tuple-element.36), channel_id=1, source_target_pairs={{0,0},{1,1},{2,2},{3,3},{4,4},{5,5},{6,6},{7,7},{8,14},{9,15},{10,... | collective-permute-start | bytes 1572872 | tf_op jit(solution)/shard_map/ppermute | solution.py:132
  46.2 0.8 copy-start.7
  47.0 137.1 %all-gather.5.cloned.1.call-start = ((), (), s32[]{:S(2)}) async-start(), calls=%async_computation.2 | async-start | bytes 4718592 | tf_op jit(solution)/shard_map/all_gather | solution.py:211
  47.0 18.5 %collective-permute-start.5 = (bf16[2,2,256,512]{3,2,1,0:T(8,128)(2,1)S(1)}, bf16[2,2,256,512]{3,2,1,0:T(8,128)(2,1)S(1)}, u32[]{:S(2)}, u32[]{:S(2)}) collective-permute-start(bf16[2,2,256,512]{3,2,1,0:T(8,128)(2,1)S(1)} %pad_maximum_fusion.8), channel_id=1, source_target_pairs={{0,1},{1,0},{2,3},{3,2},{4,5},{5,4},{6,7},{7,6},{8,9},{9,8},{10,11... | collective-permute-start | bytes 3145736 | tf_op jit(solution)/shard_map/ppermute | solution.py:132
  48.9 0.7 collective-permute-start.6
  49.6 0.8 copy-start.8
  66.6 307.0 %reduce-scatter.2.cloned.1.call-start = ((), (), s32[]{:S(2)}) async-start(), calls=%async_computation.1 | async-start | bytes 9437184 | tf_op jit(solution)/shard_map/reduce_scatter | solution.py:285
  68.2 73.9 %collective-permute-start.7 = (bf16[2048,512]{1,0:T(8,128)(2,1)S(1)}, bf16[2048,512]{1,0:T(8,128)(2,1)S(1)}, u32[]{:S(2)}, u32[]{:S(2)}) collective-permute-start(bf16[2048,512]{1,0:T(8,128)(2,1)S(1)} %bitcast.84), channel_id=1, source_target_pairs={{0,16},{1,17},{2,18},{3,19},{4,20},{5,21},{6,22},{7,23},{8,24},{9,... | collective-permute-start | bytes 6291464 | tf_op jit(solution)/shard_map/ppermute | solution.py:132
  142.1 2.7 copy-start.1
  144.8 33.1 %collective-permute-start.8 = (bf16[2048,1024]{1,0:T(8,128)(2,1)}, bf16[2048,1024]{1,0:T(8,128)(2,1)}, u32[]{:S(2)}, u32[]{:S(2)}) collective-permute-start(bf16[2048,1024]{1,0:T(8,128)(2,1)} %pad_maximum_fusion.2), channel_id=1, source_target_pairs={{0,8},{1,9},{2,10},{3,11},{4,12},{5,13},{6,14},{7,15},{8,0},{9,1},... | collective-permute-start | bytes 12582920 | tf_op jit(solution)/shard_map/ppermute | solution.py:132
  167.9 9.9 %copy-start.2 = (bf16[2048,512]{1,0:T(8,128)(2,1)S(1)}, bf16[2048,512]{1,0:T(8,128)(2,1)}, u32[]{:S(2)}) copy-start(bf16[2048,512]{1,0:T(8,128)(2,1)} %copy-done.1) | copy-start | bytes 6291460
  184.1 11.3 %copy-start = (bf16[2048,2048]{1,0:T(8,128)(2,1)S(1)}, bf16[2048,2048]{1,0:T(8,128)(2,1)}, u32[]{:S(2)}) copy-start(bf16[2048,2048]{1,0:T(8,128)(2,1)} %pad_maximum_fusion) | copy-start | bytes 25165828
  195.4 3.5 copy-start.11
  198.4 1.8 copy-start.10
  198.4 4.6 %collective-permute-start.9 = (bf16[512,512]{1,0:T(8,128)(2,1)S(1)}, bf16[512,512]{1,0:T(8,128)(2,1)S(1)}, u32[]{:S(2)}, u32[]{:S(2)}) collective-permute-start(bf16[512,512]{1,0:T(8,128)(2,1)S(1)} %fusion.34), channel_id=1, source_target_pairs={{0,8},{1,9},{2,10},{3,11},{4,12},{5,13},{6,14},{7,15},{8,0},{9,1},... | collective-permute-start | bytes 1572872 | tf_op jit(solution)/shard_map/ppermute | solution.py:132
  201.5 9.2 %collective-permute-start.13 = (bf16[512,512]{1,0:T(8,128)(2,1)S(1)}, bf16[512,512]{1,0:T(8,128)(2,1)S(1)}, u32[]{:S(2)}, u32[]{:S(2)}) collective-permute-start(bf16[512,512]{1,0:T(8,128)(2,1)S(1)} %fusion.37), channel_id=1, source_target_pairs={{0,8},{1,9},{2,10},{3,11},{4,12},{5,13},{6,14},{7,15},{8,0},{9,1},... | collective-permute-start | bytes 1572872 | tf_op jit(solution)/shard_map/ppermute | solution.py:132
  203.2 14.2 %collective-permute-start.11 = (bf16[512,512]{1,0:T(8,128)(2,1)S(1)}, bf16[512,512]{1,0:T(8,128)(2,1)S(1)}, u32[]{:S(2)}, u32[]{:S(2)}) collective-permute-start(bf16[512,512]{1,0:T(8,128)(2,1)S(1)} %add_convert_fusion.2), channel_id=1, source_target_pairs={{0,16},{1,17},{2,18},{3,19},{4,20},{5,21},{6,22},{7,23},{8,24},{9,... | collective-permute-start | bytes 1572872 | tf_op jit(solution)/shard_map/ppermute | solution.py:132
  208.8 16.4 %collective-permute-start.12 = (bf16[512,512]{1,0:T(8,128)(2,1)S(1)}, bf16[512,512]{1,0:T(8,128)(2,1)S(1)}, u32[]{:S(2)}, u32[]{:S(2)}) collective-permute-start(bf16[512,512]{1,0:T(8,128)(2,1)S(1)} %fusion.25), channel_id=1, source_target_pairs={{0,8},{1,9},{2,10},{3,11},{4,12},{5,13},{6,14},{7,15},{8,0},{9,1},... | collective-permute-start | bytes 1572872 | tf_op jit(solution)/shard_map/ppermute | solution.py:132
  208.9 10.2 %collective-permute-start.10 = (bf16[512,512]{1,0:T(8,128)(2,1)S(1)}, bf16[512,512]{1,0:T(8,128)(2,1)S(1)}, u32[]{:S(2)}, u32[]{:S(2)}) collective-permute-start(bf16[512,512]{1,0:T(8,128)(2,1)S(1)} %fusion.22), channel_id=1, source_target_pairs={{0,8},{1,9},{2,10},{3,11},{4,12},{5,13},{6,14},{7,15},{8,0},{9,1},... | collective-permute-start | bytes 1572872 | tf_op jit(solution)/shard_map/ppermute | solution.py:132
  209.4 9.9 %copy-start.5 = (f32[512,1024]{1,0:T(8,128)S(1)}, f32[512,1024]{1,0:T(8,128)}, u32[]{:S(2)}) copy-start(f32[512,1024]{1,0:T(8,128)} %param.11) | copy-start | bytes 6291460
  210.7 8.6 %copy-start.4 = (f32[512,1024]{1,0:T(8,128)S(1)}, f32[512,1024]{1,0:T(8,128)}, u32[]{:S(2)}) copy-start(f32[512,1024]{1,0:T(8,128)} %param.10) | copy-start | bytes 6291460
  217.4 14.9 %collective-permute-start.14 = (bf16[512,512]{1,0:T(8,128)(2,1)S(1)}, bf16[512,512]{1,0:T(8,128)(2,1)S(1)}, u32[]{:S(2)}, u32[]{:S(2)}) collective-permute-start(bf16[512,512]{1,0:T(8,128)(2,1)S(1)} %add_convert_fusion), channel_id=1, source_target_pairs={{0,16},{1,17},{2,18},{3,19},{4,20},{5,21},{6,22},{7,23},{8,24},{9,... | collective-permute-start | bytes 1572872 | tf_op jit(solution)/shard_map/ppermute | solution.py:132
  221.1 20.8 %collective-permute-start.15 = (bf16[512,512]{1,0:T(8,128)(2,1)S(1)}, bf16[512,512]{1,0:T(8,128)(2,1)S(1)}, u32[]{:S(2)}, u32[]{:S(2)}) collective-permute-start(bf16[512,512]{1,0:T(8,128)(2,1)S(1)} %get-tuple-element.70), channel_id=1, source_target_pairs={{0,16},{1,17},{2,18},{3,19},{4,20},{5,21},{6,22},{7,23},{8,24},{9,... | collective-permute-start | bytes 1572872 | tf_op jit(solution)/shard_map/ppermute | solution.py:132
  225.2 3.3 copy-start.9
  243.1 3.0 collective-permute-start.16
  243.1 14.3 %collective-permute-start.17 = (bf16[512,512]{1,0:T(8,128)(2,1)S(1)}, bf16[512,512]{1,0:T(8,128)(2,1)S(1)}, u32[]{:S(2)}, u32[]{:S(2)}) collective-permute-start(bf16[512,512]{1,0:T(8,128)(2,1)S(1)} %get-tuple-element.67), channel_id=1, source_target_pairs={{0,16},{1,17},{2,18},{3,19},{4,20},{5,21},{6,22},{7,23},{8,24},{9,... | collective-permute-start | bytes 1572872 | tf_op jit(solution)/shard_map/ppermute | solution.py:132
  257.4 3.5 slice-start
  257.6 2.7 collective-permute-start.18
  260.5 2.2 slice-start.1
  282.6 1.2 copy-start.3
Sparse Core Ops, SparseCore 0:
  47.1 65.9 all-gather.6
  115.2 59.4 all-gather.4
  282.7 90.8 reduce-scatter.1

commit v8 on v6

v8 whole, which is shorter than its diff:
```python
import functools

import jax
import jax.numpy as jnp
from jax import lax
from jax.sharding import PartitionSpec as P

STEP = 4


beta_first = 0.95
beta_second = 0.95
epsilon = 1e-08

COL_PARTS = 2

low = jnp.bfloat16


def matmul(a, b):
    return lax.dot_general(a, b, (((1,), (0,)), ((), ())), preferred_element_type=jnp.float32)


def matmul_nt(a, b):
    return lax.dot_general(a, b, (((1,), (1,)), ((), ())), preferred_element_type=jnp.float32)


def per_device(gradient, left_basis, right_basis, first_moment, second_moment, *, nb, nd):
    nz = nb
    nx = nd // nz
    b = lax.axis_index("basis")
    bits = [1 << k for k in range(nb.bit_length() - 1)]

    def permute(value, target):
        pairs = []
        for bb in range(nb):
            for zz in range(nz):
                for xx in range(nx):
                    tb, tz, tx = target(bb, zz, xx)
                    pairs.append((bb * nd + zz * nx + xx, tb * nd + tz * nx + tx))
        return lax.ppermute(value, ("basis", "dp"), pairs)

    def move_b(value, t):
        return permute(value, lambda bb, zz, xx: (bb ^ t, zz, xx))

    def spread(beta):
        return (beta >> 1) ^ ((beta & 1) * (nz - 1))

    unspread = [0] * nz
    for beta in range(nb):
        unspread[spread(beta)] = beta

    def joined(mine, other, bit_set, axis):
        first = jnp.where(bit_set, other, mine)
        second = jnp.where(bit_set, mine, other)
        return jnp.stack([first, second], axis=axis)

    def after(value, *others):
        return lax.optimization_barrier((value,) + others)[0]

    ff_block = right_basis.shape[1]
    rows = first_moment.shape[0]
    out_rows = left_basis.shape[1]
    whole = rows * nb

    path = []
    for xx in range(nx):
        path += [zz * nx + xx for zz in (range(nz) if xx % 2 == 0 else reversed(range(nz)))]

    order = [0]
    for t in reversed(bits):
        order = order + [s | t for s in order]
    half_places = [[order.index(unspread[bb ^ zz] ^ bb) * rows for zz in range(nz)] for bb in range(nb)]
    path_places = [[order.index(bb ^ (dd // nx)) * rows + dd % nx * out_rows for dd in path] for bb in range(nb)]
    half_places = jnp.array(half_places, jnp.int32)[b]
    path_places = jnp.array(path_places, jnp.int32)[b]

    def together(*values):
        return lax.optimization_barrier(values)

    def round_path(value):
        return lax.all_gather(value, "dp", axis_index_groups=[path])

    width = ff_block // COL_PARTS
    right = right_basis.astype(low)
    ff_rows = right.shape[0] // nx
    right_parts = [
        [right_basis[i * ff_rows : (i + 1) * ff_rows, j * width : (j + 1) * width].astype(low) for i in range(nx)]
        for j in range(COL_PARTS)
    ]

    left_blocks = round_path(left_basis.astype(low).T)
    piece = permute(gradient, lambda bb, zz, xx: (bb, zz ^ spread(bb), xx))
    piece, half_places, path_places, right_parts = together(piece, half_places, path_places, right_parts)
    piece = permute(piece, lambda bb, zz, xx: (zz ^ spread(bb), zz, xx))
    part = rows // 2
    piece, left_blocks = together(piece, left_blocks)
    gathered = [round_path(piece[h * part : (h + 1) * part]) for h in range(2)]

    left_t = jnp.concatenate([left_blocks[path.index(dd)] for dd in range(nd)], axis=0)
    for t in reversed(bits):
        left_t = jnp.concatenate([left_t, move_b(left_t, t)], axis=1)
    left_t = lax.optimization_barrier(left_t)
    left_halves = [
        lax.optimization_barrier(
            jnp.concatenate(
                [lax.dynamic_slice_in_dim(left_t, half_places[zz] + h * part, part, 1) for zz in range(nz)], axis=1
            )
        )
        for h in range(2)
    ]

    def columns_of(blocks):
        found = []
        for i in range(nx):
            mine = blocks[i * nz : (i + 1) * nz]
            mine = mine if i % 2 == 0 else jnp.flip(mine, 0)
            found.append(mine.reshape(nz * part, ff_rows))
        return lax.optimization_barrier(found)

    def half_rotation(found, j):
        total = sum(matmul(mine, right_parts[j][i]) for i, mine in enumerate(found))
        return lax.optimization_barrier(total.astype(low))

    def product(t, h, value):
        return matmul(lax.dynamic_slice_in_dim(left_halves[h], (b ^ t) * rows, rows, 0), value)

    found = columns_of(gathered[0])
    half = [half_rotation(found, j) for j in range(COL_PARTS)]
    early = {(t, j): product(t, 0, half[j]) for j in range(COL_PARTS) for t in range(nb)}
    names = list(early)
    gathered[1], *values = together(gathered[1], *[early[name] for name in names])
    early = dict(zip(names, values))
    found = columns_of(gathered[1])
    half = [None] * COL_PARTS

    products = {}
    last = None
    odd = sorted(range(1, nb, 2), key=lambda t: -t)
    held = [{} for _ in range(COL_PARTS)]
    for group in (odd[: nb // 4], odd[nb // 4 :]):
        for j in range(COL_PARTS):
            for t in (t for pair in group for t in (pair, pair ^ 1)):
                if half[j] is None:
                    half[j] = half_rotation(found if last is None else after(found, last), j)
                value = half[j] if last is None else after(half[j], last)
                last = products[t, j] = lax.optimization_barrier((early[t, j] + product(t, 1, value)).astype(low))
        for j in range(COL_PARTS):
            for t in group:
                got = move_b(products[t, j], 1)
                held[j][t ^ 1] = products[t ^ 1, j].astype(jnp.float32) + got.astype(jnp.float32)
        last = held[0][group[-1] ^ 1] = lax.optimization_barrier(held[0][group[-1] ^ 1].astype(low))
    held[0] = {t: value.astype(jnp.float32) for t, value in held[0].items()}

    arrived = []
    for j in range(COL_PARTS):
        for t in reversed(bits[1:]):
            for s in [s for s in held[j] if s & t]:
                away = held[j].pop(s).astype(low)
                if j:
                    away = after(away, arrived[j - 1])
                got = move_b(away, t)
                held[j][s ^ t] = held[j][s ^ t] + got.astype(jnp.float32)
        arrived.append(got)

    source = after(left_t, arrived[0])
    left = jnp.concatenate(
        [lax.dynamic_slice_in_dim(source, path_places[i], out_rows, 1).T for i in range(nd)], axis=0
    )
    left = lax.optimization_barrier(left)

    first_out, second_out, directions = [], [], []
    for j in range(COL_PARTS):
        cols = slice(j * width, (j + 1) * width)
        rotated = held[j][0]
        moments = first_moment[:, cols], second_moment[:, cols]
        if j:
            moments = after(moments, directions[-1])
        first_new = beta_first * moments[0] + (1.0 - beta_first) * rotated
        second_new = beta_second * moments[1] + (1.0 - beta_second) * rotated * rotated
        first_fix = 1.0 - beta_first**STEP
        second_fix = 1.0 - beta_second**STEP
        direction = first_new / first_fix / (jnp.sqrt(second_new / second_fix) + epsilon)
        first_out.append(first_new)
        second_out.append(second_new)
        directions.append(direction.astype(low))

    back, joins = [], []
    for j, column in enumerate(directions):
        for axis, t in enumerate(reversed(bits)):
            other = move_b(column, t)
            if j:
                other = after(other, joins[axis], back[-1])
            elif not axis:
                other = after(other, left, directions[-1])
            column = joined(column, other, (b & t) != 0, axis)
            joins[axis : axis + 1] = [column]
        column = lax.optimization_barrier(column.reshape(whole, width))
        back.append(lax.optimization_barrier(matmul(left, column).astype(low)))

    back = lax.optimization_barrier(jnp.concatenate(back, axis=1))
    total = matmul_nt(back, right).astype(low)
    update = lax.psum_scatter(total, "dp", scatter_dimension=0, axis_index_groups=[path], tiled=True)
    return (
        jnp.concatenate(first_out, axis=1),
        jnp.concatenate(second_out, axis=1),
        update,
    )


def solution(mesh):
    nb, nd = mesh.shape["basis"], mesh.shape["dp"]

    return jax.shard_map(
        functools.partial(per_device, nb=nb, nd=nd),
        mesh=mesh,
        in_specs=(
            P("basis", "dp"),
            P("basis", "dp"),
            P("basis", "dp"),
            P("basis", "dp"),
            P("basis", "dp"),
        ),
        out_specs=(P("basis", "dp"), P("basis", "dp"), P("dp", "basis")),
        check_vma=False,
    )
```

time: 362 us -> 400 us (1.10); the launches traced: 361 us -> 392 us
  starting transfers between devices: 51.9 us -> 14.3 us
  local copies, waits for them, and re-layouts: 16.8 us -> 52.8 us
  between operations: 16.9 us -> 42.3 us
  matrix products: 36.2 us -> 57.9 us
  Pallas kernels: 18.7 us -> 0 us
    ppermute x19 -> x14, starting transfers between devices: 51.7 us -> 14.1 us  [permute(): return lax.ppermute(value, ('basis', 'dp'), pairs)]
    all_gather x2 -> x3, waiting for transfers between devices: 9.57 us -> 38.6 us  [round_path(): return lax.all_gather(value, 'dp', axis_index_groups=[path])]
    ppermute x19 -> x14, waiting for transfers between devices: 97.9 us -> 70 us  [permute(): return lax.ppermute(value, ('basis', 'dp'), pairs)]
    dot_general x10 -> x26, matrix products: 25.3 us -> 47 us  [matmul(): lax.dot_general(a, b, (((1,), (0,)), ((), ())), preferred_element_type=jn...]
    pallas_call x2 -> x0, Pallas kernels: 18.7 us -> none  [half_rotation(): pl.pallas_call(kernel, out_shape=outs, grid_spec=pltpu.PrefetchScalarGrid...]
    slice x1 -> x5, local copies, waits for them, and re-layouts: 1.27 us -> 14.2 us  [the longest x2 8.18 us: columns_of(): mine = blocks[i * nz:(i + 1) * nz]]
    unnamed x38 -> x78, local copies, waits for them, and re-layouts: 13.2 us -> 22.1 us
    concatenate x0 -> x3, other arithmetic: none -> 7.95 us  [the longest x2 6.44 us: per_device(): jnp.concatenate([lax.dynamic_slice_in_dim(left_t, half_places[zz] + h * p...]
  transfers between devices with their start and end apart: 22 -> 18, of which waited for: 12 -> 9; matrix products, arithmetic and copies ran while one was open for 14% -> 25% of each run, Pallas kernels for 3% -> 0%
where the time goes in v8:
time: 400 us; the launch traced here: 392 us
  waiting for transfers between devices  194 us (48%)
  matrix products  57.9 us (14%)
  local copies, waits for them, and re-layouts  52.8 us (13%)
  between operations  42.3 us (11%)
  other arithmetic  31 us (8%)
  starting transfers between devices  14.3 us (4%)
    reduce_scatter x1, waiting for transfers between devices, per_device(): lax.psum_scatter(total, 'dp', scatter_dimension=0, axis_index_groups=[pat...  85.3 us
    ppermute x14, waiting for transfers between devices, permute(): return lax.ppermute(value, ('basis', 'dp'), pairs)  70 us
    dot_general x26, matrix products, matmul(): lax.dot_general(a, b, (((1,), (0,)), ((), ())), preferred_element_type=jn...  47 us
    all_gather x3, waiting for transfers between devices, round_path(): return lax.all_gather(value, 'dp', axis_index_groups=[path])  38.6 us
    unnamed x78, local copies, waits for them, and re-layouts  22.1 us
    ppermute x14, starting transfers between devices, permute(): return lax.ppermute(value, ('basis', 'dp'), pairs)  14.1 us
    dot_general x1, matrix products, matmul_nt(): lax.dot_general(a, b, (((1,), (1,)), ((), ())), preferred_element_type=jn...  10.9 us
    slice x2, local copies, waits for them, and re-layouts, columns_of(): mine = blocks[i * nz:(i + 1) * nz]  8.18 us
  transfers between devices with their start and end apart: 18, of which 9 were waited for; matrix products, arithmetic and copies ran while one was open for 25% of the time, Pallas kernels for 0%

profile of v8, /device:TPU:0, one launch (start us, length us, event | category | flops | bytes accessed | tf_op | source)
XLA Modules:
  0.0 392.4 jit_solution(14421644214437211935)
XLA Ops:
  7.2 1.8 convert_bitcast_fusion
  9.1 1.9 collective-permute-start
  10.9 6.1 %convert.6 = bf16[2048,1024]{1,0:T(8,128)(2,1)} convert(f32[2048,1024]{1,0:T(8,128)} %param.9) | non-fusion elementwise | flops 2097152 | bytes 12582912 | tf_op jit(solution)/shard_map/convert.3
  18.4 4.3 %fusion.56 = (bf16[1024,512]{1,0:T(8,128)(2,1)}, bf16[1024,512]{1,0:T(8,128)(2,1)}, bf16[1024,512]{1,0:T(8,128)(2,1)}, bf16[1024,512]{1,0:T(8,128)(2,1)}) fusion(bf16[2048,1024]{1,0:T(8,128)(2,1)} %convert.6), kind=kLoop, calls=%fused_computation.126 | loop fusion | bytes 8388608 | tf_op jit(solution)/shard_map/slice | solution.py:88
  23.5 38.6 %all-gather.7.cloned.1.call-done = bf16[2048,512]{0,1:T(8,128)(2,1)} async-done(((bf16[256,512]{0,1:T(8,128)(2,1)}), bf16[2048,512]{0,1:T(8,128)(2,1)}) %all-gather.7.cloned.1.call-update) | async-done | bytes 2097168 | tf_op jit(solution)/shard_map/all_gather | solution.py:82
  62.1 3.9 copy.17
  74.9 4.5 %collective-permute-start.2 = (bf16[2048,512]{1,0:T(8,128)(2,1)S(1)}, bf16[2048,512]{1,0:T(8,128)(2,1)S(1)}, u32[]{:S(2)}, u32[]{:S(2)}) collective-permute-start(bf16[2048,512]{1,0:T(8,128)(2,1)S(1)} %bitcast_dynamic-update-slice_fusion.8), channel_id=1, source_target_pairs={{0,16},{1,17},{2,18},{3,19},{4,20},{5,21},{6,22},{7,23},{8,24},{9,... | collective-permute-start | bytes 6291464 | tf_op jit(solution)/shard_map/ppermute | solution.py:41
  79.4 42.7 %collective-permute-done.2 = bf16[2048,512]{1,0:T(8,128)(2,1)S(1)} collective-permute-done((bf16[2048,512]{1,0:T(8,128)(2,1)S(1)}, bf16[2048,512]{1,0:T(8,128)(2,1)S(1)}, u32[]{:S(2)}, u32[]{:S(2)}) %collective-permute-start.2) | collective-permute-done | bytes 2097184 | tf_op jit(solution)/shard_map/ppermute | solution.py:41
  122.1 1.3 copy-done.2
  123.4 2.6 pad_maximum_fusion.1
  154.3 3.9 pad_maximum_fusion
  158.2 6.5 %constant_dynamic-slice_fusion.3 = (bf16[2048,256]{1,0:T(8,128)(2,1)}, bf16[2048,256]{1,0:T(8,128)(2,1)}, bf16[2048,256]{1,0:T(8,128)(2,1)}, bf16[2048,256]{1,0:...) fusion(bf16[2048,2048]{1,0:T(8,128)(2,1)S(1)} %pad_maximum_fusi, ...), kind=kLoop, calls=%fused_computation.111 | loop fusion | bytes 16777248 | tf_op jit(solution)/shard_map/dynamic_slice | solution.py:107
  164.7 3.9 pad_maximum_fusion.3
  168.6 2.5 pad_maximum_fusion.2
  171.2 4.0 %fusion.55 = (bf16[1024,1024]{1,0:T(8,128)(2,1)S(1)}, bf16[1024,1024]{1,0:T(8,128)(2,1)}) fusion(bf16[2048,1024]{1,0:T(8,128)(2,1)} %all-gather.11.cloned.1.call-done), kind=kLoop, calls=%fused_computation.125 | loop fusion | bytes 8388608 | tf_op jit(solution)/shard_map/slice | solution.py:116
  175.2 1.5 rev.7
  176.7 3.2 fusion.61
  185.3 1.7 fusion.22
  187.0 1.7 fusion.18
  188.7 1.7 fusion.20
  190.4 1.7 fusion.24
  192.1 1.7 fusion.26
  193.8 1.7 fusion.28
  195.5 1.7 fusion.30
  197.1 1.7 fusion.32
  198.9 4.2 %fusion.54 = (bf16[4,256,1024]{2,1,0:T(8,128)(2,1)S(1)}, bf16[4,256,1024]{2,1,0:T(8,128)(2,1)}) fusion(bf16[8,256,1024]{2,1,0:T(8,128)(2,1)} %bitcast.123), kind=kLoop, calls=%fused_computation.124 | loop fusion | bytes 8388608 | tf_op jit(solution)/shard_map/slice | solution.py:116
  203.1 1.5 rev.8
  204.6 3.3 fusion.62
  213.6 1.5 add_convert_fusion
  218.1 1.7 collective-permute-start.6
  222.5 9.8 %collective-permute-done.6 = bf16[512,512]{1,0:T(8,128)(2,1)S(1)} collective-permute-done((bf16[512,512]{1,0:T(8,128)(2,1)S(1)}, bf16[512,512]{1,0:T(8,128)(2,1)S(1)}, u32[]{:S(2)}, u32[]{:S(2)}) %collective-permute-start.6) | collective-permute-done | bytes 524320 | tf_op jit(solution)/shard_map/ppermute | solution.py:41
  232.3 1.7 collective-permute-start.9
  239.1 3.3 copy-done.19
  242.4 4.8 %collective-permute-done.9 = bf16[512,512]{1,0:T(8,128)(2,1)S(1)} collective-permute-done((bf16[512,512]{1,0:T(8,128)(2,1)S(1)}, bf16[512,512]{1,0:T(8,128)(2,1)S(1)}, u32[]{:S(2)}, u32[]{:S(2)}) %collective-permute-start.9) | collective-permute-done | bytes 524320 | tf_op jit(solution)/shard_map/ppermute | solution.py:41
  247.2 2.1 divide_convert_fusion
  249.3 7.7 %collective-permute-done.10 = bf16[512,512]{1,0:T(8,128)(2,1)S(1)} collective-permute-done((bf16[512,512]{1,0:T(8,128)(2,1)S(1)}, bf16[512,512]{1,0:T(8,128)(2,1)S(1)}, u32[]{:S(2)}, u32[]{:S(2)}) %collective-permute-start.10) | collective-permute-done | bytes 524320 | tf_op jit(solution)/shard_map/ppermute | solution.py:41
  258.2 1.7 collective-permute-start.12
  259.9 1.3 collective-permute-done.11
  261.2 1.4 select_bitcast_fusion.3
  262.9 8.7 %convolution_convert_fusion.2 = bf16[2048,512]{1,0:T(8,128)(2,1)S(1)} fusion(bf16[2048,2048]{0,1:T(8,128)(2,1)} %copy-done.19, bf16[2048,512]{1,0:T(8,128)(2,1)S(1)} %bitcast.129), kind=kOutput, calls=%fused_computation.7 | convolution fusion | flops 4296015872 | bytes 12582912 | tf_op jit(solution)/shard_map/dot_general | solution.py:21
  273.0 2.6 collective-permute-done.13
  276.1 1.8 slice-done.3
  278.0 4.8 %convolution_convert_fusion.1 = bf16[2048,512]{1,0:T(8,128)(2,1)S(1)} fusion(bf16[2048,2048]{0,1:T(8,128)(2,1)S(1)} %bitcast.133, bf16[2048,512]{1,0:T(8,128)(2,1)S(1)} %bitcast.128), kind=kOutput, calls=%fused_computation.6 | convolution fusion | flops 4296015872 | bytes 12582912 | tf_op jit(solution)/shard_map/dot_general | solution.py:21
  283.4 1.5 copy-done.1
  285.0 10.9 %convolution_convert_fusion = bf16[2048,2048]{1,0:T(8,128)(2,1)} fusion(bf16[2048,1024]{1,0:T(8,128)(2,1)S(1)} %pad_maximum_fusion.4, bf16[2048,1024]{1,0:T(8,128)(2,1)S(1)} %copy-done.1), kind=kOutput, calls=%fused_computation.1 | convolution fusion | flops 8594128896 | bytes 16777216 | tf_op jit(solution)/shard_map/dot_general | solution.py:25
  297.1 1.5 pad_maximum_fusion.6
  298.6 1.5 pad_maximum_fusion.5
  300.1 85.3 %reduce-scatter.2.cloned.1.call-done = bf16[256,2048]{1,0:T(8,128)(2,1)} async-done(((bf16[2048,2048]{1,0:T(8,128)(2,1)}), bf16[256,2048]{1,0:T(8,128)(2,1)}) %reduce-scatter.2.cloned.1.call-update) | async-done | bytes 1048592 | tf_op jit(solution)/shard_map/reduce_scatter | solution.py:203
  (136 shorter events, 38.5 us)
Async XLA Ops:
  7.2 54.9 %all-gather.7.cloned.1.call-start = ((), (), s32[]{:S(2)}) async-start(), calls=%async_computation.2 | async-start | bytes 2359296 | tf_op jit(solution)/shard_map/all_gather | solution.py:82
  9.0 162.2 %all-gather.11.cloned.1.call-start = ((), (), s32[]{:S(2)}) async-start(), calls=%async_computation.4 | async-start | bytes 4718592 | tf_op jit(solution)/shard_map/all_gather | solution.py:82
  9.1 13.7 %collective-permute-start = (bf16[512,1024]{1,0:T(8,128)(2,1)}, bf16[512,1024]{1,0:T(8,128)(2,1)S(1)}, u32[]{:S(2)}, u32[]{:S(2)}) collective-permute-start(bf16[512,1024]{1,0:T(8,128)(2,1)} %param.7), channel_id=1, source_target_pairs={{0,0},{1,1},{2,2},{3,3},{4,4},{5,5},{6,6},{7,7},{8,14},{9,15},{10,... | collective-permute-start | bytes 3145736 | tf_op jit(solution)/shard_map/ppermute | solution.py:41
  22.8 43.2 %collective-permute-start.1 = (bf16[512,1024]{1,0:T(8,128)(2,1)S(1)}, bf16[512,1024]{1,0:T(8,128)(2,1)S(1)}, u32[]{:S(2)}, u32[]{:S(2)}) collective-permute-start(bf16[512,1024]{1,0:T(8,128)(2,1)S(1)} %collective-permute-done), channel_id=1, source_target_pairs={{0,0},{1,1},{2,10},{3,11},{4,20},{5,21},{6,30},{7,31},{8,24},{9,25... | collective-permute-start | bytes 3145736 | tf_op jit(solution)/shard_map/ppermute | solution.py:41
  67.1 131.8 %all-gather.9.cloned.1.call-start = ((), (), s32[]{:S(2)}) async-start(), calls=%async_computation.3 | async-start | bytes 4718592 | tf_op jit(solution)/shard_map/all_gather | solution.py:82
  74.9 47.2 %collective-permute-start.2 = (bf16[2048,512]{1,0:T(8,128)(2,1)S(1)}, bf16[2048,512]{1,0:T(8,128)(2,1)S(1)}, u32[]{:S(2)}, u32[]{:S(2)}) collective-permute-start(bf16[2048,512]{1,0:T(8,128)(2,1)S(1)} %bitcast_dynamic-update-slice_fusion.8), channel_id=1, source_target_pairs={{0,16},{1,17},{2,18},{3,19},{4,20},{5,21},{6,22},{7,23},{8,24},{9,... | collective-permute-start | bytes 6291464 | tf_op jit(solution)/shard_map/ppermute | solution.py:41
  122.1 1.3 copy-start.2
  126.1 28.3 %collective-permute-start.3 = (bf16[2048,1024]{1,0:T(8,128)(2,1)}, bf16[2048,1024]{1,0:T(8,128)(2,1)}, u32[]{:S(2)}, u32[]{:S(2)}) collective-permute-start(bf16[2048,1024]{1,0:T(8,128)(2,1)} %pad_maximum_fusion.1), channel_id=1, source_target_pairs={{0,8},{1,9},{2,10},{3,11},{4,12},{5,13},{6,14},{7,15},{8,0},{9,1},... | collective-permute-start | bytes 12582920 | tf_op jit(solution)/shard_map/ppermute | solution.py:41
  126.1 259.3 %reduce-scatter.2.cloned.1.call-start = ((), (), s32[]{:S(2)}) async-start(), calls=%async_computation.1 | async-start | bytes 9437184 | tf_op jit(solution)/shard_map/reduce_scatter | solution.py:203
  158.2 6.5 %copy-start = (bf16[2048,2048]{1,0:T(8,128)(2,1)}, bf16[2048,2048]{1,0:T(8,128)(2,1)S(1)}, u32[]{:S(2)}) copy-start(bf16[2048,2048]{1,0:T(8,128)(2,1)S(1)} %pad_maximum_fusion) | copy-start | bytes 25165828
  176.7 3.3 copy-start.13
  176.7 3.3 copy-start.14
  180.0 1.6 copy-start.11
  180.0 1.8 copy-start.18
  183.1 2.2 copy-start.4
  204.6 3.3 copy-start.12
  204.6 3.3 copy-start.17
  207.9 2.2 copy-start.3
  207.9 2.5 copy-start.27
  207.9 3.7 copy-start.26
  210.3 2.0 copy-start.10
  210.3 2.0 copy-start.15
  211.1 6.0 %collective-permute-start.4 = (bf16[512,512]{1,0:T(8,128)(2,1)S(1)}, bf16[512,512]{1,0:T(8,128)(2,1)S(1)}, u32[]{:S(2)}, u32[]{:S(2)}) collective-permute-start(bf16[512,512]{1,0:T(8,128)(2,1)S(1)} %fusion), channel_id=1, source_target_pairs={{0,8},{1,9},{2,10},{3,11},{4,12},{5,13},{6,14},{7,15},{8,0},{9,1},... | collective-permute-start | bytes 1572872 | tf_op jit(solution)/shard_map/ppermute | solution.py:41
  213.6 1.5 copy-start.25
  213.6 2.7 copy-start.24
  215.1 2.1 copy-start.23
  215.8 4.0 %copy-start.22 = (f32[512,512]{1,0:T(8,128)S(1)}, f32[512,512]{1,0:T(8,128)}, u32[]{:S(2)}) copy-start(f32[512,512]{1,0:T(8,128)} %fusion.32) | copy-start | bytes 3145732
  215.8 6.4 %collective-permute-start.8 = (bf16[512,512]{1,0:T(8,128)(2,1)S(1)}, bf16[512,512]{1,0:T(8,128)(2,1)S(1)}, u32[]{:S(2)}, u32[]{:S(2)}) collective-permute-start(bf16[512,512]{1,0:T(8,128)(2,1)S(1)} %fusion.6), channel_id=1, source_target_pairs={{0,8},{1,9},{2,10},{3,11},{4,12},{5,13},{6,14},{7,15},{8,0},{9,1},... | collective-permute-start | bytes 1572872 | tf_op jit(solution)/shard_map/ppermute | solution.py:41
  217.2 3.3 copy-start.21
  217.9 3.6 copy-start.20
  217.9 4.4 %collective-permute-start.5 = (bf16[512,512]{1,0:T(8,128)(2,1)S(1)}, bf16[512,512]{1,0:T(8,128)(2,1)S(1)}, u32[]{:S(2)}, u32[]{:S(2)}) collective-permute-start(bf16[512,512]{1,0:T(8,128)(2,1)S(1)} %fusion.2), channel_id=1, source_target_pairs={{0,8},{1,9},{2,10},{3,11},{4,12},{5,13},{6,14},{7,15},{8,0},{9,1},... | collective-permute-start | bytes 1572872 | tf_op jit(solution)/shard_map/ppermute | solution.py:41
  218.1 14.3 %collective-permute-start.6 = (bf16[512,512]{1,0:T(8,128)(2,1)S(1)}, bf16[512,512]{1,0:T(8,128)(2,1)S(1)}, u32[]{:S(2)}, u32[]{:S(2)}) collective-permute-start(bf16[512,512]{1,0:T(8,128)(2,1)S(1)} %add_convert_fusion.6), channel_id=1, source_target_pairs={{0,16},{1,17},{2,18},{3,19},{4,20},{5,21},{6,22},{7,23},{8,24},{9,... | collective-permute-start | bytes 1572872 | tf_op jit(solution)/shard_map/ppermute | solution.py:41
  221.2 12.8 %copy-start.7 = (f32[512,1024]{1,0:T(8,128)S(1)}, f32[512,1024]{1,0:T(8,128)}, u32[]{:S(2)}) copy-start(f32[512,1024]{1,0:T(8,128)} %param.10) | copy-start | bytes 6291460
  221.3 12.8 %copy-start.8 = (f32[512,1024]{1,0:T(8,128)S(1)}, f32[512,1024]{1,0:T(8,128)}, u32[]{:S(2)}) copy-start(f32[512,1024]{1,0:T(8,128)} %param.11) | copy-start | bytes 6291460
  221.3 17.8 %collective-permute-start.7 = (bf16[512,512]{1,0:T(8,128)(2,1)S(1)}, bf16[512,512]{1,0:T(8,128)(2,1)S(1)}, u32[]{:S(2)}, u32[]{:S(2)}) collective-permute-start(bf16[512,512]{1,0:T(8,128)(2,1)S(1)} %fusion.4), channel_id=1, source_target_pairs={{0,8},{1,9},{2,10},{3,11},{4,12},{5,13},{6,14},{7,15},{8,0},{9,1},... | collective-permute-start | bytes 1572872 | tf_op jit(solution)/shard_map/ppermute | solution.py:41
  221.5 13.8 %slice-start = ((s8[8388608]{0:T(1024)(128)(4,1)}), s8[4194304]{0:T(1024)(128)(4,1)S(1)}, s32[]{:S(2)}) async-start(s8[8388608]{0:T(1024)(128)(4,1)} %bitcast.112), calls=%async_computation.5 | async-start | bytes 8388608
  222.5 12.8 %slice-start.1 = ((s8[8388608]{0:T(1024)(128)(4,1)}), s8[4194304]{0:T(1024)(128)(4,1)S(1)}, s32[]{:S(2)}) async-start(s8[8388608]{0:T(1024)(128)(4,1)} %bitcast.112), calls=%async_computation.6 | async-start | bytes 8388608
  232.3 14.8 %collective-permute-start.9 = (bf16[512,512]{1,0:T(8,128)(2,1)S(1)}, bf16[512,512]{1,0:T(8,128)(2,1)S(1)}, u32[]{:S(2)}, u32[]{:S(2)}) collective-permute-start(bf16[512,512]{1,0:T(8,128)(2,1)S(1)} %add_convert_fusion.4), channel_id=1, source_target_pairs={{0,16},{1,17},{2,18},{3,19},{4,20},{5,21},{6,22},{7,23},{8,24},{9,... | collective-permute-start | bytes 1572872 | tf_op jit(solution)/shard_map/ppermute | solution.py:41
  234.9 22.1 %collective-permute-start.10 = (bf16[512,512]{1,0:T(8,128)(2,1)S(1)}, bf16[512,512]{1,0:T(8,128)(2,1)S(1)}, u32[]{:S(2)}, u32[]{:S(2)}) collective-permute-start(bf16[512,512]{1,0:T(8,128)(2,1)S(1)} %get-tuple-element.82), channel_id=1, source_target_pairs={{0,16},{1,17},{2,18},{3,19},{4,20},{5,21},{6,22},{7,23},{8,24},{9,... | collective-permute-start | bytes 1572872 | tf_op jit(solution)/shard_map/ppermute | solution.py:41
  239.1 3.3 copy-start.19
  258.2 3.0 collective-permute-start.11
  258.2 14.5 %collective-permute-start.12 = (bf16[512,512]{1,0:T(8,128)(2,1)}, bf16[512,512]{1,0:T(8,128)(2,1)S(1)}, u32[]{:S(2)}, u32[]{:S(2)}) collective-permute-start(bf16[512,512]{1,0:T(8,128)(2,1)} %get-tuple-element.79), channel_id=1, source_target_pairs={{0,16},{1,17},{2,18},{3,19},{4,20},{5,21},{6,22},{7,23},{8,24},{9,... | collective-permute-start | bytes 1572872 | tf_op jit(solution)/shard_map/ppermute | solution.py:41
  262.9 9.8 %copy-start.9 = (bf16[512,512]{1,0:T(8,128)(2,1)S(1)}, bf16[512,512]{1,0:T(8,128)(2,1)}, u32[]{:S(2)}) copy-start(bf16[512,512]{1,0:T(8,128)(2,1)} %get-tuple-element.79) | copy-start | bytes 1572868
  272.7 3.4 slice-start.2
  272.9 2.7 collective-permute-start.13
  275.8 2.2 slice-start.3
  282.8 2.2 copy-start.1
  295.9 2.7 copy-start.5
  (2 other events, 2.5 us)
Sparse Core Ops, SparseCore 0:
  10.0 52.0 all-gather.6
  67.2 49.9 all-gather.10
  126.2 49.2 all-gather.8
  296.0 89.3 reduce-scatter.1

commit v9 on v8

--- a/solution.py
+++ b/solution.py
@@ -46,9 +46,9 @@
     def spread(beta):
         return (beta >> 1) ^ ((beta & 1) * (nz - 1))
 
-    unspread = [0] * nz
-    for beta in range(nb):
-        unspread[spread(beta)] = beta
+    def unspread(w):
+        odd = (w >> (len(bits) - 1)) & 1
+        return (w ^ (odd * (nz - 1))) * 2 + odd
 
     def joined(mine, other, bit_set, axis):
         first = jnp.where(bit_set, other, mine)
@@ -67,13 +67,8 @@
     for xx in range(nx):
         path += [zz * nx + xx for zz in (range(nz) if xx % 2 == 0 else reversed(range(nz)))]
 
-    order = [0]
-    for t in reversed(bits):
-        order = order + [s | t for s in order]
-    half_places = [[order.index(unspread[bb ^ zz] ^ bb) * rows for zz in range(nz)] for bb in range(nb)]
-    path_places = [[order.index(bb ^ (dd // nx)) * rows + dd % nx * out_rows for dd in path] for bb in range(nb)]
-    half_places = jnp.array(half_places, jnp.int32)[b]
-    path_places = jnp.array(path_places, jnp.int32)[b]
+    def reversed_bits(t):
+        return sum(((t >> k) & 1) << (len(bits) - 1 - k) for k in range(len(bits)))
 
     def together(*values):
         return lax.optimization_barrier(values)
@@ -91,47 +86,30 @@
 
     left_blocks = round_path(left_basis.astype(low).T)
     piece = permute(gradient, lambda bb, zz, xx: (bb, zz ^ spread(bb), xx))
-    piece, half_places, path_places, right_parts = together(piece, half_places, path_places, right_parts)
+    piece, right_parts = together(piece, right_parts)
     piece = permute(piece, lambda bb, zz, xx: (zz ^ spread(bb), zz, xx))
-    part = rows // 2
     piece, left_blocks = together(piece, left_blocks)
-    gathered = [round_path(piece[h * part : (h + 1) * part]) for h in range(2)]
+    gathered = round_path(piece)
 
     left_t = jnp.concatenate([left_blocks[path.index(dd)] for dd in range(nd)], axis=0)
     for t in reversed(bits):
         left_t = jnp.concatenate([left_t, move_b(left_t, t)], axis=1)
     left_t = lax.optimization_barrier(left_t)
-    left_halves = [
-        lax.optimization_barrier(
-            jnp.concatenate(
-                [lax.dynamic_slice_in_dim(left_t, half_places[zz] + h * part, part, 1) for zz in range(nz)], axis=1
-            )
-        )
-        for h in range(2)
-    ]
-
-    def columns_of(blocks):
-        found = []
-        for i in range(nx):
-            mine = blocks[i * nz : (i + 1) * nz]
-            mine = mine if i % 2 == 0 else jnp.flip(mine, 0)
-            found.append(mine.reshape(nz * part, ff_rows))
-        return lax.optimization_barrier(found)
-
-    def half_rotation(found, j):
-        total = sum(matmul(mine, right_parts[j][i]) for i, mine in enumerate(found))
-        return lax.optimization_barrier(total.astype(low))
-
-    def product(t, h, value):
-        return matmul(lax.dynamic_slice_in_dim(left_halves[h], (b ^ t) * rows, rows, 0), value)
-
-    found = columns_of(gathered[0])
-    half = [half_rotation(found, j) for j in range(COL_PARTS)]
-    early = {(t, j): product(t, 0, half[j]) for j in range(COL_PARTS) for t in range(nb)}
-    names = list(early)
-    gathered[1], *values = together(gathered[1], *[early[name] for name in names])
-    early = dict(zip(names, values))
-    found = columns_of(gathered[1])
+    left_rows = jnp.concatenate(
+        [
+            lax.dynamic_slice_in_dim(left_t, reversed_bits(unspread(b ^ zz) ^ b) * rows, rows, 1)
+            for zz in range(nz)
+        ],
+        axis=1,
+    )
+    left_rows, gathered = together(left_rows, gathered)
+
+    blocks = []
+    for i in range(nx):
+        mine = gathered[i * nz : (i + 1) * nz]
+        mine = mine if i % 2 == 0 else jnp.flip(mine, 0)
+        blocks.append(mine.reshape(whole, ff_rows))
+    blocks = lax.optimization_barrier(blocks)
     half = [None] * COL_PARTS
 
     products = {}
@@ -142,9 +120,12 @@
         for j in range(COL_PARTS):
             for t in (t for pair in group for t in (pair, pair ^ 1)):
                 if half[j] is None:
-                    half[j] = half_rotation(found if last is None else after(found, last), j)
+                    found = blocks if last is None else after(blocks, last)
+                    total = sum(matmul(mine, right_parts[j][i]) for i, mine in enumerate(found))
+                    half[j] = lax.optimization_barrier(total.astype(low))
                 value = half[j] if last is None else after(half[j], last)
-                last = products[t, j] = lax.optimization_barrier((early[t, j] + product(t, 1, value)).astype(low))
+                rows_of = lax.dynamic_slice_in_dim(left_rows, (b ^ t) * rows, rows, 0)
+                last = products[t, j] = lax.optimization_barrier(matmul(rows_of, value).astype(low))
         for j in range(COL_PARTS):
             for t in group:
                 got = move_b(products[t, j], 1)
@@ -165,7 +146,13 @@
 
     source = after(left_t, arrived[0])
     left = jnp.concatenate(
-        [lax.dynamic_slice_in_dim(source, path_places[i], out_rows, 1).T for i in range(nd)], axis=0
+        [
+            lax.dynamic_slice_in_dim(
+                source, reversed_bits(b ^ (dd // nx)) * rows + dd % nx * out_rows, out_rows, 1
+            ).T
+            for dd in path
+        ],
+        axis=0,
     )
     left = lax.optimization_barrier(left)
 
@@ -185,20 +172,18 @@
         second_out.append(second_new)
         directions.append(direction.astype(low))
 
-    back, joins = [], []
+    columns, joins = [], []
     for j, column in enumerate(directions):
         for axis, t in enumerate(reversed(bits)):
             other = move_b(column, t)
             if j:
-                other = after(other, joins[axis], back[-1])
-            elif not axis:
-                other = after(other, left, directions[-1])
+                other = after(other, joins[axis])
             column = joined(column, other, (b & t) != 0, axis)
             joins[axis : axis + 1] = [column]
-        column = lax.optimization_barrier(column.reshape(whole, width))
-        back.append(lax.optimization_barrier(matmul(left, column).astype(low)))
-
-    back = lax.optimization_barrier(jnp.concatenate(back, axis=1))
+        columns.append(column.reshape(whole, width))
+
+    columns = lax.optimization_barrier(jnp.concatenate(columns, axis=1))
+    back = lax.optimization_barrier(matmul(left, columns).astype(low))
     total = matmul_nt(back, right).astype(low)
     update = lax.psum_scatter(total, "dp", scatter_dimension=0, axis_index_groups=[path], tiled=True)
     return (

time: 400 us -> 356 us (0.89); the launches traced: 392 us -> 356 us
  waiting for transfers between devices: 194 us -> 224 us
  between operations: 42.3 us -> 14.3 us
  local copies, waits for them, and re-layouts: 52.8 us -> 35.5 us
  matrix products: 57.9 us -> 42.7 us
  other arithmetic: 31 us -> 25.9 us
    all_gather x3 -> x2, waiting for transfers between devices: 38.6 us -> 55 us  [round_path(): return lax.all_gather(value, 'dp', axis_index_groups=[path])]
    ppermute x14, waiting for transfers between devices: 70 us -> 86 us  [permute(): return lax.ppermute(value, ('basis', 'dp'), pairs)]
    dot_general x26 -> x13, matrix products: 47 us -> 31.8 us  [matmul(): lax.dot_general(a, b, (((1,), (0,)), ((), ())), preferred_element_type=jn...]
    unnamed x78 -> x52, local copies, waits for them, and re-layouts: 22.1 us -> 16.1 us
    dynamic_slice x1, local copies, waits for them, and re-layouts: 6.52 us -> 1.06 us  [per_device(): lax.dynamic_slice_in_dim(left_t, reversed_bits(unspread(b ^ zz) ^ b) * ro...]
    concatenate x4 -> x2, other arithmetic: 8.59 us -> 4.63 us  [the longest x1 3.98 us: per_device(): jnp.concatenate([lax.dynamic_slice_in_dim(left_t, reversed_bits(unspread(...]
    slice x4 -> x1, local copies, waits for them, and re-layouts: 9.9 us -> 5.99 us  [per_device(): mine = gathered[i * nz:(i + 1) * nz]]
  transfers between devices with their start and end apart: 18 -> 17, of which waited for: 9 -> 10; matrix products, arithmetic and copies ran while one was open for 25% -> 15% of each run, Pallas kernels for 0% -> 0%
where the time goes in v9:
time: 356 us
  waiting for transfers between devices  224 us (63%)
  matrix products  42.7 us (12%)
  local copies, waits for them, and re-layouts  35.5 us (10%)
  other arithmetic  25.9 us (7%)
  between operations  14.3 us (4%)
  starting transfers between devices  13.2 us (4%)
    ppermute x14, waiting for transfers between devices, permute(): return lax.ppermute(value, ('basis', 'dp'), pairs)  86 us
    reduce_scatter x1, waiting for transfers between devices, per_device(): lax.psum_scatter(total, 'dp', scatter_dimension=0, axis_index_groups=[pat...  83.1 us
    all_gather x2, waiting for transfers between devices, round_path(): return lax.all_gather(value, 'dp', axis_index_groups=[path])  55 us
    dot_general x13, matrix products, matmul(): lax.dot_general(a, b, (((1,), (0,)), ((), ())), preferred_element_type=jn...  31.8 us
    unnamed x52, local copies, waits for them, and re-layouts  16.1 us
    ppermute x14, starting transfers between devices, permute(): return lax.ppermute(value, ('basis', 'dp'), pairs)  13.1 us
    dot_general x1, matrix products, matmul_nt(): lax.dot_general(a, b, (((1,), (1,)), ((), ())), preferred_element_type=jn...  11 us
  transfers between devices with their start and end apart: 17, of which 10 were waited for; matrix products, arithmetic and copies ran while one was open for 15% of the time, Pallas kernels for 0%

profile of v9, /device:TPU:0, one launch (start us, length us, event | category | flops | bytes accessed | tf_op | source)
XLA Modules:
  0.0 355.8 jit_solution(3555631357172042098)
XLA Ops:
  7.2 1.8 convert_bitcast_fusion
  9.1 1.9 collective-permute-start
  10.9 4.0 %convert.6 = bf16[2048,1024]{1,0:T(8,128)(2,1)S(1)} convert(f32[2048,1024]{1,0:T(8,128)} %param.7) | non-fusion elementwise | flops 2097152 | bytes 12582912 | tf_op jit(solution)/shard_map/convert.3
  15.0 2.3 fusion.53
  17.3 1.0 copy-done.1
  19.0 43.0 %all-gather.5.cloned.1.call-done = bf16[2048,512]{0,1:T(8,128)(2,1)} async-done(((bf16[256,512]{0,1:T(8,128)(2,1)}), bf16[2048,512]{0,1:T(8,128)(2,1)}) %all-gather.5.cloned.1.call-update) | async-done | bytes 2097168 | tf_op jit(solution)/shard_map/all_gather | solution.py:77
  62.1 3.9 %copy.15 = bf16[2048,512]{1,0:T(8,128)(2,1)} copy(bf16[2048,512]{0,1:T(8,128)(2,1)} %all-gather.5.cloned.1.call-done) | data formatting | bytes 4194304 | tf_op jit(solution)/shard_map/all_gather | solution.py:77
  68.0 1.0 bitcast_dynamic-update-slice_fusion.14
  69.0 1.0 bitcast_dynamic-update-slice_fusion.13
  74.8 4.6 %collective-permute-start.2 = (bf16[2048,512]{1,0:T(8,128)(2,1)S(1)}, bf16[2048,512]{1,0:T(8,128)(2,1)S(1)}, u32[]{:S(2)}, u32[]{:S(2)}) collective-permute-start(bf16[2048,512]{1,0:T(8,128)(2,1)S(1)} %bitcast_dynamic-update-slice_fusion.8), channel_id=1, source_target_pairs={{0,16},{1,17},{2,18},{3,19},{4,20},{5,21},{6,22},{7,23},{8,24},{9,... | collective-permute-start | bytes 6291464 | tf_op jit(solution)/shard_map/ppermute | solution.py:41
  79.4 42.6 %collective-permute-done.2 = bf16[2048,512]{1,0:T(8,128)(2,1)S(1)} collective-permute-done((bf16[2048,512]{1,0:T(8,128)(2,1)S(1)}, bf16[2048,512]{1,0:T(8,128)(2,1)S(1)}, u32[]{:S(2)}, u32[]{:S(2)}) %collective-permute-start.2) | collective-permute-done | bytes 2097184 | tf_op jit(solution)/shard_map/ppermute | solution.py:41
  122.0 1.3 copy-done.3
  123.3 2.6 pad_maximum_fusion.2
  126.0 7.5 %collective-permute-done.3 = bf16[2048,1024]{1,0:T(8,128)(2,1)} collective-permute-done((bf16[2048,1024]{1,0:T(8,128)(2,1)}, bf16[2048,1024]{1,0:T(8,128)(2,1)}, u32[]{:S(2)}, u32[]{:S(2)}) %collective-permute-start.3) | collective-permute-done | bytes 4194336 | tf_op jit(solution)/shard_map/ppermute | solution.py:41
  133.5 3.7 %pad_maximum_fusion = bf16[2048,2048]{1,0:T(8,128)(2,1)S(1)} fusion(bf16[2048,1024]{1,0:T(8,128)(2,1)} %collective-permute-done.3, bf16[2048,512]{1,0:T(8,128)(2,1)} %copy-done.3, bf16[2048,512]{1,0:T(8,128)(2,1)S(1)} %bitcast_dynamic-update-slice_fusion.8), kind=kLoop, calls=%fused_computation | loop fusion | flops 25165824 | bytes 16777216 | tf_op jit(solution)/shard_map/concatenate | solution.py:96
  137.2 1.1 constant_dynamic-slice_fusion.3
  138.3 2.2 copy-done
  140.5 4.0 %pad_maximum_fusion.1 = bf16[2048,2048]{1,0:T(8,128)(2,1)} fusion(bf16[2048,512]{1,0:T(8,128)(2,1)S(1)} %get-tuple-element.64, bf16[2048,512]{1,0:T(8,128)(2,1)S(1)} %get-tuple-element.65, bf16[2048,512]{1,0:T(8,128)(2,1)S(1)} %get-tuple-element.66, bf16[2048,512]{1,0:T(8,128)(2,1)S(1)} %get-tuple-element.63), kind=kLoop, calls=%fused_computation.1 | loop fusion | flops 33554432 | bytes 16777216 | tf_op jit(solution)/shard_map/concatenate | solution.py:98
  144.5 11.9 %all-gather.7.cloned.1.call-done = bf16[4096,1024]{1,0:T(8,128)(2,1)} async-done(((bf16[512,1024]{1,0:T(8,128)(2,1)}), bf16[4096,1024]{1,0:T(8,128)(2,1)}) %all-gather.7.cloned.1.call-update) | async-done | bytes 8388624 | tf_op jit(solution)/shard_map/all_gather | solution.py:77
  156.4 6.0 %fusion.52 = (bf16[4,512,1024]{2,1,0:T(8,128)(2,1)}, bf16[4,512,1024]{2,1,0:T(8,128)(2,1)}) fusion(bf16[8,512,1024]{2,1,0:T(8,128)(2,1)} %bitcast.86), kind=kLoop, calls=%fused_computation.88 | loop fusion | bytes 16777216 | tf_op jit(solution)/shard_map/slice | solution.py:109
  162.4 4.8 %rev.4 = bf16[4,512,1024]{2,1,0:T(8,128)(2,1)} reverse(bf16[4,512,1024]{2,1,0:T(8,128)(2,1)} %get-tuple-element.61), dimensions={0} | reverse | bytes 8388608 | tf_op jit(solution)/shard_map/jit(_flip)/rev | solution.py:110
  167.2 4.7 %fusion.54 = f32[2048,512]{1,0:T(8,128)S(1)} fusion(bf16[2048,1024]{1,0:T(8,128)(2,1)} %bitcast.91, bf16[1024,512]{1,0:T(8,128)(2,1)S(1)} %copy-done.14), kind=kOutput, calls=%fused_computation.90 | convolution fusion | flops 2147483648 | bytes 9437184 | tf_op jit(solution)/shard_map/dot_general | solution.py:21
  171.9 2.5 add_convert_fusion.1
  174.5 1.2 fusion.34
  175.8 1.2 fusion.28
  178.2 2.4 fusion.55
  180.7 2.5 add_convert_fusion
  183.2 1.2 fusion.37
  184.5 1.2 fusion.31
  185.9 1.5 collective-permute-start.6
  187.5 1.5 fusion.22
  188.9 1.2 fusion.16
  190.2 1.2 fusion.25
  192.0 1.2 fusion.19
  193.4 6.9 %collective-permute-done.6 = bf16[512,512]{1,0:T(8,128)(2,1)S(1)} collective-permute-done((bf16[512,512]{1,0:T(8,128)(2,1)S(1)}, bf16[512,512]{1,0:T(8,128)(2,1)S(1)}, u32[]{:S(2)}, u32[]{:S(2)}) %collective-permute-start.6) | collective-permute-done | bytes 524320 | tf_op jit(solution)/shard_map/ppermute | solution.py:41
  200.3 1.5 collective-permute-start.9
  201.9 1.8 divide_convert_fusion.1
  204.9 10.2 %collective-permute-done.9 = bf16[512,512]{1,0:T(8,128)(2,1)S(1)} collective-permute-done((bf16[512,512]{1,0:T(8,128)(2,1)S(1)}, bf16[512,512]{1,0:T(8,128)(2,1)S(1)}, u32[]{:S(2)}, u32[]{:S(2)}) %collective-permute-start.9) | collective-permute-done | bytes 524320 | tf_op jit(solution)/shard_map/ppermute | solution.py:41
  215.1 2.2 divide_convert_fusion
  217.3 1.5 collective-permute-start.12
  218.9 7.4 %collective-permute-done.10 = bf16[512,512]{1,0:T(8,128)(2,1)S(1)} collective-permute-done((bf16[512,512]{1,0:T(8,128)(2,1)S(1)}, bf16[512,512]{1,0:T(8,128)(2,1)S(1)}, u32[]{:S(2)}, u32[]{:S(2)}) %collective-permute-start.10) | collective-permute-done | bytes 524320 | tf_op jit(solution)/shard_map/ppermute | solution.py:41
  226.6 9.7 %collective-permute-done.12 = bf16[512,512]{1,0:T(8,128)(2,1)S(1)} collective-permute-done((bf16[512,512]{1,0:T(8,128)(2,1)S(1)}, bf16[512,512]{1,0:T(8,128)(2,1)S(1)}, u32[]{:S(2)}, u32[]{:S(2)}) %collective-permute-start.12) | collective-permute-done | bytes 524320 | tf_op jit(solution)/shard_map/ppermute | solution.py:41
  237.6 1.7 collective-permute-done.13
  240.4 9.5 %convolution_convert_fusion.1 = bf16[2048,1024]{1,0:T(8,128)(2,1)S(1)} fusion(bf16[2048,2048]{0,1:T(8,128)(2,1)S(1)} %bitcast_dynamic-update-slice_fusion, bf16[2048,1024]{1,0:T(8,128)(2,1)S(1)} %pad_maximum_fusion.3), kind=kOutput, calls=%fused_computation.7 | convolution fusion | flops 8592031744 | bytes 16777216 | tf_op jit(solution)/shard_map/dot_general | solution.py:21
  249.9 11.0 %convolution_convert_fusion = bf16[2048,2048]{1,0:T(8,128)(2,1)} fusion(bf16[2048,1024]{1,0:T(8,128)(2,1)S(1)} %convolution_convert_fusion.1, bf16[2048,1024]{1,0:T(8,128)(2,1)S(1)} %copy-done.2), kind=kOutput, calls=%fused_computation.2 | convolution fusion | flops 8594128896 | bytes 16777216 | tf_op jit(solution)/shard_map/dot_general | solution.py:25
  260.9 1.2 copy-done.6
  262.4 3.7 %pad_maximum_fusion.4 = (f32[512,1024]{1,0:T(8,128)}, f32[512,1024]{1,0:T(8,128)}) fusion(f32[512,512]{1,0:T(8,128)} %get-tuple-element.57, f32[512,512]{1,0:T(8,128)S(1)} %get-tuple-element.59, f32[512,512]{1,0:T(8,128)S(1)} %copy-done.7, f32[512,512]{1,0:T(8,128)S(1)} %copy-done.6), kind=kLoop, calls=%fused_computation.8 | loop fusion | flops 1048576 | bytes 8388608 | tf_op jit(solution)/shard_map/concatenate | solution.py:190
  266.1 83.1 %reduce-scatter.2.cloned.1.call-done = bf16[256,2048]{1,0:T(8,128)(2,1)} async-done(((bf16[2048,2048]{1,0:T(8,128)(2,1)}), bf16[256,2048]{1,0:T(8,128)(2,1)}) %reduce-scatter.2.cloned.1.call-update) | async-done | bytes 1048592 | tf_op jit(solution)/shard_map/reduce_scatter | solution.py:188
  (86 shorter events, 14.1 us)
Async XLA Ops:
  7.2 54.9 %all-gather.5.cloned.1.call-start = ((), (), s32[]{:S(2)}) async-start(), calls=%async_computation.2 | async-start | bytes 2359296 | tf_op jit(solution)/shard_map/all_gather | solution.py:77
  9.0 147.4 %all-gather.7.cloned.1.call-start = ((), (), s32[]{:S(2)}) async-start(), calls=%async_computation.3 | async-start | bytes 9437184 | tf_op jit(solution)/shard_map/all_gather | solution.py:77
  9.1 9.3 %collective-permute-start = (bf16[512,1024]{1,0:T(8,128)(2,1)}, bf16[512,1024]{1,0:T(8,128)(2,1)S(1)}, u32[]{:S(2)}, u32[]{:S(2)}) collective-permute-start(bf16[512,1024]{1,0:T(8,128)(2,1)} %param.5), channel_id=1, source_target_pairs={{0,0},{1,1},{2,2},{3,3},{4,4},{5,5},{6,6},{7,7},{8,14},{9,15},{10,... | collective-permute-start | bytes 3145736 | tf_op jit(solution)/shard_map/ppermute | solution.py:41
  15.0 3.3 copy-start.1
  18.3 47.7 %collective-permute-start.1 = (bf16[512,1024]{1,0:T(8,128)(2,1)S(1)}, bf16[512,1024]{1,0:T(8,128)(2,1)S(1)}, u32[]{:S(2)}, u32[]{:S(2)}) collective-permute-start(bf16[512,1024]{1,0:T(8,128)(2,1)S(1)} %collective-permute-done), channel_id=1, source_target_pairs={{0,0},{1,1},{2,10},{3,11},{4,20},{5,21},{6,30},{7,31},{8,24},{9,25... | collective-permute-start | bytes 3145736 | tf_op jit(solution)/shard_map/ppermute | solution.py:41
  66.0 1.0 copy-start.10
  67.0 282.2 %reduce-scatter.2.cloned.1.call-start = ((), (), s32[]{:S(2)}) async-start(), calls=%async_computation.1 | async-start | bytes 9437184 | tf_op jit(solution)/shard_map/reduce_scatter | solution.py:188
  74.8 47.2 %collective-permute-start.2 = (bf16[2048,512]{1,0:T(8,128)(2,1)S(1)}, bf16[2048,512]{1,0:T(8,128)(2,1)S(1)}, u32[]{:S(2)}, u32[]{:S(2)}) collective-permute-start(bf16[2048,512]{1,0:T(8,128)(2,1)S(1)} %bitcast_dynamic-update-slice_fusion.8), channel_id=1, source_target_pairs={{0,16},{1,17},{2,18},{3,19},{4,20},{5,21},{6,22},{7,23},{8,24},{9,... | collective-permute-start | bytes 6291464 | tf_op jit(solution)/shard_map/ppermute | solution.py:41
  122.0 1.3 copy-start.3
  126.0 7.5 %collective-permute-start.3 = (bf16[2048,1024]{1,0:T(8,128)(2,1)}, bf16[2048,1024]{1,0:T(8,128)(2,1)}, u32[]{:S(2)}, u32[]{:S(2)}) collective-permute-start(bf16[2048,1024]{1,0:T(8,128)(2,1)} %pad_maximum_fusion.2), channel_id=1, source_target_pairs={{0,8},{1,9},{2,10},{3,11},{4,12},{5,13},{6,14},{7,15},{8,0},{9,1},... | collective-permute-start | bytes 12582920 | tf_op jit(solution)/shard_map/ppermute | solution.py:41
  137.2 3.3 copy-start
  162.4 4.8 %copy-start.14 = (bf16[1024,512]{1,0:T(8,128)(2,1)S(1)}, bf16[1024,512]{1,0:T(8,128)(2,1)}, u32[]{:S(2)}) copy-start(bf16[1024,512]{1,0:T(8,128)(2,1)} %get-tuple-element.37) | copy-start | bytes 3145732
  167.2 4.7 %copy-start.5 = (bf16[4,512,1024]{2,1,0:T(8,128)(2,1)S(1)}, bf16[4,512,1024]{2,1,0:T(8,128)(2,1)}, u32[]{:S(2)}) copy-start(bf16[4,512,1024]{2,1,0:T(8,128)(2,1)} %get-tuple-element.62) | copy-start | bytes 12582916
  167.2 4.7 %copy-start.13 = (bf16[1024,512]{1,0:T(8,128)(2,1)S(1)}, bf16[1024,512]{1,0:T(8,128)(2,1)}, u32[]{:S(2)}) copy-start(bf16[1024,512]{1,0:T(8,128)(2,1)} %get-tuple-element.35) | copy-start | bytes 3145732
  167.2 7.3 %slice-start.2 = ((s8[8388608]{0:T(1024)(128)(4,1)}), s8[4194304]{0:T(1024)(128)(4,1)S(1)}, s32[]{:S(2)}) async-start(s8[8388608]{0:T(1024)(128)(4,1)} %bitcast.87), calls=%async_computation.6 | async-start | bytes 8388608
  171.9 2.5 slice-start.3
  175.7 2.2 copy-start.4
  175.8 2.5 copy-start.12
  175.8 10.0 %collective-permute-start.4 = (bf16[512,512]{1,0:T(8,128)(2,1)S(1)}, bf16[512,512]{1,0:T(8,128)(2,1)S(1)}, u32[]{:S(2)}, u32[]{:S(2)}) collective-permute-start(bf16[512,512]{1,0:T(8,128)(2,1)S(1)} %fusion.34), channel_id=1, source_target_pairs={{0,8},{1,9},{2,10},{3,11},{4,12},{5,13},{6,14},{7,15},{8,0},{9,1},... | collective-permute-start | bytes 1572872 | tf_op jit(solution)/shard_map/ppermute | solution.py:41
  178.2 2.4 copy-start.11
  184.4 8.8 %collective-permute-start.8 = (bf16[512,512]{1,0:T(8,128)(2,1)S(1)}, bf16[512,512]{1,0:T(8,128)(2,1)S(1)}, u32[]{:S(2)}, u32[]{:S(2)}) collective-permute-start(bf16[512,512]{1,0:T(8,128)(2,1)S(1)} %fusion.37), channel_id=1, source_target_pairs={{0,8},{1,9},{2,10},{3,11},{4,12},{5,13},{6,14},{7,15},{8,0},{9,1},... | collective-permute-start | bytes 1572872 | tf_op jit(solution)/shard_map/ppermute | solution.py:41
  185.9 14.4 %collective-permute-start.6 = (bf16[512,512]{1,0:T(8,128)(2,1)S(1)}, bf16[512,512]{1,0:T(8,128)(2,1)S(1)}, u32[]{:S(2)}, u32[]{:S(2)}) collective-permute-start(bf16[512,512]{1,0:T(8,128)(2,1)S(1)} %add_convert_fusion.4), channel_id=1, source_target_pairs={{0,16},{1,17},{2,18},{3,19},{4,20},{5,21},{6,22},{7,23},{8,24},{9,... | collective-permute-start | bytes 1572872 | tf_op jit(solution)/shard_map/ppermute | solution.py:41
  191.4 10.5 %copy-start.8 = (f32[512,1024]{1,0:T(8,128)S(1)}, f32[512,1024]{1,0:T(8,128)}, u32[]{:S(2)}) copy-start(f32[512,1024]{1,0:T(8,128)} %param.8) | copy-start | bytes 6291460
  191.4 10.5 %copy-start.9 = (f32[512,1024]{1,0:T(8,128)S(1)}, f32[512,1024]{1,0:T(8,128)}, u32[]{:S(2)}) copy-start(f32[512,1024]{1,0:T(8,128)} %param.9) | copy-start | bytes 6291460
  191.4 13.4 %collective-permute-start.7 = (bf16[512,512]{1,0:T(8,128)(2,1)S(1)}, bf16[512,512]{1,0:T(8,128)(2,1)S(1)}, u32[]{:S(2)}, u32[]{:S(2)}) collective-permute-start(bf16[512,512]{1,0:T(8,128)(2,1)S(1)} %fusion.25), channel_id=1, source_target_pairs={{0,8},{1,9},{2,10},{3,11},{4,12},{5,13},{6,14},{7,15},{8,0},{9,1},... | collective-permute-start | bytes 1572872 | tf_op jit(solution)/shard_map/ppermute | solution.py:41
  191.7 10.1 %collective-permute-start.5 = (bf16[512,512]{1,0:T(8,128)(2,1)S(1)}, bf16[512,512]{1,0:T(8,128)(2,1)S(1)}, u32[]{:S(2)}, u32[]{:S(2)}) collective-permute-start(bf16[512,512]{1,0:T(8,128)(2,1)S(1)} %fusion.22), channel_id=1, source_target_pairs={{0,8},{1,9},{2,10},{3,11},{4,12},{5,13},{6,14},{7,15},{8,0},{9,1},... | collective-permute-start | bytes 1572872 | tf_op jit(solution)/shard_map/ppermute | solution.py:41
  192.0 12.3 %slice-start = ((s8[8388608]{0:T(1024)(128)(4,1)}), s8[4194304]{0:T(1024)(128)(4,1)S(1)}, s32[]{:S(2)}) async-start(s8[8388608]{0:T(1024)(128)(4,1)} %bitcast.76), calls=%async_computation.4 | async-start | bytes 8388608
  193.4 10.9 %slice-start.1 = ((s8[8388608]{0:T(1024)(128)(4,1)}), s8[4194304]{0:T(1024)(128)(4,1)S(1)}, s32[]{:S(2)}) async-start(s8[8388608]{0:T(1024)(128)(4,1)} %bitcast.76), calls=%async_computation.5 | async-start | bytes 8388608
  200.3 14.8 %collective-permute-start.9 = (bf16[512,512]{1,0:T(8,128)(2,1)S(1)}, bf16[512,512]{1,0:T(8,128)(2,1)S(1)}, u32[]{:S(2)}, u32[]{:S(2)}) collective-permute-start(bf16[512,512]{1,0:T(8,128)(2,1)S(1)} %add_convert_fusion.2), channel_id=1, source_target_pairs={{0,16},{1,17},{2,18},{3,19},{4,20},{5,21},{6,22},{7,23},{8,24},{9,... | collective-permute-start | bytes 1572872 | tf_op jit(solution)/shard_map/ppermute | solution.py:41
  203.7 22.6 %collective-permute-start.10 = (bf16[512,512]{1,0:T(8,128)(2,1)S(1)}, bf16[512,512]{1,0:T(8,128)(2,1)S(1)}, u32[]{:S(2)}, u32[]{:S(2)}) collective-permute-start(bf16[512,512]{1,0:T(8,128)(2,1)S(1)} %get-tuple-element.58), channel_id=1, source_target_pairs={{0,16},{1,17},{2,18},{3,19},{4,20},{5,21},{6,22},{7,23},{8,24},{9,... | collective-permute-start | bytes 1572872 | tf_op jit(solution)/shard_map/ppermute | solution.py:41
  217.3 19.0 %collective-permute-start.12 = (bf16[512,512]{1,0:T(8,128)(2,1)S(1)}, bf16[512,512]{1,0:T(8,128)(2,1)S(1)}, u32[]{:S(2)}, u32[]{:S(2)}) collective-permute-start(bf16[512,512]{1,0:T(8,128)(2,1)S(1)} %get-tuple-element.55), channel_id=1, source_target_pairs={{0,16},{1,17},{2,18},{3,19},{4,20},{5,21},{6,22},{7,23},{8,24},{9,... | collective-permute-start | bytes 1572872 | tf_op jit(solution)/shard_map/ppermute | solution.py:41
  226.6 10.5 %collective-permute-start.11 = (bf16[2,512,512]{2,1,0:T(8,128)(2,1)S(1)}, bf16[2,512,512]{2,1,0:T(8,128)(2,1)S(1)}, u32[]{:S(2)}, u32[]{:S(2)}) collective-permute-start(bf16[2,512,512]{2,1,0:T(8,128)(2,1)S(1)} %pad_maximum_fusion.8), channel_id=1, source_target_pairs={{0,8},{1,9},{2,10},{3,11},{4,12},{5,13},{6,14},{7,15},{8,0},{9,1},... | collective-permute-start | bytes 3145736 | tf_op jit(solution)/shard_map/ppermute | solution.py:41
  236.5 2.7 collective-permute-start.13
  240.4 9.5 %copy-start.2 = (bf16[2048,1024]{1,0:T(8,128)(2,1)S(1)}, bf16[2048,1024]{1,0:T(8,128)(2,1)}, u32[]{:S(2)}) copy-start(bf16[2048,1024]{1,0:T(8,128)(2,1)} %copy-done.1) | copy-start | bytes 12582916
  260.8 1.2 copy-start.6
  260.8 1.5 copy-start.7
Sparse Core Ops, SparseCore 0:
  10.0 52.0 all-gather.4
  67.1 89.2 all-gather.6
  261.0 88.1 reduce-scatter.1

commit v10 on v9

--- a/solution.py
+++ b/solution.py
@@ -74,7 +74,7 @@
         return lax.optimization_barrier(values)
 
     def round_path(value):
-        return lax.all_gather(value, "dp", axis_index_groups=[path])
+        return lax.all_gather(value, "dp", axis_index_groups=[path], tiled=True)
 
     width = ff_block // COL_PARTS
     right = right_basis.astype(low)
@@ -91,6 +91,7 @@
     piece, left_blocks = together(piece, left_blocks)
     gathered = round_path(piece)
 
+    left_blocks = left_blocks.reshape(nd, out_rows, rows)
     left_t = jnp.concatenate([left_blocks[path.index(dd)] for dd in range(nd)], axis=0)
     for t in reversed(bits):
         left_t = jnp.concatenate([left_t, move_b(left_t, t)], axis=1)
@@ -104,47 +105,52 @@
     )
     left_rows, gathered = together(left_rows, gathered)
 
-    blocks = []
-    for i in range(nx):
-        mine = gathered[i * nz : (i + 1) * nz]
-        mine = mine if i % 2 == 0 else jnp.flip(mine, 0)
-        blocks.append(mine.reshape(whole, ff_rows))
-    blocks = lax.optimization_barrier(blocks)
-    half = [None] * COL_PARTS
-
-    products = {}
+    def half_rotation(gathered, j):
+        total = None
+        for i in range(nx):
+            mine = gathered[i * whole : (i + 1) * whole]
+            term = matmul(mine, right_parts[j][i])
+            if i % 2:
+                term = lax.optimization_barrier(term).reshape(nz, rows, width)
+                term = jnp.flip(term, 0).reshape(whole, width)
+            total = term if total is None else total + term
+        return lax.optimization_barrier(total.astype(low))
+
+    odd = sorted(range(1, nb, 2), key=lambda t: -t)
+    first_group, second_group = odd[: nb // 4], odd[nb // 4 :]
+    top = bits[-1]
     last = None
-    odd = sorted(range(1, nb, 2), key=lambda t: -t)
-    held = [{} for _ in range(COL_PARTS)]
-    for group in (odd[: nb // 4], odd[nb // 4 :]):
-        for j in range(COL_PARTS):
-            for t in (t for pair in group for t in (pair, pair ^ 1)):
-                if half[j] is None:
-                    found = blocks if last is None else after(blocks, last)
-                    total = sum(matmul(mine, right_parts[j][i]) for i, mine in enumerate(found))
-                    half[j] = lax.optimization_barrier(total.astype(low))
-                value = half[j] if last is None else after(half[j], last)
-                rows_of = lax.dynamic_slice_in_dim(left_rows, (b ^ t) * rows, rows, 0)
-                last = products[t, j] = lax.optimization_barrier(matmul(rows_of, value).astype(low))
-        for j in range(COL_PARTS):
-            for t in group:
-                got = move_b(products[t, j], 1)
-                held[j][t ^ 1] = products[t ^ 1, j].astype(jnp.float32) + got.astype(jnp.float32)
-        last = held[0][group[-1] ^ 1] = lax.optimization_barrier(held[0][group[-1] ^ 1].astype(low))
-    held[0] = {t: value.astype(jnp.float32) for t, value in held[0].items()}
-
-    arrived = []
+
+    def paired(t, j):
+        nonlocal last
+        values = []
+        for u in (t, t ^ 1):
+            value = half[j] if last is None else after(half[j], last)
+            rows_of = lax.dynamic_slice_in_dim(left_rows, (b ^ u) * rows, rows, 0)
+            last = lax.optimization_barrier(matmul(rows_of, value).astype(low))
+            values.append(last)
+        return values[1].astype(jnp.float32) + move_b(values[0], 1).astype(jnp.float32)
+
+    half, arrived = [], []
     for j in range(COL_PARTS):
-        for t in reversed(bits[1:]):
-            for s in [s for s in held[j] if s & t]:
-                away = held[j].pop(s).astype(low)
-                if j:
-                    away = after(away, arrived[j - 1])
-                got = move_b(away, t)
-                held[j][s ^ t] = held[j][s ^ t] + got.astype(jnp.float32)
-        arrived.append(got)
-
-    source = after(left_t, arrived[0])
+        half.append(half_rotation(gathered if last is None else after(gathered, last), j))
+        away = [lax.optimization_barrier(paired(t, j).astype(low)) for t in first_group]
+        last = away[-1]
+        if j:
+            away = [after(value, arrived[j - 1][-1]) for value in away]
+        arrived.append([move_b(value, top) for value in away])
+    last = after(arrived[0][-1], last)
+    sums = []
+    for j in range(COL_PARTS):
+        held = {t ^ 1: paired(t, j) for t in second_group}
+        for t, got in zip(first_group, arrived[j]):
+            held[t ^ 1 ^ top] = held[t ^ 1 ^ top] + got.astype(jnp.float32)
+        for t in reversed(bits[1:-1]):
+            for s in [s for s in held if s & t]:
+                held[s ^ t] = held[s ^ t] + move_b(held.pop(s).astype(low), t).astype(jnp.float32)
+        sums.append(held[0])
+
+    source = after(left_t, arrived[-1][-1])
     left = jnp.concatenate(
         [
             lax.dynamic_slice_in_dim(
@@ -159,7 +165,7 @@
     first_out, second_out, directions = [], [], []
     for j in range(COL_PARTS):
         cols = slice(j * width, (j + 1) * width)
-        rotated = held[j][0]
+        rotated = sums[j]
         moments = first_moment[:, cols], second_moment[:, cols]
         if j:
             moments = after(moments, directions[-1])

time: 356 us -> 375 us (1.053)
  matrix products: 42.7 us -> 68.5 us
  local copies, waits for them, and re-layouts: 35.5 us -> 27.4 us
    dot_general x13, matrix products: 31.8 us -> 57.3 us  [matmul(): lax.dot_general(a, b, (((1,), (0,)), ((), ())), preferred_element_type=jn...]
    slice x1 -> x0, local copies, waits for them, and re-layouts: 5.99 us -> none  [per_device(): mine = gathered[i * nz:(i + 1) * nz]]
    rev x1 -> x2, local copies, waits for them, and re-layouts: 4.78 us -> 9.37 us  [half_rotation(): term = jnp.flip(term, 0).reshape(whole, width)]
    all_gather x1 -> x0, local copies, waits for them, and re-layouts: 3.92 us -> none  [round_path(): return lax.all_gather(value, 'dp', axis_index_groups=[path])]
    unnamed x52 -> x51, local copies, waits for them, and re-layouts: 16.1 us -> 12.8 us
  transfers between devices with their start and end apart: 17 -> 17, of which waited for: 10 -> 10; matrix products, arithmetic and copies ran while one was open for 15% -> 20% of each run, Pallas kernels for 0% -> 0%
where the time goes in v10:
time: 375 us; the launch traced here: 374 us
  waiting for transfers between devices  222 us (59%)
  matrix products  68.5 us (18%)
  other arithmetic  28 us (7%)
  local copies, waits for them, and re-layouts  27.4 us (7%)
  between operations  14.3 us (4%)
  starting transfers between devices  13.9 us (4%)
    ppermute x14, waiting for transfers between devices, permute(): return lax.ppermute(value, ('basis', 'dp'), pairs)  85.2 us
    reduce_scatter x1, waiting for transfers between devices, per_device(): lax.psum_scatter(total, 'dp', scatter_dimension=0, axis_index_groups=[pat...  83.1 us
    dot_general x13, matrix products, matmul(): lax.dot_general(a, b, (((1,), (0,)), ((), ())), preferred_element_type=jn...  57.3 us
    all_gather x2, waiting for transfers between devices, round_path(): return lax.all_gather(value, 'dp', axis_index_groups=[path], tiled=True)  53.8 us
    ppermute x14, starting transfers between devices, permute(): return lax.ppermute(value, ('basis', 'dp'), pairs)  13.8 us
    unnamed x51, local copies, waits for them, and re-layouts  12.8 us
    dot_general x1, matrix products, matmul_nt(): lax.dot_general(a, b, (((1,), (1,)), ((), ())), preferred_element_type=jn...  11.2 us
    rev x2, local copies, waits for them, and re-layouts, half_rotation(): term = jnp.flip(term, 0).reshape(whole, width)  9.37 us
  transfers between devices with their start and end apart: 17, of which 10 were waited for; matrix products, arithmetic and copies ran while one was open for 20% of the time, Pallas kernels for 0%

profile of v10, /device:TPU:0, one launch (start us, length us, event | category | flops | bytes accessed | tf_op | source)
XLA Modules:
  0.0 374.2 jit_solution(13341951996041641124)
XLA Ops:
  7.2 1.8 convert_bitcast_fusion
  9.1 1.9 collective-permute-start
  10.9 4.0 %convert.6 = bf16[2048,1024]{1,0:T(8,128)(2,1)S(1)} convert(f32[2048,1024]{1,0:T(8,128)} %param.7) | non-fusion elementwise | flops 2097152 | bytes 12582912 | tf_op jit(solution)/shard_map/convert.3
  15.0 2.3 fusion.66
  17.3 1.1 copy-done.1
  19.1 43.0 %all-gather.3.cloned.1.call-done = bf16[2048,512]{0,1:T(8,128)(2,1)} async-done(((bf16[256,512]{0,1:T(8,128)(2,1)}), bf16[2048,512]{0,1:T(8,128)(2,1)}) %all-gather.3.cloned.1.call-update) | async-done | bytes 2097168 | tf_op jit(solution)/shard_map/all_gather | solution.py:77
  66.1 1.0 slice_dynamic-update-slice_fusion.2
  67.1 1.0 slice_dynamic-update-slice_fusion.1
  68.1 1.1 slice_dynamic-update-slice_fusion
  69.2 4.5 %collective-permute-start.2 = (bf16[2048,512]{0,1:T(8,128)(2,1)S(1)}, bf16[2048,512]{0,1:T(8,128)(2,1)S(1)}, u32[]{:S(2)}, u32[]{:S(2)}) collective-permute-start(bf16[2048,512]{0,1:T(8,128)(2,1)S(1)} %slice_dynamic-update-slice_fusion), channel_id=1, source_target_pairs={{0,16},{1,17},{2,18},{3,19},{4,20},{5,21},{6,22},{7,23},{8,24},{9,... | collective-permute-start | bytes 6291464 | tf_op jit(solution)/shard_map/ppermute | solution.py:41
  73.7 46.1 %collective-permute-done.2 = bf16[2048,512]{0,1:T(8,128)(2,1)S(1)} collective-permute-done((bf16[2048,512]{0,1:T(8,128)(2,1)S(1)}, bf16[2048,512]{0,1:T(8,128)(2,1)S(1)}, u32[]{:S(2)}, u32[]{:S(2)}) %collective-permute-start.2) | collective-permute-done | bytes 2097184 | tf_op jit(solution)/shard_map/ppermute | solution.py:41
  119.8 1.3 copy-done.3
  121.1 2.5 pad_maximum_fusion.2
  124.3 7.1 %collective-permute-done.3 = bf16[2048,1024]{0,1:T(8,128)(2,1)} collective-permute-done((bf16[2048,1024]{0,1:T(8,128)(2,1)}, bf16[2048,1024]{0,1:T(8,128)(2,1)}, u32[]{:S(2)}, u32[]{:S(2)}) %collective-permute-start.3) | collective-permute-done | bytes 4194336 | tf_op jit(solution)/shard_map/ppermute | solution.py:41
  131.4 3.9 %pad_maximum_fusion = bf16[2048,2048]{0,1:T(8,128)(2,1)S(1)} fusion(bf16[2048,1024]{0,1:T(8,128)(2,1)} %collective-permute-done.3, bf16[2048,512]{0,1:T(8,128)(2,1)} %copy-done.3, bf16[2048,512]{0,1:T(8,128)(2,1)S(1)} %slice_dynamic-update-slice_fusion), kind=kLoop, calls=%fused_computation | loop fusion | flops 25165824 | bytes 16777216 | tf_op jit(solution)/shard_map/concatenate | solution.py:97
  135.3 1.5 constant_dynamic-slice_fusion.3
  136.8 2.5 copy-done
  139.3 4.2 %pad_maximum_fusion.1 = bf16[2048,2048]{0,1:T(8,128)(2,1)} fusion(bf16[2048,512]{0,1:T(8,128)(2,1)S(1)} %get-tuple-element.54, bf16[2048,512]{0,1:T(8,128)(2,1)S(1)} %get-tuple-element.55, bf16[2048,512]{0,1:T(8,128)(2,1)S(1)} %get-tuple-element.56, bf16[2048,512]{0,1:T(8,128)(2,1)S(1)} %get-tuple-element.53), kind=kLoop, calls=%fused_computation.1 | loop fusion | flops 33554432 | bytes 16777216 | tf_op jit(solution)/shard_map/concatenate | solution.py:99
  143.4 10.8 %all-gather.5.cloned.1.call-done = bf16[4096,1024]{1,0:T(8,128)(2,1)} async-done(((bf16[512,1024]{1,0:T(8,128)(2,1)}), bf16[4096,1024]{1,0:T(8,128)(2,1)}) %all-gather.5.cloned.1.call-update) | async-done | bytes 8388624 | tf_op jit(solution)/shard_map/all_gather | solution.py:77
  154.2 6.6 %fusion.6 = f32[2048,512]{1,0:T(8,128)} fusion(bf16[1024,512]{1,0:T(8,128)(2,1)S(1)} %copy-done.13, bf16[4096,1024]{1,0:T(8,128)(2,1)} %all-gather.5.cloned.1.call-done), kind=kOutput, calls=%fused_computation.13 | convolution fusion | flops 2147483648 | bytes 9437184 | tf_op jit(solution)/shard_map/dot_general | solution.py:21
  160.8 4.7 %rev.7 = f32[4,512,512]{2,1,0:T(8,128)} reverse(f32[4,512,512]{2,1,0:T(8,128)} %bitcast.66), dimensions={0} | reverse | bytes 8388608 | tf_op jit(solution)/shard_map/jit(_flip)/rev | solution.py:115
  165.5 5.8 %fusion.1 = bf16[2048,512]{1,0:T(8,128)(2,1)S(1)} fusion(f32[4,512,512]{2,1,0:T(8,128)} %rev.7, bf16[1024,512]{1,0:T(8,128)(2,1)S(1)} %copy-done.12, bf16[4096,1024]{1,0:T(8,128)(2,1)} %all-gather.5.cloned.1.call-done), kind=kOutput, calls=%fused_computation.8 | convolution fusion | flops 2149580800 | bytes 11534336 | tf_op jit(solution)/shard_map/dot_general | solution.py:21
  171.3 3.0 fusion.48
  174.4 3.7 fusion.36
  178.6 3.1 fusion.42
  181.7 3.8 %fusion.30 = bf16[512,512]{1,0:T(8,128)(2,1)} fusion(bf16[2048,512]{1,0:T(8,128)(2,1)S(1)} %fusion.1, bf16[2048,2048]{0,1:T(8,128)(2,1)} %pad_maximum_fusion.1, s32[]{:T(128)S(6)} %select_n.96), kind=kOutput, calls=%fused_computation.42 | convolution fusion | flops 1074003968 | bytes 4718596 | tf_op jit(solution)/shard_map/dot_general | solution.py:21
  186.4 4.5 %fusion.2 = f32[2048,512]{1,0:T(8,128)} fusion(bf16[1024,512]{1,0:T(8,128)(2,1)S(1)} %copy-done.11, bf16[4096,1024]{1,0:T(8,128)(2,1)S(1)} %bitcast.69), kind=kOutput, calls=%fused_computation.9 | convolution fusion | flops 2147483648 | bytes 9437184 | tf_op jit(solution)/shard_map/dot_general | solution.py:21
  190.9 4.7 %rev.8 = f32[4,512,512]{2,1,0:T(8,128)} reverse(f32[4,512,512]{2,1,0:T(8,128)} %bitcast.67), dimensions={0} | reverse | bytes 8388608 | tf_op jit(solution)/shard_map/jit(_flip)/rev | solution.py:115
  195.6 6.1 %fusion = bf16[2048,512]{1,0:T(8,128)(2,1)S(1)} fusion(f32[4,512,512]{2,1,0:T(8,128)} %rev.8, bf16[1024,512]{1,0:T(8,128)(2,1)S(1)} %copy-done.10, bf16[4096,1024]{1,0:T(8,128)(2,1)} %all-gather.5.cloned.1.call-done), kind=kOutput, calls=%fused_computation.6 | convolution fusion | flops 2149580800 | bytes 11534336 | tf_op jit(solution)/shard_map/dot_general | solution.py:21
  201.7 2.9 fusion.51
  204.7 1.5 collective-permute-start.6
  206.2 2.9 fusion.39
  209.3 3.0 fusion.45
  212.5 6.5 %collective-permute-done.6 = bf16[512,512]{1,0:T(8,128)(2,1)S(1)} collective-permute-done((bf16[512,512]{1,0:T(8,128)(2,1)S(1)}, bf16[512,512]{1,0:T(8,128)(2,1)S(1)}, u32[]{:S(2)}, u32[]{:S(2)}) %collective-permute-start.6) | collective-permute-done | bytes 524320 | tf_op jit(solution)/shard_map/ppermute | solution.py:41
  219.0 1.5 collective-permute-start.9
  220.5 2.9 divide_convert_fusion.1
  224.0 3.0 fusion.33
  227.0 6.9 %collective-permute-done.9 = bf16[512,512]{1,0:T(8,128)(2,1)S(1)} collective-permute-done((bf16[512,512]{1,0:T(8,128)(2,1)S(1)}, bf16[512,512]{1,0:T(8,128)(2,1)S(1)}, u32[]{:S(2)}, u32[]{:S(2)}) %collective-permute-start.9) | collective-permute-done | bytes 524320 | tf_op jit(solution)/shard_map/ppermute | solution.py:41
  233.8 2.2 divide_convert_fusion
  236.0 1.5 collective-permute-start.12
  237.5 7.6 %collective-permute-done.10 = bf16[512,512]{1,0:T(8,128)(2,1)S(1)} collective-permute-done((bf16[512,512]{1,0:T(8,128)(2,1)S(1)}, bf16[512,512]{1,0:T(8,128)(2,1)S(1)}, u32[]{:S(2)}, u32[]{:S(2)}) %collective-permute-start.10) | collective-permute-done | bytes 524320 | tf_op jit(solution)/shard_map/ppermute | solution.py:41
  245.8 9.2 %collective-permute-done.12 = bf16[512,512]{1,0:T(8,128)(2,1)S(1)} collective-permute-done((bf16[512,512]{1,0:T(8,128)(2,1)S(1)}, bf16[512,512]{1,0:T(8,128)(2,1)S(1)}, u32[]{:S(2)}, u32[]{:S(2)}) %collective-permute-start.12) | collective-permute-done | bytes 524320 | tf_op jit(solution)/shard_map/ppermute | solution.py:41
  256.0 1.9 collective-permute-done.13
  259.0 9.0 %convolution_convert_fusion.1 = bf16[2048,1024]{1,0:T(8,128)(2,1)S(1)} fusion(bf16[2048,2048]{1,0:T(8,128)(2,1)S(1)} %bitcast_dynamic-update-slice_fusion, bf16[2048,1024]{1,0:T(8,128)(2,1)S(1)} %pad_maximum_fusion.3), kind=kOutput, calls=%fused_computation.17 | convolution fusion | flops 8592031744 | bytes 16777216 | tf_op jit(solution)/shard_map/dot_general | solution.py:21
  268.0 11.2 %convolution_convert_fusion = bf16[2048,2048]{1,0:T(8,128)(2,1)} fusion(bf16[2048,1024]{1,0:T(8,128)(2,1)S(1)} %convolution_convert_fusion.1, bf16[2048,1024]{1,0:T(8,128)(2,1)S(1)} %copy-done.2), kind=kOutput, calls=%fused_computation.2 | convolution fusion | flops 8594128896 | bytes 16777216 | tf_op jit(solution)/shard_map/dot_general | solution.py:25
  279.3 1.2 copy-done.4
  280.8 3.7 pad_maximum_fusion.4
  284.5 83.1 %reduce-scatter.2.cloned.1.call-done = bf16[256,2048]{1,0:T(8,128)(2,1)} async-done(((bf16[2048,2048]{1,0:T(8,128)(2,1)}), bf16[256,2048]{1,0:T(8,128)(2,1)}) %reduce-scatter.2.cloned.1.call-update) | async-done | bytes 1048592 | tf_op jit(solution)/shard_map/reduce_scatter | solution.py:194
  (83 shorter events, 11.0 us)
Async XLA Ops:
  7.2 54.9 %all-gather.3.cloned.1.call-start = ((), (), s32[]{:S(2)}) async-start(), calls=%async_computation.1 | async-start | bytes 2359296 | tf_op jit(solution)/shard_map/all_gather | solution.py:77
  9.0 145.2 %all-gather.5.cloned.1.call-start = ((), (), s32[]{:S(2)}) async-start(), calls=%async_computation.2 | async-start | bytes 9437184 | tf_op jit(solution)/shard_map/all_gather | solution.py:77
  9.1 9.3 %collective-permute-start = (bf16[512,1024]{1,0:T(8,128)(2,1)}, bf16[512,1024]{1,0:T(8,128)(2,1)S(1)}, u32[]{:S(2)}, u32[]{:S(2)}) collective-permute-start(bf16[512,1024]{1,0:T(8,128)(2,1)} %param.5), channel_id=1, source_target_pairs={{0,0},{1,1},{2,2},{3,3},{4,4},{5,5},{6,6},{7,7},{8,14},{9,15},{10,... | collective-permute-start | bytes 3145736 | tf_op jit(solution)/shard_map/ppermute | solution.py:41
  15.0 3.3 copy-start.1
  18.3 0.7 collective-permute-start.1
  19.1 43.0 %copy-start.9 = (bf16[512,1024]{1,0:T(8,128)(2,1)}, bf16[512,1024]{1,0:T(8,128)(2,1)S(1)}, u32[]{:S(2)}) copy-start(bf16[512,1024]{1,0:T(8,128)(2,1)S(1)} %collective-permute-done.1) | copy-start | bytes 3145732
  62.1 305.6 %reduce-scatter.2.cloned.1.call-start = ((), (), s32[]{:S(2)}) async-start(), calls=%async_computation.3 | async-start | bytes 9437184 | tf_op jit(solution)/shard_map/reduce_scatter | solution.py:194
  69.2 50.6 %collective-permute-start.2 = (bf16[2048,512]{0,1:T(8,128)(2,1)S(1)}, bf16[2048,512]{0,1:T(8,128)(2,1)S(1)}, u32[]{:S(2)}, u32[]{:S(2)}) collective-permute-start(bf16[2048,512]{0,1:T(8,128)(2,1)S(1)} %slice_dynamic-update-slice_fusion), channel_id=1, source_target_pairs={{0,16},{1,17},{2,18},{3,19},{4,20},{5,21},{6,22},{7,23},{8,24},{9,... | collective-permute-start | bytes 6291464 | tf_op jit(solution)/shard_map/ppermute | solution.py:41
  119.8 1.3 copy-start.3
  123.6 7.7 %collective-permute-start.3 = (bf16[2048,1024]{0,1:T(8,128)(2,1)}, bf16[2048,1024]{0,1:T(8,128)(2,1)}, u32[]{:S(2)}, u32[]{:S(2)}) collective-permute-start(bf16[2048,1024]{0,1:T(8,128)(2,1)} %pad_maximum_fusion.2), channel_id=1, source_target_pairs={{0,8},{1,9},{2,10},{3,11},{4,12},{5,13},{6,14},{7,15},{8,0},{9,1},... | collective-permute-start | bytes 12582920 | tf_op jit(solution)/shard_map/ppermute | solution.py:41
  135.3 3.9 %copy-start = (bf16[2048,2048]{0,1:T(8,128)(2,1)}, bf16[2048,2048]{0,1:T(8,128)(2,1)S(1)}, u32[]{:S(2)}) copy-start(bf16[2048,2048]{0,1:T(8,128)(2,1)S(1)} %pad_maximum_fusion) | copy-start | bytes 25165828
  139.3 14.9 %copy-start.13 = (bf16[1024,512]{1,0:T(8,128)(2,1)S(1)}, bf16[1024,512]{1,0:T(8,128)(2,1)}, u32[]{:S(2)}) copy-start(bf16[1024,512]{1,0:T(8,128)(2,1)} %get-tuple-element.31) | copy-start | bytes 3145732
  160.8 4.7 %copy-start.12 = (bf16[1024,512]{1,0:T(8,128)(2,1)S(1)}, bf16[1024,512]{1,0:T(8,128)(2,1)}, u32[]{:S(2)}) copy-start(bf16[1024,512]{1,0:T(8,128)(2,1)} %get-tuple-element.30) | copy-start | bytes 3145732
  171.3 15.1 %slice-start.2 = ((s8[8388608]{0:T(1024)(128)(4,1)}), s8[4194304]{0:T(1024)(128)(4,1)S(1)}, s32[]{:S(2)}) async-start(s8[8388608]{0:T(1024)(128)(4,1)} %bitcast.68), calls=%async_computation.6 | async-start | bytes 8388608
  174.4 11.1 %collective-permute-start.5 = (bf16[512,512]{1,0:T(8,128)(2,1)S(1)}, bf16[512,512]{1,0:T(8,128)(2,1)S(1)}, u32[]{:S(2)}, u32[]{:S(2)}) collective-permute-start(bf16[512,512]{1,0:T(8,128)(2,1)S(1)} %fusion.48), channel_id=1, source_target_pairs={{0,8},{1,9},{2,10},{3,11},{4,12},{5,13},{6,14},{7,15},{8,0},{9,1},... | collective-permute-start | bytes 1572872 | tf_op jit(solution)/shard_map/ppermute | solution.py:41
  178.1 8.3 %slice-start.3 = ((s8[8388608]{0:T(1024)(128)(4,1)}), s8[4194304]{0:T(1024)(128)(4,1)S(1)}, s32[]{:S(2)}) async-start(s8[8388608]{0:T(1024)(128)(4,1)} %bitcast.68), calls=%async_computation.7 | async-start | bytes 8388608
  178.1 42.4 %collective-permute-start.4 = (bf16[512,512]{1,0:T(8,128)(2,1)}, bf16[512,512]{1,0:T(8,128)(2,1)}, u32[]{:S(2)}, u32[]{:S(2)}) collective-permute-start(bf16[512,512]{1,0:T(8,128)(2,1)} %fusion.36), channel_id=1, source_target_pairs={{0,8},{1,9},{2,10},{3,11},{4,12},{5,13},{6,14},{7,15},{8,0},{9,1},... | collective-permute-start | bytes 1572872 | tf_op jit(solution)/shard_map/ppermute | solution.py:41
  181.7 4.7 %copy-start.11 = (bf16[1024,512]{1,0:T(8,128)(2,1)S(1)}, bf16[1024,512]{1,0:T(8,128)(2,1)}, u32[]{:S(2)}) copy-start(bf16[1024,512]{1,0:T(8,128)(2,1)} %get-tuple-element.37) | copy-start | bytes 3145732
  190.9 4.7 %copy-start.10 = (bf16[1024,512]{1,0:T(8,128)(2,1)S(1)}, bf16[1024,512]{1,0:T(8,128)(2,1)}, u32[]{:S(2)}) copy-start(bf16[1024,512]{1,0:T(8,128)(2,1)} %get-tuple-element.36) | copy-start | bytes 3145732
  201.6 3.0 copy-start.14
  204.6 7.8 %collective-permute-start.8 = (bf16[512,512]{1,0:T(8,128)(2,1)S(1)}, bf16[512,512]{1,0:T(8,128)(2,1)S(1)}, u32[]{:S(2)}, u32[]{:S(2)}) collective-permute-start(bf16[512,512]{1,0:T(8,128)(2,1)S(1)} %fusion.51), channel_id=1, source_target_pairs={{0,8},{1,9},{2,10},{3,11},{4,12},{5,13},{6,14},{7,15},{8,0},{9,1},... | collective-permute-start | bytes 1572872 | tf_op jit(solution)/shard_map/ppermute | solution.py:41
  204.7 14.3 %collective-permute-start.6 = (bf16[512,512]{1,0:T(8,128)(2,1)S(1)}, bf16[512,512]{1,0:T(8,128)(2,1)S(1)}, u32[]{:S(2)}, u32[]{:S(2)}) collective-permute-start(bf16[512,512]{1,0:T(8,128)(2,1)S(1)} %copy-done.14), channel_id=1, source_target_pairs={{0,16},{1,17},{2,18},{3,19},{4,20},{5,21},{6,22},{7,23},{8,24},{9,... | collective-permute-start | bytes 1572872 | tf_op jit(solution)/shard_map/ppermute | solution.py:41
  209.1 11.4 %copy-start.6 = (f32[512,1024]{1,0:T(8,128)S(1)}, f32[512,1024]{1,0:T(8,128)}, u32[]{:S(2)}) copy-start(f32[512,1024]{1,0:T(8,128)} %param.8) | copy-start | bytes 6291460
  209.1 11.4 %copy-start.7 = (f32[512,1024]{1,0:T(8,128)S(1)}, f32[512,1024]{1,0:T(8,128)}, u32[]{:S(2)}) copy-start(f32[512,1024]{1,0:T(8,128)} %param.9) | copy-start | bytes 6291460
  209.1 11.4 %copy-start.8 = (bf16[512,512]{1,0:T(8,128)(2,1)S(1)}, bf16[512,512]{1,0:T(8,128)(2,1)}, u32[]{:S(2)}) copy-start(bf16[512,512]{1,0:T(8,128)(2,1)} %fusion.30) | copy-start | bytes 1572868
  209.1 24.7 %collective-permute-start.7 = (bf16[512,512]{1,0:T(8,128)(2,1)S(1)}, bf16[512,512]{1,0:T(8,128)(2,1)S(1)}, u32[]{:S(2)}, u32[]{:S(2)}) collective-permute-start(bf16[512,512]{1,0:T(8,128)(2,1)S(1)} %fusion.39), channel_id=1, source_target_pairs={{0,8},{1,9},{2,10},{3,11},{4,12},{5,13},{6,14},{7,15},{8,0},{9,1},... | collective-permute-start | bytes 1572872 | tf_op jit(solution)/shard_map/ppermute | solution.py:41
  219.0 14.8 %collective-permute-start.9 = (bf16[512,512]{1,0:T(8,128)(2,1)S(1)}, bf16[512,512]{1,0:T(8,128)(2,1)S(1)}, u32[]{:S(2)}, u32[]{:S(2)}) collective-permute-start(bf16[512,512]{1,0:T(8,128)(2,1)S(1)} %add_convert_fusion), channel_id=1, source_target_pairs={{0,16},{1,17},{2,18},{3,19},{4,20},{5,21},{6,22},{7,23},{8,24},{9,... | collective-permute-start | bytes 1572872 | tf_op jit(solution)/shard_map/ppermute | solution.py:41
  223.4 21.7 %collective-permute-start.10 = (bf16[512,512]{1,0:T(8,128)(2,1)S(1)}, bf16[512,512]{1,0:T(8,128)(2,1)S(1)}, u32[]{:S(2)}, u32[]{:S(2)}) collective-permute-start(bf16[512,512]{1,0:T(8,128)(2,1)S(1)} %get-tuple-element.50), channel_id=1, source_target_pairs={{0,16},{1,17},{2,18},{3,19},{4,20},{5,21},{6,22},{7,23},{8,24},{9,... | collective-permute-start | bytes 1572872 | tf_op jit(solution)/shard_map/ppermute | solution.py:41
  224.0 21.4 %slice-start = ((s8[8388608]{0:T(1024)(128)(4,1)}), s8[4194304]{0:T(1024)(128)(4,1)S(1)}, s32[]{:S(2)}) async-start(s8[8388608]{0:T(1024)(128)(4,1)} %bitcast.62), calls=%async_computation.4 | async-start | bytes 8388608
  227.0 18.4 %slice-start.1 = ((s8[8388608]{0:T(1024)(128)(4,1)}), s8[4194304]{0:T(1024)(128)(4,1)S(1)}, s32[]{:S(2)}) async-start(s8[8388608]{0:T(1024)(128)(4,1)} %bitcast.62), calls=%async_computation.5 | async-start | bytes 8388608
  236.0 18.9 %collective-permute-start.12 = (bf16[512,512]{1,0:T(8,128)(2,1)S(1)}, bf16[512,512]{1,0:T(8,128)(2,1)S(1)}, u32[]{:S(2)}, u32[]{:S(2)}) collective-permute-start(bf16[512,512]{1,0:T(8,128)(2,1)S(1)} %get-tuple-element.47), channel_id=1, source_target_pairs={{0,16},{1,17},{2,18},{3,19},{4,20},{5,21},{6,22},{7,23},{8,24},{9,... | collective-permute-start | bytes 1572872 | tf_op jit(solution)/shard_map/ppermute | solution.py:41
  245.3 10.2 %collective-permute-start.11 = (bf16[2,512,512]{2,1,0:T(8,128)(2,1)S(1)}, bf16[2,512,512]{2,1,0:T(8,128)(2,1)S(1)}, u32[]{:S(2)}, u32[]{:S(2)}) collective-permute-start(bf16[2,512,512]{2,1,0:T(8,128)(2,1)S(1)} %pad_maximum_fusion.8), channel_id=1, source_target_pairs={{0,8},{1,9},{2,10},{3,11},{4,12},{5,13},{6,14},{7,15},{8,0},{9,1},... | collective-permute-start | bytes 3145736 | tf_op jit(solution)/shard_map/ppermute | solution.py:41
  255.1 2.7 collective-permute-start.13
  259.0 9.0 %copy-start.2 = (bf16[2048,1024]{1,0:T(8,128)(2,1)S(1)}, bf16[2048,1024]{1,0:T(8,128)(2,1)}, u32[]{:S(2)}) copy-start(bf16[2048,1024]{1,0:T(8,128)(2,1)} %copy-done.1) | copy-start | bytes 12582916
  279.3 1.2 copy-start.4
  279.3 1.5 copy-start.5
Sparse Core Ops, SparseCore 0:
  10.0 52.0 all-gather.2
  63.6 90.5 all-gather.4
  279.4 88.1 reduce-scatter.1

commit v11 on v10

--- a/solution.py
+++ b/solution.py
@@ -3,6 +3,8 @@
 import jax
 import jax.numpy as jnp
 from jax import lax
+from jax.experimental import pallas as pl
+from jax.experimental.pallas import tpu as pltpu
 from jax.sharding import PartitionSpec as P
 
 STEP = 4
@@ -14,6 +16,8 @@
 
 COL_PARTS = 2
 
+VMEM_BYTES = 52 * 1024 * 1024
+
 low = jnp.bfloat16
 
 
@@ -23,6 +27,41 @@
 
 def matmul_nt(a, b):
     return lax.dot_general(a, b, (((1,), (1,)), ((), ())), preferred_element_type=jnp.float32)
+
+
+def half_rotation(gathered, right, places, nz):
+    count, rows, cols = gathered.shape
+    nx = count // nz
+    width = right.shape[1]
+
+    def kernel(places_ref, *refs):
+        blocks, right_ref, out = refs[:nx], refs[nx], refs[nx + 1]
+        total = matmul(blocks[0][...], right_ref[:cols])
+        for i in range(1, nx):
+            total += matmul(blocks[i][...], right_ref[i * cols : (i + 1) * cols])
+        out[...] = total.astype(out.dtype)
+
+    def block_of(i):
+        if i % 2 == 0:
+            return pl.BlockSpec((None, rows, cols), lambda k, p: (i * nz + k, 0, 0))
+        return pl.BlockSpec((None, rows, cols), lambda k, p: (i * nz + nz - 1 - k, 0, 0))
+
+    out = jax.ShapeDtypeStruct((nz * rows, width), low)
+    size = sum(a.size * a.dtype.itemsize for a in (gathered, right, out))
+    return pl.pallas_call(
+        kernel,
+        out_shape=out,
+        grid_spec=pltpu.PrefetchScalarGridSpec(
+            num_scalar_prefetch=1,
+            grid=(nz,),
+            in_specs=[block_of(i) for i in range(nx)]
+            + [pl.BlockSpec(right.shape, lambda k, p: (0, 0), pipeline_mode=pl.Buffered(1))],
+            out_specs=pl.BlockSpec((rows, width), lambda k, p: (p[k], 0)),
+        ),
+        compiler_params=pltpu.CompilerParams(vmem_limit_bytes=VMEM_BYTES),
+        cost_estimate=pl.CostEstimate(flops=2 * gathered.size * width, bytes_accessed=size, transcendentals=0),
+        name="half_rotation",
+    )(places, *([gathered] * nx), right)
 
 
 def per_device(gradient, left_basis, right_basis, first_moment, second_moment, *, nb, nd):
@@ -78,15 +117,12 @@
 
     width = ff_block // COL_PARTS
     right = right_basis.astype(low)
-    ff_rows = right.shape[0] // nx
-    right_parts = [
-        [right_basis[i * ff_rows : (i + 1) * ff_rows, j * width : (j + 1) * width].astype(low) for i in range(nx)]
-        for j in range(COL_PARTS)
-    ]
+    right_parts = [right_basis[:, j * width : (j + 1) * width].astype(low) for j in range(COL_PARTS)]
+    places = jnp.stack([reversed_bits(unspread(b ^ zz) ^ b) for zz in range(nz)]).astype(jnp.int32)
 
     left_blocks = round_path(left_basis.astype(low).T)
     piece = permute(gradient, lambda bb, zz, xx: (bb, zz ^ spread(bb), xx))
-    piece, right_parts = together(piece, right_parts)
+    piece, right_parts, places = together(piece, right_parts, places)
     piece = permute(piece, lambda bb, zz, xx: (zz ^ spread(bb), zz, xx))
     piece, left_blocks = together(piece, left_blocks)
     gathered = round_path(piece)
@@ -95,26 +131,7 @@
     left_t = jnp.concatenate([left_blocks[path.index(dd)] for dd in range(nd)], axis=0)
     for t in reversed(bits):
         left_t = jnp.concatenate([left_t, move_b(left_t, t)], axis=1)
-    left_t = lax.optimization_barrier(left_t)
-    left_rows = jnp.concatenate(
-        [
-            lax.dynamic_slice_in_dim(left_t, reversed_bits(unspread(b ^ zz) ^ b) * rows, rows, 1)
-            for zz in range(nz)
-        ],
-        axis=1,
-    )
-    left_rows, gathered = together(left_rows, gathered)
-
-    def half_rotation(gathered, j):
-        total = None
-        for i in range(nx):
-            mine = gathered[i * whole : (i + 1) * whole]
-            term = matmul(mine, right_parts[j][i])
-            if i % 2:
-                term = lax.optimization_barrier(term).reshape(nz, rows, width)
-                term = jnp.flip(term, 0).reshape(whole, width)
-            total = term if total is None else total + term
-        return lax.optimization_barrier(total.astype(low))
+    left_t, gathered = together(left_t, gathered.reshape(nd, rows, ff_block))
 
     odd = sorted(range(1, nb, 2), key=lambda t: -t)
     first_group, second_group = odd[: nb // 4], odd[nb // 4 :]
@@ -126,20 +143,21 @@
         values = []
         for u in (t, t ^ 1):
             value = half[j] if last is None else after(half[j], last)
-            rows_of = lax.dynamic_slice_in_dim(left_rows, (b ^ u) * rows, rows, 0)
+            rows_of = lax.dynamic_slice_in_dim(left_t, (b ^ u) * rows, rows, 0)
             last = lax.optimization_barrier(matmul(rows_of, value).astype(low))
             values.append(last)
         return values[1].astype(jnp.float32) + move_b(values[0], 1).astype(jnp.float32)
 
     half, arrived = [], []
     for j in range(COL_PARTS):
-        half.append(half_rotation(gathered if last is None else after(gathered, last), j))
+        found = gathered if last is None else after(gathered, last)
+        half.append(half_rotation(found, right_parts[j], places, nz))
         away = [lax.optimization_barrier(paired(t, j).astype(low)) for t in first_group]
         last = away[-1]
         if j:
             away = [after(value, arrived[j - 1][-1]) for value in away]
         arrived.append([move_b(value, top) for value in away])
-    last = after(arrived[0][-1], last)
+    last = arrived[0][-1]
     sums = []
     for j in range(COL_PARTS):
         held = {t ^ 1: paired(t, j) for t in second_group}
@@ -150,7 +168,7 @@
                 held[s ^ t] = held[s ^ t] + move_b(held.pop(s).astype(low), t).astype(jnp.float32)
         sums.append(held[0])
 
-    source = after(left_t, arrived[-1][-1])
+    source = after(left_t, arrived[0][-1])
     left = jnp.concatenate(
         [
             lax.dynamic_slice_in_dim(

time: 375 us -> 351 us (0.936)
  matrix products: 68.5 us -> 36.1 us
  Pallas kernels: 0 us -> 18.6 us
  local copies, waits for them, and re-layouts: 27.4 us -> 20 us
    dot_general x13 -> x9, matrix products: 57.3 us -> 25.1 us  [matmul(): lax.dot_general(a, b, (((1,), (0,)), ((), ())), preferred_element_type=jn...]
    pallas_call x0 -> x2, Pallas kernels: none -> 18.6 us  [half_rotation(): pl.pallas_call(kernel, out_shape=out, grid_spec=pltpu.PrefetchScalarGridS...]
    rev x2 -> x0, local copies, waits for them, and re-layouts: 9.37 us -> none  [half_rotation(): term = jnp.flip(term, 0).reshape(whole, width)]
    ppermute x14, waiting for transfers between devices: 85.2 us -> 79.7 us  [permute(): return lax.ppermute(value, ('basis', 'dp'), pairs)]
    all_gather x2, waiting for transfers between devices: 53.8 us -> 58.2 us  [round_path(): return lax.all_gather(value, 'dp', axis_index_groups=[path], tiled=True)]
    concatenate x1 -> x0, other arithmetic: 4.16 us -> none  [per_device(): jnp.concatenate([lax.dynamic_slice_in_dim(left_t, reversed_bits(unspread(...]
    unnamed x51 -> x37, local copies, waits for them, and re-layouts: 12.8 us -> 13.9 us
  transfers between devices with their start and end apart: 17 -> 17, of which waited for: 10 -> 8; matrix products, arithmetic and copies ran while one was open for 20% -> 14% of each run, Pallas kernels for 0% -> 3%
where the time goes in v11:
time: 351 us; the launch traced here: 350 us
  waiting for transfers between devices  222 us (63%)
  matrix products  36.1 us (10%)
  other arithmetic  25.6 us (7%)
  local copies, waits for them, and re-layouts  20 us (6%)
  Pallas kernels  18.6 us (5%)
  between operations  14.3 us (4%)
  starting transfers between devices  13.3 us (4%)
    reduce_scatter x1, waiting for transfers between devices, per_device(): lax.psum_scatter(total, 'dp', scatter_dimension=0, axis_index_groups=[pat...  84.3 us
    ppermute x14, waiting for transfers between devices, permute(): return lax.ppermute(value, ('basis', 'dp'), pairs)  79.7 us
    all_gather x2, waiting for transfers between devices, round_path(): return lax.all_gather(value, 'dp', axis_index_groups=[path], tiled=True)  58.2 us
    dot_general x9, matrix products, matmul(): lax.dot_general(a, b, (((1,), (0,)), ((), ())), preferred_element_type=jn...  25.1 us
    pallas_call x2, Pallas kernels, half_rotation(): pl.pallas_call(kernel, out_shape=out, grid_spec=pltpu.PrefetchScalarGridS...  18.6 us
    unnamed x37, local copies, waits for them, and re-layouts  13.9 us
    ppermute x14, starting transfers between devices, permute(): return lax.ppermute(value, ('basis', 'dp'), pairs)  13.1 us
    dot_general x1, matrix products, matmul_nt(): lax.dot_general(a, b, (((1,), (1,)), ((), ())), preferred_element_type=jn...  11 us
  transfers between devices with their start and end apart: 17, of which 8 were waited for; matrix products, arithmetic and copies ran while one was open for 14% of the time, Pallas kernels for 3%

profile of v11, /device:TPU:0, one launch (start us, length us, event | category | flops | bytes accessed | tf_op | source)
XLA Modules:
  0.0 350.0 jit_solution(1299969002637390675)
XLA Ops:
  7.2 1.8 convert_bitcast_fusion
  9.1 1.9 collective-permute-start
  10.9 6.0 %convert.4 = bf16[2048,1024]{1,0:T(8,128)(2,1)} convert(f32[2048,1024]{1,0:T(8,128)} %param.7) | non-fusion elementwise | flops 2097152 | bytes 12582912 | tf_op jit(solution)/shard_map/convert.1
  17.0 4.6 %fusion.52 = (bf16[2048,512]{1,0:T(8,128)(2,1)}, bf16[2048,512]{1,0:T(8,128)(2,1)}) fusion(bf16[2048,1024]{1,0:T(8,128)(2,1)} %convert.4), kind=kLoop, calls=%fused_computation.80 | loop fusion | bytes 8388608 | tf_op jit(solution)/shard_map/slice | solution.py:120
  21.6 0.7 collective-permute-start.1
  22.4 39.4 %all-gather.3.cloned.1.call-done = bf16[2048,512]{0,1:T(8,128)(2,1)} async-done(((bf16[256,512]{0,1:T(8,128)(2,1)}), bf16[2048,512]{0,1:T(8,128)(2,1)}) %all-gather.3.cloned.1.call-update) | async-done | bytes 2097168 | tf_op jit(solution)/shard_map/all_gather | solution.py:116
  61.9 1.0 slice_dynamic-update-slice_fusion.6
  62.8 1.0 slice_dynamic-update-slice_fusion.5
  63.8 1.0 slice_dynamic-update-slice_fusion.4
  64.8 1.0 slice_dynamic-update-slice_fusion.3
  65.8 1.0 slice_dynamic-update-slice_fusion.2
  66.8 1.0 slice_dynamic-update-slice_fusion.1
  67.8 1.1 slice_dynamic-update-slice_fusion
  68.9 3.9 %collective-permute-start.2 = (bf16[2048,512]{0,1:T(8,128)(2,1)S(1)}, bf16[2048,512]{0,1:T(8,128)(2,1)S(1)}, u32[]{:S(2)}, u32[]{:S(2)}) collective-permute-start(bf16[2048,512]{0,1:T(8,128)(2,1)S(1)} %slice_dynamic-update-slice_fusion), channel_id=1, source_target_pairs={{0,16},{1,17},{2,18},{3,19},{4,20},{5,21},{6,22},{7,23},{8,24},{9,... | collective-permute-start | bytes 6291464 | tf_op jit(solution)/shard_map/ppermute | solution.py:80
  72.8 45.7 %collective-permute-done.2 = bf16[2048,512]{0,1:T(8,128)(2,1)S(1)} collective-permute-done((bf16[2048,512]{0,1:T(8,128)(2,1)S(1)}, bf16[2048,512]{0,1:T(8,128)(2,1)S(1)}, u32[]{:S(2)}, u32[]{:S(2)}) %collective-permute-start.2) | collective-permute-done | bytes 2097184 | tf_op jit(solution)/shard_map/ppermute | solution.py:80
  118.5 2.7 pad_maximum_fusion.1
  121.2 1.0 collective-permute-start.3
  122.2 7.1 %collective-permute-done.3 = bf16[2048,1024]{0,1:T(8,128)(2,1)} collective-permute-done((bf16[2048,1024]{0,1:T(8,128)(2,1)}, bf16[2048,1024]{0,1:T(8,128)(2,1)}, u32[]{:S(2)}, u32[]{:S(2)}) %collective-permute-start.3) | collective-permute-done | bytes 4194336 | tf_op jit(solution)/shard_map/ppermute | solution.py:80
  129.4 6.6 %pad_maximum_fusion = bf16[2048,2048]{0,1:T(8,128)(2,1)} fusion(bf16[2048,1024]{0,1:T(8,128)(2,1)} %collective-permute-done.3, bf16[2048,512]{0,1:T(8,128)(2,1)} %copy-done.3, bf16[2048,512]{0,1:T(8,128)(2,1)S(1)} %slice_dynamic-update-slice_fusion), kind=kLoop, calls=%fused_computation | loop fusion | flops 25165824 | bytes 16777216 | tf_op jit(solution)/shard_map/concatenate | solution.py:133
  136.0 18.8 %all-gather.5.cloned.1.call-done = bf16[4096,1024]{1,0:T(8,128)(2,1)} async-done(((bf16[512,1024]{1,0:T(8,128)(2,1)}), bf16[4096,1024]{1,0:T(8,128)(2,1)}) %all-gather.5.cloned.1.call-update) | async-done | bytes 8388624 | tf_op jit(solution)/shard_map/all_gather | solution.py:116
  154.8 9.2 %half_rotation.2 = bf16[2048,512]{1,0:T(8,128)(2,1)} custom-call(s32[4]{0:T(128)S(1)} %pad_add_fusion.places_ref, bf16[8,512,1024]{2,1,0:T(8,128)(2,1)} %bitcast.55, bf16[8,512,1024]{2,1,0:T(8,128)(2,1)} %bitcast.56, bf16[2048,512]{1,0:T(8,128)(2,1)} %get-tuple-element.31.refs_2_), custom_call_target="tpu_custom_call" | custom-call | flops 4294967296 | bytes 12582912 | tf_op jit(solution)/shard_map/half_rotation/pallas_call | solution.py:51
  164.0 3.7 %fusion.34 = bf16[512,512]{1,0:T(8,128)(2,1)S(1)} fusion(bf16[2048,512]{1,0:T(8,128)(2,1)} %half_rotation.2, bf16[2048,2048]{0,1:T(8,128)(2,1)} %pad_maximum_fusion, s32[]{:T(128)S(6)} %select_n.83), kind=kOutput, calls=%fused_computation.35 | convolution fusion | flops 1074003968 | bytes 4718596 | tf_op jit(solution)/shard_map/dot_general | solution.py:25
  167.8 2.9 fusion.28
  170.8 1.6 collective-permute-start.5
  172.4 9.4 %half_rotation.3 = bf16[2048,512]{1,0:T(8,128)(2,1)} custom-call(s32[4]{0:T(128)S(1)} %pad_add_fusion.places_ref, bf16[8,512,1024]{2,1,0:T(8,128)(2,1)} %bitcast.57, bf16[8,512,1024]{2,1,0:T(8,128)(2,1)} %bitcast.58, bf16[2048,512]{1,0:T(8,128)(2,1)} %get-tuple-element.37.refs_2_), custom_call_target="tpu_custom_call" | custom-call | flops 4294967296 | bytes 12582912 | tf_op jit(solution)/shard_map/half_rotation/pallas_call | solution.py:51
  181.8 3.0 fusion.37
  185.3 1.3 fusion.31
  186.7 1.3 fusion.22
  188.0 1.3 fusion.16
  189.3 1.3 fusion.25
  191.4 0.7 collective-permute-start.9
  192.0 1.3 fusion.19
  193.9 1.3 copy-done.4
  195.2 0.6 copy-done.5
  195.8 0.9 divide_convert_fusion.1
  196.7 1.5 collective-permute-start.10
  198.2 8.0 %collective-permute-done.9 = bf16[512,512]{1,0:T(8,128)(2,1)S(1)} collective-permute-done((bf16[512,512]{1,0:T(8,128)(2,1)S(1)}, bf16[512,512]{1,0:T(8,128)(2,1)S(1)}, u32[]{:S(2)}, u32[]{:S(2)}) %collective-permute-start.9) | collective-permute-done | bytes 524320 | tf_op jit(solution)/shard_map/ppermute | solution.py:80
  206.2 1.8 divide_convert_fusion
  208.7 8.7 %collective-permute-done.10 = bf16[512,512]{1,0:T(8,128)(2,1)S(1)} collective-permute-done((bf16[512,512]{1,0:T(8,128)(2,1)S(1)}, bf16[512,512]{1,0:T(8,128)(2,1)S(1)}, u32[]{:S(2)}, u32[]{:S(2)}) %collective-permute-start.10) | collective-permute-done | bytes 524320 | tf_op jit(solution)/shard_map/ppermute | solution.py:80
  217.7 10.1 %collective-permute-done.12 = bf16[512,512]{1,0:T(8,128)(2,1)S(1)} collective-permute-done((bf16[512,512]{1,0:T(8,128)(2,1)S(1)}, bf16[512,512]{1,0:T(8,128)(2,1)S(1)}, u32[]{:S(2)}, u32[]{:S(2)}) %collective-permute-start.12) | collective-permute-done | bytes 524320 | tf_op jit(solution)/shard_map/ppermute | solution.py:80
  229.0 2.8 copy-done.7
  232.3 0.6 pad_maximum_fusion.2
  232.9 1.2 slice-done.2
  234.1 1.4 slice-done.3
  235.5 9.0 %convolution_convert_fusion.1 = bf16[2048,1024]{1,0:T(8,128)(2,1)S(1)} fusion(bf16[2048,2048]{1,0:T(8,128)(2,1)S(1)} %bitcast.62, bf16[2048,1024]{1,0:T(8,128)(2,1)S(1)} %pad_maximum_fusion.2), kind=kOutput, calls=%fused_computation.4 | convolution fusion | flops 8592031744 | bytes 16777216 | tf_op jit(solution)/shard_map/dot_general | solution.py:25
  244.5 11.0 %convolution_convert_fusion = bf16[2048,2048]{1,0:T(8,128)(2,1)} fusion(bf16[2048,1024]{1,0:T(8,128)(2,1)S(1)} %convolution_convert_fusion.1, bf16[2048,1024]{1,0:T(8,128)(2,1)S(1)} %copy-done.2), kind=kOutput, calls=%fused_computation.1 | convolution fusion | flops 8594128896 | bytes 16777216 | tf_op jit(solution)/shard_map/dot_general | solution.py:29
  255.5 3.7 %pad_maximum_fusion.3 = (f32[512,1024]{1,0:T(8,128)}, f32[512,1024]{1,0:T(8,128)}) fusion(f32[512,512]{1,0:T(8,128)} %get-tuple-element.49, f32[512,512]{1,0:T(8,128)S(1)} %get-tuple-element.51, f32[512,512]{1,0:T(8,128)S(1)} %get-tuple-element.48, f32[512,512]{1,0:T(8,128)S(1)} %get-tuple-element.52), kind=kLoop, calls=%fused_computation.5 | loop fusion | flops 1048576 | bytes 8388608 | tf_op jit(solution)/shard_map/concatenate | solution.py:214
  259.2 84.3 %reduce-scatter.2.cloned.1.call-done = bf16[256,2048]{1,0:T(8,128)(2,1)} async-done(((bf16[2048,2048]{1,0:T(8,128)(2,1)}), bf16[256,2048]{1,0:T(8,128)(2,1)}) %reduce-scatter.2.cloned.1.call-update) | async-done | bytes 1048592 | tf_op jit(solution)/shard_map/reduce_scatter | solution.py:212
  (64 shorter events, 4.7 us)
Async XLA Ops:
  7.2 54.6 %all-gather.3.cloned.1.call-start = ((), (), s32[]{:S(2)}) async-start(), calls=%async_computation.1 | async-start | bytes 2359296 | tf_op jit(solution)/shard_map/all_gather | solution.py:116
  9.0 145.8 %all-gather.5.cloned.1.call-start = ((), (), s32[]{:S(2)}) async-start(), calls=%async_computation.2 | async-start | bytes 9437184 | tf_op jit(solution)/shard_map/all_gather | solution.py:116
  9.1 12.6 %collective-permute-start = (bf16[512,1024]{1,0:T(8,128)(2,1)}, bf16[512,1024]{1,0:T(8,128)(2,1)S(1)}, u32[]{:S(2)}, u32[]{:S(2)}) collective-permute-start(bf16[512,1024]{1,0:T(8,128)(2,1)} %param.5), channel_id=1, source_target_pairs={{0,0},{1,1},{2,2},{3,3},{4,4},{5,5},{6,6},{7,7},{8,14},{9,15},{10,... | collective-permute-start | bytes 3145736 | tf_op jit(solution)/shard_map/ppermute | solution.py:80
  21.6 0.7 collective-permute-start.1
  22.4 39.4 %copy-start.6 = (bf16[512,1024]{1,0:T(8,128)(2,1)}, bf16[512,1024]{1,0:T(8,128)(2,1)S(1)}, u32[]{:S(2)}) copy-start(bf16[512,1024]{1,0:T(8,128)(2,1)S(1)} %collective-permute-done.1) | copy-start | bytes 3145732
  61.8 281.7 %reduce-scatter.2.cloned.1.call-start = ((), (), s32[]{:S(2)}) async-start(), calls=%async_computation.3 | async-start | bytes 9437184 | tf_op jit(solution)/shard_map/reduce_scatter | solution.py:212
  68.9 49.6 %collective-permute-start.2 = (bf16[2048,512]{0,1:T(8,128)(2,1)S(1)}, bf16[2048,512]{0,1:T(8,128)(2,1)S(1)}, u32[]{:S(2)}, u32[]{:S(2)}) collective-permute-start(bf16[2048,512]{0,1:T(8,128)(2,1)S(1)} %slice_dynamic-update-slice_fusion), channel_id=1, source_target_pairs={{0,16},{1,17},{2,18},{3,19},{4,20},{5,21},{6,22},{7,23},{8,24},{9,... | collective-permute-start | bytes 6291464 | tf_op jit(solution)/shard_map/ppermute | solution.py:80
  118.5 2.7 copy-start.3
  121.2 8.2 %collective-permute-start.3 = (bf16[2048,1024]{0,1:T(8,128)(2,1)}, bf16[2048,1024]{0,1:T(8,128)(2,1)}, u32[]{:S(2)}, u32[]{:S(2)}) collective-permute-start(bf16[2048,1024]{0,1:T(8,128)(2,1)} %pad_maximum_fusion.1), channel_id=1, source_target_pairs={{0,8},{1,9},{2,10},{3,11},{4,12},{5,13},{6,14},{7,15},{8,0},{9,1},... | collective-permute-start | bytes 12582920 | tf_op jit(solution)/shard_map/ppermute | solution.py:80
  164.0 3.8 %copy-start = (bf16[2048,512]{1,0:T(8,128)(2,1)S(1)}, bf16[2048,512]{1,0:T(8,128)(2,1)}, u32[]{:S(2)}) copy-start(bf16[2048,512]{1,0:T(8,128)(2,1)} %half_rotation.2) | copy-start | bytes 6291460
  167.7 3.0 collective-permute-start.4
  170.7 11.1 %slice-start = ((s8[8388608]{0:T(1024)(128)(4,1)}), s8[4194304]{0:T(1024)(128)(4,1)S(1)}, s32[]{:S(2)}) async-start(s8[8388608]{0:T(1024)(128)(4,1)} %bitcast.53), calls=%async_computation.4 | async-start | bytes 8388608
  170.8 10.9 %slice-start.1 = ((s8[8388608]{0:T(1024)(128)(4,1)}), s8[4194304]{0:T(1024)(128)(4,1)S(1)}, s32[]{:S(2)}) async-start(s8[8388608]{0:T(1024)(128)(4,1)} %bitcast.53), calls=%async_computation.5 | async-start | bytes 8388608
  170.8 15.8 %collective-permute-start.5 = (bf16[512,512]{1,0:T(8,128)(2,1)S(1)}, bf16[512,512]{1,0:T(8,128)(2,1)S(1)}, u32[]{:S(2)}, u32[]{:S(2)}) collective-permute-start(bf16[512,512]{1,0:T(8,128)(2,1)S(1)} %add_convert_fusion.1), channel_id=1, source_target_pairs={{0,16},{1,17},{2,18},{3,19},{4,20},{5,21},{6,22},{7,23},{8,24},{9,... | collective-permute-start | bytes 1572872 | tf_op jit(solution)/shard_map/ppermute | solution.py:80
  181.8 3.5 %copy-start.1 = (bf16[2048,512]{1,0:T(8,128)(2,1)S(1)}, bf16[2048,512]{1,0:T(8,128)(2,1)}, u32[]{:S(2)}) copy-start(bf16[2048,512]{1,0:T(8,128)(2,1)} %half_rotation.3) | copy-start | bytes 6291460
  184.8 6.4 %collective-permute-start.8 = (bf16[512,512]{1,0:T(8,128)(2,1)S(1)}, bf16[512,512]{1,0:T(8,128)(2,1)S(1)}, u32[]{:S(2)}, u32[]{:S(2)}) collective-permute-start(bf16[512,512]{1,0:T(8,128)(2,1)S(1)} %fusion.37), channel_id=1, source_target_pairs={{0,8},{1,9},{2,10},{3,11},{4,12},{5,13},{6,14},{7,15},{8,0},{9,1},... | collective-permute-start | bytes 1572872 | tf_op jit(solution)/shard_map/ppermute | solution.py:80
  190.6 15.6 %collective-permute-start.7 = (bf16[512,512]{1,0:T(8,128)(2,1)S(1)}, bf16[512,512]{1,0:T(8,128)(2,1)S(1)}, u32[]{:S(2)}, u32[]{:S(2)}) collective-permute-start(bf16[512,512]{1,0:T(8,128)(2,1)S(1)} %fusion.25), channel_id=1, source_target_pairs={{0,8},{1,9},{2,10},{3,11},{4,12},{5,13},{6,14},{7,15},{8,0},{9,1},... | collective-permute-start | bytes 1572872 | tf_op jit(solution)/shard_map/ppermute | solution.py:80
  190.8 3.1 collective-permute-start.6
  191.4 14.8 %collective-permute-start.9 = (bf16[512,512]{1,0:T(8,128)(2,1)S(1)}, bf16[512,512]{1,0:T(8,128)(2,1)S(1)}, u32[]{:S(2)}, u32[]{:S(2)}) collective-permute-start(bf16[512,512]{1,0:T(8,128)(2,1)S(1)} %add_convert_fusion), channel_id=1, source_target_pairs={{0,16},{1,17},{2,18},{3,19},{4,20},{5,21},{6,22},{7,23},{8,24},{9,... | collective-permute-start | bytes 1572872 | tf_op jit(solution)/shard_map/ppermute | solution.py:80
  193.6 1.6 copy-start.4
  193.6 2.2 copy-start.5
  196.7 20.7 %collective-permute-start.10 = (bf16[512,512]{1,0:T(8,128)(2,1)S(1)}, bf16[512,512]{1,0:T(8,128)(2,1)S(1)}, u32[]{:S(2)}, u32[]{:S(2)}) collective-permute-start(bf16[512,512]{1,0:T(8,128)(2,1)S(1)} %get-tuple-element.50), channel_id=1, source_target_pairs={{0,16},{1,17},{2,18},{3,19},{4,20},{5,21},{6,22},{7,23},{8,24},{9,... | collective-permute-start | bytes 1572872 | tf_op jit(solution)/shard_map/ppermute | solution.py:80
  208.0 19.8 %collective-permute-start.12 = (bf16[512,512]{1,0:T(8,128)(2,1)S(1)}, bf16[512,512]{1,0:T(8,128)(2,1)S(1)}, u32[]{:S(2)}, u32[]{:S(2)}) collective-permute-start(bf16[512,512]{1,0:T(8,128)(2,1)S(1)} %get-tuple-element.47), channel_id=1, source_target_pairs={{0,16},{1,17},{2,18},{3,19},{4,20},{5,21},{6,22},{7,23},{8,24},{9,... | collective-permute-start | bytes 1572872 | tf_op jit(solution)/shard_map/ppermute | solution.py:80
  217.6 10.9 %collective-permute-start.11 = (bf16[2,512,512]{2,1,0:T(8,128)(2,1)S(1)}, bf16[2,512,512]{2,1,0:T(8,128)(2,1)S(1)}, u32[]{:S(2)}, u32[]{:S(2)}) collective-permute-start(bf16[2,512,512]{2,1,0:T(8,128)(2,1)S(1)} %pad_maximum_fusion.7), channel_id=1, source_target_pairs={{0,8},{1,9},{2,10},{3,11},{4,12},{5,13},{6,14},{7,15},{8,0},{9,1},... | collective-permute-start | bytes 3145736 | tf_op jit(solution)/shard_map/ppermute | solution.py:80
  228.0 3.7 %collective-permute-start.13 = (bf16[2,512,512]{2,1,0:T(8,128)(2,1)S(1)}, bf16[2,512,512]{2,1,0:T(8,128)(2,1)S(1)}, u32[]{:S(2)}, u32[]{:S(2)}) collective-permute-start(bf16[2,512,512]{2,1,0:T(8,128)(2,1)S(1)} %pad_maximum_fusion.8), channel_id=1, source_target_pairs={{0,8},{1,9},{2,10},{3,11},{4,12},{5,13},{6,14},{7,15},{8,0},{9,1},... | collective-permute-start | bytes 3145736 | tf_op jit(solution)/shard_map/ppermute | solution.py:80
  228.5 3.3 copy-start.7
  231.9 2.2 slice-start.2
  232.3 3.2 slice-start.3
  235.5 9.0 %copy-start.2 = (bf16[2048,1024]{1,0:T(8,128)(2,1)S(1)}, bf16[2048,1024]{1,0:T(8,128)(2,1)}, u32[]{:S(2)}) copy-start(bf16[2048,1024]{1,0:T(8,128)(2,1)} %convert.4) | copy-start | bytes 12582916
Sparse Core Ops, SparseCore 0:
  9.5 52.2 all-gather.2
  63.9 90.8 all-gather.4
  255.6 87.8 reduce-scatter.1

commit v12 on v11

--- a/solution.py
+++ b/solution.py
@@ -16,7 +16,7 @@
 
 COL_PARTS = 2
 
-VMEM_BYTES = 52 * 1024 * 1024
+VMEM_BYTES = 16 * 1024 * 1024
 
 low = jnp.bfloat16
 
@@ -34,17 +34,30 @@
     nx = count // nz
     width = right.shape[1]
 
-    def kernel(places_ref, *refs):
-        blocks, right_ref, out = refs[:nx], refs[nx], refs[nx + 1]
-        total = matmul(blocks[0][...], right_ref[:cols])
-        for i in range(1, nx):
-            total += matmul(blocks[i][...], right_ref[i * cols : (i + 1) * cols])
-        out[...] = total.astype(out.dtype)
-
-    def block_of(i):
-        if i % 2 == 0:
-            return pl.BlockSpec((None, rows, cols), lambda k, p: (i * nz + k, 0, 0))
-        return pl.BlockSpec((None, rows, cols), lambda k, p: (i * nz + nz - 1 - k, 0, 0))
+    def kernel(places_ref, gathered_ref, right_ref, out_ref, held, arrived):
+        def copies(k):
+            return [
+                pltpu.make_async_copy(
+                    gathered_ref.at[i * nz + (k if i % 2 == 0 else nz - 1 - k)],
+                    held.at[k % 2, i],
+                    arrived.at[k % 2, i],
+                )
+                for i in range(nx)
+            ]
+
+        for copy in copies(0):
+            copy.start()
+        for k in range(nz):
+            if k + 1 < nz:
+                for copy in copies(k + 1):
+                    copy.start()
+            for copy in copies(k):
+                copy.wait()
+            total = matmul(held[k % 2, 0], right_ref[:cols])
+            for i in range(1, nx):
+                total += matmul(held[k % 2, i], right_ref[i * cols : (i + 1) * cols])
+            start = pl.multiple_of(places_ref[k] * rows, rows)
+            out_ref[pl.ds(start, rows)] = total.astype(out_ref.dtype)
 
     out = jax.ShapeDtypeStruct((nz * rows, width), low)
     size = sum(a.size * a.dtype.itemsize for a in (gathered, right, out))
@@ -53,15 +66,21 @@
         out_shape=out,
         grid_spec=pltpu.PrefetchScalarGridSpec(
             num_scalar_prefetch=1,
-            grid=(nz,),
-            in_specs=[block_of(i) for i in range(nx)]
-            + [pl.BlockSpec(right.shape, lambda k, p: (0, 0), pipeline_mode=pl.Buffered(1))],
-            out_specs=pl.BlockSpec((rows, width), lambda k, p: (p[k], 0)),
+            grid=(1,),
+            in_specs=[
+                pl.BlockSpec(memory_space=pltpu.HBM),
+                pl.BlockSpec(right.shape, lambda k, p: (0, 0), pipeline_mode=pl.Buffered(1)),
+            ],
+            out_specs=pl.BlockSpec(out.shape, lambda k, p: (0, 0)),
+            scratch_shapes=[
+                pltpu.VMEM((2, nx, rows, cols), gathered.dtype),
+                pltpu.SemaphoreType.DMA((2, nx)),
+            ],
         ),
         compiler_params=pltpu.CompilerParams(vmem_limit_bytes=VMEM_BYTES),
         cost_estimate=pl.CostEstimate(flops=2 * gathered.size * width, bytes_accessed=size, transcendentals=0),
         name="half_rotation",
-    )(places, *([gathered] * nx), right)
+    )(places, gathered, right)
 
 
 def per_device(gradient, left_basis, right_basis, first_moment, second_moment, *, nb, nd):

time: 351 us -> 351 us (level)
  Pallas kernels: 18.6 us -> 12.5 us
    pallas_call x2, Pallas kernels: 18.6 us -> 12.5 us  [half_rotation(): pl.pallas_call(kernel, out_shape=out, grid_spec=pltpu.PrefetchScalarGridS...]
    unnamed x37 -> x33, local copies, waits for them, and re-layouts: 13.9 us -> 17 us
  transfers between devices with their start and end apart: 17 -> 17, of which waited for: 8 -> 10; matrix products, arithmetic and copies ran while one was open for 14% -> 13% of each run, Pallas kernels for 3% -> 2%
where the time goes in v12:
time: 351 us; the launch traced here: 350 us
  waiting for transfers between devices  224 us (64%)
  matrix products  37.6 us (11%)
  other arithmetic  25.5 us (7%)
  local copies, waits for them, and re-layouts  23 us (7%)
  between operations  14.2 us (4%)
  starting transfers between devices  13.9 us (4%)
  Pallas kernels  12.5 us (4%)
    reduce_scatter x1, waiting for transfers between devices, per_device(): lax.psum_scatter(total, 'dp', scatter_dimension=0, axis_index_groups=[pat...  84.6 us
    ppermute x14, waiting for transfers between devices, permute(): return lax.ppermute(value, ('basis', 'dp'), pairs)  80.9 us
    all_gather x2, waiting for transfers between devices, round_path(): return lax.all_gather(value, 'dp', axis_index_groups=[path], tiled=True)  58.2 us
    dot_general x9, matrix products, matmul(): lax.dot_general(a, b, (((1,), (0,)), ((), ())), preferred_element_type=jn...  24.2 us
    unnamed x33, local copies, waits for them, and re-layouts  17 us
    ppermute x14, starting transfers between devices, permute(): return lax.ppermute(value, ('basis', 'dp'), pairs)  13.8 us
    dot_general x1, matrix products, matmul_nt(): lax.dot_general(a, b, (((1,), (1,)), ((), ())), preferred_element_type=jn...  13.4 us
    pallas_call x2, Pallas kernels, half_rotation(): pl.pallas_call(kernel, out_shape=out, grid_spec=pltpu.PrefetchScalarGridS...  12.5 us
  transfers between devices with their start and end apart: 17, of which 10 were waited for; matrix products, arithmetic and copies ran while one was open for 13% of the time, Pallas kernels for 2%

profile of v12, /device:TPU:0, one launch (start us, length us, event | category | flops | bytes accessed | tf_op | source)
XLA Modules:
  0.0 350.5 jit_solution(4394338470375225056)
XLA Ops:
  7.2 1.8 convert_bitcast_fusion
  9.1 1.9 collective-permute-start
  10.9 6.0 %convert.4 = bf16[2048,1024]{1,0:T(8,128)(2,1)} convert(f32[2048,1024]{1,0:T(8,128)} %param.7) | non-fusion elementwise | flops 2097152 | bytes 12582912 | tf_op jit(solution)/shard_map/convert.1
  17.0 4.6 %fusion.52 = (bf16[2048,512]{1,0:T(8,128)(2,1)}, bf16[2048,512]{1,0:T(8,128)(2,1)}) fusion(bf16[2048,1024]{1,0:T(8,128)(2,1)} %convert.4), kind=kLoop, calls=%fused_computation.80 | loop fusion | bytes 8388608 | tf_op jit(solution)/shard_map/slice | solution.py:139
  21.6 0.7 collective-permute-start.1
  22.4 39.4 %all-gather.3.cloned.1.call-done = bf16[2048,512]{0,1:T(8,128)(2,1)} async-done(((bf16[256,512]{0,1:T(8,128)(2,1)}), bf16[2048,512]{0,1:T(8,128)(2,1)}) %all-gather.3.cloned.1.call-update) | async-done | bytes 2097168 | tf_op jit(solution)/shard_map/all_gather | solution.py:135
  61.9 1.0 slice_dynamic-update-slice_fusion.6
  62.8 1.0 slice_dynamic-update-slice_fusion.5
  63.8 1.0 slice_dynamic-update-slice_fusion.4
  64.8 1.0 slice_dynamic-update-slice_fusion.3
  65.8 1.0 slice_dynamic-update-slice_fusion.2
  66.8 1.0 slice_dynamic-update-slice_fusion.1
  67.8 1.1 slice_dynamic-update-slice_fusion
  68.9 3.9 %collective-permute-start.2 = (bf16[2048,512]{0,1:T(8,128)(2,1)S(1)}, bf16[2048,512]{0,1:T(8,128)(2,1)S(1)}, u32[]{:S(2)}, u32[]{:S(2)}) collective-permute-start(bf16[2048,512]{0,1:T(8,128)(2,1)S(1)} %slice_dynamic-update-slice_fusion), channel_id=1, source_target_pairs={{0,16},{1,17},{2,18},{3,19},{4,20},{5,21},{6,22},{7,23},{8,24},{9,... | collective-permute-start | bytes 6291464 | tf_op jit(solution)/shard_map/ppermute | solution.py:99
  72.8 45.7 %collective-permute-done.2 = bf16[2048,512]{0,1:T(8,128)(2,1)S(1)} collective-permute-done((bf16[2048,512]{0,1:T(8,128)(2,1)S(1)}, bf16[2048,512]{0,1:T(8,128)(2,1)S(1)}, u32[]{:S(2)}, u32[]{:S(2)}) %collective-permute-start.2) | collective-permute-done | bytes 2097184 | tf_op jit(solution)/shard_map/ppermute | solution.py:99
  118.5 2.7 pad_maximum_fusion.1
  121.2 1.0 collective-permute-start.3
  122.2 7.1 %collective-permute-done.3 = bf16[2048,1024]{0,1:T(8,128)(2,1)} collective-permute-done((bf16[2048,1024]{0,1:T(8,128)(2,1)}, bf16[2048,1024]{0,1:T(8,128)(2,1)}, u32[]{:S(2)}, u32[]{:S(2)}) %collective-permute-start.3) | collective-permute-done | bytes 4194336 | tf_op jit(solution)/shard_map/ppermute | solution.py:99
  129.3 6.6 %pad_maximum_fusion = bf16[2048,2048]{0,1:T(8,128)(2,1)} fusion(bf16[2048,1024]{0,1:T(8,128)(2,1)} %collective-permute-done.3, bf16[2048,512]{0,1:T(8,128)(2,1)} %copy-done.6, bf16[2048,512]{0,1:T(8,128)(2,1)S(1)} %slice_dynamic-update-slice_fusion), kind=kLoop, calls=%fused_computation | loop fusion | flops 25165824 | bytes 16777216 | tf_op jit(solution)/shard_map/concatenate | solution.py:152
  136.0 18.8 %all-gather.5.cloned.1.call-done = bf16[4096,1024]{1,0:T(8,128)(2,1)} async-done(((bf16[512,1024]{1,0:T(8,128)(2,1)}), bf16[4096,1024]{1,0:T(8,128)(2,1)}) %all-gather.5.cloned.1.call-update) | async-done | bytes 8388624 | tf_op jit(solution)/shard_map/all_gather | solution.py:135
  154.8 1.6 copy-done.1
  156.4 3.4 copy-done.2
  159.8 6.1 %half_rotation.2 = bf16[2048,512]{1,0:T(8,128)(2,1)S(1)} custom-call(s32[4]{0:T(128)S(1)} %pad_add_fusion.places_ref, bf16[8,512,1024]{2,1,0:T(8,128)(2,1)S(1)} %bitcast.53, bf16[2048,512]{1,0:T(8,128)(2,1)S(1)} %copy-done.1), custom_call_target="tpu_custom_call" | custom-call | flops 4294967296 | bytes 12582912 | tf_op jit(solution)/shard_map/half_rotation/pallas_call | solution.py:64
  165.9 2.9 fusion.34
  168.9 3.0 fusion.28
  172.1 1.5 collective-permute-start.5
  173.7 3.4 copy-done.3
  177.1 6.3 %half_rotation.3 = bf16[2048,512]{1,0:T(8,128)(2,1)S(1)} custom-call(s32[4]{0:T(128)S(1)} %pad_add_fusion.places_ref, bf16[8,512,1024]{2,1,0:T(8,128)(2,1)S(1)} %bitcast.54, bf16[2048,512]{1,0:T(8,128)(2,1)S(1)} %copy-done), custom_call_target="tpu_custom_call" | custom-call | flops 4294967296 | bytes 12582912 | tf_op jit(solution)/shard_map/half_rotation/pallas_call | solution.py:64
  183.4 1.3 fusion.37
  184.9 1.3 fusion.31
  186.5 1.3 fusion.22
  187.8 1.3 fusion.16
  189.0 1.3 fusion.25
  191.1 1.5 collective-permute-start.9
  192.6 1.3 fusion.19
  194.4 1.3 copy-done.7
  196.3 0.9 divide_convert_fusion.1
  197.9 8.0 %collective-permute-done.9 = bf16[512,512]{1,0:T(8,128)(2,1)S(1)} collective-permute-done((bf16[512,512]{1,0:T(8,128)(2,1)S(1)}, bf16[512,512]{1,0:T(8,128)(2,1)S(1)}, u32[]{:S(2)}, u32[]{:S(2)}) %collective-permute-start.9) | collective-permute-done | bytes 524320 | tf_op jit(solution)/shard_map/ppermute | solution.py:99
  205.9 1.8 divide_convert_fusion
  207.7 1.5 collective-permute-start.12
  209.3 7.8 %collective-permute-done.10 = bf16[512,512]{1,0:T(8,128)(2,1)S(1)} collective-permute-done((bf16[512,512]{1,0:T(8,128)(2,1)S(1)}, bf16[512,512]{1,0:T(8,128)(2,1)S(1)}, u32[]{:S(2)}, u32[]{:S(2)}) %collective-permute-start.10) | collective-permute-done | bytes 524320 | tf_op jit(solution)/shard_map/ppermute | solution.py:99
  217.4 10.1 %collective-permute-done.12 = bf16[512,512]{1,0:T(8,128)(2,1)S(1)} collective-permute-done((bf16[512,512]{1,0:T(8,128)(2,1)S(1)}, bf16[512,512]{1,0:T(8,128)(2,1)S(1)}, u32[]{:S(2)}, u32[]{:S(2)}) %collective-permute-start.12) | collective-permute-done | bytes 524320 | tf_op jit(solution)/shard_map/ppermute | solution.py:99
  228.7 1.8 collective-permute-done.13
  230.9 0.6 pad_maximum_fusion.2
  231.6 10.6 %convolution_convert_fusion.1 = bf16[2048,1024]{1,0:T(8,128)(2,1)} fusion(bf16[2048,2048]{1,0:T(8,128)(2,1)S(1)} %bitcast_dynamic-update-slice_fusion, bf16[2048,1024]{1,0:T(8,128)(2,1)S(1)} %pad_maximum_fusion.2), kind=kOutput, calls=%fused_computation.4 | convolution fusion | flops 8592031744 | bytes 16777216 | tf_op jit(solution)/shard_map/dot_general | solution.py:25
  242.2 13.4 %convolution_convert_fusion = bf16[2048,2048]{1,0:T(8,128)(2,1)} fusion(bf16[2048,1024]{1,0:T(8,128)(2,1)} %convolution_convert_fusion.1, bf16[2048,1024]{1,0:T(8,128)(2,1)S(1)} %copy-done.5), kind=kOutput, calls=%fused_computation.1 | convolution fusion | flops 8594128896 | bytes 16777216 | tf_op jit(solution)/shard_map/dot_general | solution.py:29
  255.6 3.7 %pad_maximum_fusion.3 = (f32[512,1024]{1,0:T(8,128)}, f32[512,1024]{1,0:T(8,128)}) fusion(f32[512,512]{1,0:T(8,128)} %get-tuple-element.49, f32[512,512]{1,0:T(8,128)S(1)} %get-tuple-element.51, f32[512,512]{1,0:T(8,128)S(1)} %get-tuple-element.48, f32[512,512]{1,0:T(8,128)S(1)} %get-tuple-element.52), kind=kLoop, calls=%fused_computation.5 | loop fusion | flops 1048576 | bytes 8388608 | tf_op jit(solution)/shard_map/concatenate | solution.py:233
  259.4 84.6 %reduce-scatter.2.cloned.1.call-done = bf16[256,2048]{1,0:T(8,128)(2,1)} async-done(((bf16[2048,2048]{1,0:T(8,128)(2,1)}), bf16[256,2048]{1,0:T(8,128)(2,1)}) %reduce-scatter.2.cloned.1.call-update) | async-done | bytes 1048592 | tf_op jit(solution)/shard_map/reduce_scatter | solution.py:231
  (58 shorter events, 5.2 us)
Async XLA Ops:
  7.2 54.6 %all-gather.3.cloned.1.call-start = ((), (), s32[]{:S(2)}) async-start(), calls=%async_computation.1 | async-start | bytes 2359296 | tf_op jit(solution)/shard_map/all_gather | solution.py:135
  9.0 145.8 %all-gather.5.cloned.1.call-start = ((), (), s32[]{:S(2)}) async-start(), calls=%async_computation.2 | async-start | bytes 9437184 | tf_op jit(solution)/shard_map/all_gather | solution.py:135
  9.1 12.6 %collective-permute-start = (bf16[512,1024]{1,0:T(8,128)(2,1)}, bf16[512,1024]{1,0:T(8,128)(2,1)S(1)}, u32[]{:S(2)}, u32[]{:S(2)}) collective-permute-start(bf16[512,1024]{1,0:T(8,128)(2,1)} %param.5), channel_id=1, source_target_pairs={{0,0},{1,1},{2,2},{3,3},{4,4},{5,5},{6,6},{7,7},{8,14},{9,15},{10,... | collective-permute-start | bytes 3145736 | tf_op jit(solution)/shard_map/ppermute | solution.py:99
  21.6 0.7 collective-permute-start.1
  22.4 39.4 %copy-start.9 = (bf16[512,1024]{1,0:T(8,128)(2,1)}, bf16[512,1024]{1,0:T(8,128)(2,1)S(1)}, u32[]{:S(2)}) copy-start(bf16[512,1024]{1,0:T(8,128)(2,1)S(1)} %collective-permute-done.1) | copy-start | bytes 3145732
  61.8 282.1 %reduce-scatter.2.cloned.1.call-start = ((), (), s32[]{:S(2)}) async-start(), calls=%async_computation.3 | async-start | bytes 9437184 | tf_op jit(solution)/shard_map/reduce_scatter | solution.py:231
  68.9 49.6 %collective-permute-start.2 = (bf16[2048,512]{0,1:T(8,128)(2,1)S(1)}, bf16[2048,512]{0,1:T(8,128)(2,1)S(1)}, u32[]{:S(2)}, u32[]{:S(2)}) collective-permute-start(bf16[2048,512]{0,1:T(8,128)(2,1)S(1)} %slice_dynamic-update-slice_fusion), channel_id=1, source_target_pairs={{0,16},{1,17},{2,18},{3,19},{4,20},{5,21},{6,22},{7,23},{8,24},{9,... | collective-permute-start | bytes 6291464 | tf_op jit(solution)/shard_map/ppermute | solution.py:99
  118.5 2.7 copy-start.6
  121.2 8.2 %collective-permute-start.3 = (bf16[2048,1024]{0,1:T(8,128)(2,1)}, bf16[2048,1024]{0,1:T(8,128)(2,1)}, u32[]{:S(2)}, u32[]{:S(2)}) collective-permute-start(bf16[2048,1024]{0,1:T(8,128)(2,1)} %pad_maximum_fusion.1), channel_id=1, source_target_pairs={{0,8},{1,9},{2,10},{3,11},{4,12},{5,13},{6,14},{7,15},{8,0},{9,1},... | collective-permute-start | bytes 12582920 | tf_op jit(solution)/shard_map/ppermute | solution.py:99
  154.8 1.6 copy-start.1
  156.4 3.4 copy-start.2
  168.8 3.2 collective-permute-start.4
  168.9 4.7 %copy-start = (bf16[2048,512]{1,0:T(8,128)(2,1)S(1)}, bf16[2048,512]{1,0:T(8,128)(2,1)}, u32[]{:S(2)}) copy-start(bf16[2048,512]{1,0:T(8,128)(2,1)} %get-tuple-element.37.right_ref) | copy-start | bytes 6291460
  172.1 14.3 %collective-permute-start.5 = (bf16[512,512]{1,0:T(8,128)(2,1)S(1)}, bf16[512,512]{1,0:T(8,128)(2,1)S(1)}, u32[]{:S(2)}, u32[]{:S(2)}) collective-permute-start(bf16[512,512]{1,0:T(8,128)(2,1)S(1)} %add_convert_fusion.1), channel_id=1, source_target_pairs={{0,16},{1,17},{2,18},{3,19},{4,20},{5,21},{6,22},{7,23},{8,24},{9,... | collective-permute-start | bytes 1572872 | tf_op jit(solution)/shard_map/ppermute | solution.py:99
  173.7 3.4 copy-start.3
  177.1 6.4 %copy-start.4 = (bf16[2048,2048]{0,1:T(8,128)(2,1)S(1)}, bf16[2048,2048]{0,1:T(8,128)(2,1)}, u32[]{:S(2)}) copy-start(bf16[2048,2048]{0,1:T(8,128)(2,1)} %pad_maximum_fusion) | copy-start | bytes 25165828
  184.7 6.2 %collective-permute-start.8 = (bf16[512,512]{1,0:T(8,128)(2,1)S(1)}, bf16[512,512]{1,0:T(8,128)(2,1)S(1)}, u32[]{:S(2)}, u32[]{:S(2)}) collective-permute-start(bf16[512,512]{1,0:T(8,128)(2,1)S(1)} %fusion.37), channel_id=1, source_target_pairs={{0,8},{1,9},{2,10},{3,11},{4,12},{5,13},{6,14},{7,15},{8,0},{9,1},... | collective-permute-start | bytes 1572872 | tf_op jit(solution)/shard_map/ppermute | solution.py:99
  190.3 15.6 %collective-permute-start.7 = (bf16[512,512]{1,0:T(8,128)(2,1)S(1)}, bf16[512,512]{1,0:T(8,128)(2,1)S(1)}, u32[]{:S(2)}, u32[]{:S(2)}) collective-permute-start(bf16[512,512]{1,0:T(8,128)(2,1)S(1)} %fusion.25), channel_id=1, source_target_pairs={{0,8},{1,9},{2,10},{3,11},{4,12},{5,13},{6,14},{7,15},{8,0},{9,1},... | collective-permute-start | bytes 1572872 | tf_op jit(solution)/shard_map/ppermute | solution.py:99
  190.5 3.9 %collective-permute-start.6 = (bf16[512,512]{1,0:T(8,128)(2,1)S(1)}, bf16[512,512]{1,0:T(8,128)(2,1)S(1)}, u32[]{:S(2)}, u32[]{:S(2)}) collective-permute-start(bf16[512,512]{1,0:T(8,128)(2,1)S(1)} %fusion.22), channel_id=1, source_target_pairs={{0,8},{1,9},{2,10},{3,11},{4,12},{5,13},{6,14},{7,15},{8,0},{9,1},... | collective-permute-start | bytes 1572872 | tf_op jit(solution)/shard_map/ppermute | solution.py:99
  191.1 14.8 %collective-permute-start.9 = (bf16[512,512]{1,0:T(8,128)(2,1)S(1)}, bf16[512,512]{1,0:T(8,128)(2,1)S(1)}, u32[]{:S(2)}, u32[]{:S(2)}) collective-permute-start(bf16[512,512]{1,0:T(8,128)(2,1)S(1)} %add_convert_fusion), channel_id=1, source_target_pairs={{0,16},{1,17},{2,18},{3,19},{4,20},{5,21},{6,22},{7,23},{8,24},{9,... | collective-permute-start | bytes 1572872 | tf_op jit(solution)/shard_map/ppermute | solution.py:99
  194.1 1.6 copy-start.7
  194.1 2.2 copy-start.8
  197.2 19.9 %collective-permute-start.10 = (bf16[512,512]{1,0:T(8,128)(2,1)S(1)}, bf16[512,512]{1,0:T(8,128)(2,1)S(1)}, u32[]{:S(2)}, u32[]{:S(2)}) collective-permute-start(bf16[512,512]{1,0:T(8,128)(2,1)S(1)} %get-tuple-element.50), channel_id=1, source_target_pairs={{0,16},{1,17},{2,18},{3,19},{4,20},{5,21},{6,22},{7,23},{8,24},{9,... | collective-permute-start | bytes 1572872 | tf_op jit(solution)/shard_map/ppermute | solution.py:99
  207.7 19.8 %collective-permute-start.12 = (bf16[512,512]{1,0:T(8,128)(2,1)S(1)}, bf16[512,512]{1,0:T(8,128)(2,1)S(1)}, u32[]{:S(2)}, u32[]{:S(2)}) collective-permute-start(bf16[512,512]{1,0:T(8,128)(2,1)S(1)} %get-tuple-element.47), channel_id=1, source_target_pairs={{0,16},{1,17},{2,18},{3,19},{4,20},{5,21},{6,22},{7,23},{8,24},{9,... | collective-permute-start | bytes 1572872 | tf_op jit(solution)/shard_map/ppermute | solution.py:99
  217.3 10.8 %collective-permute-start.11 = (bf16[2,512,512]{2,1,0:T(8,128)(2,1)S(1)}, bf16[2,512,512]{2,1,0:T(8,128)(2,1)S(1)}, u32[]{:S(2)}, u32[]{:S(2)}) collective-permute-start(bf16[2,512,512]{2,1,0:T(8,128)(2,1)S(1)} %pad_maximum_fusion.7), channel_id=1, source_target_pairs={{0,8},{1,9},{2,10},{3,11},{4,12},{5,13},{6,14},{7,15},{8,0},{9,1},... | collective-permute-start | bytes 3145736 | tf_op jit(solution)/shard_map/ppermute | solution.py:99
  227.7 2.7 collective-permute-start.13
  231.6 10.6 %copy-start.5 = (bf16[2048,1024]{1,0:T(8,128)(2,1)S(1)}, bf16[2048,1024]{1,0:T(8,128)(2,1)}, u32[]{:S(2)}) copy-start(bf16[2048,1024]{1,0:T(8,128)(2,1)} %convert.4) | copy-start | bytes 12582916
Sparse Core Ops, SparseCore 0:
  9.5 52.2 all-gather.2
  63.9 90.8 all-gather.4
  255.8 88.1 reduce-scatter.1

commit v13 on v12

--- a/solution.py
+++ b/solution.py
@@ -16,7 +16,7 @@
 
 COL_PARTS = 2
 
-VMEM_BYTES = 16 * 1024 * 1024
+VMEM_BYTES = 52 * 1024 * 1024
 
 low = jnp.bfloat16
 
@@ -150,7 +150,17 @@
     left_t = jnp.concatenate([left_blocks[path.index(dd)] for dd in range(nd)], axis=0)
     for t in reversed(bits):
         left_t = jnp.concatenate([left_t, move_b(left_t, t)], axis=1)
-    left_t, gathered = together(left_t, gathered.reshape(nd, rows, ff_block))
+    left_t = lax.optimization_barrier(left_t)
+    left = jnp.concatenate(
+        [
+            lax.dynamic_slice_in_dim(
+                left_t, reversed_bits(b ^ (dd // nx)) * rows + dd % nx * out_rows, out_rows, 1
+            ).T
+            for dd in path
+        ],
+        axis=0,
+    )
+    left_t, left, gathered = together(left_t, left, gathered.reshape(nd, rows, ff_block))
 
     odd = sorted(range(1, nb, 2), key=lambda t: -t)
     first_group, second_group = odd[: nb // 4], odd[nb // 4 :]
@@ -187,18 +197,6 @@
                 held[s ^ t] = held[s ^ t] + move_b(held.pop(s).astype(low), t).astype(jnp.float32)
         sums.append(held[0])
 
-    source = after(left_t, arrived[0][-1])
-    left = jnp.concatenate(
-        [
-            lax.dynamic_slice_in_dim(
-                source, reversed_bits(b ^ (dd // nx)) * rows + dd % nx * out_rows, out_rows, 1
-            ).T
-            for dd in path
-        ],
-        axis=0,
-    )
-    left = lax.optimization_barrier(left)
-
     first_out, second_out, directions = [], [], []
     for j in range(COL_PARTS):
         cols = slice(j * width, (j + 1) * width)

time: 351 us -> 356 us (1.014)
  waiting for transfers between devices: 224 us -> 214 us
  Pallas kernels: 12.5 us -> 20.5 us
  other arithmetic: 25.5 us -> 31 us
    pallas_call x2, Pallas kernels: 12.5 us -> 20.5 us  [half_rotation(): pl.pallas_call(kernel, out_shape=out, grid_spec=pltpu.PrefetchScalarGridS...]
    all_gather x2, waiting for transfers between devices: 58.2 us -> 51.3 us  [round_path(): return lax.all_gather(value, 'dp', axis_index_groups=[path], tiled=True)]
    another operation x8, other arithmetic: 1.02 us -> 7.62 us  [joined(): return jnp.stack([first, second], axis=axis)]
    unnamed x33 -> x47, local copies, waits for them, and re-layouts: 17 us -> 16 us
  transfers between devices with their start and end apart: 17 -> 17, of which waited for: 10 -> 9; matrix products, arithmetic and copies ran while one was open for 13% -> 17% of each run, Pallas kernels for 2% -> 3%
where the time goes in v13:
time: 356 us; the launch traced here: 355 us
  waiting for transfers between devices  214 us (60%)
  matrix products  38.6 us (11%)
  other arithmetic  31 us (9%)
  local copies, waits for them, and re-layouts  23.1 us (6%)
  Pallas kernels  20.5 us (6%)
  between operations  14.2 us (4%)
  starting transfers between devices  12.7 us (4%)
    reduce_scatter x1, waiting for transfers between devices, per_device(): lax.psum_scatter(total, 'dp', scatter_dimension=0, axis_index_groups=[pat...  82.6 us
    ppermute x14, waiting for transfers between devices, permute(): return lax.ppermute(value, ('basis', 'dp'), pairs)  80.5 us
    all_gather x2, waiting for transfers between devices, round_path(): return lax.all_gather(value, 'dp', axis_index_groups=[path], tiled=True)  51.3 us
    dot_general x9, matrix products, matmul(): lax.dot_general(a, b, (((1,), (0,)), ((), ())), preferred_element_type=jn...  27.7 us
    pallas_call x2, Pallas kernels, half_rotation(): pl.pallas_call(kernel, out_shape=out, grid_spec=pltpu.PrefetchScalarGridS...  20.5 us
    unnamed x47, local copies, waits for them, and re-layouts  16 us
    ppermute x14, starting transfers between devices, permute(): return lax.ppermute(value, ('basis', 'dp'), pairs)  12.6 us
    dot_general x1, matrix products, matmul_nt(): lax.dot_general(a, b, (((1,), (1,)), ((), ())), preferred_element_type=jn...  11 us
  transfers between devices with their start and end apart: 17, of which 9 were waited for; matrix products, arithmetic and copies ran while one was open for 17% of the time, Pallas kernels for 3%

profile of v13, /device:TPU:0, one launch (start us, length us, event | category | flops | bytes accessed | tf_op | source)
XLA Modules:
  0.0 354.6 jit_solution(11736290925646232676)
XLA Ops:
  7.2 1.8 convert_bitcast_fusion
  9.1 1.9 collective-permute-start
  10.9 6.1 %convert.4 = bf16[2048,1024]{1,0:T(8,128)(2,1)} convert(f32[2048,1024]{1,0:T(8,128)} %param.7) | non-fusion elementwise | flops 2097152 | bytes 12582912 | tf_op jit(solution)/shard_map/convert.1
  17.1 4.6 %fusion.52 = (bf16[2048,512]{1,0:T(8,128)(2,1)}, bf16[2048,512]{1,0:T(8,128)(2,1)}) fusion(bf16[2048,1024]{1,0:T(8,128)(2,1)} %convert.4), kind=kLoop, calls=%fused_computation.80 | loop fusion | bytes 8388608 | tf_op jit(solution)/shard_map/slice | solution.py:139
  22.4 39.6 %all-gather.3.cloned.1.call-done = bf16[2048,512]{0,1:T(8,128)(2,1)} async-done(((bf16[256,512]{0,1:T(8,128)(2,1)}), bf16[2048,512]{0,1:T(8,128)(2,1)}) %all-gather.3.cloned.1.call-update) | async-done | bytes 2097168 | tf_op jit(solution)/shard_map/all_gather | solution.py:135
  68.0 1.1 slice_dynamic-update-slice_fusion
  69.1 3.7 %collective-permute-start.2 = (bf16[2048,512]{0,1:T(8,128)(2,1)S(1)}, bf16[2048,512]{0,1:T(8,128)(2,1)S(1)}, u32[]{:S(2)}, u32[]{:S(2)}) collective-permute-start(bf16[2048,512]{0,1:T(8,128)(2,1)S(1)} %slice_dynamic-update-slice_fusion), channel_id=1, source_target_pairs={{0,16},{1,17},{2,18},{3,19},{4,20},{5,21},{6,22},{7,23},{8,24},{9,... | collective-permute-start | bytes 6291464 | tf_op jit(solution)/shard_map/ppermute | solution.py:99
  72.8 45.8 %collective-permute-done.2 = bf16[2048,512]{0,1:T(8,128)(2,1)S(1)} collective-permute-done((bf16[2048,512]{0,1:T(8,128)(2,1)S(1)}, bf16[2048,512]{0,1:T(8,128)(2,1)S(1)}, u32[]{:S(2)}, u32[]{:S(2)}) %collective-permute-start.2) | collective-permute-done | bytes 2097184 | tf_op jit(solution)/shard_map/ppermute | solution.py:99
  118.6 2.6 pad_maximum_fusion.1
  122.2 7.1 %collective-permute-done.3 = bf16[2048,1024]{0,1:T(8,128)(2,1)} collective-permute-done((bf16[2048,1024]{0,1:T(8,128)(2,1)}, bf16[2048,1024]{0,1:T(8,128)(2,1)}, u32[]{:S(2)}, u32[]{:S(2)}) %collective-permute-start.3) | collective-permute-done | bytes 4194336 | tf_op jit(solution)/shard_map/ppermute | solution.py:99
  129.3 4.1 %pad_maximum_fusion = bf16[2048,2048]{0,1:T(8,128)(2,1)S(1)} fusion(bf16[2048,1024]{0,1:T(8,128)(2,1)} %collective-permute-done.3, bf16[2048,512]{0,1:T(8,128)(2,1)} %copy-done.4, bf16[2048,512]{0,1:T(8,128)(2,1)S(1)} %slice_dynamic-update-slice_fusion), kind=kLoop, calls=%fused_computation | loop fusion | flops 25165824 | bytes 16777216 | tf_op jit(solution)/shard_map/concatenate | solution.py:152
  133.4 1.2 bitcast_dynamic-update-slice_fusion.7
  134.6 1.7 bitcast_dynamic-update-slice_fusion.6
  136.4 1.2 bitcast_dynamic-update-slice_fusion.5
  137.6 1.1 bitcast_dynamic-update-slice_fusion.4
  138.7 1.1 bitcast_dynamic-update-slice_fusion.3
  139.8 1.1 bitcast_dynamic-update-slice_fusion.2
  140.9 1.1 bitcast_dynamic-update-slice_fusion.1
  142.0 1.2 bitcast_dynamic-update-slice_fusion
  143.1 11.7 %all-gather.5.cloned.1.call-done = bf16[4096,1024]{1,0:T(8,128)(2,1)} async-done(((bf16[512,1024]{1,0:T(8,128)(2,1)}), bf16[4096,1024]{1,0:T(8,128)(2,1)}) %all-gather.5.cloned.1.call-update) | async-done | bytes 8388624 | tf_op jit(solution)/shard_map/all_gather | solution.py:135
  154.8 10.1 %half_rotation.2 = bf16[2048,512]{1,0:T(8,128)(2,1)} custom-call(s32[4]{0:T(128)S(1)} %pad_add_fusion.places_ref, bf16[8,512,1024]{2,1,0:T(8,128)(2,1)} %bitcast.57, bf16[2048,512]{1,0:T(8,128)(2,1)} %get-tuple-element.31.right_ref), custom_call_target="tpu_custom_call" | custom-call | flops 4294967296 | bytes 12582912 | tf_op jit(solution)/shard_map/half_rotation/pallas_call | solution.py:64
  164.9 3.7 %fusion.34 = bf16[512,512]{1,0:T(8,128)(2,1)S(1)} fusion(bf16[2048,512]{1,0:T(8,128)(2,1)} %half_rotation.2, bf16[2048,2048]{0,1:T(8,128)(2,1)} %copy-done, s32[]{:T(128)S(6)} %select_n.91), kind=kOutput, calls=%fused_computation.35 | convolution fusion | flops 1074003968 | bytes 4718596 | tf_op jit(solution)/shard_map/dot_general | solution.py:25
  168.7 2.9 fusion.28
  171.8 1.5 collective-permute-start.5
  173.3 10.4 %half_rotation.3 = bf16[2048,512]{1,0:T(8,128)(2,1)} custom-call(s32[4]{0:T(128)S(1)} %pad_add_fusion.places_ref, bf16[8,512,1024]{2,1,0:T(8,128)(2,1)} %bitcast.58, bf16[2048,512]{1,0:T(8,128)(2,1)} %get-tuple-element.37.right_ref), custom_call_target="tpu_custom_call" | custom-call | flops 4294967296 | bytes 12582912 | tf_op jit(solution)/shard_map/half_rotation/pallas_call | solution.py:64
  183.7 3.0 fusion.37
  187.3 1.3 fusion.31
  188.6 1.3 fusion.22
  190.1 1.3 fusion.16
  191.4 1.5 fusion.25
  194.3 1.9 divide_convert_fusion.1
  196.1 1.5 collective-permute-start.10
  197.6 1.3 fusion.19
  199.0 9.5 %collective-permute-done.9 = bf16[512,512]{1,0:T(8,128)(2,1)S(1)} collective-permute-done((bf16[512,512]{1,0:T(8,128)(2,1)S(1)}, bf16[512,512]{1,0:T(8,128)(2,1)S(1)}, u32[]{:S(2)}, u32[]{:S(2)}) %collective-permute-start.9) | collective-permute-done | bytes 524320 | tf_op jit(solution)/shard_map/ppermute | solution.py:99
  208.5 2.2 divide_convert_fusion
  211.1 8.7 %collective-permute-done.10 = bf16[512,512]{1,0:T(8,128)(2,1)} collective-permute-done((bf16[512,512]{1,0:T(8,128)(2,1)S(1)}, bf16[512,512]{1,0:T(8,128)(2,1)}, u32[]{:S(2)}, u32[]{:S(2)}) %collective-permute-start.10) | collective-permute-done | bytes 524320 | tf_op jit(solution)/shard_map/ppermute | solution.py:99
  219.8 1.1 select_bitcast_fusion.7
  222.0 8.1 %collective-permute-done.12 = bf16[512,512]{1,0:T(8,128)(2,1)} collective-permute-done((bf16[512,512]{1,0:T(8,128)(2,1)S(1)}, bf16[512,512]{1,0:T(8,128)(2,1)}, u32[]{:S(2)}, u32[]{:S(2)}) %collective-permute-start.12) | collective-permute-done | bytes 524320 | tf_op jit(solution)/shard_map/ppermute | solution.py:99
  230.2 1.3 select_bitcast_fusion.5
  231.4 1.1 pad_maximum_fusion.8
  232.5 1.4 select_bitcast_fusion.3
  234.2 1.3 collective-permute-done.13
  235.5 1.4 select_bitcast_fusion.1
  237.9 11.3 %convolution_convert_fusion.1 = bf16[2048,1024]{1,0:T(8,128)(2,1)S(1)} fusion(bf16[2048,2048]{1,0:T(8,128)(2,1)} %bitcast_dynamic-update-slice_fusion, bf16[2048,1024]{1,0:T(8,128)(2,1)S(1)} %pad_maximum_fusion.2), kind=kOutput, calls=%fused_computation.4 | convolution fusion | flops 8592031744 | bytes 16777216 | tf_op jit(solution)/shard_map/dot_general | solution.py:25
  249.2 11.0 %convolution_convert_fusion = bf16[2048,2048]{1,0:T(8,128)(2,1)} fusion(bf16[2048,1024]{1,0:T(8,128)(2,1)S(1)} %convolution_convert_fusion.1, bf16[2048,1024]{1,0:T(8,128)(2,1)S(1)} %copy-done.3), kind=kOutput, calls=%fused_computation.1 | convolution fusion | flops 8594128896 | bytes 16777216 | tf_op jit(solution)/shard_map/dot_general | solution.py:29
  260.2 1.2 copy-done.5
  261.7 3.7 %pad_maximum_fusion.3 = (f32[512,1024]{1,0:T(8,128)}, f32[512,1024]{1,0:T(8,128)}) fusion(f32[512,512]{1,0:T(8,128)} %get-tuple-element.49, f32[512,512]{1,0:T(8,128)S(1)} %get-tuple-element.51, f32[512,512]{1,0:T(8,128)S(1)} %copy-done.6, f32[512,512]{1,0:T(8,128)S(1)} %copy-done.5), kind=kLoop, calls=%fused_computation.5 | loop fusion | flops 1048576 | bytes 8388608 | tf_op jit(solution)/shard_map/concatenate | solution.py:231
  265.5 82.6 %reduce-scatter.2.cloned.1.call-done = bf16[256,2048]{1,0:T(8,128)(2,1)} async-done(((bf16[2048,2048]{1,0:T(8,128)(2,1)}), bf16[256,2048]{1,0:T(8,128)(2,1)}) %reduce-scatter.2.cloned.1.call-update) | async-done | bytes 1048592 | tf_op jit(solution)/shard_map/reduce_scatter | solution.py:229
  (73 shorter events, 13.2 us)
Async XLA Ops:
  7.2 54.9 %all-gather.3.cloned.1.call-start = ((), (), s32[]{:S(2)}) async-start(), calls=%async_computation.1 | async-start | bytes 2359296 | tf_op jit(solution)/shard_map/all_gather | solution.py:135
  9.0 145.8 %all-gather.5.cloned.1.call-start = ((), (), s32[]{:S(2)}) async-start(), calls=%async_computation.2 | async-start | bytes 9437184 | tf_op jit(solution)/shard_map/all_gather | solution.py:135
  9.1 12.6 %collective-permute-start = (bf16[512,1024]{1,0:T(8,128)(2,1)}, bf16[512,1024]{1,0:T(8,128)(2,1)S(1)}, u32[]{:S(2)}, u32[]{:S(2)}) collective-permute-start(bf16[512,1024]{1,0:T(8,128)(2,1)} %param.5), channel_id=1, source_target_pairs={{0,0},{1,1},{2,2},{3,3},{4,4},{5,5},{6,6},{7,7},{8,14},{9,15},{10,... | collective-permute-start | bytes 3145736 | tf_op jit(solution)/shard_map/ppermute | solution.py:99
  21.7 0.7 collective-permute-start.1
  22.4 39.6 %copy-start.12 = (bf16[512,1024]{1,0:T(8,128)(2,1)}, bf16[512,1024]{1,0:T(8,128)(2,1)S(1)}, u32[]{:S(2)}) copy-start(bf16[512,1024]{1,0:T(8,128)(2,1)S(1)} %collective-permute-done.1) | copy-start | bytes 3145732
  62.1 286.0 %reduce-scatter.2.cloned.1.call-start = ((), (), s32[]{:S(2)}) async-start(), calls=%async_computation.3 | async-start | bytes 9437184 | tf_op jit(solution)/shard_map/reduce_scatter | solution.py:229
  69.1 49.4 %collective-permute-start.2 = (bf16[2048,512]{0,1:T(8,128)(2,1)S(1)}, bf16[2048,512]{0,1:T(8,128)(2,1)S(1)}, u32[]{:S(2)}, u32[]{:S(2)}) collective-permute-start(bf16[2048,512]{0,1:T(8,128)(2,1)S(1)} %slice_dynamic-update-slice_fusion), channel_id=1, source_target_pairs={{0,16},{1,17},{2,18},{3,19},{4,20},{5,21},{6,22},{7,23},{8,24},{9,... | collective-permute-start | bytes 6291464 | tf_op jit(solution)/shard_map/ppermute | solution.py:99
  118.6 2.6 copy-start.4
  121.2 8.1 %collective-permute-start.3 = (bf16[2048,1024]{0,1:T(8,128)(2,1)}, bf16[2048,1024]{0,1:T(8,128)(2,1)}, u32[]{:S(2)}, u32[]{:S(2)}) collective-permute-start(bf16[2048,1024]{0,1:T(8,128)(2,1)} %pad_maximum_fusion.1), channel_id=1, source_target_pairs={{0,8},{1,9},{2,10},{3,11},{4,12},{5,13},{6,14},{7,15},{8,0},{9,1},... | collective-permute-start | bytes 12582920 | tf_op jit(solution)/shard_map/ppermute | solution.py:99
  133.4 8.5 %copy-start = (bf16[2048,2048]{0,1:T(8,128)(2,1)}, bf16[2048,2048]{0,1:T(8,128)(2,1)S(1)}, u32[]{:S(2)}) copy-start(bf16[2048,2048]{0,1:T(8,128)(2,1)S(1)} %pad_maximum_fusion) | copy-start | bytes 25165828
  164.9 3.8 %copy-start.1 = (bf16[2048,512]{1,0:T(8,128)(2,1)S(1)}, bf16[2048,512]{1,0:T(8,128)(2,1)}, u32[]{:S(2)}) copy-start(bf16[2048,512]{1,0:T(8,128)(2,1)} %half_rotation.2) | copy-start | bytes 6291460
  168.6 3.0 collective-permute-start.4
  171.6 12.1 %slice-start = ((s8[8388608]{0:T(1024)(128)(4,1)}), s8[4194304]{0:T(1024)(128)(4,1)S(1)}, s32[]{:S(2)}) async-start(s8[8388608]{0:T(1024)(128)(4,1)} %bitcast.53), calls=%async_computation.4 | async-start | bytes 8388608
  171.8 11.9 %slice-start.1 = ((s8[8388608]{0:T(1024)(128)(4,1)}), s8[4194304]{0:T(1024)(128)(4,1)S(1)}, s32[]{:S(2)}) async-start(s8[8388608]{0:T(1024)(128)(4,1)} %bitcast.53), calls=%async_computation.5 | async-start | bytes 8388608
  171.8 16.8 %collective-permute-start.5 = (bf16[512,512]{1,0:T(8,128)(2,1)S(1)}, bf16[512,512]{1,0:T(8,128)(2,1)S(1)}, u32[]{:S(2)}, u32[]{:S(2)}) collective-permute-start(bf16[512,512]{1,0:T(8,128)(2,1)S(1)} %add_convert_fusion.1), channel_id=1, source_target_pairs={{0,16},{1,17},{2,18},{3,19},{4,20},{5,21},{6,22},{7,23},{8,24},{9,... | collective-permute-start | bytes 1572872 | tf_op jit(solution)/shard_map/ppermute | solution.py:99
  183.7 3.6 %copy-start.2 = (bf16[2048,512]{1,0:T(8,128)(2,1)S(1)}, bf16[2048,512]{1,0:T(8,128)(2,1)}, u32[]{:S(2)}) copy-start(bf16[2048,512]{1,0:T(8,128)(2,1)} %half_rotation.3) | copy-start | bytes 6291460
  186.8 6.7 %collective-permute-start.8 = (bf16[512,512]{1,0:T(8,128)(2,1)S(1)}, bf16[512,512]{1,0:T(8,128)(2,1)S(1)}, u32[]{:S(2)}, u32[]{:S(2)}) collective-permute-start(bf16[512,512]{1,0:T(8,128)(2,1)S(1)} %fusion.37), channel_id=1, source_target_pairs={{0,8},{1,9},{2,10},{3,11},{4,12},{5,13},{6,14},{7,15},{8,0},{9,1},... | collective-permute-start | bytes 1572872 | tf_op jit(solution)/shard_map/ppermute | solution.py:99
  188.6 1.3 copy-start.13
  190.0 4.3 %collective-permute-start.6 = (bf16[512,512]{1,0:T(8,128)(2,1)S(1)}, bf16[512,512]{1,0:T(8,128)(2,1)S(1)}, u32[]{:S(2)}, u32[]{:S(2)}) collective-permute-start(bf16[512,512]{1,0:T(8,128)(2,1)S(1)} %fusion.22), channel_id=1, source_target_pairs={{0,8},{1,9},{2,10},{3,11},{4,12},{5,13},{6,14},{7,15},{8,0},{9,1},... | collective-permute-start | bytes 1572872 | tf_op jit(solution)/shard_map/ppermute | solution.py:99
  191.4 2.8 copy-start.7
  191.4 2.8 copy-start.8
  191.4 2.8 copy-start.14
  193.0 15.5 %collective-permute-start.7 = (bf16[512,512]{1,0:T(8,128)(2,1)S(1)}, bf16[512,512]{1,0:T(8,128)(2,1)S(1)}, u32[]{:S(2)}, u32[]{:S(2)}) collective-permute-start(bf16[512,512]{1,0:T(8,128)(2,1)S(1)} %fusion.25), channel_id=1, source_target_pairs={{0,8},{1,9},{2,10},{3,11},{4,12},{5,13},{6,14},{7,15},{8,0},{9,1},... | collective-permute-start | bytes 1572872 | tf_op jit(solution)/shard_map/ppermute | solution.py:99
  193.6 14.8 %collective-permute-start.9 = (bf16[512,512]{1,0:T(8,128)(2,1)S(1)}, bf16[512,512]{1,0:T(8,128)(2,1)S(1)}, u32[]{:S(2)}, u32[]{:S(2)}) collective-permute-start(bf16[512,512]{1,0:T(8,128)(2,1)S(1)} %add_convert_fusion), channel_id=1, source_target_pairs={{0,16},{1,17},{2,18},{3,19},{4,20},{5,21},{6,22},{7,23},{8,24},{9,... | collective-permute-start | bytes 1572872 | tf_op jit(solution)/shard_map/ppermute | solution.py:99
  196.1 2.8 copy-start.9
  196.1 23.7 %collective-permute-start.10 = (bf16[512,512]{1,0:T(8,128)(2,1)S(1)}, bf16[512,512]{1,0:T(8,128)(2,1)}, u32[]{:S(2)}, u32[]{:S(2)}) collective-permute-start(bf16[512,512]{1,0:T(8,128)(2,1)S(1)} %get-tuple-element.50), channel_id=1, source_target_pairs={{0,16},{1,17},{2,18},{3,19},{4,20},{5,21},{6,22},{7,23},{8,24},{9,... | collective-permute-start | bytes 1572872 | tf_op jit(solution)/shard_map/ppermute | solution.py:99
  199.0 20.9 %copy-start.10 = (bf16[512,512]{1,0:T(8,128)(2,1)S(1)}, bf16[512,512]{1,0:T(8,128)(2,1)}, u32[]{:S(2)}) copy-start(bf16[512,512]{1,0:T(8,128)(2,1)} %copy-done.9) | copy-start | bytes 1572868
  210.7 11.4 %copy-start.11 = (bf16[512,512]{1,0:T(8,128)(2,1)}, bf16[512,512]{1,0:T(8,128)(2,1)S(1)}, u32[]{:S(2)}) copy-start(bf16[512,512]{1,0:T(8,128)(2,1)S(1)} %get-tuple-element.47) | copy-start | bytes 1572868
  210.7 19.5 %collective-permute-start.12 = (bf16[512,512]{1,0:T(8,128)(2,1)S(1)}, bf16[512,512]{1,0:T(8,128)(2,1)}, u32[]{:S(2)}, u32[]{:S(2)}) collective-permute-start(bf16[512,512]{1,0:T(8,128)(2,1)S(1)} %get-tuple-element.47), channel_id=1, source_target_pairs={{0,16},{1,17},{2,18},{3,19},{4,20},{5,21},{6,22},{7,23},{8,24},{9,... | collective-permute-start | bytes 1572872 | tf_op jit(solution)/shard_map/ppermute | solution.py:99
  222.0 10.5 %collective-permute-start.11 = (bf16[2,512,512]{2,1,0:T(8,128)(2,1)}, bf16[2,512,512]{2,1,0:T(8,128)(2,1)}, u32[]{:S(2)}, u32[]{:S(2)}) collective-permute-start(bf16[2,512,512]{2,1,0:T(8,128)(2,1)} %pad_maximum_fusion.7), channel_id=1, source_target_pairs={{0,8},{1,9},{2,10},{3,11},{4,12},{5,13},{6,14},{7,15},{8,0},{9,1},... | collective-permute-start | bytes 3145736 | tf_op jit(solution)/shard_map/ppermute | solution.py:99
  232.5 3.0 collective-permute-start.13
  237.9 11.4 %copy-start.3 = (bf16[2048,1024]{1,0:T(8,128)(2,1)S(1)}, bf16[2048,1024]{1,0:T(8,128)(2,1)}, u32[]{:S(2)}) copy-start(bf16[2048,1024]{1,0:T(8,128)(2,1)} %convert.4) | copy-start | bytes 12582916
  260.2 1.2 copy-start.5
  260.2 1.5 copy-start.6
Sparse Core Ops, SparseCore 0:
  9.5 52.5 all-gather.2
  64.1 90.5 all-gather.4
  260.4 87.6 reduce-scatter.1

commit v14 on v11

--- a/solution.py
+++ b/solution.py
@@ -29,37 +29,40 @@
     return lax.dot_general(a, b, (((1,), (1,)), ((), ())), preferred_element_type=jnp.float32)
 
 
-def half_rotation(gathered, right, places, nz):
+def half_rotation(gathered, right, places, nz, parts):
     count, rows, cols = gathered.shape
     nx = count // nz
-    width = right.shape[1]
+    width = right.shape[1] // parts
 
     def kernel(places_ref, *refs):
-        blocks, right_ref, out = refs[:nx], refs[nx], refs[nx + 1]
-        total = matmul(blocks[0][...], right_ref[:cols])
-        for i in range(1, nx):
-            total += matmul(blocks[i][...], right_ref[i * cols : (i + 1) * cols])
-        out[...] = total.astype(out.dtype)
+        blocks, right_ref, outs = refs[:nx], refs[nx], refs[nx + 1 :]
+        for j, out in enumerate(outs):
+            total = matmul(blocks[0][...], right_ref[:cols, j * width : (j + 1) * width])
+            for i in range(1, nx):
+                total += matmul(blocks[i][...], right_ref[i * cols : (i + 1) * cols, j * width : (j + 1) * width])
+            out[...] = total.astype(out.dtype)
 
     def block_of(i):
         if i % 2 == 0:
             return pl.BlockSpec((None, rows, cols), lambda k, p: (i * nz + k, 0, 0))
         return pl.BlockSpec((None, rows, cols), lambda k, p: (i * nz + nz - 1 - k, 0, 0))
 
-    out = jax.ShapeDtypeStruct((nz * rows, width), low)
-    size = sum(a.size * a.dtype.itemsize for a in (gathered, right, out))
+    outs = [jax.ShapeDtypeStruct((nz * rows, width), low)] * parts
+    size = sum(a.size * a.dtype.itemsize for a in (gathered, right, *outs))
     return pl.pallas_call(
         kernel,
-        out_shape=out,
+        out_shape=outs,
         grid_spec=pltpu.PrefetchScalarGridSpec(
             num_scalar_prefetch=1,
             grid=(nz,),
             in_specs=[block_of(i) for i in range(nx)]
             + [pl.BlockSpec(right.shape, lambda k, p: (0, 0), pipeline_mode=pl.Buffered(1))],
-            out_specs=pl.BlockSpec((rows, width), lambda k, p: (p[k], 0)),
+            out_specs=[pl.BlockSpec((rows, width), lambda k, p: (p[k], 0))] * parts,
         ),
         compiler_params=pltpu.CompilerParams(vmem_limit_bytes=VMEM_BYTES),
-        cost_estimate=pl.CostEstimate(flops=2 * gathered.size * width, bytes_accessed=size, transcendentals=0),
+        cost_estimate=pl.CostEstimate(
+            flops=2 * gathered.size * right.shape[1], bytes_accessed=size, transcendentals=0
+        ),
         name="half_rotation",
     )(places, *([gathered] * nx), right)
 
@@ -117,12 +120,11 @@
 
     width = ff_block // COL_PARTS
     right = right_basis.astype(low)
-    right_parts = [right_basis[:, j * width : (j + 1) * width].astype(low) for j in range(COL_PARTS)]
     places = jnp.stack([reversed_bits(unspread(b ^ zz) ^ b) for zz in range(nz)]).astype(jnp.int32)
 
     left_blocks = round_path(left_basis.astype(low).T)
     piece = permute(gradient, lambda bb, zz, xx: (bb, zz ^ spread(bb), xx))
-    piece, right_parts, places = together(piece, right_parts, places)
+    piece, right, places = together(piece, right, places)
     piece = permute(piece, lambda bb, zz, xx: (zz ^ spread(bb), zz, xx))
     piece, left_blocks = together(piece, left_blocks)
     gathered = round_path(piece)
@@ -148,10 +150,9 @@
             values.append(last)
         return values[1].astype(jnp.float32) + move_b(values[0], 1).astype(jnp.float32)
 
-    half, arrived = [], []
+    half = half_rotation(gathered, right, places, nz, COL_PARTS)
+    arrived = []
     for j in range(COL_PARTS):
-        found = gathered if last is None else after(gathered, last)
-        half.append(half_rotation(found, right_parts[j], places, nz))
         away = [lax.optimization_barrier(paired(t, j).astype(low)) for t in first_group]
         last = away[-1]
         if j:

time: 351 us -> 354 us (level)
  waiting for transfers between devices: 222 us -> 234 us
  local copies, waits for them, and re-layouts: 20 us -> 10.1 us
  matrix products: 36.1 us -> 41.6 us
  Pallas kernels: 18.6 us -> 13.7 us
    ppermute x14, waiting for transfers between devices: 79.7 us -> 87.7 us  [permute(): return lax.ppermute(value, ('basis', 'dp'), pairs)]
    convert_element_type x0 -> x1, other arithmetic: none -> 6.03 us  [per_device(): right = right_basis.astype(low)]
    another operation x1 -> x0, other arithmetic: 6.02 us -> none
    unnamed x37 -> x31, local copies, waits for them, and re-layouts: 13.9 us -> 8.61 us
    pallas_call x2 -> x1, Pallas kernels: 18.6 us -> 13.7 us  [half_rotation(): pl.pallas_call(kernel, out_shape=outs, grid_spec=pltpu.PrefetchScalarGrid...]
    slice x1 -> x0, local copies, waits for them, and re-layouts: 4.57 us -> none  [per_device(): right_basis[:, j * width:(j + 1) * width].astype(low)]
  transfers between devices with their start and end apart: 17 -> 17, of which waited for: 8 -> 10; matrix products, arithmetic and copies ran while one was open for 14% -> 13% of each run, Pallas kernels for 3% -> 0%
where the time goes in v14:
time: 354 us; the launch traced here: 353 us
  waiting for transfers between devices  234 us (66%)
  matrix products  41.6 us (12%)
  other arithmetic  25.8 us (7%)
  between operations  14.2 us (4%)
  starting transfers between devices  14 us (4%)
  Pallas kernels  13.7 us (4%)
  local copies, waits for them, and re-layouts  10.1 us (3%)
    ppermute x14, waiting for transfers between devices, permute(): return lax.ppermute(value, ('basis', 'dp'), pairs)  87.7 us
    reduce_scatter x1, waiting for transfers between devices, per_device(): lax.psum_scatter(total, 'dp', scatter_dimension=0, axis_index_groups=[pat...  84.6 us
    all_gather x2, waiting for transfers between devices, round_path(): return lax.all_gather(value, 'dp', axis_index_groups=[path], tiled=True)  61.7 us
    dot_general x9, matrix products, matmul(): lax.dot_general(a, b, (((1,), (0,)), ((), ())), preferred_element_type=jn...  28.2 us
    ppermute x14, starting transfers between devices, permute(): return lax.ppermute(value, ('basis', 'dp'), pairs)  13.9 us
    pallas_call x1, Pallas kernels, half_rotation(): pl.pallas_call(kernel, out_shape=outs, grid_spec=pltpu.PrefetchScalarGrid...  13.7 us
    dot_general x1, matrix products, matmul_nt(): lax.dot_general(a, b, (((1,), (1,)), ((), ())), preferred_element_type=jn...  13.5 us
    concatenate x2, other arithmetic, per_device(): left_t = jnp.concatenate([left_t, move_b(left_t, t)], axis=1)  9.3 us
  transfers between devices with their start and end apart: 17, of which 10 were waited for; matrix products, arithmetic and copies ran while one was open for 13% of the time, Pallas kernels for 0%

profile of v14, /device:TPU:0, one launch (start us, length us, event | category | flops | bytes accessed | tf_op | source)
XLA Modules:
  0.0 353.4 jit_solution(11453963402962719639)
XLA Ops:
  7.2 1.8 convert_bitcast_fusion
  9.1 1.9 collective-permute-start
  10.9 6.0 %convert_element_type.78.refs_2_ = bf16[2048,1024]{1,0:T(8,128)(2,1)} convert(f32[2048,1024]{1,0:T(8,128)} %param.7) | non-fusion elementwise | flops 2097152 | bytes 12582912 | tf_op jit(solution)/shard_map/convert_element_type | solution.py:122
  17.1 0.7 collective-permute-start.1
  17.8 44.3 %all-gather.3.cloned.1.call-done = bf16[2048,512]{0,1:T(8,128)(2,1)} async-done(((bf16[256,512]{0,1:T(8,128)(2,1)}), bf16[2048,512]{0,1:T(8,128)(2,1)}) %all-gather.3.cloned.1.call-update) | async-done | bytes 2097168 | tf_op jit(solution)/shard_map/all_gather | solution.py:119
  62.2 1.0 slice_dynamic-update-slice_fusion.6
  63.1 1.0 slice_dynamic-update-slice_fusion.5
  64.1 1.0 slice_dynamic-update-slice_fusion.4
  65.1 1.0 slice_dynamic-update-slice_fusion.3
  66.1 1.0 slice_dynamic-update-slice_fusion.2
  67.1 1.0 slice_dynamic-update-slice_fusion.1
  68.1 1.1 slice_dynamic-update-slice_fusion
  69.2 4.5 %collective-permute-start.2 = (bf16[2048,512]{0,1:T(8,128)(2,1)S(1)}, bf16[2048,512]{0,1:T(8,128)(2,1)S(1)}, u32[]{:S(2)}, u32[]{:S(2)}) collective-permute-start(bf16[2048,512]{0,1:T(8,128)(2,1)S(1)} %slice_dynamic-update-slice_fusion), channel_id=1, source_target_pairs={{0,16},{1,17},{2,18},{3,19},{4,20},{5,21},{6,22},{7,23},{8,24},{9,... | collective-permute-start | bytes 6291464 | tf_op jit(solution)/shard_map/ppermute | solution.py:83
  73.7 46.1 %collective-permute-done.2 = bf16[2048,512]{0,1:T(8,128)(2,1)S(1)} collective-permute-done((bf16[2048,512]{0,1:T(8,128)(2,1)S(1)}, bf16[2048,512]{0,1:T(8,128)(2,1)S(1)}, u32[]{:S(2)}, u32[]{:S(2)}) %collective-permute-start.2) | collective-permute-done | bytes 2097184 | tf_op jit(solution)/shard_map/ppermute | solution.py:83
  119.8 2.7 pad_maximum_fusion.1
  122.5 0.6 collective-permute-start.3
  123.1 7.1 %collective-permute-done.3 = bf16[2048,1024]{0,1:T(8,128)(2,1)} collective-permute-done((bf16[2048,1024]{0,1:T(8,128)(2,1)}, bf16[2048,1024]{0,1:T(8,128)(2,1)}, u32[]{:S(2)}, u32[]{:S(2)}) %collective-permute-start.3) | collective-permute-done | bytes 4194336 | tf_op jit(solution)/shard_map/ppermute | solution.py:83
  130.2 6.6 %pad_maximum_fusion = bf16[2048,2048]{0,1:T(8,128)(2,1)} fusion(bf16[2048,1024]{0,1:T(8,128)(2,1)} %collective-permute-done.3, bf16[2048,512]{0,1:T(8,128)(2,1)} %copy-done.2, bf16[2048,512]{0,1:T(8,128)(2,1)S(1)} %slice_dynamic-update-slice_fusion), kind=kLoop, calls=%fused_computation | loop fusion | flops 25165824 | bytes 16777216 | tf_op jit(solution)/shard_map/concatenate | solution.py:135
  136.8 17.4 %all-gather.5.cloned.1.call-done = bf16[4096,1024]{1,0:T(8,128)(2,1)} async-done(((bf16[512,1024]{1,0:T(8,128)(2,1)}), bf16[4096,1024]{1,0:T(8,128)(2,1)}) %all-gather.5.cloned.1.call-update) | async-done | bytes 8388624 | tf_op jit(solution)/shard_map/all_gather | solution.py:119
  154.2 13.7 %half_rotation.1 = (bf16[2048,512]{1,0:T(8,128)(2,1)}, bf16[2048,512]{1,0:T(8,128)(2,1)}) custom-call(s32[4]{0:T(128)S(1)} %pad_add_fusion.places_ref, bf16[8,512,1024]{2,1,0:T(8,128)(2,1)} %bitcast.57, bf16[8,512,1024]{2,1,0:T(8,128)(2,1)} %bitcast.58, bf16[2048,1024]{1,0:T(8,128)(2,1)} %convert_element_type.78.refs_2_), custom_call_target="tpu_custom_call" | custom-call | flops 8589934592 | bytes 16777216 | tf_op jit(solution)/shard_map/half_rotation/pallas_call | solution.py:52
  167.9 3.7 %fusion.34 = bf16[512,512]{1,0:T(8,128)(2,1)S(1)} fusion(bf16[2048,512]{1,0:T(8,128)(2,1)} %get-tuple-element.35, bf16[2048,2048]{0,1:T(8,128)(2,1)} %pad_maximum_fusion, s32[]{:T(128)S(6)} %select_n.83), kind=kOutput, calls=%fused_computation.35 | convolution fusion | flops 1074003968 | bytes 4718596 | tf_op jit(solution)/shard_map/dot_general | solution.py:25
  171.7 3.0 fusion.28
  174.9 1.5 collective-permute-start.5
  176.4 3.0 fusion.37
  179.4 0.2 collective-permute-start.8
  179.7 2.9 fusion.31
  182.5 6.7 %collective-permute-done.5 = bf16[512,512]{1,0:T(8,128)(2,1)S(1)} collective-permute-done((bf16[512,512]{1,0:T(8,128)(2,1)S(1)}, bf16[512,512]{1,0:T(8,128)(2,1)S(1)}, u32[]{:S(2)}, u32[]{:S(2)}) %collective-permute-start.5) | collective-permute-done | bytes 524320 | tf_op jit(solution)/shard_map/ppermute | solution.py:83
  189.2 1.3 fusion.22
  190.5 1.3 fusion.16
  191.9 1.3 fusion.25
  193.2 0.5 collective-permute-start.6
  193.9 1.5 collective-permute-start.9
  195.4 1.3 fusion.19
  197.2 1.3 copy-done.4
  198.5 0.6 copy-done.5
  199.1 0.9 divide_convert_fusion.1
  200.0 0.6 collective-permute-start.10
  200.7 8.0 %collective-permute-done.9 = bf16[512,512]{1,0:T(8,128)(2,1)S(1)} collective-permute-done((bf16[512,512]{1,0:T(8,128)(2,1)S(1)}, bf16[512,512]{1,0:T(8,128)(2,1)S(1)}, u32[]{:S(2)}, u32[]{:S(2)}) %collective-permute-start.9) | collective-permute-done | bytes 524320 | tf_op jit(solution)/shard_map/ppermute | solution.py:83
  208.7 1.8 divide_convert_fusion
  210.5 1.5 collective-permute-start.12
  212.1 7.9 %collective-permute-done.10 = bf16[512,512]{1,0:T(8,128)(2,1)S(1)} collective-permute-done((bf16[512,512]{1,0:T(8,128)(2,1)S(1)}, bf16[512,512]{1,0:T(8,128)(2,1)S(1)}, u32[]{:S(2)}, u32[]{:S(2)}) %collective-permute-start.10) | collective-permute-done | bytes 524320 | tf_op jit(solution)/shard_map/ppermute | solution.py:83
  220.2 10.1 %collective-permute-done.12 = bf16[512,512]{1,0:T(8,128)(2,1)S(1)} collective-permute-done((bf16[512,512]{1,0:T(8,128)(2,1)S(1)}, bf16[512,512]{1,0:T(8,128)(2,1)S(1)}, u32[]{:S(2)}, u32[]{:S(2)}) %collective-permute-start.12) | collective-permute-done | bytes 524320 | tf_op jit(solution)/shard_map/ppermute | solution.py:83
  231.5 1.8 collective-permute-done.13
  233.8 0.8 pad_maximum_fusion.2
  234.6 10.4 %convolution_convert_fusion.1 = bf16[2048,1024]{1,0:T(8,128)(2,1)} fusion(bf16[2048,2048]{1,0:T(8,128)(2,1)S(1)} %bitcast_dynamic-update-slice_fusion, bf16[2048,1024]{1,0:T(8,128)(2,1)S(1)} %pad_maximum_fusion.2), kind=kOutput, calls=%fused_computation.4 | convolution fusion | flops 8592031744 | bytes 16777216 | tf_op jit(solution)/shard_map/dot_general | solution.py:25
  245.1 13.5 %convolution_convert_fusion = bf16[2048,2048]{1,0:T(8,128)(2,1)} fusion(bf16[2048,1024]{1,0:T(8,128)(2,1)} %convolution_convert_fusion.1, bf16[2048,1024]{1,0:T(8,128)(2,1)S(1)} %copy-done.3), kind=kOutput, calls=%fused_computation.1 | convolution fusion | flops 8594128896 | bytes 16777216 | tf_op jit(solution)/shard_map/dot_general | solution.py:29
  258.5 3.7 %pad_maximum_fusion.3 = (f32[512,1024]{1,0:T(8,128)}, f32[512,1024]{1,0:T(8,128)}) fusion(f32[512,512]{1,0:T(8,128)} %get-tuple-element.49, f32[512,512]{1,0:T(8,128)S(1)} %get-tuple-element.51, f32[512,512]{1,0:T(8,128)S(1)} %get-tuple-element.48, f32[512,512]{1,0:T(8,128)S(1)} %get-tuple-element.52), kind=kLoop, calls=%fused_computation.5 | loop fusion | flops 1048576 | bytes 8388608 | tf_op jit(solution)/shard_map/concatenate | solution.py:215
  262.3 84.6 %reduce-scatter.2.cloned.1.call-done = bf16[256,2048]{1,0:T(8,128)(2,1)} async-done(((bf16[2048,2048]{1,0:T(8,128)(2,1)}), bf16[256,2048]{1,0:T(8,128)(2,1)}) %reduce-scatter.2.cloned.1.call-update) | async-done | bytes 1048592 | tf_op jit(solution)/shard_map/reduce_scatter | solution.py:213
  (55 shorter events, 3.1 us)
Async XLA Ops:
  7.2 54.9 %all-gather.3.cloned.1.call-start = ((), (), s32[]{:S(2)}) async-start(), calls=%async_computation.1 | async-start | bytes 2359296 | tf_op jit(solution)/shard_map/all_gather | solution.py:119
  9.0 145.2 %all-gather.5.cloned.1.call-start = ((), (), s32[]{:S(2)}) async-start(), calls=%async_computation.2 | async-start | bytes 9437184 | tf_op jit(solution)/shard_map/all_gather | solution.py:119
  9.1 8.0 %collective-permute-start = (bf16[512,1024]{1,0:T(8,128)(2,1)}, bf16[512,1024]{1,0:T(8,128)(2,1)S(1)}, u32[]{:S(2)}, u32[]{:S(2)}) collective-permute-start(bf16[512,1024]{1,0:T(8,128)(2,1)} %param.5), channel_id=1, source_target_pairs={{0,0},{1,1},{2,2},{3,3},{4,4},{5,5},{6,6},{7,7},{8,14},{9,15},{10,... | collective-permute-start | bytes 3145736 | tf_op jit(solution)/shard_map/ppermute | solution.py:83
  17.1 0.7 collective-permute-start.1
  17.8 44.3 %copy-start.6 = (bf16[512,1024]{1,0:T(8,128)(2,1)}, bf16[512,1024]{1,0:T(8,128)(2,1)S(1)}, u32[]{:S(2)}) copy-start(bf16[512,1024]{1,0:T(8,128)(2,1)S(1)} %collective-permute-done.1) | copy-start | bytes 3145732
  62.1 284.8 %reduce-scatter.2.cloned.1.call-start = ((), (), s32[]{:S(2)}) async-start(), calls=%async_computation.3 | async-start | bytes 9437184 | tf_op jit(solution)/shard_map/reduce_scatter | solution.py:213
  69.2 50.6 %collective-permute-start.2 = (bf16[2048,512]{0,1:T(8,128)(2,1)S(1)}, bf16[2048,512]{0,1:T(8,128)(2,1)S(1)}, u32[]{:S(2)}, u32[]{:S(2)}) collective-permute-start(bf16[2048,512]{0,1:T(8,128)(2,1)S(1)} %slice_dynamic-update-slice_fusion), channel_id=1, source_target_pairs={{0,16},{1,17},{2,18},{3,19},{4,20},{5,21},{6,22},{7,23},{8,24},{9,... | collective-permute-start | bytes 6291464 | tf_op jit(solution)/shard_map/ppermute | solution.py:83
  119.8 2.7 copy-start.2
  122.5 7.7 %collective-permute-start.3 = (bf16[2048,1024]{0,1:T(8,128)(2,1)}, bf16[2048,1024]{0,1:T(8,128)(2,1)}, u32[]{:S(2)}, u32[]{:S(2)}) collective-permute-start(bf16[2048,1024]{0,1:T(8,128)(2,1)} %pad_maximum_fusion.1), channel_id=1, source_target_pairs={{0,8},{1,9},{2,10},{3,11},{4,12},{5,13},{6,14},{7,15},{8,0},{9,1},... | collective-permute-start | bytes 12582920 | tf_op jit(solution)/shard_map/ppermute | solution.py:83
  167.9 3.8 %copy-start.1 = (bf16[2048,512]{1,0:T(8,128)(2,1)S(1)}, bf16[2048,512]{1,0:T(8,128)(2,1)}, u32[]{:S(2)}) copy-start(bf16[2048,512]{1,0:T(8,128)(2,1)} %get-tuple-element.35) | copy-start | bytes 6291460
  171.5 3.2 collective-permute-start.4
  171.7 4.7 %copy-start = (bf16[2048,512]{1,0:T(8,128)(2,1)S(1)}, bf16[2048,512]{1,0:T(8,128)(2,1)}, u32[]{:S(2)}) copy-start(bf16[2048,512]{1,0:T(8,128)(2,1)} %get-tuple-element.39) | copy-start | bytes 6291460
  171.7 17.5 %slice-start = ((s8[8388608]{0:T(1024)(128)(4,1)}), s8[4194304]{0:T(1024)(128)(4,1)S(1)}, s32[]{:S(2)}) async-start(s8[8388608]{0:T(1024)(128)(4,1)} %bitcast.53), calls=%async_computation.4 | async-start | bytes 8388608
  174.9 14.3 %collective-permute-start.5 = (bf16[512,512]{1,0:T(8,128)(2,1)S(1)}, bf16[512,512]{1,0:T(8,128)(2,1)S(1)}, u32[]{:S(2)}, u32[]{:S(2)}) collective-permute-start(bf16[512,512]{1,0:T(8,128)(2,1)S(1)} %add_convert_fusion.1), channel_id=1, source_target_pairs={{0,16},{1,17},{2,18},{3,19},{4,20},{5,21},{6,22},{7,23},{8,24},{9,... | collective-permute-start | bytes 1572872 | tf_op jit(solution)/shard_map/ppermute | solution.py:83
  176.4 12.8 %slice-start.1 = ((s8[8388608]{0:T(1024)(128)(4,1)}), s8[4194304]{0:T(1024)(128)(4,1)S(1)}, s32[]{:S(2)}) async-start(s8[8388608]{0:T(1024)(128)(4,1)} %bitcast.53), calls=%async_computation.5 | async-start | bytes 8388608
  179.4 14.3 %collective-permute-start.8 = (bf16[512,512]{1,0:T(8,128)(2,1)S(1)}, bf16[512,512]{1,0:T(8,128)(2,1)S(1)}, u32[]{:S(2)}, u32[]{:S(2)}) collective-permute-start(bf16[512,512]{1,0:T(8,128)(2,1)S(1)} %fusion.37), channel_id=1, source_target_pairs={{0,8},{1,9},{2,10},{3,11},{4,12},{5,13},{6,14},{7,15},{8,0},{9,1},... | collective-permute-start | bytes 1572872 | tf_op jit(solution)/shard_map/ppermute | solution.py:83
  193.1 15.6 %collective-permute-start.7 = (bf16[512,512]{1,0:T(8,128)(2,1)S(1)}, bf16[512,512]{1,0:T(8,128)(2,1)S(1)}, u32[]{:S(2)}, u32[]{:S(2)}) collective-permute-start(bf16[512,512]{1,0:T(8,128)(2,1)S(1)} %fusion.25), channel_id=1, source_target_pairs={{0,8},{1,9},{2,10},{3,11},{4,12},{5,13},{6,14},{7,15},{8,0},{9,1},... | collective-permute-start | bytes 1572872 | tf_op jit(solution)/shard_map/ppermute | solution.py:83
  193.2 4.0 %collective-permute-start.6 = (bf16[512,512]{1,0:T(8,128)(2,1)S(1)}, bf16[512,512]{1,0:T(8,128)(2,1)S(1)}, u32[]{:S(2)}, u32[]{:S(2)}) collective-permute-start(bf16[512,512]{1,0:T(8,128)(2,1)S(1)} %fusion.22), channel_id=1, source_target_pairs={{0,8},{1,9},{2,10},{3,11},{4,12},{5,13},{6,14},{7,15},{8,0},{9,1},... | collective-permute-start | bytes 1572872 | tf_op jit(solution)/shard_map/ppermute | solution.py:83
  193.9 14.8 %collective-permute-start.9 = (bf16[512,512]{1,0:T(8,128)(2,1)S(1)}, bf16[512,512]{1,0:T(8,128)(2,1)S(1)}, u32[]{:S(2)}, u32[]{:S(2)}) collective-permute-start(bf16[512,512]{1,0:T(8,128)(2,1)S(1)} %add_convert_fusion), channel_id=1, source_target_pairs={{0,16},{1,17},{2,18},{3,19},{4,20},{5,21},{6,22},{7,23},{8,24},{9,... | collective-permute-start | bytes 1572872 | tf_op jit(solution)/shard_map/ppermute | solution.py:83
  196.9 1.6 copy-start.4
  196.9 2.2 copy-start.5
  200.0 19.9 %collective-permute-start.10 = (bf16[512,512]{1,0:T(8,128)(2,1)S(1)}, bf16[512,512]{1,0:T(8,128)(2,1)S(1)}, u32[]{:S(2)}, u32[]{:S(2)}) collective-permute-start(bf16[512,512]{1,0:T(8,128)(2,1)S(1)} %get-tuple-element.50), channel_id=1, source_target_pairs={{0,16},{1,17},{2,18},{3,19},{4,20},{5,21},{6,22},{7,23},{8,24},{9,... | collective-permute-start | bytes 1572872 | tf_op jit(solution)/shard_map/ppermute | solution.py:83
  210.5 19.8 %collective-permute-start.12 = (bf16[512,512]{1,0:T(8,128)(2,1)S(1)}, bf16[512,512]{1,0:T(8,128)(2,1)S(1)}, u32[]{:S(2)}, u32[]{:S(2)}) collective-permute-start(bf16[512,512]{1,0:T(8,128)(2,1)S(1)} %get-tuple-element.47), channel_id=1, source_target_pairs={{0,16},{1,17},{2,18},{3,19},{4,20},{5,21},{6,22},{7,23},{8,24},{9,... | collective-permute-start | bytes 1572872 | tf_op jit(solution)/shard_map/ppermute | solution.py:83
  220.1 10.9 %collective-permute-start.11 = (bf16[2,512,512]{2,1,0:T(8,128)(2,1)S(1)}, bf16[2,512,512]{2,1,0:T(8,128)(2,1)S(1)}, u32[]{:S(2)}, u32[]{:S(2)}) collective-permute-start(bf16[2,512,512]{2,1,0:T(8,128)(2,1)S(1)} %pad_maximum_fusion.7), channel_id=1, source_target_pairs={{0,8},{1,9},{2,10},{3,11},{4,12},{5,13},{6,14},{7,15},{8,0},{9,1},... | collective-permute-start | bytes 3145736 | tf_op jit(solution)/shard_map/ppermute | solution.py:83
  230.6 2.7 collective-permute-start.13
  234.6 10.4 %copy-start.3 = (bf16[2048,1024]{1,0:T(8,128)(2,1)S(1)}, bf16[2048,1024]{1,0:T(8,128)(2,1)}, u32[]{:S(2)}) copy-start(bf16[2048,1024]{1,0:T(8,128)(2,1)} %convert_element_type.78.refs_2_) | copy-start | bytes 12582916
Sparse Core Ops, SparseCore 0:
  10.0 52.0 all-gather.2
  64.2 89.9 all-gather.4
  258.7 88.1 reduce-scatter.1

commit v15 on v14

--- a/solution.py
+++ b/solution.py
@@ -16,7 +16,7 @@
 
 COL_PARTS = 2
 
-VMEM_BYTES = 52 * 1024 * 1024
+VMEM_BYTES = 20 * 1024 * 1024
 
 low = jnp.bfloat16
 
@@ -158,7 +158,6 @@
         if j:
             away = [after(value, arrived[j - 1][-1]) for value in away]
         arrived.append([move_b(value, top) for value in away])
-    last = arrived[0][-1]
     sums = []
     for j in range(COL_PARTS):
         held = {t ^ 1: paired(t, j) for t in second_group}

time: 354 us -> 355 us (level)
  waiting for transfers between devices: 234 us -> 227 us
  local copies, waits for them, and re-layouts: 10.1 us -> 15.7 us
  matrix products: 41.6 us -> 47.1 us
  Pallas kernels: 13.7 us -> 10.1 us
    ppermute x14, waiting for transfers between devices: 87.7 us -> 81.9 us  [permute(): return lax.ppermute(value, ('basis', 'dp'), pairs)]
    unnamed x31 -> x35, local copies, waits for them, and re-layouts: 8.61 us -> 14.2 us
    dot_general x9, matrix products: 28.2 us -> 33.6 us  [matmul(): lax.dot_general(a, b, (((1,), (0,)), ((), ())), preferred_element_type=jn...]
    pallas_call x1, Pallas kernels: 13.7 us -> 10.1 us  [half_rotation(): pl.pallas_call(kernel, out_shape=outs, grid_spec=pltpu.PrefetchScalarGrid...]
  transfers between devices with their start and end apart: 17 -> 17, of which waited for: 10 -> 9; matrix products, arithmetic and copies ran while one was open for 13% -> 14% of each run, Pallas kernels for 0% -> 0%
where the time goes in v15:
time: 355 us; the launch traced here: 354 us
  waiting for transfers between devices  227 us (64%)
  matrix products  47.1 us (13%)
  other arithmetic  26.7 us (8%)
  local copies, waits for them, and re-layouts  15.7 us (4%)
  between operations  14.2 us (4%)
  starting transfers between devices  13.4 us (4%)
  Pallas kernels  10.1 us (3%)
    reduce_scatter x1, waiting for transfers between devices, per_device(): lax.psum_scatter(total, 'dp', scatter_dimension=0, axis_index_groups=[pat...  83.8 us
    ppermute x14, waiting for transfers between devices, permute(): return lax.ppermute(value, ('basis', 'dp'), pairs)  81.9 us
    all_gather x2, waiting for transfers between devices, round_path(): return lax.all_gather(value, 'dp', axis_index_groups=[path], tiled=True)  61.7 us
    dot_general x9, matrix products, matmul(): lax.dot_general(a, b, (((1,), (0,)), ((), ())), preferred_element_type=jn...  33.6 us
    unnamed x35, local copies, waits for them, and re-layouts  14.2 us
    dot_general x1, matrix products, matmul_nt(): lax.dot_general(a, b, (((1,), (1,)), ((), ())), preferred_element_type=jn...  13.5 us
    ppermute x14, starting transfers between devices, permute(): return lax.ppermute(value, ('basis', 'dp'), pairs)  13.2 us
    pallas_call x1, Pallas kernels, half_rotation(): pl.pallas_call(kernel, out_shape=outs, grid_spec=pltpu.PrefetchScalarGrid...  10.1 us
  transfers between devices with their start and end apart: 17, of which 9 were waited for; matrix products, arithmetic and copies ran while one was open for 14% of the time, Pallas kernels for 0%

profile of v15, /device:TPU:0, one launch (start us, length us, event | category | flops | bytes accessed | tf_op | source)
XLA Modules:
  0.0 354.4 jit_solution(14321501453595299641)
XLA Ops:
  7.2 1.8 convert_bitcast_fusion
  9.1 1.9 collective-permute-start
  10.9 6.0 %convert_element_type.78.refs_2_ = bf16[2048,1024]{1,0:T(8,128)(2,1)} convert(f32[2048,1024]{1,0:T(8,128)} %param.7) | non-fusion elementwise | flops 2097152 | bytes 12582912 | tf_op jit(solution)/shard_map/convert_element_type | solution.py:122
  17.0 0.7 collective-permute-start.1
  17.8 44.3 %all-gather.3.cloned.1.call-done = bf16[2048,512]{0,1:T(8,128)(2,1)} async-done(((bf16[256,512]{0,1:T(8,128)(2,1)}), bf16[2048,512]{0,1:T(8,128)(2,1)}) %all-gather.3.cloned.1.call-update) | async-done | bytes 2097168 | tf_op jit(solution)/shard_map/all_gather | solution.py:119
  62.2 1.0 slice_dynamic-update-slice_fusion.6
  63.1 1.0 slice_dynamic-update-slice_fusion.5
  64.1 1.0 slice_dynamic-update-slice_fusion.4
  65.1 1.0 slice_dynamic-update-slice_fusion.3
  66.1 1.0 slice_dynamic-update-slice_fusion.2
  67.1 1.0 slice_dynamic-update-slice_fusion.1
  68.1 1.1 slice_dynamic-update-slice_fusion
  69.2 4.5 %collective-permute-start.2 = (bf16[2048,512]{0,1:T(8,128)(2,1)S(1)}, bf16[2048,512]{0,1:T(8,128)(2,1)S(1)}, u32[]{:S(2)}, u32[]{:S(2)}) collective-permute-start(bf16[2048,512]{0,1:T(8,128)(2,1)S(1)} %slice_dynamic-update-slice_fusion), channel_id=1, source_target_pairs={{0,16},{1,17},{2,18},{3,19},{4,20},{5,21},{6,22},{7,23},{8,24},{9,... | collective-permute-start | bytes 6291464 | tf_op jit(solution)/shard_map/ppermute | solution.py:83
  73.7 46.1 %collective-permute-done.2 = bf16[2048,512]{0,1:T(8,128)(2,1)S(1)} collective-permute-done((bf16[2048,512]{0,1:T(8,128)(2,1)S(1)}, bf16[2048,512]{0,1:T(8,128)(2,1)S(1)}, u32[]{:S(2)}, u32[]{:S(2)}) %collective-permute-start.2) | collective-permute-done | bytes 2097184 | tf_op jit(solution)/shard_map/ppermute | solution.py:83
  119.8 2.7 pad_maximum_fusion.1
  122.5 0.6 collective-permute-start.3
  123.1 7.1 %collective-permute-done.3 = bf16[2048,1024]{0,1:T(8,128)(2,1)} collective-permute-done((bf16[2048,1024]{0,1:T(8,128)(2,1)}, bf16[2048,1024]{0,1:T(8,128)(2,1)}, u32[]{:S(2)}, u32[]{:S(2)}) %collective-permute-start.3) | collective-permute-done | bytes 4194336 | tf_op jit(solution)/shard_map/ppermute | solution.py:83
  130.2 6.6 %pad_maximum_fusion = bf16[2048,2048]{0,1:T(8,128)(2,1)} fusion(bf16[2048,1024]{0,1:T(8,128)(2,1)} %collective-permute-done.3, bf16[2048,512]{0,1:T(8,128)(2,1)} %copy-done.5, bf16[2048,512]{0,1:T(8,128)(2,1)S(1)} %slice_dynamic-update-slice_fusion), kind=kLoop, calls=%fused_computation | loop fusion | flops 25165824 | bytes 16777216 | tf_op jit(solution)/shard_map/concatenate | solution.py:135
  136.8 17.4 %all-gather.5.cloned.1.call-done = bf16[4096,1024]{1,0:T(8,128)(2,1)} async-done(((bf16[512,1024]{1,0:T(8,128)(2,1)}), bf16[4096,1024]{1,0:T(8,128)(2,1)}) %all-gather.5.cloned.1.call-update) | async-done | bytes 8388624 | tf_op jit(solution)/shard_map/all_gather | solution.py:119
  154.2 2.2 copy-done.2
  156.4 3.4 copy-done.4
  159.8 10.1 %half_rotation.1 = (bf16[2048,512]{1,0:T(8,128)(2,1)S(1)}, bf16[2048,512]{1,0:T(8,128)(2,1)S(1)}) custom-call(s32[4]{0:T(128)S(1)} %pad_add_fusion.places_ref, bf16[8,512,1024]{2,1,0:T(8,128)(2,1)S(1)} %bitcast.53, bf16[8,512,1024]{2,1,0:T(8,128)(2,1)S(1)} %bitcast.54, bf16[2048,1024]{1,0:T(8,128)(2,1)S(1)} %copy-done.2), custom_call_target="tpu_custom_call" | custom-call | flops 8589934592 | bytes 16777216 | tf_op jit(solution)/shard_map/half_rotation/pallas_call | solution.py:52
  169.9 3.6 %fusion.34 = bf16[512,512]{1,0:T(8,128)(2,1)S(1)} fusion(bf16[2048,512]{1,0:T(8,128)(2,1)S(1)} %get-tuple-element.38, bf16[2048,2048]{0,1:T(8,128)(2,1)} %pad_maximum_fusion, s32[]{:T(128)S(6)} %select_n.83), kind=kOutput, calls=%fused_computation.35 | convolution fusion | flops 1074003968 | bytes 4718596 | tf_op jit(solution)/shard_map/dot_general | solution.py:25
  173.6 3.5 fusion.28
  177.3 2.9 fusion.37
  180.7 1.5 collective-permute-start.7
  182.2 2.9 fusion.31
  185.0 1.3 add_convert_fusion
  186.4 2.9 fusion.22
  189.3 3.0 fusion.16
  192.4 2.9 fusion.25
  195.8 0.6 collective-permute-start.9
  196.5 1.3 fusion.19
  198.3 1.3 copy-done.6
  199.6 0.6 copy-done.7
  200.2 0.9 divide_convert_fusion.1
  201.1 1.5 collective-permute-start.10
  202.6 8.0 %collective-permute-done.9 = bf16[512,512]{1,0:T(8,128)(2,1)S(1)} collective-permute-done((bf16[512,512]{1,0:T(8,128)(2,1)S(1)}, bf16[512,512]{1,0:T(8,128)(2,1)S(1)}, u32[]{:S(2)}, u32[]{:S(2)}) %collective-permute-start.9) | collective-permute-done | bytes 524320 | tf_op jit(solution)/shard_map/ppermute | solution.py:83
  210.6 1.8 divide_convert_fusion
  212.4 0.6 collective-permute-start.12
  213.1 8.7 %collective-permute-done.10 = bf16[512,512]{1,0:T(8,128)(2,1)S(1)} collective-permute-done((bf16[512,512]{1,0:T(8,128)(2,1)S(1)}, bf16[512,512]{1,0:T(8,128)(2,1)S(1)}, u32[]{:S(2)}, u32[]{:S(2)}) %collective-permute-start.10) | collective-permute-done | bytes 524320 | tf_op jit(solution)/shard_map/ppermute | solution.py:83
  222.1 10.1 %collective-permute-done.12 = bf16[512,512]{1,0:T(8,128)(2,1)S(1)} collective-permute-done((bf16[512,512]{1,0:T(8,128)(2,1)S(1)}, bf16[512,512]{1,0:T(8,128)(2,1)S(1)}, u32[]{:S(2)}, u32[]{:S(2)}) %collective-permute-start.12) | collective-permute-done | bytes 524320 | tf_op jit(solution)/shard_map/ppermute | solution.py:83
  233.3 1.8 collective-permute-done.13
  235.6 0.6 pad_maximum_fusion.2
  236.3 10.7 %convolution_convert_fusion.1 = bf16[2048,1024]{1,0:T(8,128)(2,1)} fusion(bf16[2048,2048]{1,0:T(8,128)(2,1)S(1)} %bitcast_dynamic-update-slice_fusion, bf16[2048,1024]{1,0:T(8,128)(2,1)S(1)} %pad_maximum_fusion.2), kind=kOutput, calls=%fused_computation.4 | convolution fusion | flops 8592031744 | bytes 16777216 | tf_op jit(solution)/shard_map/dot_general | solution.py:25
  246.9 13.5 %convolution_convert_fusion = bf16[2048,2048]{1,0:T(8,128)(2,1)} fusion(bf16[2048,1024]{1,0:T(8,128)(2,1)} %convolution_convert_fusion.1, bf16[2048,1024]{1,0:T(8,128)(2,1)S(1)} %copy-done.3), kind=kOutput, calls=%fused_computation.1 | convolution fusion | flops 8594128896 | bytes 16777216 | tf_op jit(solution)/shard_map/dot_general | solution.py:29
  260.4 3.7 %pad_maximum_fusion.3 = (f32[512,1024]{1,0:T(8,128)}, f32[512,1024]{1,0:T(8,128)}) fusion(f32[512,512]{1,0:T(8,128)} %get-tuple-element.49, f32[512,512]{1,0:T(8,128)S(1)} %get-tuple-element.51, f32[512,512]{1,0:T(8,128)S(1)} %get-tuple-element.48, f32[512,512]{1,0:T(8,128)S(1)} %get-tuple-element.52), kind=kLoop, calls=%fused_computation.5 | loop fusion | flops 1048576 | bytes 8388608 | tf_op jit(solution)/shard_map/concatenate | solution.py:214
  264.1 83.8 %reduce-scatter.2.cloned.1.call-done = bf16[256,2048]{1,0:T(8,128)(2,1)} async-done(((bf16[2048,2048]{1,0:T(8,128)(2,1)}), bf16[256,2048]{1,0:T(8,128)(2,1)}) %reduce-scatter.2.cloned.1.call-update) | async-done | bytes 1048592 | tf_op jit(solution)/shard_map/reduce_scatter | solution.py:212
  (59 shorter events, 3.9 us)
Async XLA Ops:
  7.2 54.9 %all-gather.3.cloned.1.call-start = ((), (), s32[]{:S(2)}) async-start(), calls=%async_computation.1 | async-start | bytes 2359296 | tf_op jit(solution)/shard_map/all_gather | solution.py:119
  9.0 145.2 %all-gather.5.cloned.1.call-start = ((), (), s32[]{:S(2)}) async-start(), calls=%async_computation.2 | async-start | bytes 9437184 | tf_op jit(solution)/shard_map/all_gather | solution.py:119
  9.1 8.0 %collective-permute-start = (bf16[512,1024]{1,0:T(8,128)(2,1)}, bf16[512,1024]{1,0:T(8,128)(2,1)S(1)}, u32[]{:S(2)}, u32[]{:S(2)}) collective-permute-start(bf16[512,1024]{1,0:T(8,128)(2,1)} %param.5), channel_id=1, source_target_pairs={{0,0},{1,1},{2,2},{3,3},{4,4},{5,5},{6,6},{7,7},{8,14},{9,15},{10,... | collective-permute-start | bytes 3145736 | tf_op jit(solution)/shard_map/ppermute | solution.py:83
  17.0 0.7 collective-permute-start.1
  17.8 44.3 %copy-start.8 = (bf16[512,1024]{1,0:T(8,128)(2,1)}, bf16[512,1024]{1,0:T(8,128)(2,1)S(1)}, u32[]{:S(2)}) copy-start(bf16[512,1024]{1,0:T(8,128)(2,1)S(1)} %collective-permute-done.1) | copy-start | bytes 3145732
  62.1 285.8 %reduce-scatter.2.cloned.1.call-start = ((), (), s32[]{:S(2)}) async-start(), calls=%async_computation.3 | async-start | bytes 9437184 | tf_op jit(solution)/shard_map/reduce_scatter | solution.py:212
  69.2 50.6 %collective-permute-start.2 = (bf16[2048,512]{0,1:T(8,128)(2,1)S(1)}, bf16[2048,512]{0,1:T(8,128)(2,1)S(1)}, u32[]{:S(2)}, u32[]{:S(2)}) collective-permute-start(bf16[2048,512]{0,1:T(8,128)(2,1)S(1)} %slice_dynamic-update-slice_fusion), channel_id=1, source_target_pairs={{0,16},{1,17},{2,18},{3,19},{4,20},{5,21},{6,22},{7,23},{8,24},{9,... | collective-permute-start | bytes 6291464 | tf_op jit(solution)/shard_map/ppermute | solution.py:83
  119.8 2.7 copy-start.5
  122.5 7.7 %collective-permute-start.3 = (bf16[2048,1024]{0,1:T(8,128)(2,1)}, bf16[2048,1024]{0,1:T(8,128)(2,1)}, u32[]{:S(2)}, u32[]{:S(2)}) collective-permute-start(bf16[2048,1024]{0,1:T(8,128)(2,1)} %pad_maximum_fusion.1), channel_id=1, source_target_pairs={{0,8},{1,9},{2,10},{3,11},{4,12},{5,13},{6,14},{7,15},{8,0},{9,1},... | collective-permute-start | bytes 12582920 | tf_op jit(solution)/shard_map/ppermute | solution.py:83
  154.2 2.2 copy-start.2
  156.4 3.4 copy-start.4
  169.8 3.6 %copy-start = (bf16[2048,512]{1,0:T(8,128)(2,1)}, bf16[2048,512]{1,0:T(8,128)(2,1)S(1)}, u32[]{:S(2)}) copy-start(bf16[2048,512]{1,0:T(8,128)(2,1)S(1)} %get-tuple-element.38) | copy-start | bytes 6291460
  173.5 3.6 %collective-permute-start.4 = (bf16[512,512]{1,0:T(8,128)(2,1)S(1)}, bf16[512,512]{1,0:T(8,128)(2,1)S(1)}, u32[]{:S(2)}, u32[]{:S(2)}) collective-permute-start(bf16[512,512]{1,0:T(8,128)(2,1)S(1)} %fusion.34), channel_id=1, source_target_pairs={{0,8},{1,9},{2,10},{3,11},{4,12},{5,13},{6,14},{7,15},{8,0},{9,1},... | collective-permute-start | bytes 1572872 | tf_op jit(solution)/shard_map/ppermute | solution.py:83
  180.1 4.9 %collective-permute-start.5 = (bf16[512,512]{1,0:T(8,128)(2,1)S(1)}, bf16[512,512]{1,0:T(8,128)(2,1)}, u32[]{:S(2)}, u32[]{:S(2)}) collective-permute-start(bf16[512,512]{1,0:T(8,128)(2,1)S(1)} %fusion.37), channel_id=1, source_target_pairs={{0,8},{1,9},{2,10},{3,11},{4,12},{5,13},{6,14},{7,15},{8,0},{9,1},... | collective-permute-start | bytes 1572872 | tf_op jit(solution)/shard_map/ppermute | solution.py:83
  180.7 5.7 %copy-start.1 = (bf16[2048,512]{1,0:T(8,128)(2,1)S(1)}, bf16[2048,512]{1,0:T(8,128)(2,1)}, u32[]{:S(2)}) copy-start(bf16[2048,512]{1,0:T(8,128)(2,1)} %copy-done) | copy-start | bytes 6291460
  180.7 15.2 %collective-permute-start.7 = (bf16[512,512]{1,0:T(8,128)(2,1)S(1)}, bf16[512,512]{1,0:T(8,128)(2,1)S(1)}, u32[]{:S(2)}, u32[]{:S(2)}) collective-permute-start(bf16[512,512]{1,0:T(8,128)(2,1)S(1)} %add_convert_fusion.1), channel_id=1, source_target_pairs={{0,16},{1,17},{2,18},{3,19},{4,20},{5,21},{6,22},{7,23},{8,24},{9,... | collective-permute-start | bytes 1572872 | tf_op jit(solution)/shard_map/ppermute | solution.py:83
  185.0 11.4 %slice-start = ((s8[8388608]{0:T(1024)(128)(4,1)}), s8[4194304]{0:T(1024)(128)(4,1)S(1)}, s32[]{:S(2)}) async-start(s8[8388608]{0:T(1024)(128)(4,1)} %bitcast.55), calls=%async_computation.4 | async-start | bytes 8388608
  189.3 7.1 %slice-start.1 = ((s8[8388608]{0:T(1024)(128)(4,1)}), s8[4194304]{0:T(1024)(128)(4,1)S(1)}, s32[]{:S(2)}) async-start(s8[8388608]{0:T(1024)(128)(4,1)} %bitcast.55), calls=%async_computation.5 | async-start | bytes 8388608
  195.3 15.4 %collective-permute-start.8 = (bf16[512,512]{1,0:T(8,128)(2,1)S(1)}, bf16[512,512]{1,0:T(8,128)(2,1)S(1)}, u32[]{:S(2)}, u32[]{:S(2)}) collective-permute-start(bf16[512,512]{1,0:T(8,128)(2,1)S(1)} %fusion.25), channel_id=1, source_target_pairs={{0,8},{1,9},{2,10},{3,11},{4,12},{5,13},{6,14},{7,15},{8,0},{9,1},... | collective-permute-start | bytes 1572872 | tf_op jit(solution)/shard_map/ppermute | solution.py:83
  195.3 2.9 collective-permute-start.6
  195.8 14.8 %collective-permute-start.9 = (bf16[512,512]{1,0:T(8,128)(2,1)S(1)}, bf16[512,512]{1,0:T(8,128)(2,1)S(1)}, u32[]{:S(2)}, u32[]{:S(2)}) collective-permute-start(bf16[512,512]{1,0:T(8,128)(2,1)S(1)} %add_convert_fusion), channel_id=1, source_target_pairs={{0,16},{1,17},{2,18},{3,19},{4,20},{5,21},{6,22},{7,23},{8,24},{9,... | collective-permute-start | bytes 1572872 | tf_op jit(solution)/shard_map/ppermute | solution.py:83
  198.0 1.6 copy-start.6
  198.0 2.2 copy-start.7
  201.1 20.7 %collective-permute-start.10 = (bf16[512,512]{1,0:T(8,128)(2,1)S(1)}, bf16[512,512]{1,0:T(8,128)(2,1)S(1)}, u32[]{:S(2)}, u32[]{:S(2)}) collective-permute-start(bf16[512,512]{1,0:T(8,128)(2,1)S(1)} %get-tuple-element.50), channel_id=1, source_target_pairs={{0,16},{1,17},{2,18},{3,19},{4,20},{5,21},{6,22},{7,23},{8,24},{9,... | collective-permute-start | bytes 1572872 | tf_op jit(solution)/shard_map/ppermute | solution.py:83
  212.4 19.8 %collective-permute-start.12 = (bf16[512,512]{1,0:T(8,128)(2,1)S(1)}, bf16[512,512]{1,0:T(8,128)(2,1)S(1)}, u32[]{:S(2)}, u32[]{:S(2)}) collective-permute-start(bf16[512,512]{1,0:T(8,128)(2,1)S(1)} %get-tuple-element.47), channel_id=1, source_target_pairs={{0,16},{1,17},{2,18},{3,19},{4,20},{5,21},{6,22},{7,23},{8,24},{9,... | collective-permute-start | bytes 1572872 | tf_op jit(solution)/shard_map/ppermute | solution.py:83
  222.0 10.8 %collective-permute-start.11 = (bf16[2,512,512]{2,1,0:T(8,128)(2,1)S(1)}, bf16[2,512,512]{2,1,0:T(8,128)(2,1)S(1)}, u32[]{:S(2)}, u32[]{:S(2)}) collective-permute-start(bf16[2,512,512]{2,1,0:T(8,128)(2,1)S(1)} %pad_maximum_fusion.7), channel_id=1, source_target_pairs={{0,8},{1,9},{2,10},{3,11},{4,12},{5,13},{6,14},{7,15},{8,0},{9,1},... | collective-permute-start | bytes 3145736 | tf_op jit(solution)/shard_map/ppermute | solution.py:83
  232.4 2.7 collective-permute-start.13
  236.3 10.7 %copy-start.3 = (bf16[2048,1024]{1,0:T(8,128)(2,1)S(1)}, bf16[2048,1024]{1,0:T(8,128)(2,1)}, u32[]{:S(2)}) copy-start(bf16[2048,1024]{1,0:T(8,128)(2,1)} %convert_element_type.78.refs_2_) | copy-start | bytes 12582916
Sparse Core Ops, SparseCore 0:
  10.0 52.0 all-gather.2
  64.2 89.9 all-gather.4
  260.5 87.3 reduce-scatter.1
